TPU v7x, 128 devices: a whole 4x4x4 slice. The times are simulated.
128 devices in a mesh: grp: 2 (over x_hi), tp: 8 (over y, core), sq: 8 (over x_lo, z).
Axes of the slice: x: 4 (x_hi: 2, x_lo: 2; x = x_hi * 2 + x_lo), y: 4, z: 4, core: 2. Of those that a mesh axis runs over, the one named last changes fastest.
Arguments:
- neighbour_inputs: bfloat16 [128, 128, 896], P(('grp', 'tp', 'sq')), may hold values from -6 to 6
- encoder_gain: float32 [896], replicated, may hold values from 0.5 to 1.5
- encoder_project: bfloat16 [896, 2688], replicated, may hold values from -0.1875 to 0.1875
- encoder_mix: bfloat16 [896, 896], replicated, may hold values from -0.1875 to 0.1875
- decoder_queries: bfloat16 [64, 64, 8192], P(('grp', 'sq'), None, 'tp'), may hold values from -6 to 6
- cross_pairs: bfloat16 [896, 2, 8192], P(None, None, 'tp'), may hold values from -0.1875 to 0.1875
- span_neighbours: int32 [64, 2], P(('grp', 'sq')), may hold values from 0 to 127, as said below
- grad_output: bfloat16 [64, 64, 8192], P(('grp', 'sq'), None, 'tp'), may hold values from -6 to 6
Outputs:
- cross_output: bfloat16 [64, 64, 8192], P(('grp', 'sq'), None, 'tp')
- grad_queries: bfloat16 [64, 64, 8192], P(('grp', 'sq'), None, 'tp')
- grad_cross_pairs: float32 [896, 2, 8192], P(None, None, 'tp')
- grad_encoder_project: float32 [896, 2688], P(('grp', 'tp', 'sq'))
- grad_encoder_mix: float32 [896, 896], P(('grp', 'tp', 'sq'))
- grad_neighbour_inputs: bfloat16 [128, 128, 896], P(('grp', 'tp', 'sq'))
Inputs may be any that keep to these rules, and one draw needn't show every extreme that they name: `span_neighbours`: for every k, the spans k * 4 to (k + 1) * 4 - 1 together name each of the neighbours 2 * k * 4 to 2 * (k + 1) * 4 - 1 exactly once.
All inputs are finite; a program needn't handle non-finite values.
Results may differ from a plain program's by a relative error of at most 0.02.
Values may be sent and summed in bfloat16 or wider, within the bound.
No kernel may reach another device: no remote copies, remote signals or barrier semaphores. Data moves between devices by JAX's collectives and lax.ppermute only.
A program may use at most 128 MiB of HBM per device.

v0:
```python
import math

import jax
import jax.numpy as jnp
from jax import lax
from jax.sharding import PartitionSpec as P

HS = 128
EHS = 128


full_precision = lax.Precision.HIGHEST
epsilon = 1e-06


def in_order(pieces, dim):
    dims = list(pieces.shape[1:])
    dims[dim] *= pieces.shape[0]
    return jnp.moveaxis(pieces, 0, dim).reshape(dims)


def from_everyone(x, axis):
    length = lax.axis_size(axis)
    return lax.all_to_all(jnp.broadcast_to(x[None], (length, *x.shape)), axis, 0, 0, tiled=True)


def collect(x, axis, dim):
    return in_order(from_everyone(x, axis), dim)


def rows_for(lines, length):
    spare = -lines.shape[0] % length
    if not spare:
        return lines
    return jnp.concatenate([lines, jnp.zeros((spare, *lines.shape[1:]), lines.dtype)])


def total_of(x, axis):
    lines = x.reshape(-1, *x.shape[1:][-1:])
    own = lax.psum_scatter(
        rows_for(lines, lax.axis_size(axis)), axis, scatter_dimension=0, tiled=True
    )
    whole = lax.all_gather(own, axis).reshape(-1, *lines.shape[1:])
    return lax.slice_in_dim(whole, 0, len(lines)).reshape(x.shape)


def in_blocks(x, dim, length):
    dims = x.shape
    pieces = x.reshape(*dims[:dim], length, dims[dim] // length, *dims[dim + 1 :])
    return jnp.moveaxis(pieces, dim, 0)


def sent_and_summed(x, axis, dim):
    length = lax.axis_size(axis)
    pieces = lax.all_to_all(in_blocks(x, dim, length), axis, 0, 0, tiled=True)
    return jnp.sum(pieces.astype(jnp.float32), axis=0)


def one_scatter(arrays, axis, dims):
    length = lax.axis_size(axis)
    pieces = [in_blocks(a, dim, length) for a, dim in zip(arrays, dims)]
    lines = jnp.concatenate([b.reshape(length, -1) for b in pieces], axis=1)
    rows = max(16, -(-lines.shape[1] // 1024) * 8)
    lines = jnp.pad(lines, ((0, 0), (0, rows * 128 - lines.shape[1]))).reshape(-1, 128)
    flat, at, gathered = (lax.psum_scatter(lines, axis, tiled=True).reshape(-1), 0, [])
    for b in pieces:
        part = b[0]
        gathered.append(flat[at : at + part.size].reshape(part.shape))
        at += part.size
    return tuple(gathered)


def rounded(value):
    return lax.optimization_barrier(value.astype(jnp.bfloat16)).astype(jnp.float32)


def encode(source_rows, gain_vector, project_weight, mix_weight):
    groups, length, enc_width = source_rows.shape
    heads_enc = enc_width // EHS
    variance = jnp.mean(source_rows * source_rows, axis=-1, keepdims=True)
    normed = rounded(source_rows * lax.rsqrt(variance + epsilon) * gain_vector)
    projected = rounded(jnp.einsum("ntc,cf->ntf", normed, project_weight, precision=full_precision))
    projected = projected.reshape(groups, length, 3, heads_enc, EHS)
    scores = jnp.einsum(
        "nqhd,nkhd->nhqk", projected[:, :, 0], projected[:, :, 1], precision=full_precision
    ) / math.sqrt(EHS)
    weights = rounded(jax.nn.softmax(scores, axis=-1))
    mixed_heads = rounded(
        jnp.einsum("nhqk,nkhd->nqhd", weights, projected[:, :, 2], precision=full_precision)
    )
    mixed_heads = mixed_heads.reshape(groups, length, enc_width)
    return source_rows + jnp.einsum(
        "ntc,cf->ntf", mixed_heads, mix_weight, precision=full_precision
    )


def cross(sources, queries, grad_out, weight_pair):
    spans, keylen, enc_width = sources.shape
    inner_width = weight_pair.shape[1] // 2
    head_many = inner_width // HS
    score_scale = 1.0 / math.sqrt(HS)
    flat_rows = sources.reshape(spans * keylen, enc_width)
    projected = jnp.dot(flat_rows, weight_pair, preferred_element_type=jnp.float32).astype(
        jnp.bfloat16
    )
    key_rows = projected[:, :inner_width].reshape(spans, keylen, head_many, HS)
    value_rows = projected[:, inner_width:].reshape(spans, keylen, head_many, HS)
    query_rows = queries.reshape(spans, -1, head_many, HS)
    scores = (
        jnp.einsum("cqhd,ckhd->chqk", query_rows, key_rows, preferred_element_type=jnp.float32)
        * score_scale
    )
    probs_full = jax.nn.softmax(scores, axis=-1)
    probs_low = probs_full.astype(jnp.bfloat16)
    attended = jnp.einsum(
        "chqk,ckhd->cqhd", probs_low, value_rows, preferred_element_type=jnp.float32
    )
    result = attended.astype(jnp.bfloat16).reshape(queries.shape)
    upstream = grad_out.reshape(query_rows.shape)
    grad_probs = jnp.einsum(
        "cqhd,ckhd->chqk", upstream, value_rows, preferred_element_type=jnp.float32
    )
    grad_values = jnp.einsum(
        "chqk,cqhd->ckhd", probs_low, upstream, preferred_element_type=jnp.float32
    )
    grad_scores = (
        probs_full * (grad_probs - jnp.sum(probs_full * grad_probs, axis=-1, keepdims=True))
    ).astype(jnp.bfloat16)
    grad_query = (
        jnp.einsum("chqk,ckhd->cqhd", grad_scores, key_rows, preferred_element_type=jnp.float32)
        * score_scale
    ).astype(jnp.bfloat16)
    grad_keys = (
        jnp.einsum("chqk,cqhd->ckhd", grad_scores, query_rows, preferred_element_type=jnp.float32)
        * score_scale
    )
    grad_pairs = jnp.concatenate(
        [
            grad_keys.reshape(spans * keylen, inner_width),
            grad_values.reshape(spans * keylen, inner_width),
        ],
        axis=1,
    ).astype(jnp.bfloat16)
    grad_weight = jnp.einsum("nc,nf->cf", flat_rows, grad_pairs, preferred_element_type=jnp.float32)
    grad_sources = jnp.einsum(
        "nf,cf->nc", grad_pairs, weight_pair, preferred_element_type=jnp.float32
    )
    return (
        result,
        grad_query.reshape(queries.shape),
        grad_sources.reshape(spans, keylen, enc_width),
        grad_weight,
    )


def shards(
    neighbour_inputs,
    encoder_gain,
    encoder_project,
    encoder_mix,
    decoder_queries,
    cross_pairs,
    span_neighbours,
    grad_output,
):
    tp_count = lax.axis_size("tp")
    sq_count = lax.axis_size("sq")
    local_many, length, enc_width = neighbour_inputs.shape
    source_rows = neighbour_inputs.astype(jnp.float32)

    def run_encoder(rows_in, project_weight, mix_weight):
        return encode(rows_in, encoder_gain, project_weight, mix_weight)

    encoded_full, pull_back = jax.vjp(
        run_encoder,
        source_rows,
        encoder_project.astype(jnp.float32),
        encoder_mix.astype(jnp.float32),
    )
    encoded = encoded_full.astype(jnp.bfloat16)
    spread = collect(encoded, "tp", 0).reshape(tp_count, local_many, length, enc_width)
    arrived = lax.all_to_all(spread, "sq", split_axis=0, concat_axis=1, tiled=True).reshape(
        sq_count * local_many, length, enc_width
    )
    span_many = decoder_queries.shape[0]
    picked = (span_neighbours % (2 * span_many)).reshape(-1)
    keyed_rows = jnp.take(arrived, picked, axis=0).reshape(span_many, 2 * length, enc_width)
    weight_pair = cross_pairs.reshape(enc_width, -1)
    result, grad_query, grad_sources, grad_weight = cross(
        keyed_rows, decoder_queries, grad_output, weight_pair
    )
    grad_pair = (
        total_of(grad_weight.astype(jnp.bfloat16), ("grp", "sq"))
        .astype(jnp.float32)
        .reshape(cross_pairs.shape)
    )
    by_slot = (
        jnp.zeros((sq_count * local_many, length, enc_width), jnp.float32)
        .at[picked]
        .add(grad_sources.reshape(2 * span_many, length, enc_width))
    )
    routed = lax.all_to_all(
        by_slot.reshape(1, sq_count, local_many, length, enc_width).astype(jnp.bfloat16),
        "sq",
        split_axis=1,
        concat_axis=0,
        tiled=True,
    )
    own_block = sent_and_summed(routed, "tp", 0)[0]
    grad_encoded = rounded(own_block.reshape(local_many, length, enc_width))
    grad_inputs, grad_project, grad_mix = pull_back(grad_encoded)
    summed_project, summed_mix = one_scatter((grad_project, grad_mix), ("grp", "tp", "sq"), (0, 0))
    return (
        result,
        grad_query,
        grad_pair,
        summed_project,
        summed_mix,
        grad_inputs.astype(jnp.bfloat16),
    )


def solution(mesh):
    placed = (
        P(("grp", "tp", "sq"), None, None),
        P(),
        P(),
        P(),
        P(("grp", "sq"), None, "tp"),
        P(None, None, "tp"),
        P(("grp", "sq"), None),
        P(("grp", "sq"), None, "tp"),
    )
    return jax.shard_map(
        shards,
        mesh=mesh,
        in_specs=placed,
        out_specs=(
            P(("grp", "sq"), None, "tp"),
            P(("grp", "sq"), None, "tp"),
            P(None, None, "tp"),
            P(("grp", "tp", "sq"), None),
            P(("grp", "tp", "sq"), None),
            P(("grp", "tp", "sq"), None, None),
        ),
        check_vma=False,
    )
```

profile of v0, /device:TPU:1, one launch (start us, length us, event | category | flops | bytes accessed | tf_op | source)
XLA Modules:
  0.0 449.9 jit_solution(9958984355121986865)
XLA Ops:
  8.0 1.2 fusion.76
  9.2 1.1 fusion.78
  11.0 3.3 fusion.13
  18.5 29.5 %all_to_all.28 = bf16[8,1,128,896]{3,2,1,0:T(8,128)(2,1)} all-to-all(bf16[8,1,128,896]{3,2,1,0:T(8,128)(2,1)S(1)} %broadcast_in_dim.59), channel_id=1, replica_groups=mesh['grp'=2,'tp'=8,'sq'=8] {'tp'}, dimensions={0} | all-to-all | bytes 3670016 | tf_op jit(solution)/shard_map/all_to_all | solution.py:24
  48.0 6.3 %all-to-all-start.1 = ((bf16[8,1,128,896]{3,2,1,0:T(8,128)(2,1)}), bf16[8,1,128,896]{3,2,1,0:T(8,128)(2,1)S(1)}, u32[]{:S(2)}, u32[]{:S(2)}) async-start(bf16[8,1,128,896]{3,2,1,0:T(8,128)(2,1)} %all_to_all.28), calls=%async_computation.1 | async-start | bytes 3670016 | tf_op jit(solution)/shard_map/all_to_all | solution.py:182
  54.6 7.1 %reshape.371 = bf16[896,2048,1]{1,0,2:T(8,128)(2,1)} reshape(bf16[896,2,1024]{2,1,0:T(2,128)(2,1)} %param.13) | data formatting | bytes 7340032 | tf_op jit(solution)/shard_map/reshape | solution.py:188
  61.8 5.1 %copy.108 = bf16[112,8,2,1024]{3,1,2,0:T(8,128)(2,1)} copy(bf16[112,8,2,1024]{3,2,1,0:T(2,128)(2,1)} %bitcast.228) | data formatting | bytes 7340032
  67.0 10.7 %all-to-all-done.1 = bf16[8,1,128,896]{3,2,1,0:T(8,128)(2,1)S(1)} async-done(((bf16[8,1,128,896]{3,2,1,0:T(8,128)(2,1)}), bf16[8,1,128,896]{3,2,1,0:T(8,128)(2,1)S(1)}, u32[]{:S(2)}, u32[]{:S(2)}) %all-to-all-start.1) | async-done | bytes 1835040 | tf_op jit(solution)/shard_map/all_to_all | solution.py:182
  77.7 1.3 copy-done.4
  78.9 2.3 gather_fusion
  81.5 1.8 copy-done.15
  83.3 4.7 %convolution_convert_fusion = bf16[1024,2048]{1,0:T(8,128)(2,1)S(1)} fusion(bf16[1024,896]{1,0:T(8,128)(2,1)S(1)} %bitcast.247, bf16[896,2048]{1,0:T(8,128)(2,1)S(1)} %bitcast.242), kind=kOutput, calls=%fused_computation.15 | convolution fusion | flops 3760193536 | bytes 9699328 | tf_op jit(solution)/shard_map/dot_general | solution.py:103
  88.0 1.2 slice_bitcast_fusion.1
  89.8 2.0 copy.110
  92.7 2.0 fusion.107
  94.7 7.9 %convert_bitcast_fusion = bf16[4,256,8,128]{3,1,2,0:T(8,128)(2,1)} fusion(f32[4,8,64]{2,1,0:T(8,128)S(1)} %get-tuple-element.10, f32[4,8,256,64]{2,3,1,0:T(8,128)} %copy-done.2, bf16[4,64,1024]{2,1,0:T(8,128)(2,1)} %param.15), kind=kOutput, calls=%fused_computation.32 | convolution fusion | flops 137890048 | bytes 4726784 | tf_op jit(solution)/shard_map/chqk,cqhd->ckhd/dot_general | solution.py:123
  102.6 4.5 copy.81
  107.1 2.0 fusion.14
  109.1 0.9 fusion.16
  110.1 0.9 copy-done.7
  111.9 2.7 copy.79
  114.5 4.2 concatenate.16
  118.7 4.2 concatenate.17
  122.8 9.7 %fusion.6 = f32[8,128,896]{2,1,0:T(8,128)} fusion(bf16[896,2048,1]{1,0,2:T(8,128)(2,1)} %reshape.371, bf16[8,128,1024]{2,1,0:T(8,128)(2,1)} %concatenate.17, bf16[8,128,1024]{2,1,0:T(8,128)(2,1)} %concatenate.16), kind=kOutput, calls=%fused_computation.10 | convolution fusion | flops 3766484992 | bytes 11534336 | tf_op jit(solution)/shard_map/nf,cf->nc/dot_general | solution.py:145
  132.5 2.1 broadcast_in_dim.65
  134.7 8.6 %scatter_fusion = f32[8,128,896]{2,1,0:T(8,128)} fusion(f32[8,128,896]{2,1,0:T(8,128)} %broadcast_in_dim.65, s32[8]{0:T(128)S(1)} %fusion.91, f32[8,128,896]{2,1,0:T(8,128)} %fusion.6), kind=kCustom, calls=%fused_computation.1 | custom fusion | flops 917504 | bytes 11010080 | tf_op jit(solution)/shard_map/scatter-add | solution.py:200
  143.3 3.5 convert_bitcast_fusion.1
  146.8 4.3 all-to-all-start.2
  151.2 3.5 copy_bitcast_fusion
  155.2 5.7 %fusion.10 = bf16[896,2048]{1,0:T(8,128)(2,1)} fusion(bf16[1024,896]{1,0:T(8,128)(2,1)S(1)} %bitcast_select_fusion, bf16[1024,1024]{1,0:T(8,128)(2,1)S(1)} %get-tuple-element.14, bf16[1024,1024]{1,0:T(8,128)(2,1)S(1)} %get-tuple-element.15), kind=kOutput, calls=%fused_computation.17 | convolution fusion | flops 3768320000 | bytes 9699328 | tf_op jit(solution)/shard_map/nc,nf->cf/dot_general | solution.py:144
  160.9 14.5 %all-to-all-done.2 = bf16[1,8,1,128,896]{4,3,2,0,1:T(8,128)(2,1)} async-done(((bf16[1,8,1,128,896]{4,3,2,0,1:T(8,128)(2,1)}), bf16[1,8,1,128,896]{4,3,2,0,1:T(8,128)(2,1)}, u32[]{:S(2)}, u32[]{:S(2)}) %all-to-all-start.2) | async-done | bytes 1835040 | tf_op jit(solution)/shard_map/all_to_all | solution.py:202
  175.4 4.7 %all-to-all-start.3 = ((bf16[8,1,1,1,128,896]{5,4,3,2,1,0:T(8,128)(2,1)}), bf16[8,1,1,1,128,896]{5,4,3,2,1,0:T(8,128)(2,1)S(1)}, u32[]{:S(2)}, u32[]{:S(2)}) async-start(bf16[8,1,1,1,128,896]{5,4,3,2,1,0:T(8,128)(2,1)} %bitcast.26), calls=%async_computation.3 | async-start | bytes 3670016 | tf_op jit(solution)/shard_map/all_to_all | solution.py:55
  180.3 23.3 %all-to-all-done.3 = bf16[8,1,1,1,128,896]{5,4,3,2,1,0:T(8,128)(2,1)S(1)} async-done(((bf16[8,1,1,1,128,896]{5,4,3,2,1,0:T(8,128)(2,1)}), bf16[8,1,1,1,128,896]{5,4,3,2,1,0:T(8,128)(2,1)S(1)}, u32[]{:S(2)}, u32[]{:S(2)}) %all-to-all-start.3) | async-done | bytes 1835040 | tf_op jit(solution)/shard_map/all_to_all | solution.py:55
  203.6 1.0 reduce_sum.78
  204.6 1.6 fusion.54
  208.5 2.2 fusion.83
  210.7 4.4 reshape_reshape.9
  215.2 5.1 %fusion.57 = f32[896,2688]{1,0:T(8,128)} fusion(bf16[1,128,2688]{1,2,0:T(8,128)(2,1)S(1)} %bitcast.232, bf16[1,128,896]{2,1,0:T(8,128)(2,1)S(1)} %copy-done.17), kind=kOutput, calls=%fused_computation.77 | convolution fusion | flops 616562688 | bytes 10551296 | tf_op jit(solution)/shard_map/transpose(jvp(ntc,cf->ntf))/dot_general | solution.py:82
  220.3 10.4 %reshape_reshape.8 = f32[128,18816]{1,0:T(8,128)} reshape(f32[896,2688]{1,0:T(8,128)} %fusion.57) | data formatting | bytes 19267584 | tf_op jit(solution)/shard_map/reshape;reshape | solution.py:62
  230.7 9.6 %select_maximum_fusion = f32[128,25600]{1,0:T(8,128)} fusion(f32[128,6272]{1,0:T(8,128)} %reshape_reshape.9, f32[128,18816]{1,0:T(8,128)} %reshape_reshape.8), kind=kLoop, calls=%fused_computation.4 | loop fusion | flops 13107200 | bytes 25952256 | tf_op jit(solution)/shard_map/concatenate | solution.py:62
  240.4 12.1 %reshape.348 = f32[25600,128]{1,0:T(8,128)} reshape(f32[128,25600]{1,0:T(8,128)} %select_maximum_fusion) | data formatting | bytes 26214400 | tf_op jit(solution)/shard_map/reshape | solution.py:64
  253.3 7.4 %fusion.44 = bf16[4,8,8,8,128]{4,3,2,1,0:T(8,128)(2,1)} fusion(bf16[4,256,8,128]{3,2,1,0:T(8,128)(2,1)} %bitcast.243, f32[4,8,64]{2,1,0:T(8,128)S(1)} %get-tuple-element.10, f32[4,8,256,64]{2,3,1,0:T(8,128)} %copy-done.2), kind=kOutput, calls=%fused_computation.52 | convolution fusion | flops 137103616 | bytes 4726784 | tf_op jit(solution)/shard_map/chqk,ckhd->cqhd/dot_general | solution.py:115
  260.7 2.1 fusion.41
  262.9 1.1 copy_bitcast_fusion.2
  264.0 4.3 fusion.53
  268.5 0.9 fusion.75
  269.4 159.3 %all-reduce.8.cloned.1.call-done = f32[25600,128]{1,0:T(8,128)} async-done(((f32[25600,128]{1,0:T(8,128)}), f32[25600,128]{1,0:T(8,128)}) %all-reduce.8.cloned.1.call-update) | async-done | bytes 13107216
  431.6 10.4 %reshape.351 = f32[896,2,1024]{2,1,0:T(2,128)} reshape(bf16[896,2048]{1,0:T(8,128)(2,1)} %all-gather.3.cloned.1.call-done) | data formatting | bytes 11010048 | tf_op jit(solution)/shard_map/convert_element_type | solution.py:194
  (96 shorter events, 14.6 us)
Async XLA Ops:
  8.0 9.8 %copy-start = (bf16[896,896]{1,0:T(8,128)(2,1)S(1)}, bf16[896,896]{1,0:T(8,128)(2,1)}, u32[]{:S(2)}) copy-start(bf16[896,896]{1,0:T(8,128)(2,1)} %param.11) | copy-start | bytes 4816900
  10.3 0.7 copy-start.16
  14.3 3.5 copy-start.5
  14.7 3.6 copy-start.11
  15.4 0.8 copy-start.9
  16.2 0.7 copy-start.23
  17.1 0.7 copy-start.21
  48.0 6.3 %copy-start.27 = (s32[4,2]{0,1:T(2,128)S(1)}, s32[4,2]{0,1:T(2,128)}, u32[]{:S(2)}) copy-start(s32[4,2]{0,1:T(2,128)} %param.14) | copy-start | bytes 100
  48.0 29.6 %all-to-all-start.1 = ((bf16[8,1,128,896]{3,2,1,0:T(8,128)(2,1)}), bf16[8,1,128,896]{3,2,1,0:T(8,128)(2,1)S(1)}, u32[]{:S(2)}, u32[]{:S(2)}) async-start(bf16[8,1,128,896]{3,2,1,0:T(8,128)(2,1)} %all_to_all.28), calls=%async_computation.1 | async-start | bytes 3670016 | tf_op jit(solution)/shard_map/all_to_all | solution.py:182
  77.7 1.3 copy-start.4
  81.3 2.0 copy-start.15
  89.8 2.0 copy-start.1
  89.8 2.0 copy-start.18
  92.7 2.0 copy-start.2
  102.6 4.5 copy-start.3
  102.6 4.5 copy-start.20
  109.1 1.9 copy-start.19
  110.1 1.0 copy-start.7
  146.8 28.5 %all-to-all-start.2 = ((bf16[1,8,1,128,896]{4,3,2,0,1:T(8,128)(2,1)}), bf16[1,8,1,128,896]{4,3,2,0,1:T(8,128)(2,1)}, u32[]{:S(2)}, u32[]{:S(2)}) async-start(bf16[1,8,1,128,896]{4,3,2,0,1:T(8,128)(2,1)} %convert_bitcast_fusion.1), calls=%async_computation.2 | async-start | bytes 3670016 | tf_op jit(solution)/shard_map/all_to_all | solution.py:202
  151.1 101.5 %reduce-scatter.4.cloned.1.call-start = ((), (), s32[]{:S(2)}) async-start(), calls=%async_computation.7 | async-start | bytes 3899392
  175.4 28.2 %all-to-all-start.3 = ((bf16[8,1,1,1,128,896]{5,4,3,2,1,0:T(8,128)(2,1)}), bf16[8,1,1,1,128,896]{5,4,3,2,1,0:T(8,128)(2,1)S(1)}, u32[]{:S(2)}, u32[]{:S(2)}) async-start(bf16[8,1,1,1,128,896]{5,4,3,2,1,0:T(8,128)(2,1)} %bitcast.26), calls=%async_computation.3 | async-start | bytes 3670016 | tf_op jit(solution)/shard_map/all_to_all | solution.py:55
  180.0 248.6 %all-reduce.8.cloned.1.call-start = ((), (), s32[]{:S(2)}) async-start(), calls=%async_computation.6 | async-start | bytes 26214400
  204.6 1.7 copy-start.12
  204.6 2.0 copy-start.10
  204.6 2.1 copy-start.24
  207.5 0.9 copy-start.13
  207.5 1.0 copy-start.22
  210.7 4.4 copy-start.17
  252.5 179.1 %all-gather.3.cloned.1.call-start = ((), (), s32[]{:S(2)}) async-start(), calls=%async_computation.5 | async-start | bytes 3899392 | tf_op jit(solution)/shard_map/all_gather | solution.py:43
  253.3 7.4 %copy-start.8 = (bf16[4,8,64,256]{3,2,1,0:T(8,128)(2,1)S(1)}, bf16[4,8,64,256]{3,2,1,0:T(8,128)(2,1)}, u32[]{:S(2)}) copy-start(bf16[4,8,64,256]{3,2,1,0:T(8,128)(2,1)} %copy-done.7) | copy-start | bytes 3145732
  260.7 2.1 copy-start.25
  264.0 4.3 copy-start.6
  264.0 4.3 copy-start.26
  264.0 4.5 copy-start.14
Sparse Core Ops, SparseCore 0:
  161.0 74.3 reduce-scatter.3
  255.6 53.9 all-gather.2
Sparse Core Ops, SparseCore 1:
  252.6 176.0 all-reduce.7
where the time goes:
time: 454 us; the launch traced here: 450 us
  waiting for transfers between devices  208 us (46%)
  local copies, waits for them, and re-layouts  89 us (20%)
  matrix products  60.4 us (13%)
  other arithmetic  30.4 us (7%)
  blocking collectives  29.5 us (6%)
  between operations  16.4 us (4%)
  starting transfers between devices  15.6 us (3%)
    unnamed x5, waiting for transfers between devices  160 us
    all_to_all x1, blocking collectives, from_everyone(): lax.all_to_all(jnp.broadcast_to(x[None], (length, *x.shape)), axis, 0, 0,...  29.5 us
    all_to_all x1, waiting for transfers between devices, sent_and_summed(): pieces = lax.all_to_all(in_blocks(x, dim, length), axis, 0, 0, tiled=True)  23.3 us
    unnamed x60, local copies, waits for them, and re-layouts  16 us
    another operation x2, local copies, waits for them, and re-layouts, one_scatter(): lines = jnp.concatenate([b.reshape(length, -1) for b in pieces], axis=1)  14.9 us
    all_to_all x1, waiting for transfers between devices, shards(): lax.all_to_all(by_slot.reshape(1, sq_count, local_many, length, enc_width...  14.5 us
    dot_general x3, matrix products, encode(): jnp.einsum('ntc,cf->ntf', normed, project_weight, precision=full_precision)  12.7 us
    reshape x1, local copies, waits for them, and re-layouts, one_scatter(): jnp.pad(lines, ((0, 0), (0, rows * 128 - lines.shape[1]))).reshape(-1, 128)  12.1 us
  transfers between devices with their start and end apart: 6, of which 4 were waited for; matrix products, arithmetic and copies ran while one was open for 20% of the time, Pallas kernels for 0%

commit v1 on v0

v1 whole, which is shorter than its diff:
```python
import functools
import math

import jax
import jax.numpy as jnp
from jax import lax
from jax.experimental import pallas as pl
from jax.experimental.pallas import tpu as pltpu
from jax.sharding import Mesh
from jax.sharding import PartitionSpec as P

HS = 128
TOK = 128
ENC = 896
epsilon = 1e-06
f32 = jnp.float32
bf16 = jnp.bfloat16

FINE = ("xh", "y", "c", "xl", "z")
TP = ("y", "c")
PLANE = ("xh", "xl", "z")
LANES = 512
PARTS = 8


def turned(axis, length, by):
    pairs = [(i, (i + by) % length) for i in range(length)]
    return lambda x: lax.ppermute(x, axis, pairs)


def across(x):
    return lax.ppermute(x, "c", [(0, 1), (1, 0)])


def flipped(x):
    pairs = [(t * 8 + s, s * 8 + t) for t in range(8) for s in range(8)]
    return lax.ppermute(x, ("y", "c", "xl", "z"), pairs)


def dot(a, b, contract):
    return lax.dot_general(a, b, ((contract[:1], contract[1:]), ((), ())), preferred_element_type=f32)


def nn(a, b):
    return dot(a, b, (1, 0))


def nt(a, b):
    return dot(a, b, (1, 1))


def tn(a, b):
    return dot(a, b, (0, 0))


def params(mib, n=0):
    more = {"dimension_semantics": ("arbitrary",) * n} if n else {}
    return pltpu.CompilerParams(vmem_limit_bytes=mib * 2**20, **more)


def cost(flops, size):
    return pl.CostEstimate(flops=flops, bytes_accessed=size, transcendentals=0)


def softmax(scores):
    e = jnp.exp(scores - jnp.max(scores, axis=-1, keepdims=True))
    return e / jnp.sum(e, axis=-1, keepdims=True)


def head(ref, h, block=0):
    start = block * ENC + h * HS
    return ref[:, start : start + HS]


def encode_kernel(x_ref, gain_ref, project_ref, mix_ref, encoded_ref, normed_ref, projected_ref, mixed_ref):
    x = x_ref[...].astype(f32)
    r = lax.rsqrt(jnp.mean(x * x, axis=-1, keepdims=True) + epsilon)
    normed_ref[...] = (x * r * gain_ref[...]).astype(bf16)
    projected_ref[...] = nn(normed_ref[...], project_ref[...]).astype(bf16)
    for h in range(ENC // HS):
        q, k, v = (head(projected_ref, h, b) for b in range(3))
        w = softmax(nt(q, k) / math.sqrt(HS)).astype(bf16)
        mixed_ref[:, h * HS : (h + 1) * HS] = nn(w, v).astype(bf16)
    encoded_ref[...] = (x + nn(mixed_ref[...], mix_ref[...])).astype(bf16)


def encode(x, gain, project, mix):
    shape = jax.ShapeDtypeStruct((TOK, ENC), bf16)
    wide = jax.ShapeDtypeStruct((TOK, 3 * ENC), bf16)
    return pl.pallas_call(
        encode_kernel,
        out_shape=(shape, shape, wide, shape),
        compiler_params=params(24),
        cost_estimate=cost(10**9, 8 * 10**6),
    )(x, gain, project, mix)


def spread_kernel(normed_ref, mixed_ref, out_ref):
    column = lax.broadcasted_iota(jnp.int32, (ENC, 1024), 1)
    row = lax.broadcasted_iota(jnp.int32, (ENC, 1024), 0)
    place = jnp.where((column % 8 < 7) & (row == column // 8 * 7 + column % 8), 1.0, 0.0).astype(bf16)
    out_ref[:, :1024] = nn(normed_ref[...], place).astype(bf16)
    out_ref[:, 1024:] = nn(mixed_ref[...], place).astype(bf16)


def spread(normed, mixed):
    return pl.pallas_call(
        spread_kernel,
        out_shape=jax.ShapeDtypeStruct((TOK, 2048), bf16),
        compiler_params=params(24),
        cost_estimate=cost(5 * 10**8, 10**6),
    )(normed, mixed)


def pairs_kernel(first_ref, second_ref, weight_ref, *rest):
    held_ref, out_ref = rest[-2:]
    held_ref[0, 0] = first_ref[...]
    held_ref[1, 0] = second_ref[...]
    out_ref[0, 0] = nn(first_ref[...], weight_ref[...]).astype(bf16)
    out_ref[1, 0] = nn(second_ref[...], weight_ref[...]).astype(bf16)


def pairs_of(step, first, second, weight, before):
    many = 4
    width = weight.shape[1] // many
    kept = [pl.BlockSpec(memory_space=pl.ANY)] * len(before)
    return pl.pallas_call(
        pairs_kernel,
        grid=(many,),
        in_specs=[
            pl.BlockSpec((TOK, ENC), lambda i: (0, 0)),
            pl.BlockSpec((TOK, ENC), lambda i: (0, 0)),
            pl.BlockSpec((ENC, width), lambda i: (0, i)),
            *kept,
        ],
        out_specs=(
            pl.BlockSpec((2, 1, TOK, ENC), lambda i: (0, step, 0, 0)),
            pl.BlockSpec((2, 1, TOK, width), lambda i: (0, step, 0, i)),
        ),
        out_shape=(
            jax.ShapeDtypeStruct((2, 4, TOK, ENC), bf16),
            jax.ShapeDtypeStruct((2, 4, TOK, weight.shape[1]), bf16),
        ),
        input_output_aliases={3: 0, 4: 1} if before else {},
        compiler_params=params(16, 1),
        cost_estimate=cost(10**9, 6 * 10**6),
    )(first, second, weight, *before)


def cross_kernel(slots_ref, q_ref, up_ref, one_ref, two_ref, out_ref, grad_ref, pairs_ref):
    span = pl.program_id(0)
    slots = (slots_ref[2 * span], slots_ref[2 * span + 1])
    inner = q_ref.shape[2]
    scale = 1.0 / math.sqrt(HS)
    for h in range(inner // HS):
        at = slice(h * HS, (h + 1) * HS)
        up = slice(inner + h * HS, inner + (h + 1) * HS)
        q = q_ref[0, :, at]
        g = up_ref[0, :, at]
        k = jnp.concatenate([one_ref[0, :, at], two_ref[0, :, at]], axis=0)
        v = jnp.concatenate([one_ref[0, :, up], two_ref[0, :, up]], axis=0)
        probs = softmax(nt(q, k) * scale)
        low = probs.astype(bf16)
        out_ref[0, :, at] = nn(low, v).astype(bf16)
        grad_probs = nt(g, v)
        grad_values = tn(low, g).astype(bf16)
        total = jnp.sum(probs * grad_probs, axis=-1, keepdims=True)
        grad_scores = (probs * (grad_probs - total)).astype(bf16)
        grad_ref[0, :, at] = (nn(grad_scores, k) * scale).astype(bf16)
        grad_keys = (tn(grad_scores, q) * scale).astype(bf16)
        for n in range(2):
            pairs_ref[slots[n], :, at] = grad_keys[n * TOK : (n + 1) * TOK]
            pairs_ref[slots[n], :, up] = grad_values[n * TOK : (n + 1) * TOK]


def cross(slots, queries, upstream, pairs):
    spans, length, inner = queries.shape
    whole = pl.BlockSpec((1, length, inner), lambda i, s: (i, 0, 0))
    return pl.pallas_call(
        cross_kernel,
        grid_spec=pltpu.PrefetchScalarGridSpec(
            num_scalar_prefetch=1,
            grid=(spans,),
            in_specs=[
                whole,
                whole,
                pl.BlockSpec((1, TOK, 2 * inner), lambda i, s: (s[2 * i], 0, 0)),
                pl.BlockSpec((1, TOK, 2 * inner), lambda i, s: (s[2 * i + 1], 0, 0)),
            ],
            out_specs=(
                whole,
                whole,
                pl.BlockSpec((2 * spans, TOK, 2 * inner), lambda i, s: (0, 0, 0)),
            ),
        ),
        out_shape=(
            jax.ShapeDtypeStruct(queries.shape, bf16),
            jax.ShapeDtypeStruct(queries.shape, bf16),
            jax.ShapeDtypeStruct((2 * spans, TOK, 2 * inner), bf16),
        ),
        compiler_params=params(32, 1),
        cost_estimate=cost(3 * 10**9, 12 * 10**6),
    )(slots, queries, upstream, pairs, pairs)


def columns_of(at):
    return at // LANES, slice(at % LANES, at % LANES + HS)


def backward_kernel(grad_ref, projected_ref, mix_ref, out_ref):
    grad = grad_ref[...]
    grad_mixed = nt(grad, mix_ref[...]).astype(bf16)
    heads = ENC // HS
    for j in range(PARTS * LANES // HS):
        part, lanes = columns_of(j * HS)
        if j < 3 * heads:
            continue
        near = j - 24
        if 0 <= near < heads:
            out_ref[part, :, lanes] = grad[:, near * HS : (near + 1) * HS]
        else:
            out_ref[part, :, lanes] = jnp.zeros((TOK, HS), bf16)
    for h in range(heads):
        q, k, v = (head(projected_ref, h, b) for b in range(3))
        g = grad_mixed[:, h * HS : (h + 1) * HS]
        probs = softmax(nt(q, k) / math.sqrt(HS))
        grad_probs = nt(g, v).astype(bf16).astype(f32)
        total = jnp.sum(probs * grad_probs, axis=-1, keepdims=True)
        grad_scores = (probs * (grad_probs - total) / math.sqrt(HS)).astype(bf16)
        for b, value in enumerate(
            (nn(grad_scores, k), tn(grad_scores, q), tn(probs.astype(bf16), g))
        ):
            part, lanes = columns_of(b * ENC + h * HS)
            out_ref[part, :, lanes] = value.astype(bf16)


def backward(grad, projected, mix):
    return pl.pallas_call(
        backward_kernel,
        out_shape=jax.ShapeDtypeStruct((PARTS, TOK, LANES), bf16),
        compiler_params=params(24),
        cost_estimate=cost(6 * 10**8, 4 * 10**6),
    )(grad, projected, mix)


def inputs_kernel(x_ref, gain_ref, project_ref, parts_ref, grad_ref, out_ref):
    many = 3 * ENC // LANES
    total = nt(parts_ref[0], project_ref[:, :LANES])
    for j in range(1, many):
        total += nt(parts_ref[j], project_ref[:, j * LANES : (j + 1) * LANES])
    rest = 3 * ENC - many * LANES
    total += nt(parts_ref[many][:, :rest], project_ref[:, many * LANES :])
    u = total.astype(bf16).astype(f32) * gain_ref[...]
    x = x_ref[...].astype(f32)
    r = lax.rsqrt(jnp.mean(x * x, axis=-1, keepdims=True) + epsilon)
    slope = jnp.mean(x * u, axis=-1, keepdims=True) * (r * r * r)
    out_ref[...] = (r * u - x * slope + grad_ref[...].astype(f32)).astype(bf16)


def inputs_grad(x, gain, project, parts, grad):
    return pl.pallas_call(
        inputs_kernel,
        out_shape=jax.ShapeDtypeStruct((TOK, ENC), bf16),
        compiler_params=params(24),
        cost_estimate=cost(6 * 10**8, 6 * 10**6),
    )(x, gain, project, parts, grad)


def shards(
    neighbour_inputs,
    encoder_gain,
    encoder_project,
    encoder_mix,
    decoder_queries,
    cross_pairs,
    span_neighbours,
    grad_output,
):
    gain = encoder_gain.reshape(1, ENC)
    y, core = lax.axis_index("y"), lax.axis_index("c")
    inner = cross_pairs.shape[2]
    x = flipped(neighbour_inputs[0])
    weight = lax.optimization_barrier(cross_pairs.reshape(ENC, 2 * inner))
    encoded, normed, projected, mixed = encode(x, gain, encoder_project, encoder_mix)

    before = ()
    for step in range(4):
        first = encoded if step == 0 else turned("y", 4, -step)(encoded)
        before = pairs_of(step, first, across(first), weight, before)
    sources, pairs = before
    operands = lax.all_gather(spread(normed, mixed), TP, tiled=True)

    named = span_neighbours.reshape(-1) % 8
    slots = (named % 2 != core) * 4 + (named // 2 - y) % 4
    result, grad_queries, grad_pairs = cross(
        slots.astype(jnp.int32), decoder_queries, grad_output, pairs.reshape(8, TOK, 2 * inner)
    )

    far = nt(grad_pairs[4:].reshape(4 * TOK, 2 * inner), weight).astype(bf16)
    brought = across(far)
    near = nt(grad_pairs[:4].reshape(4 * TOK, 2 * inner), weight)
    grad_weight = tn(sources.reshape(8 * TOK, ENC), grad_pairs.reshape(8 * TOK, 2 * inner)).astype(bf16)
    summed = (near + brought.astype(f32)).reshape(4, TOK, ENC)
    total = summed[0]
    for step in range(1, 4):
        total += turned("y", 4, step)(summed[step].astype(bf16)).astype(f32)
    grad_encoded = total.astype(bf16)

    grad_cross = lax.psum(grad_weight, PLANE)
    grad_cross = grad_cross.astype(f32).reshape(cross_pairs.shape)

    parts = backward(grad_encoded, projected, encoder_mix)
    all_parts = lax.all_to_all(parts, TP, 0, 0, tiled=True).reshape(8 * TOK, LANES)
    mine = jnp.where(y * 2 + core < 6, operands[:, :1024], operands[:, 1024:])
    encoder_grad = tn(mine, all_parts).astype(bf16).reshape(128, 8, LANES)
    arrived = lax.all_to_all(encoder_grad, FINE, 0, 0, tiled=True).astype(f32)
    arrived = arrived.reshape(2, 8, 8, 8, LANES).sum(axis=(0, 2))
    rows = jnp.swapaxes(arrived, 0, 1).reshape(8, 8 * LANES)[:7]
    grad_inputs = flipped(inputs_grad(x, gain, encoder_project, parts, grad_encoded))
    return (
        result,
        grad_queries,
        grad_cross,
        rows[:, : 3 * ENC],
        rows[:, 6 * LANES : 6 * LANES + ENC],
        grad_inputs[None],
    )


def solution(mesh):
    fine = Mesh(mesh.devices.reshape(2, 4, 2, 2, 4), FINE)
    heads = P(PLANE, None, TP)
    placed = (
        P(FINE, None, None),
        P(),
        P(),
        P(),
        heads,
        P(None, None, TP),
        P(PLANE, None),
        heads,
    )
    return jax.shard_map(
        shards,
        mesh=fine,
        in_specs=placed,
        out_specs=(
            heads,
            heads,
            P(None, None, TP),
            P(FINE, None),
            P(FINE, None),
            P(FINE, None, None),
        ),
        check_vma=False,
    )
```

time: 454 us -> 226 us (0.50)
  waiting for transfers between devices: 208 us -> 82 us
  local copies, waits for them, and re-layouts: 89 us -> 19.9 us
  matrix products: 60.4 us -> 18 us
  Pallas kernels: 0 us -> 38.4 us
  blocking collectives: 29.5 us -> 0 us
  starting transfers between devices: 15.6 us -> 43.6 us
  other arithmetic: 30.4 us -> 7.87 us
    unnamed x5 -> x2, waiting for transfers between devices: 160 us -> 0.03 us
    dot_general x21 -> x4, matrix products: 60.4 us -> 18 us  [dot(): lax.dot_general(a, b, ((contract[:1], contract[1:]), ((), ())), preferred...]
    pallas_call x0 -> x9, Pallas kernels: none -> 38.4 us  [the longest x1 16 us: cross(): pl.pallas_call(cross_kernel, grid_spec=pltpu.PrefetchScalarGridSpec(num_s...]
    ppermute x0 -> x13, waiting for transfers between devices: none -> 33.7 us  [the longest x2 17.2 us: flipped(): return lax.ppermute(x, ('y', 'c', 'xl', 'z'), pairs)]
    all_to_all x3 -> x2, waiting for transfers between devices: 48.5 us -> 15.1 us  [the longest x1 15.1 us: shards(): lax.all_to_all(parts, TP, 0, 0, tiled=True).reshape(8 * TOK, LANES)]
    psum x0 -> x1, waiting for transfers between devices: none -> 33.2 us  [shards(): grad_cross = lax.psum(grad_weight, PLANE)]
    ppermute x0 -> x13, starting transfers between devices: none -> 30.7 us  [the longest x6 15.7 us: turned(): return lambda x: lax.ppermute(x, axis, pairs)]
    all_to_all x1 -> x0, blocking collectives: 29.5 us -> none  [from_everyone(): lax.all_to_all(jnp.broadcast_to(x[None], (length, *x.shape)), axis, 0, 0,...]
  transfers between devices with their start and end apart: 6 -> 17, of which waited for: 4 -> 8; matrix products, arithmetic and copies ran while one was open for 20% -> 17% of each run, Pallas kernels for 0% -> 15%
where the time goes in v1:
time: 226 us
  waiting for transfers between devices  82 us (36%)
  starting transfers between devices  43.6 us (19%)
  Pallas kernels  38.4 us (17%)
  local copies, waits for them, and re-layouts  19.9 us (9%)
  matrix products  18 us (8%)
  between operations  15.7 us (7%)
  other arithmetic  7.87 us (3%)
    psum x1, waiting for transfers between devices, shards(): grad_cross = lax.psum(grad_weight, PLANE)  33.2 us
    dot_general x4, matrix products, dot(): lax.dot_general(a, b, ((contract[:1], contract[1:]), ((), ())), preferred...  18 us
    ppermute x2, waiting for transfers between devices, flipped(): return lax.ppermute(x, ('y', 'c', 'xl', 'z'), pairs)  17.2 us
    ppermute x6, waiting for transfers between devices, turned(): return lambda x: lax.ppermute(x, axis, pairs)  16.5 us
    pallas_call x1, Pallas kernels, cross(): pl.pallas_call(cross_kernel, grid_spec=pltpu.PrefetchScalarGridSpec(num_s...  16 us
    ppermute x6, starting transfers between devices, turned(): return lambda x: lax.ppermute(x, axis, pairs)  15.7 us
    all_to_all x1, waiting for transfers between devices, shards(): lax.all_to_all(parts, TP, 0, 0, tiled=True).reshape(8 * TOK, LANES)  15.1 us
    unnamed x19, local copies, waits for them, and re-layouts  10.3 us
  transfers between devices with their start and end apart: 17, of which 8 were waited for; matrix products, arithmetic and copies ran while one was open for 17% of the time, Pallas kernels for 15%

profile of v1, /device:TPU:1, one launch (start us, length us, event | category | flops | bytes accessed | tf_op | source)
XLA Modules:
  0.0 225.5 jit_solution(18235844591345457365)
XLA Ops:
  8.0 4.9 %collective-permute-start = (bf16[128,896]{1,0:T(8,128)(2,1)}, bf16[128,896]{1,0:T(8,128)(2,1)S(1)}, u32[]{:S(2)}, u32[]{:S(2)}) collective-permute-start(bf16[128,896]{1,0:T(8,128)(2,1)} %bitcast.42), channel_id=1, source_target_pairs={{0,0},{1,8},{2,16},{3,24},{4,32},{5,40},{6,48},{7,56},{8,1},{9,9},... | collective-permute-start | bytes 688136 | tf_op jit(solution)/shard_map/ppermute | solution.py:37
  13.0 0.7 reshape.66.gain_ref
  13.7 3.2 %collective-permute-done.x_ref = bf16[128,896]{1,0:T(8,128)(2,1)S(1)} collective-permute-done((bf16[128,896]{1,0:T(8,128)(2,1)}, bf16[128,896]{1,0:T(8,128)(2,1)S(1)}, u32[]{:S(2)}, u32[]{:S(2)}) %collective-permute-start) | collective-permute-done | bytes 229408 | tf_op jit(solution)/shard_map/ppermute | solution.py:37
  16.9 2.4 %copy-done.1 = bf16[896,2688]{1,0:T(8,128)(2,1)S(1)} copy-done((bf16[896,2688]{1,0:T(8,128)(2,1)S(1)}, bf16[896,2688]{1,0:T(8,128)(2,1)}, u32[]{:S(2)}) %copy-start.1) | copy-done | bytes 4816920
  19.3 1.4 copy-done.3
  20.7 3.5 %shard_map.127 = (bf16[128,896]{1,0:T(8,128)(2,1)S(1)}, bf16[128,896]{1,0:T(8,128)(2,1)S(1)}, bf16[128,2688]{1,0:T(8,128)(2,1)S(1)}, bf16[128,896]{1,0:T(8,128)(2,1)S(1)}) custom-call(bf16[128,896]{1,0:T(8,128)(2,1)S(1)} %collective-permute-done.x_ref, f32[1,896]{1,0:T(1,128)S(1)} %reshape.66.gain_ref, bf16[896,2688]{1,0:T(8,128)(2,1)S(1)} %copy-done.1, ...), custom_call_target="tpu_custom_call" | custom-call | flops 1000000000 | bytes 8000000 | tf_op jit(solution)/shard_map/pallas_call | solution.py:90
  24.2 1.7 shard_map.133
  26.0 11.9 %collective-permute-start.5 = (bf16[128,896]{1,0:T(8,128)(2,1)S(1)}, bf16[128,896]{1,0:T(8,128)(2,1)S(1)}, u32[]{:S(2)}, u32[]{:S(2)}) collective-permute-start(bf16[128,896]{1,0:T(8,128)(2,1)S(1)} %get-tuple-element.21.first_ref), channel_id=1, source_target_pairs={{0,48},{16,0},{32,16},{48,32},{1,49},{17,1},{33,17},{49,33},{2,50}... | collective-permute-start | bytes 688136 | tf_op jit(solution)/shard_map/ppermute | solution.py:28
  37.9 0.1 collective-permute-start.3
  38.1 0.8 collective-permute-start.1
  38.9 3.1 %collective-permute-start.7 = (bf16[128,896]{1,0:T(8,128)(2,1)S(1)}, bf16[128,896]{1,0:T(8,128)(2,1)S(1)}, u32[]{:S(2)}, u32[]{:S(2)}) collective-permute-start(bf16[128,896]{1,0:T(8,128)(2,1)S(1)} %get-tuple-element.21.first_ref), channel_id=1, source_target_pairs={{0,8},{8,0},{1,9},{9,1},{2,10},{10,2},{3,11},{11,3},{4,12},{12,4},... | collective-permute-start | bytes 688136 | tf_op jit(solution)/shard_map/ppermute | solution.py:32
  42.1 5.3 %collective-permute-done.5.first_ref = bf16[128,896]{1,0:T(8,128)(2,1)S(1)} collective-permute-done((bf16[128,896]{1,0:T(8,128)(2,1)S(1)}, bf16[128,896]{1,0:T(8,128)(2,1)S(1)}, u32[]{:S(2)}, u32[]{:S(2)}) %collective-permute-start.5) | collective-permute-done | bytes 229408 | tf_op jit(solution)/shard_map/ppermute | solution.py:28
  47.4 1.4 collective-permute-start.6
  48.8 1.2 collective-permute-start.4
  50.1 3.3 %copy.23 = bf16[112,8,2,1024]{3,1,2,0:T(8,128)(2,1)S(1)} copy(bf16[112,8,2,1024]{3,2,1,0:T(2,128)(2,1)} %bitcast.35) | data formatting | bytes 7340032
  53.4 0.3 collective-permute-start.2
  53.6 2.4 %shard_map.128 = (bf16[2,4,128,896]{3,2,1,0:T(8,128)(2,1)S(1)}, bf16[2,4,128,2048]{3,2,1,0:T(8,128)(2,1)S(1)}) custom-call(bf16[128,896]{1,0:T(8,128)(2,1)S(1)} %get-tuple-element.21.first_ref, bf16[128,896]{1,0:T(8,128)(2,1)S(1)} %collective-permute-done.7.second_ref, bf16[896,2048]{1,0:T(8,128)(2,1)S(1)} %bitcast.24), custom_call_target="tpu_custom_call" | custom-call | flops 1000000000 | bytes 6000000 | tf_op jit(solution)/shard_map/pallas_call | solution.py:127
  56.0 2.4 %shard_map.129 = (bf16[2,4,128,896]{3,2,1,0:T(8,128)(2,1)S(1)}, bf16[2,4,128,2048]{3,2,1,0:T(8,128)(2,1)S(1)}) custom-call(bf16[128,896]{1,0:T(8,128)(2,1)S(1)} %collective-permute-done.5.first_ref, bf16[128,896]{1,0:T(8,128)(2,1)S(1)} %collective-permute-done.6.second_ref, ...), custom_call_target="tpu_custom_call", output_to_operand_aliasing={{0}: (3, {}), {1}: (4, {})} | custom-call | flops 1000000000 | bytes 6000000 | tf_op jit(solution)/shard_map/pallas_call | solution.py:127
  58.4 2.4 %shard_map.130 = (bf16[2,4,128,896]{3,2,1,0:T(8,128)(2,1)S(1)}, bf16[2,4,128,2048]{3,2,1,0:T(8,128)(2,1)S(1)}) custom-call(bf16[128,896]{1,0:T(8,128)(2,1)S(1)} %collective-permute-done.3.first_ref, bf16[128,896]{1,0:T(8,128)(2,1)S(1)} %collective-permute-done.4.second_ref, ...), custom_call_target="tpu_custom_call", output_to_operand_aliasing={{0}: (3, {}), {1}: (4, {})} | custom-call | flops 1000000000 | bytes 6000000 | tf_op jit(solution)/shard_map/pallas_call | solution.py:127
  60.8 2.4 %shard_map.131 = (bf16[2,4,128,896]{3,2,1,0:T(8,128)(2,1)S(1)}, bf16[2,4,128,2048]{3,2,1,0:T(8,128)(2,1)S(1)}) custom-call(bf16[128,896]{1,0:T(8,128)(2,1)S(1)} %collective-permute-done.1.first_ref, bf16[128,896]{1,0:T(8,128)(2,1)S(1)} %collective-permute-done.2.second_ref, ...), custom_call_target="tpu_custom_call", output_to_operand_aliasing={{0}: (3, {}), {1}: (4, {})} | custom-call | flops 1000000000 | bytes 6000000 | tf_op jit(solution)/shard_map/pallas_call | solution.py:127
  63.2 16.0 %shard_map.132 = (bf16[4,64,1024]{2,1,0:T(8,128)(2,1)}, bf16[4,64,1024]{2,1,0:T(8,128)(2,1)}, bf16[8,128,2048]{2,1,0:T(8,128)(2,1)S(1)}) custom-call(s32[8]{0:T(128)S(1)} %fusion.8.slots_ref, bf16[4,64,1024]{2,1,0:T(8,128)(2,1)S(1)} %copy-done.5, bf16[4,64,1024]{2,1,0:T(8,128)(2,1)S(1)} %copy-done.6, bf16[8,128,2048]{2,1,0:T(8,128)(2,1)S(1)} %bitcast.30, ...), custom_call_target="tpu_custom_call" | custom-call | flops 3000000000 | bytes 12000000 | tf_op jit(solution)/shard_map/pallas_call | solution.py:179
  79.2 0.4 fusion.12
  79.7 3.3 %convolution_convert_fusion.1 = bf16[512,896]{1,0:T(8,128)(2,1)} fusion(bf16[512,2048]{1,0:T(8,128)(2,1)S(1)} %bitcast.37, bf16[896,2048]{1,0:T(8,128)(2,1)S(1)} %bitcast.28), kind=kOutput, calls=%fused_computation.8 | convolution fusion | flops 1879506944 | bytes 6684672 | tf_op jit(solution)/shard_map/dot_general | solution.py:41
  83.0 0.5 collective-permute-start.8
  83.5 5.5 %convolution_convert_fusion = bf16[896,2048]{1,0:T(8,128)(2,1)} fusion(bf16[1024,896]{1,0:T(8,128)(2,1)S(1)} %bitcast.32, bf16[1024,2048]{1,0:T(8,128)(2,1)S(1)} %bitcast.33), kind=kOutput, calls=%fused_computation | convolution fusion | flops 3759931392 | bytes 9699328 | tf_op jit(solution)/shard_map/dot_general | solution.py:41
  89.0 7.1 %reshape.71 = bf16[896,2,1024]{2,1,0:T(2,128)(2,1)} reshape(bf16[896,2048]{1,0:T(8,128)(2,1)} %convolution_convert_fusion) | data formatting | bytes 7340032 | tf_op jit(solution)/shard_map/reshape | solution.py:310
  96.1 4.7 %fusion.11 = (bf16[512,896]{1,0:T(8,128)(2,1)S(1)}, f32[512,896]{1,0:T(8,128)S(1)}) fusion(bf16[512,896]{1,0:T(8,128)(2,1)} %collective-permute-done.8, bf16[512,2048]{1,0:T(8,128)(2,1)S(1)} %bitcast.36, bf16[896,2048]{1,0:T(8,128)(2,1)} %bitcast.29), kind=kOutput, calls=%fused_computation.29 | convolution fusion | flops 1880424448 | bytes 9437184 | tf_op jit(solution)/shard_map/dot_general | solution.py:41
  100.9 0.6 collective-permute-start.10
  101.5 2.2 collective-permute-start.11
  103.8 6.0 %collective-permute-done.10 = bf16[128,896]{1,0:T(8,128)(2,1)S(1)} collective-permute-done((bf16[128,896]{1,0:T(8,128)(2,1)S(1)}, bf16[128,896]{1,0:T(8,128)(2,1)S(1)}, u32[]{:S(2)}, u32[]{:S(2)}) %collective-permute-start.10) | collective-permute-done | bytes 229408 | tf_op jit(solution)/shard_map/ppermute | solution.py:28
  109.8 4.3 %collective-permute-done.11 = bf16[128,896]{1,0:T(8,128)(2,1)S(1)} collective-permute-done((bf16[128,896]{1,0:T(8,128)(2,1)S(1)}, bf16[128,896]{1,0:T(8,128)(2,1)S(1)}, u32[]{:S(2)}, u32[]{:S(2)}) %collective-permute-start.11) | collective-permute-done | bytes 229408 | tf_op jit(solution)/shard_map/ppermute | solution.py:28
  114.1 0.9 collective-permute-done.9
  114.9 0.1 fusion.7.grad_ref
  115.0 4.6 %shard_map.134.parts_ref = bf16[8,128,512]{2,1,0:T(8,128)(2,1)} custom-call(bf16[128,896]{1,0:T(8,128)(2,1)S(1)} %fusion.7.grad_ref, bf16[128,2688]{1,0:T(8,128)(2,1)S(1)} %get-tuple-element.35.projected_ref, bf16[896,896]{1,0:T(8,128)(2,1)S(1)} %copy-done.4), custom_call_target="tpu_custom_call" | custom-call | flops 600000000 | bytes 4000000 | tf_op jit(solution)/shard_map/pallas_call | solution.py:238
  119.7 4.3 %all-to-all-start = ((bf16[8,128,512]{2,1,0:T(8,128)(2,1)}), bf16[8,128,512]{2,1,0:T(8,128)(2,1)S(1)}, u32[]{:S(2)}, u32[]{:S(2)}) async-start(bf16[8,128,512]{2,1,0:T(8,128)(2,1)} %shard_map.134.parts_ref), calls=%async_computation | async-start | bytes 2097152 | tf_op jit(solution)/shard_map/all_to_all | solution.py:313
  123.9 15.1 %all-to-all-done = bf16[8,128,512]{2,1,0:T(8,128)(2,1)S(1)} async-done(((bf16[8,128,512]{2,1,0:T(8,128)(2,1)}), bf16[8,128,512]{2,1,0:T(8,128)(2,1)S(1)}, u32[]{:S(2)}, u32[]{:S(2)}) %all-to-all-start) | async-done | bytes 1048608 | tf_op jit(solution)/shard_map/all_to_all | solution.py:313
  139.0 4.5 %fusion.4 = bf16[128,8,512]{2,1,0:T(8,128)(2,1)} fusion(bf16[1024,512]{1,0:T(8,128)(2,1)S(1)} %bitcast.38, bf16[1024,2048]{1,0:T(8,128)(2,1)} %all-gather.2.cloned.1.call-done, pred[]{:T(512)S(6)} %lt.20), kind=kOutput, calls=%fused_computation.9 | convolution fusion | flops 1075314688 | bytes 6291457 | tf_op jit(solution)/shard_map/dot_general | solution.py:41
  143.6 8.5 %all-to-all-start.1 = ((bf16[128,8,512]{2,1,0:T(8,128)(2,1)}), bf16[128,8,512]{2,1,0:T(8,128)(2,1)S(1)}, u32[]{:S(2)}, u32[]{:S(2)}) async-start(bf16[128,8,512]{2,1,0:T(8,128)(2,1)} %fusion.4), calls=%async_computation.1 | async-start | bytes 2097152 | tf_op jit(solution)/shard_map/all_to_all | solution.py:316
  152.1 2.4 %copy-done.2 = bf16[896,2688]{1,0:T(8,128)(2,1)S(1)} copy-done((bf16[896,2688]{1,0:T(8,128)(2,1)S(1)}, bf16[896,2688]{1,0:T(8,128)(2,1)}, u32[]{:S(2)}) %copy-start.2) | copy-done | bytes 4816920
  154.5 3.0 %shard_map.135 = bf16[128,896]{1,0:T(8,128)(2,1)S(1)} custom-call(bf16[128,896]{1,0:T(8,128)(2,1)S(1)} %collective-permute-done.x_ref, f32[1,896]{1,0:T(1,128)S(1)} %reshape.66.gain_ref, bf16[896,2688]{1,0:T(8,128)(2,1)S(1)} %copy-done.2, bf16[8,128,512]{2,1,0:T(8,128)(2,1)} %shard_map.134.parts_ref, bf16[128,896]{1,0:T(8,128)(2,1)S(1)} %fusion.7.grad_ref), custom_call_target="tpu_custom_call" | custom-call | flops 600000000 | bytes 6000000 | tf_op jit(solution)/shard_map/pallas_call | solution.py:261
  157.6 3.7 %collective-permute-start.12 = (bf16[128,896]{1,0:T(8,128)(2,1)S(1)}, bf16[128,896]{1,0:T(8,128)(2,1)S(1)}, u32[]{:S(2)}, u32[]{:S(2)}) collective-permute-start(bf16[128,896]{1,0:T(8,128)(2,1)S(1)} %shard_map.135), channel_id=1, source_target_pairs={{0,0},{1,8},{2,16},{3,24},{4,32},{5,40},{6,48},{7,56},{8,1},{9,9},... | collective-permute-start | bytes 688136 | tf_op jit(solution)/shard_map/ppermute | solution.py:37
  161.2 14.0 %collective-permute-done.12 = bf16[128,896]{1,0:T(8,128)(2,1)S(1)} collective-permute-done((bf16[128,896]{1,0:T(8,128)(2,1)S(1)}, bf16[128,896]{1,0:T(8,128)(2,1)S(1)}, u32[]{:S(2)}, u32[]{:S(2)}) %collective-permute-start.12) | collective-permute-done | bytes 229408 | tf_op jit(solution)/shard_map/ppermute | solution.py:37
  175.2 33.2 %all-reduce.2.cloned.1.call-done = bf16[896,2,1024]{2,1,0:T(2,128)(2,1)} async-done(((bf16[896,2,1024]{2,1,0:T(2,128)(2,1)}), bf16[896,2,1024]{2,1,0:T(2,128)(2,1)}) %all-reduce.2.cloned.1.call-update) | async-done | bytes 3670032 | tf_op jit(solution)/shard_map/psum | solution.py:309
  208.4 7.6 %reshape.72 = f32[896,2,1024]{2,1,0:T(2,128)} convert(bf16[896,2,1024]{2,1,0:T(2,128)(2,1)} %all-reduce.2.cloned.1.call-done) | non-fusion elementwise | flops 1835008 | bytes 11010048 | tf_op jit(solution)/shard_map/reshape | solution.py:310
  216.0 0.1 convert_reduce_fusion
  216.1 0.6 slice.62
  216.8 0.6 slice.63
  217.4 0.7 copy.32
  (31 shorter events, 0.5 us)
Async XLA Ops:
  8.0 131.0 %all-gather.2.cloned.1.call-start = ((), (), s32[]{:S(2)}) async-start(), calls=%async_computation.3 | async-start | bytes 4718592 | tf_op jit(solution)/shard_map/all_gather | solution.py:291
  8.0 8.8 %collective-permute-start = (bf16[128,896]{1,0:T(8,128)(2,1)}, bf16[128,896]{1,0:T(8,128)(2,1)S(1)}, u32[]{:S(2)}, u32[]{:S(2)}) collective-permute-start(bf16[128,896]{1,0:T(8,128)(2,1)} %bitcast.42), channel_id=1, source_target_pairs={{0,0},{1,8},{2,16},{3,24},{4,32},{5,40},{6,48},{7,56},{8,1},{9,9},... | collective-permute-start | bytes 688136 | tf_op jit(solution)/shard_map/ppermute | solution.py:37
  16.9 2.4 %copy-start.1 = (bf16[896,2688]{1,0:T(8,128)(2,1)S(1)}, bf16[896,2688]{1,0:T(8,128)(2,1)}, u32[]{:S(2)}) copy-start(bf16[896,2688]{1,0:T(8,128)(2,1)} %project_ref.3) | copy-start | bytes 14450692
  19.3 1.4 copy-start.3
  24.2 17.8 %copy-start.7 = (s32[4,2]{0,1:T(2,128)S(1)}, s32[4,2]{0,1:T(2,128)}, u32[]{:S(2)}) copy-start(s32[4,2]{0,1:T(2,128)} %param.14) | copy-start | bytes 100
  26.0 182.4 %all-reduce.2.cloned.1.call-start = ((), (), s32[]{:S(2)}) async-start(), calls=%async_computation.2 | async-start | bytes 7340032 | tf_op jit(solution)/shard_map/psum | solution.py:309
  26.0 21.4 %collective-permute-start.5 = (bf16[128,896]{1,0:T(8,128)(2,1)S(1)}, bf16[128,896]{1,0:T(8,128)(2,1)S(1)}, u32[]{:S(2)}, u32[]{:S(2)}) collective-permute-start(bf16[128,896]{1,0:T(8,128)(2,1)S(1)} %get-tuple-element.21.first_ref), channel_id=1, source_target_pairs={{0,48},{16,0},{32,16},{48,32},{1,49},{17,1},{33,17},{49,33},{2,50}... | collective-permute-start | bytes 688136 | tf_op jit(solution)/shard_map/ppermute | solution.py:28
  37.9 10.8 %collective-permute-start.3 = (bf16[128,896]{1,0:T(8,128)(2,1)S(1)}, bf16[128,896]{1,0:T(8,128)(2,1)S(1)}, u32[]{:S(2)}, u32[]{:S(2)}) collective-permute-start(bf16[128,896]{1,0:T(8,128)(2,1)S(1)} %get-tuple-element.21.first_ref), channel_id=1, source_target_pairs={{0,32},{16,48},{32,0},{48,16},{1,33},{17,49},{33,1},{49,17},{2,34}... | collective-permute-start | bytes 688136 | tf_op jit(solution)/shard_map/ppermute | solution.py:28
  38.1 15.3 %collective-permute-start.1 = (bf16[128,896]{1,0:T(8,128)(2,1)S(1)}, bf16[128,896]{1,0:T(8,128)(2,1)S(1)}, u32[]{:S(2)}, u32[]{:S(2)}) collective-permute-start(bf16[128,896]{1,0:T(8,128)(2,1)S(1)} %get-tuple-element.21.first_ref), channel_id=1, source_target_pairs={{0,16},{16,32},{32,48},{48,0},{1,17},{17,33},{33,49},{49,1},{2,18}... | collective-permute-start | bytes 688136 | tf_op jit(solution)/shard_map/ppermute | solution.py:28
  38.9 14.8 %collective-permute-start.7 = (bf16[128,896]{1,0:T(8,128)(2,1)S(1)}, bf16[128,896]{1,0:T(8,128)(2,1)S(1)}, u32[]{:S(2)}, u32[]{:S(2)}) collective-permute-start(bf16[128,896]{1,0:T(8,128)(2,1)S(1)} %get-tuple-element.21.first_ref), channel_id=1, source_target_pairs={{0,8},{8,0},{1,9},{9,1},{2,10},{10,2},{3,11},{11,3},{4,12},{12,4},... | collective-permute-start | bytes 688136 | tf_op jit(solution)/shard_map/ppermute | solution.py:32
  47.4 8.6 %collective-permute-start.6 = (bf16[128,896]{1,0:T(8,128)(2,1)S(1)}, bf16[128,896]{1,0:T(8,128)(2,1)S(1)}, u32[]{:S(2)}, u32[]{:S(2)}) collective-permute-start(bf16[128,896]{1,0:T(8,128)(2,1)S(1)} %collective-permute-done.5.first_ref), channel_id=1, source_target_pairs={{0,8},{8,0},{1,9},{9,1},{2,10},{10,2},{3,11},{11,3},{4,12},{12,4},... | collective-permute-start | bytes 688136 | tf_op jit(solution)/shard_map/ppermute | solution.py:32
  48.8 9.6 %collective-permute-start.4 = (bf16[128,896]{1,0:T(8,128)(2,1)S(1)}, bf16[128,896]{1,0:T(8,128)(2,1)S(1)}, u32[]{:S(2)}, u32[]{:S(2)}) collective-permute-start(bf16[128,896]{1,0:T(8,128)(2,1)S(1)} %collective-permute-done.3.first_ref), channel_id=1, source_target_pairs={{0,8},{8,0},{1,9},{9,1},{2,10},{10,2},{3,11},{11,3},{4,12},{12,4},... | collective-permute-start | bytes 688136 | tf_op jit(solution)/shard_map/ppermute | solution.py:32
  53.3 26.3 %copy-start = (bf16[112,8,2,1024]{3,1,2,0:T(8,128)(2,1)}, bf16[112,8,2,1024]{3,1,2,0:T(8,128)(2,1)S(1)}, u32[]{:S(2)}) copy-start(bf16[112,8,2,1024]{3,1,2,0:T(8,128)(2,1)S(1)} %copy.23) | copy-start | bytes 11010052
  53.4 7.5 %collective-permute-start.2 = (bf16[128,896]{1,0:T(8,128)(2,1)S(1)}, bf16[128,896]{1,0:T(8,128)(2,1)S(1)}, u32[]{:S(2)}, u32[]{:S(2)}) collective-permute-start(bf16[128,896]{1,0:T(8,128)(2,1)S(1)} %collective-permute-done.1.first_ref), channel_id=1, source_target_pairs={{0,8},{8,0},{1,9},{9,1},{2,10},{10,2},{3,11},{11,3},{4,12},{12,4},... | collective-permute-start | bytes 688136 | tf_op jit(solution)/shard_map/ppermute | solution.py:32
  60.8 2.4 %copy-start.5 = (bf16[4,64,1024]{2,1,0:T(8,128)(2,1)S(1)}, bf16[4,64,1024]{2,1,0:T(8,128)(2,1)}, u32[]{:S(2)}) copy-start(bf16[4,64,1024]{2,1,0:T(8,128)(2,1)} %q_ref.1) | copy-start | bytes 1572868
  60.8 2.4 %copy-start.6 = (bf16[4,64,1024]{2,1,0:T(8,128)(2,1)S(1)}, bf16[4,64,1024]{2,1,0:T(8,128)(2,1)}, u32[]{:S(2)}) copy-start(bf16[4,64,1024]{2,1,0:T(8,128)(2,1)} %up_ref.1) | copy-start | bytes 1572868
  83.0 13.2 %collective-permute-start.8 = (bf16[512,896]{1,0:T(8,128)(2,1)}, bf16[512,896]{1,0:T(8,128)(2,1)}, u32[]{:S(2)}, u32[]{:S(2)}) collective-permute-start(bf16[512,896]{1,0:T(8,128)(2,1)} %convolution_convert_fusion.1), channel_id=1, source_target_pairs={{0,8},{8,0},{1,9},{9,1},{2,10},{10,2},{3,11},{11,3},{4,12},{12,4},... | collective-permute-start | bytes 2752520 | tf_op jit(solution)/shard_map/ppermute | solution.py:32
  100.8 14.2 %copy-start.4 = (bf16[896,896]{1,0:T(8,128)(2,1)S(1)}, bf16[896,896]{1,0:T(8,128)(2,1)}, u32[]{:S(2)}) copy-start(bf16[896,896]{1,0:T(8,128)(2,1)} %mix_ref.3) | copy-start | bytes 4816900
  100.9 8.8 %collective-permute-start.10 = (bf16[128,896]{1,0:T(8,128)(2,1)S(1)}, bf16[128,896]{1,0:T(8,128)(2,1)S(1)}, u32[]{:S(2)}, u32[]{:S(2)}) collective-permute-start(bf16[128,896]{1,0:T(8,128)(2,1)S(1)} %get-tuple-element.42), channel_id=1, source_target_pairs={{0,32},{16,48},{32,0},{48,16},{1,33},{17,49},{33,1},{49,17},{2,34}... | collective-permute-start | bytes 688136 | tf_op jit(solution)/shard_map/ppermute | solution.py:28
  101.5 12.6 %collective-permute-start.11 = (bf16[128,896]{1,0:T(8,128)(2,1)S(1)}, bf16[128,896]{1,0:T(8,128)(2,1)S(1)}, u32[]{:S(2)}, u32[]{:S(2)}) collective-permute-start(bf16[128,896]{1,0:T(8,128)(2,1)S(1)} %get-tuple-element.41), channel_id=1, source_target_pairs={{0,48},{16,0},{32,16},{48,32},{1,49},{17,1},{33,17},{49,33},{2,50}... | collective-permute-start | bytes 688136 | tf_op jit(solution)/shard_map/ppermute | solution.py:28
  103.7 11.3 %collective-permute-start.9 = (bf16[128,896]{1,0:T(8,128)(2,1)S(1)}, bf16[128,896]{1,0:T(8,128)(2,1)S(1)}, u32[]{:S(2)}, u32[]{:S(2)}) collective-permute-start(bf16[128,896]{1,0:T(8,128)(2,1)S(1)} %get-tuple-element.40), channel_id=1, source_target_pairs={{0,16},{16,32},{32,48},{48,0},{1,17},{17,33},{33,49},{49,1},{2,18}... | collective-permute-start | bytes 688136 | tf_op jit(solution)/shard_map/ppermute | solution.py:28
  119.7 19.4 %all-to-all-start = ((bf16[8,128,512]{2,1,0:T(8,128)(2,1)}), bf16[8,128,512]{2,1,0:T(8,128)(2,1)S(1)}, u32[]{:S(2)}, u32[]{:S(2)}) async-start(bf16[8,128,512]{2,1,0:T(8,128)(2,1)} %shard_map.134.parts_ref), calls=%async_computation | async-start | bytes 2097152 | tf_op jit(solution)/shard_map/all_to_all | solution.py:313
  143.6 72.4 %all-to-all-start.1 = ((bf16[128,8,512]{2,1,0:T(8,128)(2,1)}), bf16[128,8,512]{2,1,0:T(8,128)(2,1)S(1)}, u32[]{:S(2)}, u32[]{:S(2)}) async-start(bf16[128,8,512]{2,1,0:T(8,128)(2,1)} %fusion.4), calls=%async_computation.1 | async-start | bytes 2097152 | tf_op jit(solution)/shard_map/all_to_all | solution.py:316
  152.1 2.4 %copy-start.2 = (bf16[896,2688]{1,0:T(8,128)(2,1)S(1)}, bf16[896,2688]{1,0:T(8,128)(2,1)}, u32[]{:S(2)}) copy-start(bf16[896,2688]{1,0:T(8,128)(2,1)} %project_ref.3) | copy-start | bytes 14450692
  157.6 17.7 %collective-permute-start.12 = (bf16[128,896]{1,0:T(8,128)(2,1)S(1)}, bf16[128,896]{1,0:T(8,128)(2,1)S(1)}, u32[]{:S(2)}, u32[]{:S(2)}) collective-permute-start(bf16[128,896]{1,0:T(8,128)(2,1)S(1)} %shard_map.135), channel_id=1, source_target_pairs={{0,0},{1,8},{2,16},{3,24},{4,32},{5,40},{6,48},{7,56},{8,1},{9,9},... | collective-permute-start | bytes 688136 | tf_op jit(solution)/shard_map/ppermute | solution.py:37
Sparse Core Ops, SparseCore 0:
  26.1 44.3 all-gather.1
Sparse Core Ops, SparseCore 1:
  96.2 112.1 all-reduce.1

commit v2 on v1

--- a/solution.py
+++ b/solution.py
@@ -112,95 +112,138 @@
     )(normed, mixed)
 
 
-def pairs_kernel(first_ref, second_ref, weight_ref, *rest):
-    held_ref, out_ref = rest[-2:]
-    held_ref[0, 0] = first_ref[...]
-    held_ref[1, 0] = second_ref[...]
-    out_ref[0, 0] = nn(first_ref[...], weight_ref[...]).astype(bf16)
-    out_ref[1, 0] = nn(second_ref[...], weight_ref[...]).astype(bf16)
-
-
-def pairs_of(step, first, second, weight, before):
-    many = 4
-    width = weight.shape[1] // many
-    kept = [pl.BlockSpec(memory_space=pl.ANY)] * len(before)
-    return pl.pallas_call(
-        pairs_kernel,
-        grid=(many,),
-        in_specs=[
-            pl.BlockSpec((TOK, ENC), lambda i: (0, 0)),
-            pl.BlockSpec((TOK, ENC), lambda i: (0, 0)),
-            pl.BlockSpec((ENC, width), lambda i: (0, i)),
-            *kept,
-        ],
-        out_specs=(
-            pl.BlockSpec((2, 1, TOK, ENC), lambda i: (0, step, 0, 0)),
-            pl.BlockSpec((2, 1, TOK, width), lambda i: (0, step, 0, i)),
-        ),
-        out_shape=(
-            jax.ShapeDtypeStruct((2, 4, TOK, ENC), bf16),
-            jax.ShapeDtypeStruct((2, 4, TOK, weight.shape[1]), bf16),
-        ),
-        input_output_aliases={3: 0, 4: 1} if before else {},
-        compiler_params=params(16, 1),
-        cost_estimate=cost(10**9, 6 * 10**6),
-    )(first, second, weight, *before)
-
-
-def cross_kernel(slots_ref, q_ref, up_ref, one_ref, two_ref, out_ref, grad_ref, pairs_ref):
-    span = pl.program_id(0)
-    slots = (slots_ref[2 * span], slots_ref[2 * span + 1])
-    inner = q_ref.shape[2]
+def cross_kernel(slots_ref, q_ref, up_ref, weight_ref, *rest):
+    sources, (out_ref, grad_ref, pairs_ref, rows_ref, held_ref) = rest[:8], rest[8:]
+
+    @pl.when(pl.program_id(0) == 0)
+    def _():
+        for n, source in enumerate(sources):
+            rows_ref[n * TOK : (n + 1) * TOK] = source[...]
+
+    held_ref[...] = nn(rows_ref[...], weight_ref[...]).astype(bf16)
     scale = 1.0 / math.sqrt(HS)
-    for h in range(inner // HS):
-        at = slice(h * HS, (h + 1) * HS)
-        up = slice(inner + h * HS, inner + (h + 1) * HS)
-        q = q_ref[0, :, at]
-        g = up_ref[0, :, at]
-        k = jnp.concatenate([one_ref[0, :, at], two_ref[0, :, at]], axis=0)
-        v = jnp.concatenate([one_ref[0, :, up], two_ref[0, :, up]], axis=0)
-        probs = softmax(nt(q, k) * scale)
-        low = probs.astype(bf16)
-        out_ref[0, :, at] = nn(low, v).astype(bf16)
-        grad_probs = nt(g, v)
-        grad_values = tn(low, g).astype(bf16)
-        total = jnp.sum(probs * grad_probs, axis=-1, keepdims=True)
-        grad_scores = (probs * (grad_probs - total)).astype(bf16)
-        grad_ref[0, :, at] = (nn(grad_scores, k) * scale).astype(bf16)
-        grad_keys = (tn(grad_scores, q) * scale).astype(bf16)
+    spans = range(q_ref.shape[0])
+    rows = [
+        [pl.ds(pl.multiple_of(slots_ref[2 * c + n] * TOK, TOK), TOK) for n in range(2)]
+        for c in spans
+    ]
+    k = [jnp.concatenate([held_ref[r, :HS] for r in rows[c]], axis=0) for c in spans]
+    v = [jnp.concatenate([held_ref[r, HS:] for r in rows[c]], axis=0) for c in spans]
+    scores = [nt(q_ref[c], k[c]) * scale for c in spans]
+    grad_probs = [nt(up_ref[c], v[c]) for c in spans]
+    probs = [softmax(scores[c]) for c in spans]
+    low = [probs[c].astype(bf16) for c in spans]
+    totals = [jnp.sum(probs[c] * grad_probs[c], axis=-1, keepdims=True) for c in spans]
+    grad_scores = [(probs[c] * (grad_probs[c] - totals[c])).astype(bf16) for c in spans]
+    for c in spans:
+        out_ref[c] = nn(low[c], v[c]).astype(bf16)
+        grad_ref[c] = (nn(grad_scores[c], k[c]) * scale).astype(bf16)
+    for c in spans:
+        grad_keys = (tn(grad_scores[c], q_ref[c]) * scale).astype(bf16)
+        grad_values = tn(low[c], up_ref[c]).astype(bf16)
         for n in range(2):
-            pairs_ref[slots[n], :, at] = grad_keys[n * TOK : (n + 1) * TOK]
-            pairs_ref[slots[n], :, up] = grad_values[n * TOK : (n + 1) * TOK]
-
-
-def cross(slots, queries, upstream, pairs):
+            pairs_ref[rows[c][n], :HS] = grad_keys[n * TOK : (n + 1) * TOK]
+            pairs_ref[rows[c][n], HS:] = grad_values[n * TOK : (n + 1) * TOK]
+
+
+def cross(slots, queries, upstream, weight, sources):
     spans, length, inner = queries.shape
-    whole = pl.BlockSpec((1, length, inner), lambda i, s: (i, 0, 0))
+    rows = len(sources) * TOK
+    column = pl.BlockSpec((spans, length, HS), lambda i, s: (0, 0, i))
     return pl.pallas_call(
         cross_kernel,
         grid_spec=pltpu.PrefetchScalarGridSpec(
             num_scalar_prefetch=1,
-            grid=(spans,),
+            grid=(inner // HS,),
             in_specs=[
-                whole,
-                whole,
-                pl.BlockSpec((1, TOK, 2 * inner), lambda i, s: (s[2 * i], 0, 0)),
-                pl.BlockSpec((1, TOK, 2 * inner), lambda i, s: (s[2 * i + 1], 0, 0)),
+                column,
+                column,
+                pl.BlockSpec((ENC, 2 * HS), lambda i, s: (0, i)),
+                *[pl.BlockSpec((TOK, ENC), lambda i, s: (0, 0))] * len(sources),
             ],
-            out_specs=(
-                whole,
-                whole,
-                pl.BlockSpec((2 * spans, TOK, 2 * inner), lambda i, s: (0, 0, 0)),
-            ),
+            out_specs=(column, column, pl.BlockSpec((rows, 2 * HS), lambda i, s: (0, i))),
+            scratch_shapes=[pltpu.VMEM((rows, ENC), bf16), pltpu.VMEM((rows, 2 * HS), bf16)],
         ),
         out_shape=(
             jax.ShapeDtypeStruct(queries.shape, bf16),
             jax.ShapeDtypeStruct(queries.shape, bf16),
-            jax.ShapeDtypeStruct((2 * spans, TOK, 2 * inner), bf16),
+            jax.ShapeDtypeStruct((rows, 2 * inner), bf16),
         ),
-        compiler_params=params(32, 1),
-        cost_estimate=cost(3 * 10**9, 12 * 10**6),
-    )(slots, queries, upstream, pairs, pairs)
+        compiler_params=params(24, 1),
+        cost_estimate=cost(12 * 10**9, 12 * 10**6),
+    )(slots, queries, upstream, weight, *sources)
+
+
+def weight_kernel(order_ref, pairs_ref, *rest):
+    sources, outs, turned_ref = rest[:8], rest[8:-1], rest[-1]
+    for n, source in enumerate(sources):
+        turned_ref[:, n * TOK : (n + 1) * TOK] = source[...].T
+    for i, out in enumerate(outs):
+        at = pl.ds(pl.multiple_of(order_ref[i] * 2 * HS, 2 * HS), 2 * HS)
+        out[...] = nn(turned_ref[...], pairs_ref[:, at]).astype(bf16)
+
+
+def weight_blocks(order, pairs, sources):
+    heads = pairs.shape[1] // (2 * HS)
+    vmem = pl.BlockSpec(memory_space=pltpu.VMEM)
+    return pl.pallas_call(
+        weight_kernel,
+        in_specs=[pl.BlockSpec(memory_space=pltpu.SMEM)] + [vmem] * (1 + len(sources)),
+        out_specs=(vmem,) * heads,
+        out_shape=(jax.ShapeDtypeStruct((ENC, 2 * HS), bf16),) * heads,
+        scratch_shapes=[pltpu.VMEM((ENC, len(sources) * TOK), bf16)],
+        compiler_params=params(24),
+        cost_estimate=cost(4 * 10**9, 10**7),
+    )(order, pairs, *sources)
+
+
+def plane_sum(blocks, first, second, at_second):
+    total = blocks[0].astype(f32)
+    for d in range(1, 4):
+        total += turned(first, 4, d)(blocks[d]).astype(f32)
+    total = total.astype(bf16)
+    size = total.shape[0] // 4
+    cuts = [lax.dynamic_slice_in_dim(total, (at_second + d) % 4 * size, size) for d in range(4)]
+    piece = cuts[0].astype(f32)
+    for d in range(1, 4):
+        piece += turned(second, 4, d)(cuts[d]).astype(f32)
+    piece = piece.astype(bf16)
+    line = jnp.stack([piece] + [turned(second, 4, -d)(piece) for d in range(1, 4)])
+    return [line] + [turned(first, 4, -d)(line) for d in range(1, 4)]
+
+
+def place_kernel(at_ref, *rest):
+    lines, out_ref = rest[:8], rest[8]
+    size = lines[0].shape[1]
+    for half in range(2):
+        for h in range(4):
+            for d in range(4):
+
+                @pl.when((at_ref[half] + d) % 4 == h)
+                def _():
+                    for b in range(2):
+                        value = lines[4 * half + d][0, :, b * HS : (b + 1) * HS]
+                        start = (half * 4 + h) * 2 + b
+                        out_ref[pl.ds(start, size, stride=16), :] = value.astype(f32)
+
+
+def placed_blocks(at, lines):
+    size = lines[0].shape[1]
+    return pl.pallas_call(
+        place_kernel,
+        grid_spec=pltpu.PrefetchScalarGridSpec(
+            num_scalar_prefetch=1,
+            grid=(4,),
+            in_specs=[
+                pl.BlockSpec((1, size, 2 * HS), lambda i, s, o=1 - n // 4: ((i - s[o] + 4) % 4, 0, 0))
+                for n in range(8)
+            ],
+            out_specs=pl.BlockSpec((size * 16, HS), lambda i, s: (i, 0)),
+        ),
+        out_shape=jax.ShapeDtypeStruct((4 * size * 16, HS), f32),
+        compiler_params=params(16, 1),
+        cost_estimate=cost(10**6, 11 * 10**6),
+    )(at, *lines)
 
 
 def columns_of(at):
@@ -280,34 +323,42 @@
     y, core = lax.axis_index("y"), lax.axis_index("c")
     inner = cross_pairs.shape[2]
     x = flipped(neighbour_inputs[0])
-    weight = lax.optimization_barrier(cross_pairs.reshape(ENC, 2 * inner))
+    heads = inner // HS
+    weight = cross_pairs.reshape(ENC, 2, heads, HS).swapaxes(1, 2).reshape(ENC, 2 * inner)
+    weight = lax.optimization_barrier(weight)
     encoded, normed, projected, mixed = encode(x, gain, encoder_project, encoder_mix)
 
-    before = ()
-    for step in range(4):
-        first = encoded if step == 0 else turned("y", 4, -step)(encoded)
-        before = pairs_of(step, first, across(first), weight, before)
-    sources, pairs = before
+    column = [encoded] + [turned("y", 4, -step)(encoded) for step in range(1, 4)]
+    sources = column + [across(one) for one in column]
+    normed, mixed, _ = lax.optimization_barrier((normed, mixed, sources[6]))
     operands = lax.all_gather(spread(normed, mixed), TP, tiled=True)
 
     named = span_neighbours.reshape(-1) % 8
     slots = (named % 2 != core) * 4 + (named // 2 - y) % 4
     result, grad_queries, grad_pairs = cross(
-        slots.astype(jnp.int32), decoder_queries, grad_output, pairs.reshape(8, TOK, 2 * inner)
+        slots.astype(jnp.int32), decoder_queries, grad_output, weight, sources
     )
 
-    far = nt(grad_pairs[4:].reshape(4 * TOK, 2 * inner), weight).astype(bf16)
+    far = nt(grad_pairs[4 * TOK :], weight).astype(bf16)
     brought = across(far)
-    near = nt(grad_pairs[:4].reshape(4 * TOK, 2 * inner), weight)
-    grad_weight = tn(sources.reshape(8 * TOK, ENC), grad_pairs.reshape(8 * TOK, 2 * inner)).astype(bf16)
+    near = nt(grad_pairs[: 4 * TOK], weight)
+
+    at_x = lax.axis_index("xh") * 2 + lax.axis_index("xl")
+    at_z = lax.axis_index("z")
+    steps = jnp.arange(4, dtype=jnp.int32)
+    order = jnp.concatenate([(at_x + steps) % 4, 4 + (at_z + steps) % 4])
+    blocks = weight_blocks(order, grad_pairs, sources)
+    lines = plane_sum(blocks[:4], ("xh", "xl"), "z", at_z) + plane_sum(
+        blocks[4:], "z", ("xh", "xl"), at_x
+    )
+    grad_cross = placed_blocks(jnp.stack([at_x, at_z]).astype(jnp.int32), lines)
+    grad_cross = grad_cross.reshape(ENC, heads, 2, HS).swapaxes(1, 2).reshape(cross_pairs.shape)
+
     summed = (near + brought.astype(f32)).reshape(4, TOK, ENC)
     total = summed[0]
     for step in range(1, 4):
         total += turned("y", 4, step)(summed[step].astype(bf16)).astype(f32)
     grad_encoded = total.astype(bf16)
-
-    grad_cross = lax.psum(grad_weight, PLANE)
-    grad_cross = grad_cross.astype(f32).reshape(cross_pairs.shape)
 
     parts = backward(grad_encoded, projected, encoder_mix)
     all_parts = lax.all_to_all(parts, TP, 0, 0, tiled=True).reshape(8 * TOK, LANES)

time: 226 us -> 251 us (1.11)
  starting transfers between devices: 43.6 us -> 82.7 us
  waiting for transfers between devices: 82 us -> 66.9 us
  Pallas kernels: 38.4 us -> 45.3 us
  matrix products: 18 us -> 13.5 us
    ppermute x6 -> x30, waiting for transfers between devices: 16.5 us -> 59.9 us  [turned(): return lambda x: lax.ppermute(x, axis, pairs)]
    ppermute x6 -> x30, starting transfers between devices: 15.7 us -> 53.8 us  [turned(): return lambda x: lax.ppermute(x, axis, pairs)]
    psum x1 -> x0, waiting for transfers between devices: 33.2 us -> none  [shards(): grad_cross = lax.psum(grad_weight, PLANE)]
    all_to_all x1, waiting for transfers between devices: 15.1 us -> 0.01 us  [shards(): lax.all_to_all(parts, TP, 0, 0, tiled=True).reshape(8 * TOK, LANES)]
    ppermute x2, waiting for transfers between devices: 17.2 us -> 3.21 us  [flipped(): return lax.ppermute(x, ('y', 'c', 'xl', 'z'), pairs)]
    reshape x1 -> x0, other arithmetic: 7.6 us -> none  [shards(): grad_cross = grad_cross.astype(f32).reshape(cross_pairs.shape)]
    dot_general x4 -> x3, matrix products: 18 us -> 13.5 us  [dot(): lax.dot_general(a, b, ((contract[:1], contract[1:]), ((), ())), preferred...]
    convert_element_type x0 -> x4, other arithmetic: none -> 4.27 us  [the longest x2 3.19 us: plane_sum(): total = total.astype(bf16)]
  transfers between devices with their start and end apart: 17 -> 40, of which waited for: 8 -> 12; matrix products, arithmetic and copies ran while one was open for 17% -> 11% of each run, Pallas kernels for 15% -> 16%
where the time goes in v2:
time: 251 us; the launch traced here: 250 us
  starting transfers between devices  82.7 us (33%)
  waiting for transfers between devices  66.9 us (27%)
  Pallas kernels  45.3 us (18%)
  local copies, waits for them, and re-layouts  20.8 us (8%)
  between operations  14.3 us (6%)
  matrix products  13.5 us (5%)
  other arithmetic  6.09 us (2%)
    ppermute x30, waiting for transfers between devices, turned(): return lambda x: lax.ppermute(x, axis, pairs)  59.9 us
    ppermute x30, starting transfers between devices, turned(): return lambda x: lax.ppermute(x, axis, pairs)  53.8 us
    pallas_call x1, Pallas kernels, cross(): pl.pallas_call(cross_kernel, grid_spec=pltpu.PrefetchScalarGridSpec(num_s...  20 us
    dot_general x3, matrix products, dot(): lax.dot_general(a, b, ((contract[:1], contract[1:]), ((), ())), preferred...  13.5 us
    all_to_all x1, starting transfers between devices, shards(): arrived = lax.all_to_all(encoder_grad, FINE, 0, 0, tiled=True).astype(f32)  11.3 us
    unnamed x42, local copies, waits for them, and re-layouts  10.6 us
    reshape x1, local copies, waits for them, and re-layouts, shards(): cross_pairs.reshape(ENC, 2, heads, HS).swapaxes(1, 2)  7.24 us
    all_to_all x1, starting transfers between devices, shards(): lax.all_to_all(parts, TP, 0, 0, tiled=True).reshape(8 * TOK, LANES)  7.14 us
  transfers between devices with their start and end apart: 40, of which 12 were waited for; matrix products, arithmetic and copies ran while one was open for 11% of the time, Pallas kernels for 16%

profile of v2, /device:TPU:1, one launch (start us, length us, event | category | flops | bytes accessed | tf_op | source)
XLA Modules:
  0.0 249.7 jit_solution(3315672841544166593)
XLA Ops:
  7.2 4.9 %collective-permute-start = (bf16[128,896]{1,0:T(8,128)(2,1)}, bf16[128,896]{1,0:T(8,128)(2,1)S(1)}, u32[]{:S(2)}, u32[]{:S(2)}) collective-permute-start(bf16[128,896]{1,0:T(8,128)(2,1)} %bitcast.45), channel_id=1, source_target_pairs={{0,0},{1,8},{2,16},{3,24},{4,32},{5,40},{6,48},{7,56},{8,1},{9,9},... | collective-permute-start | bytes 688136 | tf_op jit(solution)/shard_map/ppermute | solution.py:37
  12.8 3.2 %collective-permute-done.x_ref = bf16[128,896]{1,0:T(8,128)(2,1)S(1)} collective-permute-done((bf16[128,896]{1,0:T(8,128)(2,1)}, bf16[128,896]{1,0:T(8,128)(2,1)S(1)}, u32[]{:S(2)}, u32[]{:S(2)}) %collective-permute-start) | collective-permute-done | bytes 229408 | tf_op jit(solution)/shard_map/ppermute | solution.py:37
  16.1 2.4 copy-done
  18.4 1.4 copy-done.2
  19.8 3.5 %shard_map.127 = (bf16[128,896]{1,0:T(8,128)(2,1)S(1)}, bf16[128,896]{1,0:T(8,128)(2,1)S(1)}, bf16[128,2688]{1,0:T(8,128)(2,1)S(1)}, bf16[128,896]{1,0:T(8,128)(2,1)S(1)}) custom-call(bf16[128,896]{1,0:T(8,128)(2,1)S(1)} %collective-permute-done.x_ref, f32[1,896]{1,0:T(1,128)S(1)} %reshape.56.gain_ref, bf16[896,2688]{1,0:T(8,128)(2,1)S(1)} %copy-done, ...), custom_call_target="tpu_custom_call" | custom-call | flops 1000000000 | bytes 8000000 | tf_op jit(solution)/shard_map/pallas_call | solution.py:90
  23.4 11.9 %collective-permute-start.2 = (bf16[128,896]{1,0:T(8,128)(2,1)S(1)}, bf16[128,896]{1,0:T(8,128)(2,1)S(1)}, u32[]{:S(2)}, u32[]{:S(2)}) collective-permute-start(bf16[128,896]{1,0:T(8,128)(2,1)S(1)} %get-tuple-element.23.rest_0_), channel_id=1, source_target_pairs={{0,32},{16,48},{32,0},{48,16},{1,33},{17,49},{33,1},{49,17},{2,34}... | collective-permute-start | bytes 688136 | tf_op jit(solution)/shard_map/ppermute | solution.py:28
  35.3 4.4 %collective-permute-done.2.rest_2_ = bf16[128,896]{1,0:T(8,128)(2,1)S(1)} collective-permute-done((bf16[128,896]{1,0:T(8,128)(2,1)S(1)}, bf16[128,896]{1,0:T(8,128)(2,1)S(1)}, u32[]{:S(2)}, u32[]{:S(2)}) %collective-permute-start.2) | collective-permute-done | bytes 229408 | tf_op jit(solution)/shard_map/ppermute | solution.py:28
  39.7 1.5 collective-permute-done.6.rest_6_
  41.2 1.8 shard_map.131
  43.0 5.6 %collective-permute-start.1 = (bf16[128,896]{1,0:T(8,128)(2,1)S(1)}, bf16[128,896]{1,0:T(8,128)(2,1)S(1)}, u32[]{:S(2)}, u32[]{:S(2)}) collective-permute-start(bf16[128,896]{1,0:T(8,128)(2,1)S(1)} %get-tuple-element.23.rest_0_), channel_id=1, source_target_pairs={{0,48},{16,0},{32,16},{48,32},{1,49},{17,1},{33,17},{49,33},{2,50}... | collective-permute-start | bytes 688136 | tf_op jit(solution)/shard_map/ppermute | solution.py:28
  49.2 3.9 %collective-permute-done.1.rest_1_ = bf16[128,896]{1,0:T(8,128)(2,1)S(1)} collective-permute-done((bf16[128,896]{1,0:T(8,128)(2,1)S(1)}, bf16[128,896]{1,0:T(8,128)(2,1)S(1)}, u32[]{:S(2)}, u32[]{:S(2)}) %collective-permute-start.1) | collective-permute-done | bytes 229408 | tf_op jit(solution)/shard_map/ppermute | solution.py:28
  54.4 1.9 collective-permute-done.3.rest_3_
  56.3 1.5 collective-permute-start.7
  58.0 7.2 %reshape.55.weight_ref = bf16[896,2048]{1,0:T(8,128)(2,1)} reshape(bf16[896,8,2,128]{3,2,1,0:T(2,128)(2,1)} %bitcast.33) | data formatting | bytes 7340032 | tf_op jit(solution)/shard_map/reshape | solution.py:327
  65.3 2.1 copy-done.4
  67.4 20.0 %shard_map.128 = (bf16[4,64,1024]{2,1,0:T(8,128)(2,1)}, bf16[4,64,1024]{2,1,0:T(8,128)(2,1)}, bf16[1024,2048]{1,0:T(8,128)(2,1)S(1)}) custom-call(s32[8]{0:T(128)S(1)} %fusion.17.slots_ref, bf16[4,64,1024]{2,1,0:T(8,128)(2,1)S(1)} %copy-done.6, bf16[4,64,1024]{2,1,0:T(8,128)(2,1)S(1)} %copy-done.7, bf16[896,2048]{1,0:T(8,128)(2,1)S(1)} %copy-done.4, ...), custom_call_target="tpu_custom_call" | custom-call | flops 12000000000 | bytes 12000000 | tf_op jit(solution)/shard_map/pallas_call | solution.py:153
  87.4 2.4 fusion.10
  90.1 2.3 collective-permute-done.32
  92.3 6.3 %fusion.24 = (bf16[512,896]{1,0:T(8,128)(2,1)S(1)}, f32[512,896]{1,0:T(8,128)}) fusion(bf16[512,896]{1,0:T(8,128)(2,1)S(1)} %collective-permute-done.32, bf16[896,2048]{1,0:T(8,128)(2,1)} %reshape.55.weight_ref, bf16[1024,2048]{1,0:T(8,128)(2,1)} %copy-done.17), kind=kOutput, calls=%fused_computation.56 | convolution fusion | flops 1880424448 | bytes 9437184 | tf_op jit(solution)/shard_map/dot_general | solution.py:41
  99.5 1.6 collective-permute-start.34
  102.2 6.0 %shard_map.129 = (bf16[896,256]{1,0:T(8,128)(2,1)S(1)}, bf16[896,256]{1,0:T(8,128)(2,1)}, bf16[896,256]{1,0:T(8,128)(2,1)S(1)}, bf16[896,256]{1,0:T(8,128)(2,1)}...) custom-call(s32[8]{0:T(128)S(1)} %pad_add_fusion.1.order_ref, ...), custom_call_target="tpu_custom_call" | custom-call | flops 4000000000 | bytes 10000000 | tf_op jit(solution)/shard_map/pallas_call | solution.py:189
  109.9 1.5 collective-permute-start.20
  112.8 1.7 collective-permute-start.22
  116.0 1.4 fusion.16.grad_ref
  117.4 5.8 %collective-permute-done.20 = bf16[896,256]{1,0:T(8,128)(2,1)} collective-permute-done((bf16[896,256]{1,0:T(8,128)(2,1)}, bf16[896,256]{1,0:T(8,128)(2,1)}, u32[]{:S(2)}, u32[]{:S(2)}) %collective-permute-start.20) | collective-permute-done | bytes 458784 | tf_op jit(solution)/shard_map/ppermute | solution.py:28
  123.1 2.7 %collective-permute-start.9 = (bf16[896,256]{1,0:T(8,128)(2,1)}, bf16[896,256]{1,0:T(8,128)(2,1)}, u32[]{:S(2)}, u32[]{:S(2)}) collective-permute-start(bf16[896,256]{1,0:T(8,128)(2,1)} %copy-done.8), channel_id=1, source_target_pairs={{0,64},{4,68},{64,0},{68,4},{1,65},{5,69},{65,1},{69,5},{2,66},{6,... | collective-permute-start | bytes 1376264 | tf_op jit(solution)/shard_map/ppermute | solution.py:28
  125.9 4.6 %shard_map.132.parts_ref = bf16[8,128,512]{2,1,0:T(8,128)(2,1)} custom-call(bf16[128,896]{1,0:T(8,128)(2,1)S(1)} %fusion.16.grad_ref, bf16[128,2688]{1,0:T(8,128)(2,1)S(1)} %get-tuple-element.39.projected_ref, bf16[896,896]{1,0:T(8,128)(2,1)S(1)} %copy-done.3), custom_call_target="tpu_custom_call" | custom-call | flops 600000000 | bytes 4000000 | tf_op jit(solution)/shard_map/pallas_call | solution.py:281
  130.5 7.1 %all-to-all-start = ((bf16[8,128,512]{2,1,0:T(8,128)(2,1)}), bf16[8,128,512]{2,1,0:T(8,128)(2,1)}, u32[]{:S(2)}, u32[]{:S(2)}) async-start(bf16[8,128,512]{2,1,0:T(8,128)(2,1)} %shard_map.132.parts_ref), calls=%async_computation | async-start | bytes 2097152 | tf_op jit(solution)/shard_map/all_to_all | solution.py:364
  137.7 1.7 add_convert_fusion
  139.8 2.3 collective-permute-start.25
  142.1 1.5 add_convert_fusion.1
  143.7 5.0 %collective-permute-start.11 = (bf16[224,256]{1,0:T(8,128)(2,1)S(1)}, bf16[224,256]{1,0:T(8,128)(2,1)}, u32[]{:S(2)}, u32[]{:S(2)}) collective-permute-start(bf16[224,256]{1,0:T(8,128)(2,1)S(1)} %get-tuple-element.46), channel_id=1, source_target_pairs={{0,1},{1,2},{2,3},{3,0},{4,5},{5,6},{6,7},{7,4},{8,9},{9,10},{10,1... | collective-permute-start | bytes 344072 | tf_op jit(solution)/shard_map/ppermute | solution.py:28
  148.7 2.6 %collective-permute-start.12 = (bf16[224,256]{1,0:T(8,128)(2,1)S(1)}, bf16[224,256]{1,0:T(8,128)(2,1)}, u32[]{:S(2)}, u32[]{:S(2)}) collective-permute-start(bf16[224,256]{1,0:T(8,128)(2,1)S(1)} %get-tuple-element.48), channel_id=1, source_target_pairs={{0,2},{1,3},{2,0},{3,1},{4,6},{5,7},{6,4},{7,5},{8,10},{9,11},{10,... | collective-permute-start | bytes 344072 | tf_op jit(solution)/shard_map/ppermute | solution.py:28
  152.2 1.9 collective-permute-start.27
  154.2 4.8 %fusion.13 = bf16[128,8,512]{2,1,0:T(8,128)(2,1)} fusion(bf16[1024,512]{1,0:T(8,128)(2,1)} %bitcast.16, bf16[1024,2048]{1,0:T(8,128)(2,1)} %all-gather.2.cloned.1.call-done, pred[]{:T(512)S(6)} %lt.106), kind=kOutput, calls=%fused_computation.12 | convolution fusion | flops 1075314688 | bytes 6291457 | tf_op jit(solution)/shard_map/dot_general | solution.py:41
  158.9 11.3 %all-to-all-start.1 = ((bf16[128,8,512]{2,1,0:T(8,128)(2,1)}), bf16[128,8,512]{2,1,0:T(8,128)(2,1)S(1)}, u32[]{:S(2)}, u32[]{:S(2)}) async-start(bf16[128,8,512]{2,1,0:T(8,128)(2,1)} %fusion.13), calls=%async_computation.1 | async-start | bytes 2097152 | tf_op jit(solution)/shard_map/all_to_all | solution.py:367
  170.2 3.3 %collective-permute-start.13 = (bf16[224,256]{1,0:T(8,128)(2,1)S(1)}, bf16[224,256]{1,0:T(8,128)(2,1)S(1)}, u32[]{:S(2)}, u32[]{:S(2)}) collective-permute-start(bf16[224,256]{1,0:T(8,128)(2,1)S(1)} %get-tuple-element.47), channel_id=1, source_target_pairs={{0,3},{1,0},{2,1},{3,2},{4,7},{5,4},{6,5},{7,6},{8,11},{9,8},{10,9... | collective-permute-start | bytes 344072 | tf_op jit(solution)/shard_map/ppermute | solution.py:28
  174.0 11.4 %collective-permute-done.13 = bf16[224,256]{1,0:T(8,128)(2,1)S(1)} collective-permute-done((bf16[224,256]{1,0:T(8,128)(2,1)S(1)}, bf16[224,256]{1,0:T(8,128)(2,1)S(1)}, u32[]{:S(2)}, u32[]{:S(2)}) %collective-permute-start.13) | collective-permute-done | bytes 114720 | tf_op jit(solution)/shard_map/ppermute | solution.py:28
  186.4 3.9 %collective-permute-start.14 = (bf16[224,256]{1,0:T(8,128)(2,1)S(1)}, bf16[224,256]{1,0:T(8,128)(2,1)S(1)}, u32[]{:S(2)}, u32[]{:S(2)}) collective-permute-start(bf16[224,256]{1,0:T(8,128)(2,1)S(1)} %add_convert_fusion.3), channel_id=1, source_target_pairs={{0,3},{1,0},{2,1},{3,2},{4,7},{5,4},{6,5},{7,6},{8,11},{9,8},{10,9... | collective-permute-start | bytes 344072 | tf_op jit(solution)/shard_map/ppermute | solution.py:28
  191.0 2.3 collective-permute-start.30
  193.3 17.1 %collective-permute-done.14 = bf16[224,256]{1,0:T(8,128)(2,1)S(1)} collective-permute-done((bf16[224,256]{1,0:T(8,128)(2,1)S(1)}, bf16[224,256]{1,0:T(8,128)(2,1)S(1)}, u32[]{:S(2)}, u32[]{:S(2)}) %collective-permute-start.14) | collective-permute-done | bytes 114720 | tf_op jit(solution)/shard_map/ppermute | solution.py:28
  210.6 1.4 collective-permute-start.19
  212.0 2.4 copy-done.1
  214.3 3.0 %shard_map.133 = bf16[128,896]{1,0:T(8,128)(2,1)S(1)} custom-call(bf16[128,896]{1,0:T(8,128)(2,1)S(1)} %collective-permute-done.x_ref, f32[1,896]{1,0:T(1,128)S(1)} %reshape.56.gain_ref, bf16[896,2688]{1,0:T(8,128)(2,1)S(1)} %copy-done.1, bf16[8,128,512]{2,1,0:T(8,128)(2,1)} %shard_map.132.parts_ref, bf16[128,896]{1,0:T(8,128)(2,1)S(1)} %fusion.16.grad_ref), custom_call_target="tpu_custom_call" | custom-call | flops 600000000 | bytes 6000000 | tf_op jit(solution)/shard_map/pallas_call | solution.py:304
  217.3 1.9 collective-permute-start.36
  219.3 5.1 %collective-permute-done.31.rest_7_ = bf16[4,224,256]{2,1,0:T(8,128)(2,1)S(1)} collective-permute-done((bf16[4,224,256]{2,1,0:T(8,128)(2,1)S(1)}, bf16[4,224,256]{2,1,0:T(8,128)(2,1)S(1)}, u32[]{:S(2)}, u32[]{:S(2)}) %collective-permute-start.31) | collective-permute-done | bytes 458784 | tf_op jit(solution)/shard_map/ppermute | solution.py:28
  224.4 10.0 %collective-permute-done.19.rest_3_ = bf16[4,224,256]{2,1,0:T(8,128)(2,1)S(1)} collective-permute-done((bf16[4,224,256]{2,1,0:T(8,128)(2,1)S(1)}, bf16[4,224,256]{2,1,0:T(8,128)(2,1)S(1)}, u32[]{:S(2)}, u32[]{:S(2)}) %collective-permute-start.19) | collective-permute-done | bytes 458784 | tf_op jit(solution)/shard_map/ppermute | solution.py:28
  234.3 6.4 %shard_map.130 = f32[14336,128]{1,0:T(8,128)} custom-call(s32[2]{0:T(128)S(1)} %pad_add_fusion.at_ref, bf16[4,224,256]{2,1,0:T(8,128)(2,1)S(1)} %pad_maximum_fusion.rest_0_, bf16[4,224,256]{2,1,0:T(8,128)(2,1)S(1)} %collective-permute-done.17.rest_1_, bf16[4,224,256]{2,1,0:T(8,128)(2,1)S(1)} %collective-permute-done.18.rest_2_, ...), custom_call_target="tpu_custom_call" | custom-call | flops 1000000 | bytes 11000000 | tf_op jit(solution)/shard_map/pallas_call | solution.py:232
  (105 shorter events, 15.6 us)
Async XLA Ops:
  7.2 147.0 %all-gather.2.cloned.1.call-start = ((), (), s32[]{:S(2)}) async-start(), calls=%async_computation.2 | async-start | bytes 4718592 | tf_op jit(solution)/shard_map/all_gather | solution.py:334
  7.2 8.8 %collective-permute-start = (bf16[128,896]{1,0:T(8,128)(2,1)}, bf16[128,896]{1,0:T(8,128)(2,1)S(1)}, u32[]{:S(2)}, u32[]{:S(2)}) collective-permute-start(bf16[128,896]{1,0:T(8,128)(2,1)} %bitcast.45), channel_id=1, source_target_pairs={{0,0},{1,8},{2,16},{3,24},{4,32},{5,40},{6,48},{7,56},{8,1},{9,9},... | collective-permute-start | bytes 688136 | tf_op jit(solution)/shard_map/ppermute | solution.py:37
  19.8 38.0 %copy-start.19 = (s32[4,2]{0,1:T(2,128)S(1)}, s32[4,2]{0,1:T(2,128)}, u32[]{:S(2)}) copy-start(s32[4,2]{0,1:T(2,128)} %param.14) | copy-start | bytes 100
  23.4 16.3 %collective-permute-start.2 = (bf16[128,896]{1,0:T(8,128)(2,1)S(1)}, bf16[128,896]{1,0:T(8,128)(2,1)S(1)}, u32[]{:S(2)}, u32[]{:S(2)}) collective-permute-start(bf16[128,896]{1,0:T(8,128)(2,1)S(1)} %get-tuple-element.23.rest_0_), channel_id=1, source_target_pairs={{0,32},{16,48},{32,0},{48,16},{1,33},{17,49},{33,1},{49,17},{2,34}... | collective-permute-start | bytes 688136 | tf_op jit(solution)/shard_map/ppermute | solution.py:28
  39.7 1.5 collective-permute-start.6
  41.2 24.1 %copy-start.9 = (bf16[128,896]{1,0:T(8,128)(2,1)}, bf16[128,896]{1,0:T(8,128)(2,1)S(1)}, u32[]{:S(2)}) copy-start(bf16[128,896]{1,0:T(8,128)(2,1)S(1)} %collective-permute-done.6.rest_6_) | copy-start | bytes 688132
  43.0 10.2 %collective-permute-start.1 = (bf16[128,896]{1,0:T(8,128)(2,1)S(1)}, bf16[128,896]{1,0:T(8,128)(2,1)S(1)}, u32[]{:S(2)}, u32[]{:S(2)}) collective-permute-start(bf16[128,896]{1,0:T(8,128)(2,1)S(1)} %get-tuple-element.23.rest_0_), channel_id=1, source_target_pairs={{0,48},{16,0},{32,16},{48,32},{1,49},{17,1},{33,17},{49,33},{2,50}... | collective-permute-start | bytes 688136 | tf_op jit(solution)/shard_map/ppermute | solution.py:28
  48.6 7.7 %collective-permute-start.3 = (bf16[128,896]{1,0:T(8,128)(2,1)S(1)}, bf16[128,896]{1,0:T(8,128)(2,1)S(1)}, u32[]{:S(2)}, u32[]{:S(2)}) collective-permute-start(bf16[128,896]{1,0:T(8,128)(2,1)S(1)} %get-tuple-element.23.rest_0_), channel_id=1, source_target_pairs={{0,16},{16,32},{32,48},{48,0},{1,17},{17,33},{33,49},{49,1},{2,18}... | collective-permute-start | bytes 688136 | tf_op jit(solution)/shard_map/ppermute | solution.py:28
  48.6 16.7 %collective-permute-start.4 = (bf16[128,896]{1,0:T(8,128)(2,1)S(1)}, bf16[128,896]{1,0:T(8,128)(2,1)S(1)}, u32[]{:S(2)}, u32[]{:S(2)}) collective-permute-start(bf16[128,896]{1,0:T(8,128)(2,1)S(1)} %get-tuple-element.23.rest_0_), channel_id=1, source_target_pairs={{0,8},{8,0},{1,9},{9,1},{2,10},{10,2},{3,11},{11,3},{4,12},{12,4},... | collective-permute-start | bytes 688136 | tf_op jit(solution)/shard_map/ppermute | solution.py:32
  53.2 12.1 %collective-permute-start.5 = (bf16[128,896]{1,0:T(8,128)(2,1)S(1)}, bf16[128,896]{1,0:T(8,128)(2,1)}, u32[]{:S(2)}, u32[]{:S(2)}) collective-permute-start(bf16[128,896]{1,0:T(8,128)(2,1)S(1)} %collective-permute-done.1.rest_1_), channel_id=1, source_target_pairs={{0,8},{8,0},{1,9},{9,1},{2,10},{10,2},{3,11},{11,3},{4,12},{12,4},... | collective-permute-start | bytes 688136 | tf_op jit(solution)/shard_map/ppermute | solution.py:32
  56.3 9.0 %collective-permute-start.7 = (bf16[128,896]{1,0:T(8,128)(2,1)S(1)}, bf16[128,896]{1,0:T(8,128)(2,1)}, u32[]{:S(2)}, u32[]{:S(2)}) collective-permute-start(bf16[128,896]{1,0:T(8,128)(2,1)S(1)} %collective-permute-done.3.rest_3_), channel_id=1, source_target_pairs={{0,8},{8,0},{1,9},{9,1},{2,10},{10,2},{3,11},{11,3},{4,12},{12,4},... | collective-permute-start | bytes 688136 | tf_op jit(solution)/shard_map/ppermute | solution.py:32
  65.3 22.1 %copy-start.15 = (bf16[128,896]{1,0:T(8,128)(2,1)}, bf16[128,896]{1,0:T(8,128)(2,1)S(1)}, u32[]{:S(2)}) copy-start(bf16[128,896]{1,0:T(8,128)(2,1)S(1)} %collective-permute-done.4.rest_4_) | copy-start | bytes 688132
  89.8 2.6 %collective-permute-start.32 = (bf16[512,896]{1,0:T(8,128)(2,1)S(1)}, bf16[512,896]{1,0:T(8,128)(2,1)S(1)}, u32[]{:S(2)}, u32[]{:S(2)}) collective-permute-start(bf16[512,896]{1,0:T(8,128)(2,1)S(1)} %fusion.10), channel_id=1, source_target_pairs={{0,8},{8,0},{1,9},{9,1},{2,10},{10,2},{3,11},{11,3},{4,12},{12,4},... | collective-permute-start | bytes 2752520 | tf_op jit(solution)/shard_map/ppermute | solution.py:32
  90.1 12.2 %copy-start.12 = (bf16[128,896]{1,0:T(8,128)(2,1)S(1)}, bf16[128,896]{1,0:T(8,128)(2,1)}, u32[]{:S(2)}) copy-start(bf16[128,896]{1,0:T(8,128)(2,1)} %copy-done.11) | copy-start | bytes 688132
  90.1 12.2 %copy-start.14 = (bf16[128,896]{1,0:T(8,128)(2,1)S(1)}, bf16[128,896]{1,0:T(8,128)(2,1)}, u32[]{:S(2)}) copy-start(bf16[128,896]{1,0:T(8,128)(2,1)} %copy-done.13) | copy-start | bytes 688132
  90.1 12.2 %copy-start.16 = (bf16[128,896]{1,0:T(8,128)(2,1)S(1)}, bf16[128,896]{1,0:T(8,128)(2,1)}, u32[]{:S(2)}) copy-start(bf16[128,896]{1,0:T(8,128)(2,1)} %copy-done.15) | copy-start | bytes 688132
  90.1 12.2 %copy-start.18 = (bf16[1024,2048]{1,0:T(8,128)(2,1)S(1)}, bf16[1024,2048]{1,0:T(8,128)(2,1)}, u32[]{:S(2)}) copy-start(bf16[1024,2048]{1,0:T(8,128)(2,1)} %copy-done.17) | copy-start | bytes 12582916
  99.5 13.3 %collective-permute-start.33 = (bf16[128,896]{1,0:T(8,128)(2,1)S(1)}, bf16[128,896]{1,0:T(8,128)(2,1)}, u32[]{:S(2)}, u32[]{:S(2)}) collective-permute-start(bf16[128,896]{1,0:T(8,128)(2,1)S(1)} %get-tuple-element.40), channel_id=1, source_target_pairs={{0,16},{16,32},{32,48},{48,0},{1,17},{17,33},{33,49},{49,1},{2,18}... | collective-permute-start | bytes 688136 | tf_op jit(solution)/shard_map/ppermute | solution.py:28
  99.5 15.0 %collective-permute-start.34 = (bf16[128,896]{1,0:T(8,128)(2,1)}, bf16[128,896]{1,0:T(8,128)(2,1)}, u32[]{:S(2)}, u32[]{:S(2)}) collective-permute-start(bf16[128,896]{1,0:T(8,128)(2,1)} %get-tuple-element.42), channel_id=1, source_target_pairs={{0,32},{16,48},{32,0},{48,16},{1,33},{17,49},{33,1},{49,17},{2,34}... | collective-permute-start | bytes 688136 | tf_op jit(solution)/shard_map/ppermute | solution.py:28
  101.1 24.8 %copy-start.3 = (bf16[896,896]{1,0:T(8,128)(2,1)S(1)}, bf16[896,896]{1,0:T(8,128)(2,1)}, u32[]{:S(2)}) copy-start(bf16[896,896]{1,0:T(8,128)(2,1)} %mix_ref.3) | copy-start | bytes 4816900
  101.1 14.2 %collective-permute-start.35 = (bf16[128,896]{1,0:T(8,128)(2,1)}, bf16[128,896]{1,0:T(8,128)(2,1)}, u32[]{:S(2)}, u32[]{:S(2)}) collective-permute-start(bf16[128,896]{1,0:T(8,128)(2,1)} %get-tuple-element.41), channel_id=1, source_target_pairs={{0,48},{16,0},{32,16},{48,32},{1,49},{17,1},{33,17},{49,33},{2,50}... | collective-permute-start | bytes 688136 | tf_op jit(solution)/shard_map/ppermute | solution.py:28
  109.9 13.3 %collective-permute-start.20 = (bf16[896,256]{1,0:T(8,128)(2,1)}, bf16[896,256]{1,0:T(8,128)(2,1)}, u32[]{:S(2)}, u32[]{:S(2)}) collective-permute-start(bf16[896,256]{1,0:T(8,128)(2,1)} %get-tuple-element.32), channel_id=1, source_target_pairs={{0,1},{1,2},{2,3},{3,0},{4,5},{5,6},{6,7},{7,4},{8,9},{9,10},{10,1... | collective-permute-start | bytes 1376264 | tf_op jit(solution)/shard_map/ppermute | solution.py:28
  111.4 26.3 %collective-permute-start.21 = (bf16[896,256]{1,0:T(8,128)(2,1)}, bf16[896,256]{1,0:T(8,128)(2,1)}, u32[]{:S(2)}, u32[]{:S(2)}) collective-permute-start(bf16[896,256]{1,0:T(8,128)(2,1)} %get-tuple-element.33), channel_id=1, source_target_pairs={{0,2},{1,3},{2,0},{3,1},{4,6},{5,7},{6,4},{7,5},{8,10},{9,11},{10,... | collective-permute-start | bytes 1376264 | tf_op jit(solution)/shard_map/ppermute | solution.py:28
  112.8 24.8 %collective-permute-start.22 = (bf16[896,256]{1,0:T(8,128)(2,1)}, bf16[896,256]{1,0:T(8,128)(2,1)}, u32[]{:S(2)}, u32[]{:S(2)}) collective-permute-start(bf16[896,256]{1,0:T(8,128)(2,1)} %get-tuple-element.34), channel_id=1, source_target_pairs={{0,3},{1,0},{2,1},{3,2},{4,7},{5,4},{6,5},{7,6},{8,11},{9,8},{10,9... | collective-permute-start | bytes 1376264 | tf_op jit(solution)/shard_map/ppermute | solution.py:28
  114.5 25.2 %collective-permute-start.10 = (bf16[896,256]{1,0:T(8,128)(2,1)}, bf16[896,256]{1,0:T(8,128)(2,1)}, u32[]{:S(2)}, u32[]{:S(2)}) collective-permute-start(bf16[896,256]{1,0:T(8,128)(2,1)} %get-tuple-element.30), channel_id=1, source_target_pairs={{0,68},{4,0},{64,4},{68,64},{1,69},{5,1},{65,5},{69,65},{2,70},{6,... | collective-permute-start | bytes 1376264 | tf_op jit(solution)/shard_map/ppermute | solution.py:28
  115.3 26.8 %collective-permute-start.8 = (bf16[896,256]{1,0:T(8,128)(2,1)}, bf16[896,256]{1,0:T(8,128)(2,1)}, u32[]{:S(2)}, u32[]{:S(2)}) collective-permute-start(bf16[896,256]{1,0:T(8,128)(2,1)} %get-tuple-element.28), channel_id=1, source_target_pairs={{0,4},{4,64},{64,68},{68,0},{1,5},{5,65},{65,69},{69,1},{2,6},{6,6... | collective-permute-start | bytes 1376264 | tf_op jit(solution)/shard_map/ppermute | solution.py:28
  123.1 19.0 %collective-permute-start.9 = (bf16[896,256]{1,0:T(8,128)(2,1)}, bf16[896,256]{1,0:T(8,128)(2,1)}, u32[]{:S(2)}, u32[]{:S(2)}) collective-permute-start(bf16[896,256]{1,0:T(8,128)(2,1)} %copy-done.8), channel_id=1, source_target_pairs={{0,64},{4,68},{64,0},{68,4},{1,65},{5,69},{65,1},{69,5},{2,66},{6,... | collective-permute-start | bytes 1376264 | tf_op jit(solution)/shard_map/ppermute | solution.py:28
  130.5 23.6 %all-to-all-start = ((bf16[8,128,512]{2,1,0:T(8,128)(2,1)}), bf16[8,128,512]{2,1,0:T(8,128)(2,1)}, u32[]{:S(2)}, u32[]{:S(2)}) async-start(bf16[8,128,512]{2,1,0:T(8,128)(2,1)} %shard_map.132.parts_ref), calls=%async_computation | async-start | bytes 2097152 | tf_op jit(solution)/shard_map/all_to_all | solution.py:364
  139.4 11.9 %collective-permute-start.23 = (bf16[224,256]{1,0:T(8,128)(2,1)S(1)}, bf16[224,256]{1,0:T(8,128)(2,1)S(1)}, u32[]{:S(2)}, u32[]{:S(2)}) collective-permute-start(bf16[224,256]{1,0:T(8,128)(2,1)S(1)} %get-tuple-element.43), channel_id=1, source_target_pairs={{0,4},{4,64},{64,68},{68,0},{1,5},{5,65},{65,69},{69,1},{2,6},{6,6... | collective-permute-start | bytes 344072 | tf_op jit(solution)/shard_map/ppermute | solution.py:28
  139.4 11.8 %collective-permute-start.24 = (bf16[224,256]{1,0:T(8,128)(2,1)S(1)}, bf16[224,256]{1,0:T(8,128)(2,1)S(1)}, u32[]{:S(2)}, u32[]{:S(2)}) collective-permute-start(bf16[224,256]{1,0:T(8,128)(2,1)S(1)} %get-tuple-element.45), channel_id=1, source_target_pairs={{0,64},{4,68},{64,0},{68,4},{1,65},{5,69},{65,1},{69,5},{2,66},{6,... | collective-permute-start | bytes 344072 | tf_op jit(solution)/shard_map/ppermute | solution.py:28
  139.8 11.5 %collective-permute-start.25 = (bf16[224,256]{1,0:T(8,128)(2,1)S(1)}, bf16[224,256]{1,0:T(8,128)(2,1)S(1)}, u32[]{:S(2)}, u32[]{:S(2)}) collective-permute-start(bf16[224,256]{1,0:T(8,128)(2,1)S(1)} %get-tuple-element.44), channel_id=1, source_target_pairs={{0,68},{4,0},{64,4},{68,64},{1,69},{5,1},{65,5},{69,65},{2,70},{6,... | collective-permute-start | bytes 344072 | tf_op jit(solution)/shard_map/ppermute | solution.py:28
  143.7 30.3 %collective-permute-start.11 = (bf16[224,256]{1,0:T(8,128)(2,1)S(1)}, bf16[224,256]{1,0:T(8,128)(2,1)}, u32[]{:S(2)}, u32[]{:S(2)}) collective-permute-start(bf16[224,256]{1,0:T(8,128)(2,1)S(1)} %get-tuple-element.46), channel_id=1, source_target_pairs={{0,1},{1,2},{2,3},{3,0},{4,5},{5,6},{6,7},{7,4},{8,9},{9,10},{10,1... | collective-permute-start | bytes 344072 | tf_op jit(solution)/shard_map/ppermute | solution.py:28
  148.7 25.3 %collective-permute-start.12 = (bf16[224,256]{1,0:T(8,128)(2,1)S(1)}, bf16[224,256]{1,0:T(8,128)(2,1)}, u32[]{:S(2)}, u32[]{:S(2)}) collective-permute-start(bf16[224,256]{1,0:T(8,128)(2,1)S(1)} %get-tuple-element.48), channel_id=1, source_target_pairs={{0,2},{1,3},{2,0},{3,1},{4,6},{5,7},{6,4},{7,5},{8,10},{9,11},{10,... | collective-permute-start | bytes 344072 | tf_op jit(solution)/shard_map/ppermute | solution.py:28
  151.4 18.9 %collective-permute-start.26 = (bf16[224,256]{1,0:T(8,128)(2,1)S(1)}, bf16[224,256]{1,0:T(8,128)(2,1)S(1)}, u32[]{:S(2)}, u32[]{:S(2)}) collective-permute-start(bf16[224,256]{1,0:T(8,128)(2,1)S(1)} %add_convert_fusion.2), channel_id=1, source_target_pairs={{0,68},{4,0},{64,4},{68,64},{1,69},{5,1},{65,5},{69,65},{2,70},{6,... | collective-permute-start | bytes 344072 | tf_op jit(solution)/shard_map/ppermute | solution.py:28
  152.2 21.4 %collective-permute-start.27 = (bf16[224,256]{1,0:T(8,128)(2,1)S(1)}, bf16[224,256]{1,0:T(8,128)(2,1)S(1)}, u32[]{:S(2)}, u32[]{:S(2)}) collective-permute-start(bf16[224,256]{1,0:T(8,128)(2,1)S(1)} %add_convert_fusion.2), channel_id=1, source_target_pairs={{0,64},{4,68},{64,0},{68,4},{1,65},{5,69},{65,1},{69,5},{2,66},{6,... | collective-permute-start | bytes 344072 | tf_op jit(solution)/shard_map/ppermute | solution.py:28
  154.1 19.4 %collective-permute-start.28 = (bf16[224,256]{1,0:T(8,128)(2,1)S(1)}, bf16[224,256]{1,0:T(8,128)(2,1)S(1)}, u32[]{:S(2)}, u32[]{:S(2)}) collective-permute-start(bf16[224,256]{1,0:T(8,128)(2,1)S(1)} %add_convert_fusion.2), channel_id=1, source_target_pairs={{0,4},{4,64},{64,68},{68,0},{1,5},{5,65},{65,69},{69,1},{2,6},{6,6... | collective-permute-start | bytes 344072 | tf_op jit(solution)/shard_map/ppermute | solution.py:28
  158.9 81.8 %all-to-all-start.1 = ((bf16[128,8,512]{2,1,0:T(8,128)(2,1)}), bf16[128,8,512]{2,1,0:T(8,128)(2,1)S(1)}, u32[]{:S(2)}, u32[]{:S(2)}) async-start(bf16[128,8,512]{2,1,0:T(8,128)(2,1)} %fusion.13), calls=%async_computation.1 | async-start | bytes 2097152 | tf_op jit(solution)/shard_map/all_to_all | solution.py:367
  170.2 15.2 %collective-permute-start.13 = (bf16[224,256]{1,0:T(8,128)(2,1)S(1)}, bf16[224,256]{1,0:T(8,128)(2,1)S(1)}, u32[]{:S(2)}, u32[]{:S(2)}) collective-permute-start(bf16[224,256]{1,0:T(8,128)(2,1)S(1)} %get-tuple-element.47), channel_id=1, source_target_pairs={{0,3},{1,0},{2,1},{3,2},{4,7},{5,4},{6,5},{7,6},{8,11},{9,8},{10,9... | collective-permute-start | bytes 344072 | tf_op jit(solution)/shard_map/ppermute | solution.py:28
  173.6 37.0 %collective-permute-start.29 = (bf16[4,224,256]{2,1,0:T(8,128)(2,1)S(1)}, bf16[4,224,256]{2,1,0:T(8,128)(2,1)S(1)}, u32[]{:S(2)}, u32[]{:S(2)}) collective-permute-start(bf16[4,224,256]{2,1,0:T(8,128)(2,1)S(1)} %pad_maximum_fusion.1.rest_4_), channel_id=1, source_target_pairs={{0,3},{1,0},{2,1},{3,2},{4,7},{5,4},{6,5},{7,6},{8,11},{9,8},{10,9... | collective-permute-start | bytes 1376264 | tf_op jit(solution)/shard_map/ppermute | solution.py:28
  186.4 23.9 %collective-permute-start.14 = (bf16[224,256]{1,0:T(8,128)(2,1)S(1)}, bf16[224,256]{1,0:T(8,128)(2,1)S(1)}, u32[]{:S(2)}, u32[]{:S(2)}) collective-permute-start(bf16[224,256]{1,0:T(8,128)(2,1)S(1)} %add_convert_fusion.3), channel_id=1, source_target_pairs={{0,3},{1,0},{2,1},{3,2},{4,7},{5,4},{6,5},{7,6},{8,11},{9,8},{10,9... | collective-permute-start | bytes 344072 | tf_op jit(solution)/shard_map/ppermute | solution.py:28
  190.3 20.0 %collective-permute-start.15 = (bf16[224,256]{1,0:T(8,128)(2,1)S(1)}, bf16[224,256]{1,0:T(8,128)(2,1)S(1)}, u32[]{:S(2)}, u32[]{:S(2)}) collective-permute-start(bf16[224,256]{1,0:T(8,128)(2,1)S(1)} %add_convert_fusion.3), channel_id=1, source_target_pairs={{0,2},{1,3},{2,0},{3,1},{4,6},{5,7},{6,4},{7,5},{8,10},{9,11},{10,... | collective-permute-start | bytes 344072 | tf_op jit(solution)/shard_map/ppermute | solution.py:28
  190.3 20.0 %collective-permute-start.16 = (bf16[224,256]{1,0:T(8,128)(2,1)S(1)}, bf16[224,256]{1,0:T(8,128)(2,1)S(1)}, u32[]{:S(2)}, u32[]{:S(2)}) collective-permute-start(bf16[224,256]{1,0:T(8,128)(2,1)S(1)} %add_convert_fusion.3), channel_id=1, source_target_pairs={{0,1},{1,2},{2,3},{3,0},{4,5},{5,6},{6,7},{7,4},{8,9},{9,10},{10,1... | collective-permute-start | bytes 344072 | tf_op jit(solution)/shard_map/ppermute | solution.py:28
  191.0 26.3 %collective-permute-start.30 = (bf16[4,224,256]{2,1,0:T(8,128)(2,1)S(1)}, bf16[4,224,256]{2,1,0:T(8,128)(2,1)S(1)}, u32[]{:S(2)}, u32[]{:S(2)}) collective-permute-start(bf16[4,224,256]{2,1,0:T(8,128)(2,1)S(1)} %pad_maximum_fusion.1.rest_4_), channel_id=1, source_target_pairs={{0,2},{1,3},{2,0},{3,1},{4,6},{5,7},{6,4},{7,5},{8,10},{9,11},{10,... | collective-permute-start | bytes 1376264 | tf_op jit(solution)/shard_map/ppermute | solution.py:28
  210.3 14.0 %collective-permute-start.31 = (bf16[4,224,256]{2,1,0:T(8,128)(2,1)S(1)}, bf16[4,224,256]{2,1,0:T(8,128)(2,1)S(1)}, u32[]{:S(2)}, u32[]{:S(2)}) collective-permute-start(bf16[4,224,256]{2,1,0:T(8,128)(2,1)S(1)} %pad_maximum_fusion.1.rest_4_), channel_id=1, source_target_pairs={{0,1},{1,2},{2,3},{3,0},{4,5},{5,6},{6,7},{7,4},{8,9},{9,10},{10,1... | collective-permute-start | bytes 1376264 | tf_op jit(solution)/shard_map/ppermute | solution.py:28
  210.4 13.9 %collective-permute-start.17 = (bf16[4,224,256]{2,1,0:T(8,128)(2,1)S(1)}, bf16[4,224,256]{2,1,0:T(8,128)(2,1)S(1)}, u32[]{:S(2)}, u32[]{:S(2)}) collective-permute-start(bf16[4,224,256]{2,1,0:T(8,128)(2,1)S(1)} %pad_maximum_fusion.rest_0_), channel_id=1, source_target_pairs={{0,68},{4,0},{64,4},{68,64},{1,69},{5,1},{65,5},{69,65},{2,70},{6,... | collective-permute-start | bytes 1376264 | tf_op jit(solution)/shard_map/ppermute | solution.py:28
  210.5 13.9 %collective-permute-start.18 = (bf16[4,224,256]{2,1,0:T(8,128)(2,1)S(1)}, bf16[4,224,256]{2,1,0:T(8,128)(2,1)S(1)}, u32[]{:S(2)}, u32[]{:S(2)}) collective-permute-start(bf16[4,224,256]{2,1,0:T(8,128)(2,1)S(1)} %pad_maximum_fusion.rest_0_), channel_id=1, source_target_pairs={{0,64},{4,68},{64,0},{68,4},{1,65},{5,69},{65,1},{69,5},{2,66},{6,... | collective-permute-start | bytes 1376264 | tf_op jit(solution)/shard_map/ppermute | solution.py:28
  210.6 23.8 %collective-permute-start.19 = (bf16[4,224,256]{2,1,0:T(8,128)(2,1)S(1)}, bf16[4,224,256]{2,1,0:T(8,128)(2,1)S(1)}, u32[]{:S(2)}, u32[]{:S(2)}) collective-permute-start(bf16[4,224,256]{2,1,0:T(8,128)(2,1)S(1)} %pad_maximum_fusion.rest_0_), channel_id=1, source_target_pairs={{0,4},{4,64},{64,68},{68,0},{1,5},{5,65},{65,69},{69,1},{2,6},{6,6... | collective-permute-start | bytes 1376264 | tf_op jit(solution)/shard_map/ppermute | solution.py:28
  217.3 23.5 %collective-permute-start.36 = (bf16[128,896]{1,0:T(8,128)(2,1)S(1)}, bf16[128,896]{1,0:T(8,128)(2,1)S(1)}, u32[]{:S(2)}, u32[]{:S(2)}) collective-permute-start(bf16[128,896]{1,0:T(8,128)(2,1)S(1)} %shard_map.133), channel_id=1, source_target_pairs={{0,0},{1,8},{2,16},{3,24},{4,32},{5,40},{6,48},{7,56},{8,1},{9,9},... | collective-permute-start | bytes 688136 | tf_op jit(solution)/shard_map/ppermute | solution.py:37
  (12 other events, 60.3 us)
Sparse Core Ops, SparseCore 0:
  43.1 36.2 all-gather.1

commit v3 on v1

--- a/solution.py
+++ b/solution.py
@@ -72,25 +72,48 @@
     return ref[:, start : start + HS]
 
 
-def encode_kernel(x_ref, gain_ref, project_ref, mix_ref, encoded_ref, normed_ref, projected_ref, mixed_ref):
+def encode_kernel(
+    x_ref, gain_ref, project_ref, mix_ref, encoded_ref, normed_ref, projected_ref, mixed_ref, project, mix, sems
+):
+    thirds = [slice(b * ENC, (b + 1) * ENC) for b in range(3)]
+    copies = [
+        pltpu.make_async_copy(project_ref.at[:, at], project.at[:, at], sems.at[b])
+        for b, at in enumerate(thirds)
+    ]
+    copies.append(pltpu.make_async_copy(mix_ref, mix, sems.at[3]))
+    for copy in copies:
+        copy.start()
     x = x_ref[...].astype(f32)
     r = lax.rsqrt(jnp.mean(x * x, axis=-1, keepdims=True) + epsilon)
     normed_ref[...] = (x * r * gain_ref[...]).astype(bf16)
-    projected_ref[...] = nn(normed_ref[...], project_ref[...]).astype(bf16)
-    for h in range(ENC // HS):
-        q, k, v = (head(projected_ref, h, b) for b in range(3))
-        w = softmax(nt(q, k) / math.sqrt(HS)).astype(bf16)
-        mixed_ref[:, h * HS : (h + 1) * HS] = nn(w, v).astype(bf16)
-    encoded_ref[...] = (x + nn(mixed_ref[...], mix_ref[...])).astype(bf16)
+    for b, at in enumerate(thirds):
+        copies[b].wait()
+        projected_ref[:, at] = nn(normed_ref[...], project[:, at]).astype(bf16)
+    heads = range(ENC // HS)
+    scores = [nt(head(projected_ref, h, 0), head(projected_ref, h, 1)) / math.sqrt(HS) for h in heads]
+    weights = [softmax(s).astype(bf16) for s in scores]
+    for h in heads:
+        mixed_ref[:, h * HS : (h + 1) * HS] = nn(weights[h], head(projected_ref, h, 2)).astype(bf16)
+    copies[3].wait()
+    encoded_ref[...] = (x + nn(mixed_ref[...], mix[...])).astype(bf16)
 
 
 def encode(x, gain, project, mix):
     shape = jax.ShapeDtypeStruct((TOK, ENC), bf16)
     wide = jax.ShapeDtypeStruct((TOK, 3 * ENC), bf16)
+    vmem = pl.BlockSpec(memory_space=pltpu.VMEM)
+    far = pl.BlockSpec(memory_space=pl.ANY)
     return pl.pallas_call(
         encode_kernel,
-        out_shape=(shape, shape, wide, shape),
-        compiler_params=params(24),
+        in_specs=[vmem, vmem, far, far],
+        out_specs=[vmem] * 4,
+        out_shape=[shape, shape, wide, shape],
+        scratch_shapes=[
+            pltpu.VMEM((ENC, 3 * ENC), bf16),
+            pltpu.VMEM((ENC, ENC), bf16),
+            pltpu.SemaphoreType.DMA((4,)),
+        ],
+        compiler_params=params(58),
         cost_estimate=cost(10**9, 8 * 10**6),
     )(x, gain, project, mix)
 
@@ -112,95 +135,128 @@
     )(normed, mixed)
 
 
-def pairs_kernel(first_ref, second_ref, weight_ref, *rest):
-    held_ref, out_ref = rest[-2:]
-    held_ref[0, 0] = first_ref[...]
-    held_ref[1, 0] = second_ref[...]
-    out_ref[0, 0] = nn(first_ref[...], weight_ref[...]).astype(bf16)
-    out_ref[1, 0] = nn(second_ref[...], weight_ref[...]).astype(bf16)
-
-
-def pairs_of(step, first, second, weight, before):
-    many = 4
-    width = weight.shape[1] // many
-    kept = [pl.BlockSpec(memory_space=pl.ANY)] * len(before)
-    return pl.pallas_call(
-        pairs_kernel,
-        grid=(many,),
-        in_specs=[
-            pl.BlockSpec((TOK, ENC), lambda i: (0, 0)),
-            pl.BlockSpec((TOK, ENC), lambda i: (0, 0)),
-            pl.BlockSpec((ENC, width), lambda i: (0, i)),
-            *kept,
-        ],
-        out_specs=(
-            pl.BlockSpec((2, 1, TOK, ENC), lambda i: (0, step, 0, 0)),
-            pl.BlockSpec((2, 1, TOK, width), lambda i: (0, step, 0, i)),
-        ),
-        out_shape=(
-            jax.ShapeDtypeStruct((2, 4, TOK, ENC), bf16),
-            jax.ShapeDtypeStruct((2, 4, TOK, weight.shape[1]), bf16),
-        ),
-        input_output_aliases={3: 0, 4: 1} if before else {},
-        compiler_params=params(16, 1),
-        cost_estimate=cost(10**9, 6 * 10**6),
-    )(first, second, weight, *before)
-
-
-def cross_kernel(slots_ref, q_ref, up_ref, one_ref, two_ref, out_ref, grad_ref, pairs_ref):
-    span = pl.program_id(0)
-    slots = (slots_ref[2 * span], slots_ref[2 * span + 1])
-    inner = q_ref.shape[2]
+def cross_kernel(per, slots_ref, q_ref, up_ref, weight_ref, *rest):
+    sources, (out_ref, grad_ref, pairs_ref, sum_ref, rows_ref, turned_ref, held_ref) = rest[:8], rest[8:]
+
+    @pl.when(pl.program_id(0) == 0)
+    def _():
+        for n, source in enumerate(sources):
+            rows_ref[n * TOK : (n + 1) * TOK] = source[...]
+            turned_ref[:, n * TOK : (n + 1) * TOK] = source[...].T
+
     scale = 1.0 / math.sqrt(HS)
-    for h in range(inner // HS):
-        at = slice(h * HS, (h + 1) * HS)
-        up = slice(inner + h * HS, inner + (h + 1) * HS)
-        q = q_ref[0, :, at]
-        g = up_ref[0, :, at]
-        k = jnp.concatenate([one_ref[0, :, at], two_ref[0, :, at]], axis=0)
-        v = jnp.concatenate([one_ref[0, :, up], two_ref[0, :, up]], axis=0)
-        probs = softmax(nt(q, k) * scale)
-        low = probs.astype(bf16)
-        out_ref[0, :, at] = nn(low, v).astype(bf16)
-        grad_probs = nt(g, v)
-        grad_values = tn(low, g).astype(bf16)
-        total = jnp.sum(probs * grad_probs, axis=-1, keepdims=True)
-        grad_scores = (probs * (grad_probs - total)).astype(bf16)
-        grad_ref[0, :, at] = (nn(grad_scores, k) * scale).astype(bf16)
-        grad_keys = (tn(grad_scores, q) * scale).astype(bf16)
-        for n in range(2):
-            pairs_ref[slots[n], :, at] = grad_keys[n * TOK : (n + 1) * TOK]
-            pairs_ref[slots[n], :, up] = grad_values[n * TOK : (n + 1) * TOK]
-
-
-def cross(slots, queries, upstream, pairs):
+    length = q_ref.shape[1]
+    none = jnp.zeros((length, HS), bf16)
+    spans = range(q_ref.shape[0])
+    rows = [
+        [pl.ds(pl.multiple_of(slots_ref[2 * c + n] * TOK, TOK), TOK) for n in range(2)] for c in spans
+    ]
+    held_ref[...] = nn(rows_ref[...], weight_ref[...]).astype(bf16)
+    for first in range(0, per, 2):
+        units = []
+        for h in range(first, first + 2):
+            at, pair = slice(h * HS, (h + 1) * HS), slice(2 * h * HS, 2 * (h + 1) * HS)
+            for c in spans:
+                held = jnp.concatenate([held_ref[r, pair] for r in rows[c]], axis=0)
+                top = jnp.concatenate([q_ref[c, :, at], none], axis=1)
+                low = jnp.concatenate([none, up_ref[c, :, at]], axis=1)
+                x = jnp.concatenate([top, low], axis=0)
+                units.append((c, at, pair, held, x, nt(x, held)))
+        mixed = []
+        for c, at, pair, held, x, s in units:
+            probs = softmax(s[:length] * scale)
+            grad_probs = s[length:]
+            total = jnp.sum(probs * grad_probs, axis=-1, keepdims=True)
+            y = jnp.concatenate([probs * (grad_probs - total), probs], axis=0).astype(bf16)
+            mixed.append((c, at, pair, held, x, y))
+        for c, at, pair, held, x, y in mixed:
+            z = nn(y, held)
+            grad_ref[c, :, at] = (z[:length, :HS] * scale).astype(bf16)
+            out_ref[c, :, at] = z[length:, HS:].astype(bf16)
+            g = tn(y, x)
+            g = jnp.concatenate([g[:, :HS] * scale, g[:, HS:]], axis=1).astype(bf16)
+            for n in range(2):
+                pairs_ref[rows[c][n], pair] = g[n * TOK : (n + 1) * TOK]
+    sum_ref[...] = nn(turned_ref[...], pairs_ref[...]).astype(bf16)
+
+
+def cross(slots, queries, upstream, weight, sources, per):
     spans, length, inner = queries.shape
-    whole = pl.BlockSpec((1, length, inner), lambda i, s: (i, 0, 0))
-    return pl.pallas_call(
-        cross_kernel,
+    rows = len(sources) * TOK
+    column = pl.BlockSpec((spans, length, per * HS), lambda i, s: (0, 0, i))
+    return pl.pallas_call(
+        functools.partial(cross_kernel, per),
         grid_spec=pltpu.PrefetchScalarGridSpec(
             num_scalar_prefetch=1,
-            grid=(spans,),
+            grid=(inner // HS // per,),
             in_specs=[
-                whole,
-                whole,
-                pl.BlockSpec((1, TOK, 2 * inner), lambda i, s: (s[2 * i], 0, 0)),
-                pl.BlockSpec((1, TOK, 2 * inner), lambda i, s: (s[2 * i + 1], 0, 0)),
+                column,
+                column,
+                pl.BlockSpec((ENC, 2 * HS * per), lambda i, s: (0, i)),
+                *[pl.BlockSpec((TOK, ENC), lambda i, s: (0, 0))] * len(sources),
             ],
             out_specs=(
-                whole,
-                whole,
-                pl.BlockSpec((2 * spans, TOK, 2 * inner), lambda i, s: (0, 0, 0)),
+                column,
+                column,
+                pl.BlockSpec((rows, 2 * HS * per), lambda i, s: (0, i)),
+                pl.BlockSpec((ENC, 2 * HS * per), lambda i, s: (0, i)),
             ),
+            scratch_shapes=[
+                pltpu.VMEM((rows, ENC), bf16),
+                pltpu.VMEM((ENC, rows), bf16),
+                pltpu.VMEM((rows, 2 * HS * per), bf16),
+            ],
         ),
         out_shape=(
             jax.ShapeDtypeStruct(queries.shape, bf16),
             jax.ShapeDtypeStruct(queries.shape, bf16),
-            jax.ShapeDtypeStruct((2 * spans, TOK, 2 * inner), bf16),
+            jax.ShapeDtypeStruct((rows, 2 * inner), bf16),
+            jax.ShapeDtypeStruct((ENC, 2 * inner), bf16),
         ),
+        compiler_params=params(44, 1),
+        cost_estimate=cost(16 * 10**9, 16 * 10**6),
+    )(slots, queries, upstream, weight, *sources)
+
+
+def place_kernel(sum_ref, out_ref):
+    size, many = sum_ref.shape[0], sum_ref.shape[1] // HS
+    for j in range(many):
+        out_ref[pl.ds(j, size, stride=many), :] = sum_ref[:, j * HS : (j + 1) * HS].astype(f32)
+
+
+def placed(summed):
+    size = ENC // 4
+    many = summed.shape[1] // HS
+    return pl.pallas_call(
+        place_kernel,
+        grid=(4,),
+        in_specs=[pl.BlockSpec((size, summed.shape[1]), lambda i: (i, 0))],
+        out_specs=pl.BlockSpec((size * many, HS), lambda i: (i, 0)),
+        out_shape=jax.ShapeDtypeStruct((ENC * many, HS), f32),
+        compiler_params=params(16, 1),
+        cost_estimate=cost(10**6, 11 * 10**6),
+    )(summed)
+def near_kernel(pairs_ref, weight_ref, brought_ref, own_ref, *outs):
+    total = nt(pairs_ref[...], weight_ref[...]) + brought_ref[...].astype(f32)
+    own_ref[...] = total[:TOK]
+    for n, out in enumerate(outs):
+        out[...] = total[(n + 1) * TOK : (n + 2) * TOK].astype(bf16)
+
+
+def near_sums(pairs, weight, brought):
+    def whole(*shape):
+        return pl.BlockSpec(shape, lambda i: (0, 0))
+
+    inner = weight.shape[1]
+    return pl.pallas_call(
+        near_kernel,
+        grid=(1,),
+        in_specs=[whole(4 * TOK, inner), whole(ENC, inner), whole(4 * TOK, ENC)],
+        out_specs=[whole(TOK, ENC)] * 4,
+        out_shape=[jax.ShapeDtypeStruct((TOK, ENC), f32)] + [jax.ShapeDtypeStruct((TOK, ENC), bf16)] * 3,
         compiler_params=params(32, 1),
-        cost_estimate=cost(3 * 10**9, 12 * 10**6),
-    )(slots, queries, upstream, pairs, pairs)
+        cost_estimate=cost(2 * 10**9, 8 * 10**6),
+    )(pairs, weight, brought)
 
 
 def columns_of(at):
@@ -279,40 +335,34 @@
     gain = encoder_gain.reshape(1, ENC)
     y, core = lax.axis_index("y"), lax.axis_index("c")
     inner = cross_pairs.shape[2]
-    x = flipped(neighbour_inputs[0])
-    weight = lax.optimization_barrier(cross_pairs.reshape(ENC, 2 * inner))
+    heads = inner // HS
+    weight = cross_pairs.reshape(ENC, 2, heads, HS).swapaxes(1, 2).reshape(ENC, 2 * inner)
+    x, weight = lax.optimization_barrier((flipped(neighbour_inputs[0]), weight))
     encoded, normed, projected, mixed = encode(x, gain, encoder_project, encoder_mix)
 
-    before = ()
-    for step in range(4):
-        first = encoded if step == 0 else turned("y", 4, -step)(encoded)
-        before = pairs_of(step, first, across(first), weight, before)
-    sources, pairs = before
-    operands = lax.all_gather(spread(normed, mixed), TP, tiled=True)
+    column = [encoded] + [turned("y", 4, -step)(encoded) for step in range(1, 4)]
+    sources = column + [across(one) for one in column]
+    operands, sources = lax.optimization_barrier((spread(normed, mixed), sources))
+    operands = lax.all_gather(operands, TP, tiled=True)
 
     named = span_neighbours.reshape(-1) % 8
     slots = (named % 2 != core) * 4 + (named // 2 - y) % 4
-    result, grad_queries, grad_pairs = cross(
-        slots.astype(jnp.int32), decoder_queries, grad_output, pairs.reshape(8, TOK, 2 * inner)
+    result, grad_queries, grad_pairs, grad_weight = cross(
+        slots.astype(jnp.int32), decoder_queries, grad_output, weight, sources, heads
     )
-
-    far = nt(grad_pairs[4:].reshape(4 * TOK, 2 * inner), weight).astype(bf16)
-    brought = across(far)
-    near = nt(grad_pairs[:4].reshape(4 * TOK, 2 * inner), weight)
-    grad_weight = tn(sources.reshape(8 * TOK, ENC), grad_pairs.reshape(8 * TOK, 2 * inner)).astype(bf16)
-    summed = (near + brought.astype(f32)).reshape(4, TOK, ENC)
-    total = summed[0]
-    for step in range(1, 4):
-        total += turned("y", 4, step)(summed[step].astype(bf16)).astype(f32)
+    grad_cross = placed(lax.psum(grad_weight, PLANE))
+    grad_cross = grad_cross.reshape(ENC, heads, 2, HS).swapaxes(1, 2).reshape(cross_pairs.shape)
+
+    brought = across(nt(grad_pairs[4 * TOK :], weight).astype(bf16))
+    total, *others = near_sums(grad_pairs, weight, brought)
+    for step, other in enumerate(others):
+        total += turned("y", 4, step + 1)(other).astype(f32)
     grad_encoded = total.astype(bf16)
-
-    grad_cross = lax.psum(grad_weight, PLANE)
-    grad_cross = grad_cross.astype(f32).reshape(cross_pairs.shape)
 
     parts = backward(grad_encoded, projected, encoder_mix)
     all_parts = lax.all_to_all(parts, TP, 0, 0, tiled=True).reshape(8 * TOK, LANES)
     mine = jnp.where(y * 2 + core < 6, operands[:, :1024], operands[:, 1024:])
-    encoder_grad = tn(mine, all_parts).astype(bf16).reshape(128, 8, LANES)
+    encoder_grad = nn(lax.optimization_barrier(mine.T), all_parts).astype(bf16).reshape(128, 8, LANES)
     arrived = lax.all_to_all(encoder_grad, FINE, 0, 0, tiled=True).astype(f32)
     arrived = arrived.reshape(2, 8, 8, 8, LANES).sum(axis=(0, 2))
     rows = jnp.swapaxes(arrived, 0, 1).reshape(8, 8 * LANES)[:7]

time: 226 us -> 201 us (0.89)
  waiting for transfers between devices: 82 us -> 72.7 us
  matrix products: 18 us -> 9.23 us
  starting transfers between devices: 43.6 us -> 38.9 us
  local copies, waits for them, and re-layouts: 19.9 us -> 24.2 us
  other arithmetic: 7.87 us -> 4.03 us
  Pallas kernels: 38.4 us -> 35.9 us
    dot_general x4 -> x2, matrix products: 18 us -> 9.23 us  [dot(): lax.dot_general(a, b, ((contract[:1], contract[1:]), ((), ())), preferred...]
    reshape x1 -> x0, other arithmetic: 7.6 us -> none  [shards(): grad_cross = grad_cross.astype(f32).reshape(cross_pairs.shape)]
    psum x1, waiting for transfers between devices: 33.2 us -> 27.5 us  [shards(): grad_cross = placed(lax.psum(grad_weight, PLANE))]
    ppermute x6, starting transfers between devices: 15.7 us -> 10.7 us  [turned(): return lambda x: lax.ppermute(x, axis, pairs)]
    unnamed x19 -> x38, local copies, waits for them, and re-layouts: 10.3 us -> 15.1 us
    ppermute x2, waiting for transfers between devices: 17.2 us -> 12.5 us  [flipped(): return lax.ppermute(x, ('y', 'c', 'xl', 'z'), pairs)]
    transpose x0 -> x1, other arithmetic: none -> 3.76 us  [shards(): encoder_grad = nn(lax.optimization_barrier(mine.T), all_parts).astype(bf1...]
    all_to_all x1, waiting for transfers between devices: 15.1 us -> 11.4 us  [shards(): lax.all_to_all(parts, TP, 0, 0, tiled=True).reshape(8 * TOK, LANES)]
  transfers between devices with their start and end apart: 17 -> 17, of which waited for: 8 -> 9; matrix products, arithmetic and copies ran while one was open for 17% -> 10% of each run, Pallas kernels for 15% -> 15%
where the time goes in v3:
time: 201 us
  waiting for transfers between devices  72.7 us (36%)
  starting transfers between devices  38.9 us (19%)
  Pallas kernels  35.9 us (18%)
  local copies, waits for them, and re-layouts  24.2 us (12%)
  between operations  15.7 us (8%)
  matrix products  9.23 us (5%)
  other arithmetic  4.03 us (2%)
    psum x1, waiting for transfers between devices, shards(): grad_cross = placed(lax.psum(grad_weight, PLANE))  27.5 us
    ppermute x6, waiting for transfers between devices, turned(): return lambda x: lax.ppermute(x, axis, pairs)  18.9 us
    unnamed x38, local copies, waits for them, and re-layouts  15.1 us
    pallas_call x1, Pallas kernels, cross(): pl.pallas_call(functools.partial(cross_kernel, per), grid_spec=pltpu.Pref...  13.3 us
    ppermute x2, waiting for transfers between devices, flipped(): return lax.ppermute(x, ('y', 'c', 'xl', 'z'), pairs)  12.5 us
    all_to_all x1, waiting for transfers between devices, shards(): lax.all_to_all(parts, TP, 0, 0, tiled=True).reshape(8 * TOK, LANES)  11.4 us
    ppermute x6, starting transfers between devices, turned(): return lambda x: lax.ppermute(x, axis, pairs)  10.7 us
    dot_general x2, matrix products, dot(): lax.dot_general(a, b, ((contract[:1], contract[1:]), ((), ())), preferred...  9.23 us
  transfers between devices with their start and end apart: 17, of which 9 were waited for; matrix products, arithmetic and copies ran while one was open for 10% of the time, Pallas kernels for 15%

profile of v3, /device:TPU:1, one launch (start us, length us, event | category | flops | bytes accessed | tf_op | source)
XLA Modules:
  0.0 200.6 jit_solution(17275092548274193499)
XLA Ops:
  8.0 4.9 %collective-permute-start = (bf16[128,896]{1,0:T(8,128)(2,1)}, bf16[128,896]{1,0:T(8,128)(2,1)S(1)}, u32[]{:S(2)}, u32[]{:S(2)}) collective-permute-start(bf16[128,896]{1,0:T(8,128)(2,1)} %bitcast.30), channel_id=1, source_target_pairs={{0,0},{1,8},{2,16},{3,24},{4,32},{5,40},{6,48},{7,56},{8,1},{9,9},... | collective-permute-start | bytes 688136 | tf_op jit(solution)/shard_map/ppermute | solution.py:37
  13.0 7.2 %reshape.46.weight_ref = bf16[896,2048]{1,0:T(8,128)(2,1)} reshape(bf16[896,8,2,128]{3,2,1,0:T(2,128)(2,1)} %bitcast.25) | data formatting | bytes 7340032 | tf_op jit(solution)/shard_map/reshape | solution.py:339
  20.2 0.6 reshape.47.gain_ref
  20.8 0.7 copy-done.7
  21.5 5.4 %shard_map.127 = (bf16[128,896]{1,0:T(8,128)(2,1)}, bf16[128,896]{1,0:T(8,128)(2,1)}, bf16[128,2688]{1,0:T(8,128)(2,1)}, bf16[128,896]{1,0:T(8,128)(2,1)}) custom-call(bf16[128,896]{1,0:T(8,128)(2,1)} %copy-done.7, f32[1,896]{1,0:T(1,128)} %reshape.47.gain_ref, bf16[896,2688]{1,0:T(8,128)(2,1)} %project_ref.3, bf16[896,896]{1,0:T(8,128)(2,1)} %mix_ref.3), custom_call_target="tpu_custom_call" | custom-call | flops 1000000000 | bytes 8000000 | tf_op jit(solution)/shard_map/pallas_call | solution.py:106
  26.9 8.0 %collective-permute-start.1 = (bf16[128,896]{1,0:T(8,128)(2,1)}, bf16[128,896]{1,0:T(8,128)(2,1)S(1)}, u32[]{:S(2)}, u32[]{:S(2)}) collective-permute-start(bf16[128,896]{1,0:T(8,128)(2,1)} %get-tuple-element.34.rest_0_), channel_id=1, source_target_pairs={{0,48},{16,0},{32,16},{48,32},{1,49},{17,1},{33,17},{49,33},{2,50}... | collective-permute-start | bytes 688136 | tf_op jit(solution)/shard_map/ppermute | solution.py:28
  35.0 0.8 collective-permute-start.3
  35.8 3.1 %collective-permute-start.4 = (bf16[128,896]{1,0:T(8,128)(2,1)}, bf16[128,896]{1,0:T(8,128)(2,1)S(1)}, u32[]{:S(2)}, u32[]{:S(2)}) collective-permute-start(bf16[128,896]{1,0:T(8,128)(2,1)} %get-tuple-element.34.rest_0_), channel_id=1, source_target_pairs={{0,8},{8,0},{1,9},{9,1},{2,10},{10,2},{3,11},{11,3},{4,12},{12,4},... | collective-permute-start | bytes 688136 | tf_op jit(solution)/shard_map/ppermute | solution.py:32
  39.0 5.8 %collective-permute-done.1.rest_1_ = bf16[128,896]{1,0:T(8,128)(2,1)S(1)} collective-permute-done((bf16[128,896]{1,0:T(8,128)(2,1)}, bf16[128,896]{1,0:T(8,128)(2,1)S(1)}, u32[]{:S(2)}, u32[]{:S(2)}) %collective-permute-start.1) | collective-permute-done | bytes 229408 | tf_op jit(solution)/shard_map/ppermute | solution.py:28
  44.7 1.3 collective-permute-start.5
  46.0 1.2 collective-permute-start.6
  47.2 0.8 collective-permute-done.3.rest_3_
  48.0 1.4 collective-permute-start.7
  49.4 0.9 copy-done.14
  50.3 0.9 copy-done.15
  51.3 1.8 shard_map.128
  53.1 0.2 all-reduce.2.cloned.1.call-start
  53.6 2.0 %copy-done.1 = bf16[896,2048]{1,0:T(8,128)(2,1)S(1)} copy-done((bf16[896,2048]{1,0:T(8,128)(2,1)S(1)}, bf16[896,2048]{1,0:T(8,128)(2,1)}, u32[]{:S(2)}) %copy-start.1) | copy-done | bytes 3670040
  55.6 0.9 copy-done.13
  56.6 13.3 %shard_map.129 = (bf16[4,64,1024]{2,1,0:T(8,128)(2,1)}, bf16[4,64,1024]{2,1,0:T(8,128)(2,1)}, bf16[1024,2048]{1,0:T(8,128)(2,1)}, bf16[896,2048]{1,0:T(8,128)(2,1)S(1)}) custom-call(s32[8]{0:T(128)S(1)} %fusion.7.slots_ref, bf16[4,64,1024]{2,1,0:T(8,128)(2,1)S(1)} %copy-done.11, bf16[4,64,1024]{2,1,0:T(8,128)(2,1)S(1)} %copy-done.12, ...), custom_call_target="tpu_custom_call" | custom-call | flops 16000000000 | bytes 16000000 | tf_op jit(solution)/shard_map/pallas_call | solution.py:187
  69.9 5.3 %fusion.3 = bf16[512,896]{1,0:T(8,128)(2,1)S(1)} fusion(bf16[896,2048]{1,0:T(8,128)(2,1)S(1)} %copy-done.1, bf16[1024,2048]{1,0:T(8,128)(2,1)} %get-tuple-element.46.pairs_ref), kind=kOutput, calls=%fused_computation.6 | convolution fusion | flops 1879506944 | bytes 6684672 | tf_op jit(solution)/shard_map/dot_general | solution.py:41
  75.3 0.3 collective-permute-start.8
  75.6 2.4 %collective-permute-done.8.brought_ref = bf16[512,896]{1,0:T(8,128)(2,1)S(1)} collective-permute-done((bf16[512,896]{1,0:T(8,128)(2,1)S(1)}, bf16[512,896]{1,0:T(8,128)(2,1)S(1)}, u32[]{:S(2)}, u32[]{:S(2)}) %collective-permute-start.8) | collective-permute-done | bytes 917536 | tf_op jit(solution)/shard_map/ppermute | solution.py:32
  78.1 2.1 %copy-done.2 = bf16[896,2048]{1,0:T(8,128)(2,1)S(1)} copy-done((bf16[896,2048]{1,0:T(8,128)(2,1)S(1)}, bf16[896,2048]{1,0:T(8,128)(2,1)}, u32[]{:S(2)}) %copy-start.2) | copy-done | bytes 3670040
  80.2 2.2 %copy-done.4 = bf16[1024,2048]{1,0:T(8,128)(2,1)S(1)} copy-done((bf16[1024,2048]{1,0:T(8,128)(2,1)S(1)}, bf16[1024,2048]{1,0:T(8,128)(2,1)}, u32[]{:S(2)}) %copy-start.4) | copy-done | bytes 4194328
  82.4 2.4 %shard_map.131 = (f32[128,896]{1,0:T(8,128)S(1)}, bf16[128,896]{1,0:T(8,128)(2,1)S(1)}, bf16[128,896]{1,0:T(8,128)(2,1)S(1)}, bf16[128,896]{1,0:T(8,128)(2,1)S(1)}) custom-call(bf16[1024,2048]{1,0:T(8,128)(2,1)S(1)} %copy-done.4, bf16[896,2048]{1,0:T(8,128)(2,1)S(1)} %copy-done.2, bf16[512,896]{1,0:T(8,128)(2,1)S(1)} %collective-permute-done.8.brought_ref), custom_call_target="tpu_custom_call" | custom-call | flops 2000000000 | bytes 8000000 | tf_op jit(solution)/shard_map/pallas_call | solution.py:251
  84.8 0.3 collective-permute-start.10
  85.1 0.9 collective-permute-start.11
  86.0 0.6 collective-permute-start.9
  86.5 6.9 %collective-permute-done.10 = bf16[128,896]{1,0:T(8,128)(2,1)S(1)} collective-permute-done((bf16[128,896]{1,0:T(8,128)(2,1)S(1)}, bf16[128,896]{1,0:T(8,128)(2,1)S(1)}, u32[]{:S(2)}, u32[]{:S(2)}) %collective-permute-start.10) | collective-permute-done | bytes 229408 | tf_op jit(solution)/shard_map/ppermute | solution.py:28
  93.4 3.1 %collective-permute-done.11 = bf16[128,896]{1,0:T(8,128)(2,1)S(1)} collective-permute-done((bf16[128,896]{1,0:T(8,128)(2,1)S(1)}, bf16[128,896]{1,0:T(8,128)(2,1)S(1)}, u32[]{:S(2)}, u32[]{:S(2)}) %collective-permute-start.11) | collective-permute-done | bytes 229408 | tf_op jit(solution)/shard_map/ppermute | solution.py:28
  96.5 2.4 %collective-permute-done.9 = bf16[128,896]{1,0:T(8,128)(2,1)S(1)} collective-permute-done((bf16[128,896]{1,0:T(8,128)(2,1)S(1)}, bf16[128,896]{1,0:T(8,128)(2,1)S(1)}, u32[]{:S(2)}, u32[]{:S(2)}) %collective-permute-start.9) | collective-permute-done | bytes 229408 | tf_op jit(solution)/shard_map/ppermute | solution.py:28
  99.0 4.7 %shard_map.132.parts_ref = bf16[8,128,512]{2,1,0:T(8,128)(2,1)} custom-call(bf16[128,896]{1,0:T(8,128)(2,1)S(1)} %add_convert_fusion.grad_ref, bf16[128,2688]{1,0:T(8,128)(2,1)S(1)} %copy-done.9, bf16[896,896]{1,0:T(8,128)(2,1)S(1)} %copy-done.3), custom_call_target="tpu_custom_call" | custom-call | flops 600000000 | bytes 4000000 | tf_op jit(solution)/shard_map/pallas_call | solution.py:294
  103.7 3.8 %all-to-all-start = ((bf16[8,128,512]{2,1,0:T(8,128)(2,1)}), bf16[8,128,512]{2,1,0:T(8,128)(2,1)S(1)}, u32[]{:S(2)}, u32[]{:S(2)}) async-start(bf16[8,128,512]{2,1,0:T(8,128)(2,1)} %shard_map.132.parts_ref), calls=%async_computation | async-start | bytes 2097152 | tf_op jit(solution)/shard_map/all_to_all | solution.py:363
  107.5 3.8 %fusion = bf16[1024,1024]{0,1:T(8,128)(2,1)} fusion(bf16[1024,2048]{1,0:T(8,128)(2,1)} %all-gather.2.cloned.1.call-done, pred[]{:T(512)S(6)} %lt.20), kind=kLoop, calls=%fused_computation.1 | loop fusion | flops 1048576 | bytes 6291457 | tf_op jit(solution)/shard_map/transpose | solution.py:365
  111.3 11.4 %all-to-all-done = bf16[8,128,512]{2,1,0:T(8,128)(2,1)S(1)} async-done(((bf16[8,128,512]{2,1,0:T(8,128)(2,1)}), bf16[8,128,512]{2,1,0:T(8,128)(2,1)S(1)}, u32[]{:S(2)}, u32[]{:S(2)}) %all-to-all-start) | async-done | bytes 1048608 | tf_op jit(solution)/shard_map/all_to_all | solution.py:363
  122.7 3.9 %fusion.6 = bf16[128,8,512]{2,1,0:T(8,128)(2,1)} fusion(bf16[1024,1024]{0,1:T(8,128)(2,1)} %fusion, bf16[1024,512]{1,0:T(8,128)(2,1)S(1)} %bitcast.26), kind=kOutput, calls=%fused_computation.7 | convolution fusion | flops 1074266112 | bytes 4194304 | tf_op jit(solution)/shard_map/dot_general | solution.py:41
  126.5 8.1 %all-to-all-start.1 = ((bf16[128,8,512]{2,1,0:T(8,128)(2,1)}), bf16[128,8,512]{2,1,0:T(8,128)(2,1)S(1)}, u32[]{:S(2)}, u32[]{:S(2)}) async-start(bf16[128,8,512]{2,1,0:T(8,128)(2,1)} %fusion.6), calls=%async_computation.1 | async-start | bytes 2097152 | tf_op jit(solution)/shard_map/all_to_all | solution.py:366
  134.7 2.4 %copy-done = bf16[896,2688]{1,0:T(8,128)(2,1)S(1)} copy-done((bf16[896,2688]{1,0:T(8,128)(2,1)S(1)}, bf16[896,2688]{1,0:T(8,128)(2,1)}, u32[]{:S(2)}) %copy-start) | copy-done | bytes 4816920
  137.1 3.0 %shard_map.133 = bf16[128,896]{1,0:T(8,128)(2,1)S(1)} custom-call(bf16[128,896]{1,0:T(8,128)(2,1)S(1)} %copy-done.8, f32[1,896]{1,0:T(1,128)S(1)} %copy-done.10, bf16[896,2688]{1,0:T(8,128)(2,1)S(1)} %copy-done, bf16[8,128,512]{2,1,0:T(8,128)(2,1)} %shard_map.132.parts_ref, bf16[128,896]{1,0:T(8,128)(2,1)S(1)} %add_convert_fusion.grad_ref), custom_call_target="tpu_custom_call" | custom-call | flops 600000000 | bytes 6000000 | tf_op jit(solution)/shard_map/pallas_call | solution.py:317
  140.1 3.6 %collective-permute-start.12 = (bf16[128,896]{1,0:T(8,128)(2,1)S(1)}, bf16[128,896]{1,0:T(8,128)(2,1)S(1)}, u32[]{:S(2)}, u32[]{:S(2)}) collective-permute-start(bf16[128,896]{1,0:T(8,128)(2,1)S(1)} %shard_map.133), channel_id=1, source_target_pairs={{0,0},{1,8},{2,16},{3,24},{4,32},{5,40},{6,48},{7,56},{8,1},{9,9},... | collective-permute-start | bytes 688136 | tf_op jit(solution)/shard_map/ppermute | solution.py:37
  143.7 12.5 %collective-permute-done.12 = bf16[128,896]{1,0:T(8,128)(2,1)S(1)} collective-permute-done((bf16[128,896]{1,0:T(8,128)(2,1)S(1)}, bf16[128,896]{1,0:T(8,128)(2,1)S(1)}, u32[]{:S(2)}, u32[]{:S(2)}) %collective-permute-start.12) | collective-permute-done | bytes 229408 | tf_op jit(solution)/shard_map/ppermute | solution.py:37
  156.2 27.5 %all-reduce.2.cloned.1.call-done.sum_ref = bf16[896,2048]{1,0:T(8,128)(2,1)} async-done(((bf16[896,2048]{1,0:T(8,128)(2,1)}), bf16[896,2048]{1,0:T(8,128)(2,1)}) %all-reduce.2.cloned.1.call-update) | async-done | bytes 3670032 | tf_op jit(solution)/shard_map/psum | solution.py:353
  183.7 2.0 %copy-done.6 = bf16[896,2048]{1,0:T(8,128)(2,1)S(1)} copy-done((bf16[896,2048]{1,0:T(8,128)(2,1)S(1)}, bf16[896,2048]{1,0:T(8,128)(2,1)}, u32[]{:S(2)}) %copy-start.6) | copy-done | bytes 3670040
  185.8 5.3 %shard_map.130 = f32[14336,128]{1,0:T(8,128)} custom-call(bf16[896,2048]{1,0:T(8,128)(2,1)S(1)} %copy-done.6), custom_call_target="tpu_custom_call" | custom-call | flops 1000000 | bytes 11000000 | tf_op jit(solution)/shard_map/pallas_call | solution.py:230
  191.2 0.6 slice.31
  191.9 0.6 slice.32
  192.5 0.7 copy.25
  (44 shorter events, 0.7 us)
Async XLA Ops:
  8.0 99.5 %all-gather.2.cloned.1.call-start = ((), (), s32[]{:S(2)}) async-start(), calls=%async_computation.3 | async-start | bytes 4718592 | tf_op jit(solution)/shard_map/all_gather | solution.py:346
  8.0 12.7 %collective-permute-start = (bf16[128,896]{1,0:T(8,128)(2,1)}, bf16[128,896]{1,0:T(8,128)(2,1)S(1)}, u32[]{:S(2)}, u32[]{:S(2)}) collective-permute-start(bf16[128,896]{1,0:T(8,128)(2,1)} %bitcast.30), channel_id=1, source_target_pairs={{0,0},{1,8},{2,16},{3,24},{4,32},{5,40},{6,48},{7,56},{8,1},{9,9},... | collective-permute-start | bytes 688136 | tf_op jit(solution)/shard_map/ppermute | solution.py:37
  13.0 7.2 %copy-start.16 = (f32[896]{0:T(1024)S(1)}, f32[896]{0:T(1024)}, u32[]{:S(2)}) copy-start(f32[896]{0:T(1024)} %param.9) | copy-start | bytes 10756
  20.8 32.6 %copy-start.17 = (s32[4,2]{0,1:T(2,128)S(1)}, s32[4,2]{0,1:T(2,128)}, u32[]{:S(2)}) copy-start(s32[4,2]{0,1:T(2,128)} %param.14) | copy-start | bytes 100
  20.8 32.8 %copy-start.11 = (bf16[4,64,1024]{2,1,0:T(8,128)(2,1)S(1)}, bf16[4,64,1024]{2,1,0:T(8,128)(2,1)}, u32[]{:S(2)}) copy-start(bf16[4,64,1024]{2,1,0:T(8,128)(2,1)} %q_ref.1) | copy-start | bytes 1572868
  20.8 32.8 %copy-start.12 = (bf16[4,64,1024]{2,1,0:T(8,128)(2,1)S(1)}, bf16[4,64,1024]{2,1,0:T(8,128)(2,1)}, u32[]{:S(2)}) copy-start(bf16[4,64,1024]{2,1,0:T(8,128)(2,1)} %up_ref.1) | copy-start | bytes 1572868
  20.8 0.7 copy-start.7
  26.9 17.8 %collective-permute-start.1 = (bf16[128,896]{1,0:T(8,128)(2,1)}, bf16[128,896]{1,0:T(8,128)(2,1)S(1)}, u32[]{:S(2)}, u32[]{:S(2)}) collective-permute-start(bf16[128,896]{1,0:T(8,128)(2,1)} %get-tuple-element.34.rest_0_), channel_id=1, source_target_pairs={{0,48},{16,0},{32,16},{48,32},{1,49},{17,1},{33,17},{49,33},{2,50}... | collective-permute-start | bytes 688136 | tf_op jit(solution)/shard_map/ppermute | solution.py:28
  34.9 11.1 %collective-permute-start.2 = (bf16[128,896]{1,0:T(8,128)(2,1)}, bf16[128,896]{1,0:T(8,128)(2,1)S(1)}, u32[]{:S(2)}, u32[]{:S(2)}) collective-permute-start(bf16[128,896]{1,0:T(8,128)(2,1)} %get-tuple-element.34.rest_0_), channel_id=1, source_target_pairs={{0,32},{16,48},{32,0},{48,16},{1,33},{17,49},{33,1},{49,17},{2,34}... | collective-permute-start | bytes 688136 | tf_op jit(solution)/shard_map/ppermute | solution.py:28
  35.0 12.9 %collective-permute-start.3 = (bf16[128,896]{1,0:T(8,128)(2,1)}, bf16[128,896]{1,0:T(8,128)(2,1)S(1)}, u32[]{:S(2)}, u32[]{:S(2)}) collective-permute-start(bf16[128,896]{1,0:T(8,128)(2,1)} %get-tuple-element.34.rest_0_), channel_id=1, source_target_pairs={{0,16},{16,32},{32,48},{48,0},{1,17},{17,33},{33,49},{49,1},{2,18}... | collective-permute-start | bytes 688136 | tf_op jit(solution)/shard_map/ppermute | solution.py:28
  35.8 17.2 %collective-permute-start.4 = (bf16[128,896]{1,0:T(8,128)(2,1)}, bf16[128,896]{1,0:T(8,128)(2,1)S(1)}, u32[]{:S(2)}, u32[]{:S(2)}) collective-permute-start(bf16[128,896]{1,0:T(8,128)(2,1)} %get-tuple-element.34.rest_0_), channel_id=1, source_target_pairs={{0,8},{8,0},{1,9},{9,1},{2,10},{10,2},{3,11},{11,3},{4,12},{12,4},... | collective-permute-start | bytes 688136 | tf_op jit(solution)/shard_map/ppermute | solution.py:32
  44.7 8.4 %collective-permute-start.5 = (bf16[128,896]{1,0:T(8,128)(2,1)S(1)}, bf16[128,896]{1,0:T(8,128)(2,1)S(1)}, u32[]{:S(2)}, u32[]{:S(2)}) collective-permute-start(bf16[128,896]{1,0:T(8,128)(2,1)S(1)} %collective-permute-done.1.rest_1_), channel_id=1, source_target_pairs={{0,8},{8,0},{1,9},{9,1},{2,10},{10,2},{3,11},{11,3},{4,12},{12,4},... | collective-permute-start | bytes 688136 | tf_op jit(solution)/shard_map/ppermute | solution.py:32
  46.0 7.1 %collective-permute-start.6 = (bf16[128,896]{1,0:T(8,128)(2,1)S(1)}, bf16[128,896]{1,0:T(8,128)(2,1)S(1)}, u32[]{:S(2)}, u32[]{:S(2)}) collective-permute-start(bf16[128,896]{1,0:T(8,128)(2,1)S(1)} %collective-permute-done.2.rest_2_), channel_id=1, source_target_pairs={{0,8},{8,0},{1,9},{9,1},{2,10},{10,2},{3,11},{11,3},{4,12},{12,4},... | collective-permute-start | bytes 688136 | tf_op jit(solution)/shard_map/ppermute | solution.py:32
  48.0 5.1 %collective-permute-start.7 = (bf16[128,896]{1,0:T(8,128)(2,1)S(1)}, bf16[128,896]{1,0:T(8,128)(2,1)S(1)}, u32[]{:S(2)}, u32[]{:S(2)}) collective-permute-start(bf16[128,896]{1,0:T(8,128)(2,1)S(1)} %collective-permute-done.3.rest_3_), channel_id=1, source_target_pairs={{0,8},{8,0},{1,9},{9,1},{2,10},{10,2},{3,11},{11,3},{4,12},{12,4},... | collective-permute-start | bytes 688136 | tf_op jit(solution)/shard_map/ppermute | solution.py:32
  49.4 0.9 copy-start.14
  50.3 0.9 copy-start.15
  53.1 130.6 %all-reduce.2.cloned.1.call-start = ((), (), s32[]{:S(2)}) async-start(), calls=%async_computation.2 | async-start | bytes 7340032 | tf_op jit(solution)/shard_map/psum | solution.py:353
  53.6 2.0 %copy-start.1 = (bf16[896,2048]{1,0:T(8,128)(2,1)S(1)}, bf16[896,2048]{1,0:T(8,128)(2,1)}, u32[]{:S(2)}) copy-start(bf16[896,2048]{1,0:T(8,128)(2,1)} %reshape.46.weight_ref) | copy-start | bytes 11010052
  55.6 0.9 copy-start.13
  69.9 5.4 %copy-start.5 = (bf16[896,2048]{1,0:T(8,128)(2,1)}, bf16[896,2048]{1,0:T(8,128)(2,1)S(1)}, u32[]{:S(2)}) copy-start(bf16[896,2048]{1,0:T(8,128)(2,1)S(1)} %get-tuple-element.44) | copy-start | bytes 11010052
  75.3 2.8 %collective-permute-start.8 = (bf16[512,896]{1,0:T(8,128)(2,1)S(1)}, bf16[512,896]{1,0:T(8,128)(2,1)S(1)}, u32[]{:S(2)}, u32[]{:S(2)}) collective-permute-start(bf16[512,896]{1,0:T(8,128)(2,1)S(1)} %fusion.3), channel_id=1, source_target_pairs={{0,8},{8,0},{1,9},{9,1},{2,10},{10,2},{3,11},{11,3},{4,12},{12,4},... | collective-permute-start | bytes 2752520 | tf_op jit(solution)/shard_map/ppermute | solution.py:32
  78.1 2.1 %copy-start.2 = (bf16[896,2048]{1,0:T(8,128)(2,1)S(1)}, bf16[896,2048]{1,0:T(8,128)(2,1)}, u32[]{:S(2)}) copy-start(bf16[896,2048]{1,0:T(8,128)(2,1)} %reshape.46.weight_ref) | copy-start | bytes 11010052
  80.1 2.2 %copy-start.4 = (bf16[1024,2048]{1,0:T(8,128)(2,1)S(1)}, bf16[1024,2048]{1,0:T(8,128)(2,1)}, u32[]{:S(2)}) copy-start(bf16[1024,2048]{1,0:T(8,128)(2,1)} %get-tuple-element.46.pairs_ref) | copy-start | bytes 12582916
  82.4 16.6 %copy-start.3 = (bf16[896,896]{1,0:T(8,128)(2,1)S(1)}, bf16[896,896]{1,0:T(8,128)(2,1)}, u32[]{:S(2)}) copy-start(bf16[896,896]{1,0:T(8,128)(2,1)} %mix_ref.3) | copy-start | bytes 4816900
  82.4 16.6 %copy-start.9 = (bf16[128,2688]{1,0:T(8,128)(2,1)S(1)}, bf16[128,2688]{1,0:T(8,128)(2,1)}, u32[]{:S(2)}) copy-start(bf16[128,2688]{1,0:T(8,128)(2,1)} %get-tuple-element.51.projected_ref) | copy-start | bytes 2064388
  84.8 8.7 %collective-permute-start.10 = (bf16[128,896]{1,0:T(8,128)(2,1)S(1)}, bf16[128,896]{1,0:T(8,128)(2,1)S(1)}, u32[]{:S(2)}, u32[]{:S(2)}) collective-permute-start(bf16[128,896]{1,0:T(8,128)(2,1)S(1)} %get-tuple-element.49), channel_id=1, source_target_pairs={{0,32},{16,48},{32,0},{48,16},{1,33},{17,49},{33,1},{49,17},{2,34}... | collective-permute-start | bytes 688136 | tf_op jit(solution)/shard_map/ppermute | solution.py:28
  85.1 11.4 %collective-permute-start.11 = (bf16[128,896]{1,0:T(8,128)(2,1)S(1)}, bf16[128,896]{1,0:T(8,128)(2,1)S(1)}, u32[]{:S(2)}, u32[]{:S(2)}) collective-permute-start(bf16[128,896]{1,0:T(8,128)(2,1)S(1)} %get-tuple-element.50), channel_id=1, source_target_pairs={{0,48},{16,0},{32,16},{48,32},{1,49},{17,1},{33,17},{49,33},{2,50}... | collective-permute-start | bytes 688136 | tf_op jit(solution)/shard_map/ppermute | solution.py:28
  86.0 12.9 %collective-permute-start.9 = (bf16[128,896]{1,0:T(8,128)(2,1)S(1)}, bf16[128,896]{1,0:T(8,128)(2,1)S(1)}, u32[]{:S(2)}, u32[]{:S(2)}) collective-permute-start(bf16[128,896]{1,0:T(8,128)(2,1)S(1)} %get-tuple-element.48), channel_id=1, source_target_pairs={{0,16},{16,32},{32,48},{48,0},{1,17},{17,33},{33,49},{49,1},{2,18}... | collective-permute-start | bytes 688136 | tf_op jit(solution)/shard_map/ppermute | solution.py:28
  103.7 19.0 %all-to-all-start = ((bf16[8,128,512]{2,1,0:T(8,128)(2,1)}), bf16[8,128,512]{2,1,0:T(8,128)(2,1)S(1)}, u32[]{:S(2)}, u32[]{:S(2)}) async-start(bf16[8,128,512]{2,1,0:T(8,128)(2,1)} %shard_map.132.parts_ref), calls=%async_computation | async-start | bytes 2097152 | tf_op jit(solution)/shard_map/all_to_all | solution.py:363
  122.7 12.0 %copy-start.8 = (bf16[128,896]{1,0:T(8,128)(2,1)S(1)}, bf16[128,896]{1,0:T(8,128)(2,1)}, u32[]{:S(2)}) copy-start(bf16[128,896]{1,0:T(8,128)(2,1)} %copy-done.7) | copy-start | bytes 688132
  122.7 12.0 %copy-start.10 = (f32[1,896]{1,0:T(1,128)S(1)}, f32[1,896]{1,0:T(1,128)}, u32[]{:S(2)}) copy-start(f32[1,896]{1,0:T(1,128)} %reshape.47.gain_ref) | copy-start | bytes 10756
  126.5 64.5 %all-to-all-start.1 = ((bf16[128,8,512]{2,1,0:T(8,128)(2,1)}), bf16[128,8,512]{2,1,0:T(8,128)(2,1)S(1)}, u32[]{:S(2)}, u32[]{:S(2)}) async-start(bf16[128,8,512]{2,1,0:T(8,128)(2,1)} %fusion.6), calls=%async_computation.1 | async-start | bytes 2097152 | tf_op jit(solution)/shard_map/all_to_all | solution.py:366
  134.7 2.4 %copy-start = (bf16[896,2688]{1,0:T(8,128)(2,1)S(1)}, bf16[896,2688]{1,0:T(8,128)(2,1)}, u32[]{:S(2)}) copy-start(bf16[896,2688]{1,0:T(8,128)(2,1)} %project_ref.3) | copy-start | bytes 14450692
  140.1 16.2 %collective-permute-start.12 = (bf16[128,896]{1,0:T(8,128)(2,1)S(1)}, bf16[128,896]{1,0:T(8,128)(2,1)S(1)}, u32[]{:S(2)}, u32[]{:S(2)}) collective-permute-start(bf16[128,896]{1,0:T(8,128)(2,1)S(1)} %shard_map.133), channel_id=1, source_target_pairs={{0,0},{1,8},{2,16},{3,24},{4,32},{5,40},{6,48},{7,56},{8,1},{9,9},... | collective-permute-start | bytes 688136 | tf_op jit(solution)/shard_map/ppermute | solution.py:37
  183.7 2.0 %copy-start.6 = (bf16[896,2048]{1,0:T(8,128)(2,1)S(1)}, bf16[896,2048]{1,0:T(8,128)(2,1)}, u32[]{:S(2)}) copy-start(bf16[896,2048]{1,0:T(8,128)(2,1)} %all-reduce.2.cloned.1.call-done.sum_ref) | copy-start | bytes 11010052
Sparse Core Ops, SparseCore 0:
  53.2 31.4 all-gather.1
Sparse Core Ops, SparseCore 1:
  75.7 108.0 all-reduce.1

commit v4 on v3

--- a/solution.py
+++ b/solution.py
@@ -135,15 +135,21 @@
     )(normed, mixed)
 
 
-def cross_kernel(per, slots_ref, q_ref, up_ref, weight_ref, *rest):
-    sources, (out_ref, grad_ref, pairs_ref, sum_ref, rows_ref, turned_ref, held_ref) = rest[:8], rest[8:]
-
-    @pl.when(pl.program_id(0) == 0)
-    def _():
-        for n, source in enumerate(sources):
-            rows_ref[n * TOK : (n + 1) * TOK] = source[...]
-            turned_ref[:, n * TOK : (n + 1) * TOK] = source[...].T
-
+def cross_kernel(slots_ref, order_ref, q_ref, up_ref, far_weight_ref, *rest):
+    sources, rest = rest[:8], rest[8:]
+    (out_ref, grad_ref, sum_ref), blocks, far_ref, near = rest[:3], rest[3:7], rest[7], rest[8:12]
+    weight_ref, rows_ref, turned_ref, held_ref, pairs_ref, sems = rest[12:]
+    heads = weight_ref.shape[1] // (2 * HS)
+    width = weight_ref.shape[1] // 4
+    copies = []
+    for j in range(4):
+        at = slice(j * width, (j + 1) * width)
+        copies.append(pltpu.make_async_copy(far_weight_ref.at[:, at], weight_ref.at[:, at], sems.at[j]))
+    for copy in copies:
+        copy.start()
+    for n, source in enumerate(sources):
+        rows_ref[n * TOK : (n + 1) * TOK] = source[...]
+        turned_ref[:, n * TOK : (n + 1) * TOK] = source[...].T
     scale = 1.0 / math.sqrt(HS)
     length = q_ref.shape[1]
     none = jnp.zeros((length, HS), bf16)
@@ -151,8 +157,11 @@
     rows = [
         [pl.ds(pl.multiple_of(slots_ref[2 * c + n] * TOK, TOK), TOK) for n in range(2)] for c in spans
     ]
-    held_ref[...] = nn(rows_ref[...], weight_ref[...]).astype(bf16)
-    for first in range(0, per, 2):
+    for j, copy in enumerate(copies):
+        at = slice(j * width, (j + 1) * width)
+        copy.wait()
+        held_ref[:, at] = nn(rows_ref[...], weight_ref[:, at]).astype(bf16)
+    for first in range(0, heads, 2):
         units = []
         for h in range(first, first + 2):
             at, pair = slice(h * HS, (h + 1) * HS), slice(2 * h * HS, 2 * (h + 1) * HS)
@@ -177,86 +186,121 @@
             g = jnp.concatenate([g[:, :HS] * scale, g[:, HS:]], axis=1).astype(bf16)
             for n in range(2):
                 pairs_ref[rows[c][n], pair] = g[n * TOK : (n + 1) * TOK]
-    sum_ref[...] = nn(turned_ref[...], pairs_ref[...]).astype(bf16)
-
-
-def cross(slots, queries, upstream, weight, sources, per):
-    spans, length, inner = queries.shape
-    rows = len(sources) * TOK
-    column = pl.BlockSpec((spans, length, per * HS), lambda i, s: (0, 0, i))
-    return pl.pallas_call(
-        functools.partial(cross_kernel, per),
+    most = sum_ref.shape[1]
+    sum_ref[...] = nn(turned_ref[...], pairs_ref[:, :most]).astype(bf16)
+    for d, block in enumerate(blocks):
+        at = pl.ds(pl.multiple_of(most + order_ref[d] * HS, HS), HS)
+        block[...] = nn(turned_ref[...], pairs_ref[:, at]).astype(bf16)
+    far_ref[...] = nt(pairs_ref[4 * TOK :], weight_ref[...]).astype(bf16)
+    total = nt(pairs_ref[: 4 * TOK], weight_ref[...])
+    for n, one in enumerate(near):
+        one[...] = total[n * TOK : (n + 1) * TOK]
+
+
+def cross(slots, order, queries, upstream, weight, sources):
+    rows, wide = len(sources) * TOK, weight.shape[1]
+    vmem = pl.BlockSpec(memory_space=pltpu.VMEM)
+    smem = pl.BlockSpec(memory_space=pltpu.SMEM)
+    return pl.pallas_call(
+        cross_kernel,
+        in_specs=[smem, smem, vmem, vmem, pl.BlockSpec(memory_space=pl.ANY)] + [vmem] * len(sources),
+        out_specs=[vmem] * 12,
+        out_shape=[
+            jax.ShapeDtypeStruct(queries.shape, bf16),
+            jax.ShapeDtypeStruct(queries.shape, bf16),
+            jax.ShapeDtypeStruct((ENC, wide - 4 * HS), bf16),
+            *[jax.ShapeDtypeStruct((ENC, HS), bf16)] * 4,
+            jax.ShapeDtypeStruct((4 * TOK, ENC), bf16),
+            *[jax.ShapeDtypeStruct((TOK, ENC), f32)] * 4,
+        ],
+        scratch_shapes=[
+            pltpu.VMEM((ENC, wide), bf16),
+            pltpu.VMEM((rows, ENC), bf16),
+            pltpu.VMEM((ENC, rows), bf16),
+            pltpu.VMEM((rows, wide), bf16),
+            pltpu.VMEM((rows, wide), bf16),
+            pltpu.SemaphoreType.DMA((4,)),
+        ],
+        compiler_params=params(50),
+        cost_estimate=cost(24 * 10**9, 16 * 10**6),
+    )(slots, order, queries, upstream, weight, *sources)
+
+
+def plane_sum(blocks, first, second, at_second):
+    total = blocks[0].astype(f32)
+    for d in range(1, 4):
+        total += turned(first, 4, d)(blocks[d]).astype(f32)
+    total = total.astype(bf16)
+    size = total.shape[0] // 4
+    cuts = [lax.dynamic_slice_in_dim(total, (at_second + d) % 4 * size, size) for d in range(4)]
+    piece = cuts[0].astype(f32)
+    for d in range(1, 4):
+        piece += turned(second, 4, d)(cuts[d]).astype(f32)
+    piece = piece.astype(bf16)
+    line = jnp.stack([piece] + [turned(second, 4, -d)(piece) for d in range(1, 4)])
+    return [line] + [turned(first, 4, -d)(line) for d in range(1, 4)]
+
+
+def place_kernel(at_ref, sum_ref, *rest):
+    lines, out_ref = rest[:-1], rest[-1]
+    size, most = sum_ref.shape[0], sum_ref.shape[1] // HS
+    for j in range(most):
+        out_ref[pl.ds(j, size, stride=most + 4), :] = sum_ref[:, j * HS : (j + 1) * HS].astype(f32)
+    for h in range(4):
+        for d in range(4):
+
+            @pl.when((at_ref[0] + d) % 4 == h)
+            def _():
+                out_ref[pl.ds(most + h, size, stride=most + 4), :] = lines[d][0].astype(f32)
+
+
+def placed(at, summed, lines):
+    size, most = ENC // 4, summed.shape[1]
+    many = most // HS + 4
+    return pl.pallas_call(
+        place_kernel,
         grid_spec=pltpu.PrefetchScalarGridSpec(
             num_scalar_prefetch=1,
-            grid=(inner // HS // per,),
+            grid=(4,),
             in_specs=[
-                column,
-                column,
-                pl.BlockSpec((ENC, 2 * HS * per), lambda i, s: (0, i)),
-                *[pl.BlockSpec((TOK, ENC), lambda i, s: (0, 0))] * len(sources),
+                pl.BlockSpec((size, most), lambda i, s: (i, 0)),
+                *[pl.BlockSpec((1, size, HS), lambda i, s: ((i - s[1] + 4) % 4, 0, 0))] * 4,
             ],
-            out_specs=(
-                column,
-                column,
-                pl.BlockSpec((rows, 2 * HS * per), lambda i, s: (0, i)),
-                pl.BlockSpec((ENC, 2 * HS * per), lambda i, s: (0, i)),
-            ),
-            scratch_shapes=[
-                pltpu.VMEM((rows, ENC), bf16),
-                pltpu.VMEM((ENC, rows), bf16),
-                pltpu.VMEM((rows, 2 * HS * per), bf16),
-            ],
+            out_specs=pl.BlockSpec((size * many, HS), lambda i, s: (i, 0)),
         ),
-        out_shape=(
-            jax.ShapeDtypeStruct(queries.shape, bf16),
-            jax.ShapeDtypeStruct(queries.shape, bf16),
-            jax.ShapeDtypeStruct((rows, 2 * inner), bf16),
-            jax.ShapeDtypeStruct((ENC, 2 * inner), bf16),
-        ),
-        compiler_params=params(44, 1),
-        cost_estimate=cost(16 * 10**9, 16 * 10**6),
-    )(slots, queries, upstream, weight, *sources)
-
-
-def place_kernel(sum_ref, out_ref):
-    size, many = sum_ref.shape[0], sum_ref.shape[1] // HS
-    for j in range(many):
-        out_ref[pl.ds(j, size, stride=many), :] = sum_ref[:, j * HS : (j + 1) * HS].astype(f32)
-
-
-def placed(summed):
-    size = ENC // 4
-    many = summed.shape[1] // HS
-    return pl.pallas_call(
-        place_kernel,
-        grid=(4,),
-        in_specs=[pl.BlockSpec((size, summed.shape[1]), lambda i: (i, 0))],
-        out_specs=pl.BlockSpec((size * many, HS), lambda i: (i, 0)),
         out_shape=jax.ShapeDtypeStruct((ENC * many, HS), f32),
         compiler_params=params(16, 1),
         cost_estimate=cost(10**6, 11 * 10**6),
-    )(summed)
-def near_kernel(pairs_ref, weight_ref, brought_ref, own_ref, *outs):
-    total = nt(pairs_ref[...], weight_ref[...]) + brought_ref[...].astype(f32)
-    own_ref[...] = total[:TOK]
-    for n, out in enumerate(outs):
-        out[...] = total[(n + 1) * TOK : (n + 2) * TOK].astype(bf16)
-
-
-def near_sums(pairs, weight, brought):
-    def whole(*shape):
-        return pl.BlockSpec(shape, lambda i: (0, 0))
-
-    inner = weight.shape[1]
-    return pl.pallas_call(
-        near_kernel,
-        grid=(1,),
-        in_specs=[whole(4 * TOK, inner), whole(ENC, inner), whole(4 * TOK, ENC)],
-        out_specs=[whole(TOK, ENC)] * 4,
-        out_shape=[jax.ShapeDtypeStruct((TOK, ENC), f32)] + [jax.ShapeDtypeStruct((TOK, ENC), bf16)] * 3,
-        compiler_params=params(32, 1),
-        cost_estimate=cost(2 * 10**9, 8 * 10**6),
-    )(pairs, weight, brought)
+    )(at, summed, *lines)
+
+
+def turn_kernel(which_ref, held_ref, out_ref):
+    at = pl.ds(pl.multiple_of(which_ref[0] * 1024, 1024), 1024)
+    out_ref[...] = held_ref[:, at].T
+
+
+def turned_operand(which, held):
+    return pl.pallas_call(
+        turn_kernel,
+        in_specs=[pl.BlockSpec(memory_space=pltpu.SMEM), pl.BlockSpec(memory_space=pltpu.VMEM)],
+        out_specs=pl.BlockSpec(memory_space=pltpu.VMEM),
+        out_shape=jax.ShapeDtypeStruct((1024, held.shape[0]), bf16),
+        compiler_params=params(24),
+        cost_estimate=cost(10**4, 10**4),
+    )(which, held)
+
+
+def product_kernel(turned_ref, parts_ref, out_ref):
+    out_ref[...] = nn(turned_ref[...], parts_ref[...]).astype(bf16)
+
+
+def product(turned_rows, parts):
+    return pl.pallas_call(
+        product_kernel,
+        out_shape=jax.ShapeDtypeStruct((turned_rows.shape[0], parts.shape[1]), bf16),
+        compiler_params=params(24),
+        cost_estimate=cost(10**4, 10**4),
+    )(turned_rows, parts)
 
 
 def columns_of(at):
@@ -295,7 +339,7 @@
         backward_kernel,
         out_shape=jax.ShapeDtypeStruct((PARTS, TOK, LANES), bf16),
         compiler_params=params(24),
-        cost_estimate=cost(6 * 10**8, 4 * 10**6),
+        cost_estimate=cost(10**4, 10**4),
     )(grad, projected, mix)
 
 
@@ -318,7 +362,7 @@
         inputs_kernel,
         out_shape=jax.ShapeDtypeStruct((TOK, ENC), bf16),
         compiler_params=params(24),
-        cost_estimate=cost(6 * 10**8, 6 * 10**6),
+        cost_estimate=cost(10**4, 10**4),
     )(x, gain, project, parts, grad)
 
 
@@ -347,22 +391,28 @@
 
     named = span_neighbours.reshape(-1) % 8
     slots = (named % 2 != core) * 4 + (named // 2 - y) % 4
-    result, grad_queries, grad_pairs, grad_weight = cross(
-        slots.astype(jnp.int32), decoder_queries, grad_output, weight, sources, heads
+    at_x = lax.axis_index("xh") * 2 + lax.axis_index("xl")
+    at_z = lax.axis_index("z")
+    order = (at_x + jnp.arange(4, dtype=jnp.int32)) % 4
+    result, grad_queries, grad_weight, *rest = cross(
+        slots.astype(jnp.int32), order, decoder_queries, grad_output, weight, sources
     )
-    grad_cross = placed(lax.psum(grad_weight, PLANE))
+    summed = lax.psum(grad_weight, PLANE)
+    lines = plane_sum(rest[:4], ("xh", "xl"), "z", at_z)
+    grad_cross = placed(jnp.stack([at_x, at_z]).astype(jnp.int32), summed, lines)
     grad_cross = grad_cross.reshape(ENC, heads, 2, HS).swapaxes(1, 2).reshape(cross_pairs.shape)
 
-    brought = across(nt(grad_pairs[4 * TOK :], weight).astype(bf16))
-    total, *others = near_sums(grad_pairs, weight, brought)
-    for step, other in enumerate(others):
-        total += turned("y", 4, step + 1)(other).astype(f32)
+    brought = across(rest[4]).astype(f32)
+    near = [one + brought[n * TOK : (n + 1) * TOK] for n, one in enumerate(rest[5:])]
+    total = near[0]
+    for step in range(1, 4):
+        total += turned("y", 4, step)(near[step].astype(bf16)).astype(f32)
     grad_encoded = total.astype(bf16)
 
     parts = backward(grad_encoded, projected, encoder_mix)
     all_parts = lax.all_to_all(parts, TP, 0, 0, tiled=True).reshape(8 * TOK, LANES)
-    mine = jnp.where(y * 2 + core < 6, operands[:, :1024], operands[:, 1024:])
-    encoder_grad = nn(lax.optimization_barrier(mine.T), all_parts).astype(bf16).reshape(128, 8, LANES)
+    which = (y * 2 + core >= 6).astype(jnp.int32).reshape(1)
+    encoder_grad = product(turned_operand(which, operands), all_parts).reshape(128, 8, LANES)
     arrived = lax.all_to_all(encoder_grad, FINE, 0, 0, tiled=True).astype(f32)
     arrived = arrived.reshape(2, 8, 8, 8, LANES).sum(axis=(0, 2))
     rows = jnp.swapaxes(arrived, 0, 1).reshape(8, 8 * LANES)[:7]

time: 201 us -> 210 us (1.045)
  starting transfers between devices: 38.9 us -> 56.7 us
  Pallas kernels: 35.9 us -> 47.6 us
  matrix products: 9.23 us -> 0 us
  waiting for transfers between devices: 72.7 us -> 65 us
  local copies, waits for them, and re-layouts: 24.2 us -> 20.5 us
    ppermute x6 -> x18, waiting for transfers between devices: 18.9 us -> 46.9 us  [turned(): return lambda x: lax.ppermute(x, axis, pairs)]
    psum x1, waiting for transfers between devices: 27.5 us -> 3.82 us  [shards(): summed = lax.psum(grad_weight, PLANE)]
    ppermute x6 -> x18, starting transfers between devices: 10.7 us -> 27.5 us  [turned(): return lambda x: lax.ppermute(x, axis, pairs)]
    pallas_call x3 -> x4, Pallas kernels: 21 us -> 32.8 us  [the longest x1 23.7 us: cross(): pl.pallas_call(cross_kernel, in_specs=[smem, smem, vmem, vmem, pl.BlockSp...]
    dot_general x2 -> x0, matrix products: 9.23 us -> none  [dot(): lax.dot_general(a, b, ((contract[:1], contract[1:]), ((), ())), preferred...]
    ppermute x2, waiting for transfers between devices: 12.5 us -> 3.49 us  [flipped(): return lax.ppermute(x, ('y', 'c', 'xl', 'z'), pairs)]
    transpose x1 -> x0, other arithmetic: 3.76 us -> none  [shards(): encoder_grad = nn(lax.optimization_barrier(mine.T), all_parts).astype(bf1...]
    unnamed x38 -> x34, local copies, waits for them, and re-layouts: 15.1 us -> 11.4 us
  transfers between devices with their start and end apart: 17 -> 29, of which waited for: 9 -> 11; matrix products, arithmetic and copies ran while one was open for 10% -> 5% of each run, Pallas kernels for 15% -> 20%
where the time goes in v4:
time: 210 us; the launch traced here: 208 us
  waiting for transfers between devices  65 us (31%)
  starting transfers between devices  56.7 us (27%)
  Pallas kernels  47.6 us (23%)
  local copies, waits for them, and re-layouts  20.5 us (10%)
  between operations  15.8 us (8%)
  other arithmetic  2.17 us (1%)
    ppermute x18, waiting for transfers between devices, turned(): return lambda x: lax.ppermute(x, axis, pairs)  46.9 us
    ppermute x18, starting transfers between devices, turned(): return lambda x: lax.ppermute(x, axis, pairs)  27.5 us
    pallas_call x1, Pallas kernels, cross(): pl.pallas_call(cross_kernel, in_specs=[smem, smem, vmem, vmem, pl.BlockSp...  23.7 us
    unnamed x34, local copies, waits for them, and re-layouts  11.4 us
    ppermute x2, starting transfers between devices, flipped(): return lax.ppermute(x, ('y', 'c', 'xl', 'z'), pairs)  8.82 us
    all_to_all x1, starting transfers between devices, shards(): arrived = lax.all_to_all(encoder_grad, FINE, 0, 0, tiled=True).astype(f32)  8.28 us
    all_to_all x1, waiting for transfers between devices, shards(): lax.all_to_all(parts, TP, 0, 0, tiled=True).reshape(8 * TOK, LANES)  8.04 us
    reshape x1, local copies, waits for them, and re-layouts, shards(): cross_pairs.reshape(ENC, 2, heads, HS).swapaxes(1, 2)  7.15 us
  transfers between devices with their start and end apart: 29, of which 11 were waited for; matrix products, arithmetic and copies ran while one was open for 5% of the time, Pallas kernels for 20%

profile of v4, /device:TPU:1, one launch (start us, length us, event | category | flops | bytes accessed | tf_op | source)
XLA Modules:
  0.0 207.7 jit_solution(15568403986121708643)
XLA Ops:
  8.0 4.9 %collective-permute-start = (bf16[128,896]{1,0:T(8,128)(2,1)}, bf16[128,896]{1,0:T(8,128)(2,1)S(1)}, u32[]{:S(2)}, u32[]{:S(2)}) collective-permute-start(bf16[128,896]{1,0:T(8,128)(2,1)} %bitcast.35), channel_id=1, source_target_pairs={{0,0},{1,8},{2,16},{3,24},{4,32},{5,40},{6,48},{7,56},{8,1},{9,9},... | collective-permute-start | bytes 688136 | tf_op jit(solution)/shard_map/ppermute | solution.py:37
  13.0 7.1 %reshape.51.far_weight_ref = bf16[896,2048]{1,0:T(8,128)(2,1)} reshape(bf16[896,8,2,128]{3,2,1,0:T(2,128)(2,1)} %bitcast.27) | data formatting | bytes 7340032 | tf_op jit(solution)/shard_map/reshape | solution.py:383
  20.7 0.7 copy-done.4
  21.4 5.4 %shard_map.127 = (bf16[128,896]{1,0:T(8,128)(2,1)}, bf16[128,896]{1,0:T(8,128)(2,1)}, bf16[128,2688]{1,0:T(8,128)(2,1)}, bf16[128,896]{1,0:T(8,128)(2,1)}) custom-call(bf16[128,896]{1,0:T(8,128)(2,1)} %copy-done.4, f32[1,896]{1,0:T(1,128)} %reshape.52.gain_ref, bf16[896,2688]{1,0:T(8,128)(2,1)} %project_ref.3, bf16[896,896]{1,0:T(8,128)(2,1)} %mix_ref.3), custom_call_target="tpu_custom_call" | custom-call | flops 1000000000 | bytes 8000000 | tf_op jit(solution)/shard_map/pallas_call | solution.py:106
  26.9 8.1 %collective-permute-start.1 = (bf16[128,896]{1,0:T(8,128)(2,1)}, bf16[128,896]{1,0:T(8,128)(2,1)S(1)}, u32[]{:S(2)}, u32[]{:S(2)}) collective-permute-start(bf16[128,896]{1,0:T(8,128)(2,1)} %get-tuple-element.38.rest_0_), channel_id=1, source_target_pairs={{0,48},{16,0},{32,16},{48,32},{1,49},{17,1},{33,17},{49,33},{2,50}... | collective-permute-start | bytes 688136 | tf_op jit(solution)/shard_map/ppermute | solution.py:28
  35.0 0.8 collective-permute-start.3
  35.8 3.1 %collective-permute-start.4 = (bf16[128,896]{1,0:T(8,128)(2,1)}, bf16[128,896]{1,0:T(8,128)(2,1)S(1)}, u32[]{:S(2)}, u32[]{:S(2)}) collective-permute-start(bf16[128,896]{1,0:T(8,128)(2,1)} %get-tuple-element.38.rest_0_), channel_id=1, source_target_pairs={{0,8},{8,0},{1,9},{9,1},{2,10},{10,2},{3,11},{11,3},{4,12},{12,4},... | collective-permute-start | bytes 688136 | tf_op jit(solution)/shard_map/ppermute | solution.py:32
  39.0 5.8 %collective-permute-done.1.rest_1_ = bf16[128,896]{1,0:T(8,128)(2,1)S(1)} collective-permute-done((bf16[128,896]{1,0:T(8,128)(2,1)}, bf16[128,896]{1,0:T(8,128)(2,1)S(1)}, u32[]{:S(2)}, u32[]{:S(2)}) %collective-permute-start.1) | collective-permute-done | bytes 229408 | tf_op jit(solution)/shard_map/ppermute | solution.py:28
  44.7 1.3 collective-permute-start.5
  46.0 1.2 collective-permute-start.6
  47.2 0.8 collective-permute-done.3.rest_3_
  48.0 1.4 collective-permute-start.7
  49.4 0.9 copy-done.10
  50.3 0.9 copy-done.11
  51.3 1.7 shard_map.128
  53.5 0.9 copy-done.9
  54.5 23.7 %shard_map.129 = (bf16[4,64,1024]{2,1,0:T(8,128)(2,1)}, bf16[4,64,1024]{2,1,0:T(8,128)(2,1)}, bf16[896,1536]{1,0:T(8,128)(2,1)}, bf16[896,128]{1,0:T(8,128)(2,1)...) custom-call(s32[8]{0:T(128)S(1)} %fusion.7.slots_ref, ...), custom_call_target="tpu_custom_call" | custom-call | flops 24000000000 | bytes 16000000 | tf_op jit(solution)/shard_map/pallas_call | solution.py:204
  78.2 0.7 copy-done.7
  78.9 2.7 %collective-permute-done.20 = bf16[512,896]{1,0:T(8,128)(2,1)S(1)} collective-permute-done((bf16[512,896]{1,0:T(8,128)(2,1)}, bf16[512,896]{1,0:T(8,128)(2,1)S(1)}, u32[]{:S(2)}, u32[]{:S(2)}) %collective-permute-start.20) | collective-permute-done | bytes 917536 | tf_op jit(solution)/shard_map/ppermute | solution.py:32
  82.0 1.6 collective-permute-start.22
  83.7 1.0 collective-permute-start.23
  84.7 10.5 %collective-permute-done.21 = bf16[128,896]{1,0:T(8,128)(2,1)S(1)} collective-permute-done((bf16[128,896]{1,0:T(8,128)(2,1)S(1)}, bf16[128,896]{1,0:T(8,128)(2,1)S(1)}, u32[]{:S(2)}, u32[]{:S(2)}) %collective-permute-start.21) | collective-permute-done | bytes 229408 | tf_op jit(solution)/shard_map/ppermute | solution.py:28
  95.8 4.6 %shard_map.132.parts_ref = bf16[8,128,512]{2,1,0:T(8,128)(2,1)} custom-call(bf16[128,896]{1,0:T(8,128)(2,1)S(1)} %fusion.6.grad_ref, bf16[128,2688]{1,0:T(8,128)(2,1)S(1)} %copy-done.6, bf16[896,896]{1,0:T(8,128)(2,1)S(1)} %copy-done.1), custom_call_target="tpu_custom_call" | custom-call | flops 10000 | bytes 10000 | tf_op jit(solution)/shard_map/pallas_call | solution.py:338
  100.4 4.8 %all-to-all-start = ((bf16[8,128,512]{2,1,0:T(8,128)(2,1)}), bf16[8,128,512]{2,1,0:T(8,128)(2,1)S(1)}, u32[]{:S(2)}, u32[]{:S(2)}) async-start(bf16[8,128,512]{2,1,0:T(8,128)(2,1)} %shard_map.132.parts_ref), calls=%async_computation | async-start | bytes 2097152 | tf_op jit(solution)/shard_map/all_to_all | solution.py:413
  105.2 1.0 collective-permute-start.10
  106.6 2.8 %collective-permute-start.9 = (bf16[896,128]{1,0:T(8,128)(2,1)}, bf16[896,128]{1,0:T(8,128)(2,1)}, u32[]{:S(2)}, u32[]{:S(2)}) collective-permute-start(bf16[896,128]{1,0:T(8,128)(2,1)} %get-tuple-element.51), channel_id=1, source_target_pairs={{0,64},{4,68},{64,0},{68,4},{1,65},{5,69},{65,1},{69,5},{2,66},{6,... | collective-permute-start | bytes 688136 | tf_op jit(solution)/shard_map/ppermute | solution.py:28
  109.4 2.3 %copy-done.2 = bf16[1024,2048]{1,0:T(8,128)(2,1)S(1)} copy-done((bf16[1024,2048]{1,0:T(8,128)(2,1)S(1)}, bf16[1024,2048]{1,0:T(8,128)(2,1)}, u32[]{:S(2)}) %copy-start.2) | copy-done | bytes 4194328
  112.3 8.0 %all-to-all-done = bf16[8,128,512]{2,1,0:T(8,128)(2,1)S(1)} async-done(((bf16[8,128,512]{2,1,0:T(8,128)(2,1)}), bf16[8,128,512]{2,1,0:T(8,128)(2,1)S(1)}, u32[]{:S(2)}, u32[]{:S(2)}) %all-to-all-start) | async-done | bytes 1048608 | tf_op jit(solution)/shard_map/all_to_all | solution.py:413
  120.4 2.2 %shard_map.133 = bf16[1024,512]{1,0:T(8,128)(2,1)} custom-call(bf16[1024,1024]{1,0:T(8,128)(2,1)S(1)} %shard_map.131.turned_ref, bf16[1024,512]{1,0:T(8,128)(2,1)S(1)} %bitcast.24), custom_call_target="tpu_custom_call" | custom-call | flops 10000 | bytes 10000 | tf_op jit(solution)/shard_map/pallas_call | solution.py:298
  122.6 8.3 %all-to-all-start.1 = ((bf16[128,8,512]{2,1,0:T(8,128)(2,1)}), bf16[128,8,512]{2,1,0:T(8,128)(2,1)S(1)}, u32[]{:S(2)}, u32[]{:S(2)}) async-start(bf16[128,8,512]{2,1,0:T(8,128)(2,1)} %bitcast.14), calls=%async_computation.1 | async-start | bytes 2097152 | tf_op jit(solution)/shard_map/all_to_all | solution.py:416
  130.9 1.4 add_convert_fusion
  132.4 1.6 collective-permute-start.11
  134.0 2.9 %collective-permute-start.12 = (bf16[224,128]{1,0:T(8,128)(2,1)S(1)}, bf16[224,128]{1,0:T(8,128)(2,1)S(1)}, u32[]{:S(2)}, u32[]{:S(2)}) collective-permute-start(bf16[224,128]{1,0:T(8,128)(2,1)S(1)} %get-tuple-element.65), channel_id=1, source_target_pairs={{0,2},{1,3},{2,0},{3,1},{4,6},{5,7},{6,4},{7,5},{8,10},{9,11},{10,... | collective-permute-start | bytes 172040 | tf_op jit(solution)/shard_map/ppermute | solution.py:28
  136.9 0.9 collective-permute-start.13
  137.8 8.4 %collective-permute-done.11 = bf16[224,128]{1,0:T(8,128)(2,1)S(1)} collective-permute-done((bf16[224,128]{1,0:T(8,128)(2,1)S(1)}, bf16[224,128]{1,0:T(8,128)(2,1)S(1)}, u32[]{:S(2)}, u32[]{:S(2)}) %collective-permute-start.11) | collective-permute-done | bytes 57376 | tf_op jit(solution)/shard_map/ppermute | solution.py:28
  146.2 5.7 %collective-permute-done.12 = bf16[224,128]{1,0:T(8,128)(2,1)S(1)} collective-permute-done((bf16[224,128]{1,0:T(8,128)(2,1)S(1)}, bf16[224,128]{1,0:T(8,128)(2,1)S(1)}, u32[]{:S(2)}, u32[]{:S(2)}) %collective-permute-start.12) | collective-permute-done | bytes 57376 | tf_op jit(solution)/shard_map/ppermute | solution.py:28
  152.1 1.1 collective-permute-start.15
  153.7 2.4 %copy-done = bf16[896,2688]{1,0:T(8,128)(2,1)S(1)} copy-done((bf16[896,2688]{1,0:T(8,128)(2,1)S(1)}, bf16[896,2688]{1,0:T(8,128)(2,1)}, u32[]{:S(2)}) %copy-start) | copy-done | bytes 4816920
  156.1 2.9 %shard_map.134 = bf16[128,896]{1,0:T(8,128)(2,1)S(1)} custom-call(bf16[128,896]{1,0:T(8,128)(2,1)S(1)} %copy-done.5, f32[1,896]{1,0:T(1,128)S(1)} %copy-done.8, bf16[896,2688]{1,0:T(8,128)(2,1)S(1)} %copy-done, bf16[8,128,512]{2,1,0:T(8,128)(2,1)} %shard_map.132.parts_ref, bf16[128,896]{1,0:T(8,128)(2,1)S(1)} %fusion.6.grad_ref), custom_call_target="tpu_custom_call" | custom-call | flops 10000 | bytes 10000 | tf_op jit(solution)/shard_map/pallas_call | solution.py:361
  159.0 3.9 %collective-permute-start.24 = (bf16[128,896]{1,0:T(8,128)(2,1)S(1)}, bf16[128,896]{1,0:T(8,128)(2,1)S(1)}, u32[]{:S(2)}, u32[]{:S(2)}) collective-permute-start(bf16[128,896]{1,0:T(8,128)(2,1)S(1)} %shard_map.134), channel_id=1, source_target_pairs={{0,0},{1,8},{2,16},{3,24},{4,32},{5,40},{6,48},{7,56},{8,1},{9,9},... | collective-permute-start | bytes 688136 | tf_op jit(solution)/shard_map/ppermute | solution.py:37
  163.0 3.6 %collective-permute-start.17 = (bf16[4,224,128]{2,1,0:T(8,128)(2,1)S(1)}, bf16[4,224,128]{2,1,0:T(8,128)(2,1)S(1)}, u32[]{:S(2)}, u32[]{:S(2)}) collective-permute-start(bf16[4,224,128]{2,1,0:T(8,128)(2,1)S(1)} %pad_maximum_fusion.rest_0_), channel_id=1, source_target_pairs={{0,68},{4,0},{64,4},{68,64},{1,69},{5,1},{65,5},{69,65},{2,70},{6,... | collective-permute-start | bytes 688136 | tf_op jit(solution)/shard_map/ppermute | solution.py:28
  166.6 0.9 collective-permute-start.18
  167.5 3.5 %collective-permute-done.24 = bf16[128,896]{1,0:T(8,128)(2,1)S(1)} collective-permute-done((bf16[128,896]{1,0:T(8,128)(2,1)S(1)}, bf16[128,896]{1,0:T(8,128)(2,1)S(1)}, u32[]{:S(2)}, u32[]{:S(2)}) %collective-permute-start.24) | collective-permute-done | bytes 229408 | tf_op jit(solution)/shard_map/ppermute | solution.py:37
  171.0 15.3 %collective-permute-done.17.rest_1_ = bf16[4,224,128]{2,1,0:T(8,128)(2,1)S(1)} collective-permute-done((bf16[4,224,128]{2,1,0:T(8,128)(2,1)S(1)}, bf16[4,224,128]{2,1,0:T(8,128)(2,1)S(1)}, u32[]{:S(2)}, u32[]{:S(2)}) %collective-permute-start.17) | collective-permute-done | bytes 229408 | tf_op jit(solution)/shard_map/ppermute | solution.py:28
  186.4 3.8 %all-reduce.2.cloned.1.call-done.sum_ref = bf16[896,1536]{1,0:T(8,128)(2,1)} async-done(((bf16[896,1536]{1,0:T(8,128)(2,1)}), bf16[896,1536]{1,0:T(8,128)(2,1)}) %all-reduce.2.cloned.1.call-update) | async-done | bytes 2752528 | tf_op jit(solution)/shard_map/psum | solution.py:400
  190.2 1.8 copy-done.3
  192.0 6.2 %shard_map.130 = f32[14336,128]{1,0:T(8,128)} custom-call(s32[2]{0:T(128)S(1)} %pad_add_fusion.at_ref, bf16[896,1536]{1,0:T(8,128)(2,1)S(1)} %copy-done.3, bf16[4,224,128]{2,1,0:T(8,128)(2,1)S(1)} %pad_maximum_fusion.rest_0_, bf16[4,224,128]{2,1,0:T(8,128)(2,1)S(1)} %collective-permute-done.17.rest_1_, ...), custom_call_target="tpu_custom_call" | custom-call | flops 1000000 | bytes 11000000 | tf_op jit(solution)/shard_map/pallas_call | solution.py:260
  199.6 0.7 copy.25
  (70 shorter events, 5.5 us)
Async XLA Ops:
  8.0 101.4 %all-gather.2.cloned.1.call-start = ((), (), s32[]{:S(2)}) async-start(), calls=%async_computation.3 | async-start | bytes 4718592 | tf_op jit(solution)/shard_map/all_gather | solution.py:390
  8.0 12.7 %collective-permute-start = (bf16[128,896]{1,0:T(8,128)(2,1)}, bf16[128,896]{1,0:T(8,128)(2,1)S(1)}, u32[]{:S(2)}, u32[]{:S(2)}) collective-permute-start(bf16[128,896]{1,0:T(8,128)(2,1)} %bitcast.35), channel_id=1, source_target_pairs={{0,0},{1,8},{2,16},{3,24},{4,32},{5,40},{6,48},{7,56},{8,1},{9,9},... | collective-permute-start | bytes 688136 | tf_op jit(solution)/shard_map/ppermute | solution.py:37
  13.0 7.2 %copy-start.14 = (f32[896]{0:T(1024)S(1)}, f32[896]{0:T(1024)}, u32[]{:S(2)}) copy-start(f32[896]{0:T(1024)} %param.9) | copy-start | bytes 10756
  20.7 32.6 %copy-start.15 = (s32[4,2]{0,1:T(2,128)S(1)}, s32[4,2]{0,1:T(2,128)}, u32[]{:S(2)}) copy-start(s32[4,2]{0,1:T(2,128)} %param.14) | copy-start | bytes 100
  20.7 0.7 copy-start.4
  26.9 17.8 %collective-permute-start.1 = (bf16[128,896]{1,0:T(8,128)(2,1)}, bf16[128,896]{1,0:T(8,128)(2,1)S(1)}, u32[]{:S(2)}, u32[]{:S(2)}) collective-permute-start(bf16[128,896]{1,0:T(8,128)(2,1)} %get-tuple-element.38.rest_0_), channel_id=1, source_target_pairs={{0,48},{16,0},{32,16},{48,32},{1,49},{17,1},{33,17},{49,33},{2,50}... | collective-permute-start | bytes 688136 | tf_op jit(solution)/shard_map/ppermute | solution.py:28
  34.9 11.1 %collective-permute-start.2 = (bf16[128,896]{1,0:T(8,128)(2,1)}, bf16[128,896]{1,0:T(8,128)(2,1)S(1)}, u32[]{:S(2)}, u32[]{:S(2)}) collective-permute-start(bf16[128,896]{1,0:T(8,128)(2,1)} %get-tuple-element.38.rest_0_), channel_id=1, source_target_pairs={{0,32},{16,48},{32,0},{48,16},{1,33},{17,49},{33,1},{49,17},{2,34}... | collective-permute-start | bytes 688136 | tf_op jit(solution)/shard_map/ppermute | solution.py:28
  35.0 12.9 %collective-permute-start.3 = (bf16[128,896]{1,0:T(8,128)(2,1)}, bf16[128,896]{1,0:T(8,128)(2,1)S(1)}, u32[]{:S(2)}, u32[]{:S(2)}) collective-permute-start(bf16[128,896]{1,0:T(8,128)(2,1)} %get-tuple-element.38.rest_0_), channel_id=1, source_target_pairs={{0,16},{16,32},{32,48},{48,0},{1,17},{17,33},{33,49},{49,1},{2,18}... | collective-permute-start | bytes 688136 | tf_op jit(solution)/shard_map/ppermute | solution.py:28
  35.8 17.2 %collective-permute-start.4 = (bf16[128,896]{1,0:T(8,128)(2,1)}, bf16[128,896]{1,0:T(8,128)(2,1)S(1)}, u32[]{:S(2)}, u32[]{:S(2)}) collective-permute-start(bf16[128,896]{1,0:T(8,128)(2,1)} %get-tuple-element.38.rest_0_), channel_id=1, source_target_pairs={{0,8},{8,0},{1,9},{9,1},{2,10},{10,2},{3,11},{11,3},{4,12},{12,4},... | collective-permute-start | bytes 688136 | tf_op jit(solution)/shard_map/ppermute | solution.py:32
  44.7 8.3 %collective-permute-start.5 = (bf16[128,896]{1,0:T(8,128)(2,1)S(1)}, bf16[128,896]{1,0:T(8,128)(2,1)S(1)}, u32[]{:S(2)}, u32[]{:S(2)}) collective-permute-start(bf16[128,896]{1,0:T(8,128)(2,1)S(1)} %collective-permute-done.1.rest_1_), channel_id=1, source_target_pairs={{0,8},{8,0},{1,9},{9,1},{2,10},{10,2},{3,11},{11,3},{4,12},{12,4},... | collective-permute-start | bytes 688136 | tf_op jit(solution)/shard_map/ppermute | solution.py:32
  46.0 7.1 %collective-permute-start.6 = (bf16[128,896]{1,0:T(8,128)(2,1)S(1)}, bf16[128,896]{1,0:T(8,128)(2,1)S(1)}, u32[]{:S(2)}, u32[]{:S(2)}) collective-permute-start(bf16[128,896]{1,0:T(8,128)(2,1)S(1)} %collective-permute-done.2.rest_2_), channel_id=1, source_target_pairs={{0,8},{8,0},{1,9},{9,1},{2,10},{10,2},{3,11},{11,3},{4,12},{12,4},... | collective-permute-start | bytes 688136 | tf_op jit(solution)/shard_map/ppermute | solution.py:32
  48.0 5.1 %collective-permute-start.7 = (bf16[128,896]{1,0:T(8,128)(2,1)S(1)}, bf16[128,896]{1,0:T(8,128)(2,1)S(1)}, u32[]{:S(2)}, u32[]{:S(2)}) collective-permute-start(bf16[128,896]{1,0:T(8,128)(2,1)S(1)} %collective-permute-done.3.rest_3_), channel_id=1, source_target_pairs={{0,8},{8,0},{1,9},{9,1},{2,10},{10,2},{3,11},{11,3},{4,12},{12,4},... | collective-permute-start | bytes 688136 | tf_op jit(solution)/shard_map/ppermute | solution.py:32
  49.4 0.9 copy-start.10
  50.3 0.9 copy-start.11
  53.1 137.1 %all-reduce.2.cloned.1.call-start = ((), (), s32[]{:S(2)}) async-start(), calls=%async_computation.2 | async-start | bytes 5505024 | tf_op jit(solution)/shard_map/psum | solution.py:400
  53.5 0.9 copy-start.9
  78.2 0.7 copy-start.7
  78.9 2.7 %collective-permute-start.20 = (bf16[512,896]{1,0:T(8,128)(2,1)}, bf16[512,896]{1,0:T(8,128)(2,1)S(1)}, u32[]{:S(2)}, u32[]{:S(2)}) collective-permute-start(bf16[512,896]{1,0:T(8,128)(2,1)} %get-tuple-element.55), channel_id=1, source_target_pairs={{0,8},{8,0},{1,9},{9,1},{2,10},{10,2},{3,11},{11,3},{4,12},{12,4},... | collective-permute-start | bytes 2752520 | tf_op jit(solution)/shard_map/ppermute | solution.py:32
  78.9 2.8 %copy-start.12 = (f32[128,896]{1,0:T(8,128)S(1)}, f32[128,896]{1,0:T(8,128)}, u32[]{:S(2)}) copy-start(f32[128,896]{1,0:T(8,128)} %get-tuple-element.57) | copy-start | bytes 1376260
  78.9 2.8 %copy-start.13 = (f32[128,896]{1,0:T(8,128)S(1)}, f32[128,896]{1,0:T(8,128)}, u32[]{:S(2)}) copy-start(f32[128,896]{1,0:T(8,128)} %get-tuple-element.58) | copy-start | bytes 1376260
  81.7 14.0 %copy-start.1 = (bf16[896,896]{1,0:T(8,128)(2,1)S(1)}, bf16[896,896]{1,0:T(8,128)(2,1)}, u32[]{:S(2)}) copy-start(bf16[896,896]{1,0:T(8,128)(2,1)} %mix_ref.3) | copy-start | bytes 4816900
  81.7 14.0 %copy-start.6 = (bf16[128,2688]{1,0:T(8,128)(2,1)S(1)}, bf16[128,2688]{1,0:T(8,128)(2,1)}, u32[]{:S(2)}) copy-start(bf16[128,2688]{1,0:T(8,128)(2,1)} %get-tuple-element.59.projected_ref) | copy-start | bytes 2064388
  81.9 13.3 %collective-permute-start.21 = (bf16[128,896]{1,0:T(8,128)(2,1)S(1)}, bf16[128,896]{1,0:T(8,128)(2,1)S(1)}, u32[]{:S(2)}, u32[]{:S(2)}) collective-permute-start(bf16[128,896]{1,0:T(8,128)(2,1)S(1)} %get-tuple-element.60), channel_id=1, source_target_pairs={{0,16},{16,32},{32,48},{48,0},{1,17},{17,33},{33,49},{49,1},{2,18}... | collective-permute-start | bytes 688136 | tf_op jit(solution)/shard_map/ppermute | solution.py:28
  82.0 13.2 %collective-permute-start.22 = (bf16[128,896]{1,0:T(8,128)(2,1)S(1)}, bf16[128,896]{1,0:T(8,128)(2,1)S(1)}, u32[]{:S(2)}, u32[]{:S(2)}) collective-permute-start(bf16[128,896]{1,0:T(8,128)(2,1)S(1)} %get-tuple-element.62), channel_id=1, source_target_pairs={{0,32},{16,48},{32,0},{48,16},{1,33},{17,49},{33,1},{49,17},{2,34}... | collective-permute-start | bytes 688136 | tf_op jit(solution)/shard_map/ppermute | solution.py:28
  83.7 11.9 %collective-permute-start.23 = (bf16[128,896]{1,0:T(8,128)(2,1)S(1)}, bf16[128,896]{1,0:T(8,128)(2,1)S(1)}, u32[]{:S(2)}, u32[]{:S(2)}) collective-permute-start(bf16[128,896]{1,0:T(8,128)(2,1)S(1)} %get-tuple-element.61), channel_id=1, source_target_pairs={{0,48},{16,0},{32,16},{48,32},{1,49},{17,1},{33,17},{49,33},{2,50}... | collective-permute-start | bytes 688136 | tf_op jit(solution)/shard_map/ppermute | solution.py:28
  100.4 20.0 %all-to-all-start = ((bf16[8,128,512]{2,1,0:T(8,128)(2,1)}), bf16[8,128,512]{2,1,0:T(8,128)(2,1)S(1)}, u32[]{:S(2)}, u32[]{:S(2)}) async-start(bf16[8,128,512]{2,1,0:T(8,128)(2,1)} %shard_map.132.parts_ref), calls=%async_computation | async-start | bytes 2097152 | tf_op jit(solution)/shard_map/all_to_all | solution.py:413
  105.2 25.7 %collective-permute-start.10 = (bf16[896,128]{1,0:T(8,128)(2,1)}, bf16[896,128]{1,0:T(8,128)(2,1)}, u32[]{:S(2)}, u32[]{:S(2)}) collective-permute-start(bf16[896,128]{1,0:T(8,128)(2,1)} %get-tuple-element.52), channel_id=1, source_target_pairs={{0,68},{4,0},{64,4},{68,64},{1,69},{5,1},{65,5},{69,65},{2,70},{6,... | collective-permute-start | bytes 688136 | tf_op jit(solution)/shard_map/ppermute | solution.py:28
  106.1 24.8 %collective-permute-start.8 = (bf16[896,128]{1,0:T(8,128)(2,1)}, bf16[896,128]{1,0:T(8,128)(2,1)}, u32[]{:S(2)}, u32[]{:S(2)}) collective-permute-start(bf16[896,128]{1,0:T(8,128)(2,1)} %get-tuple-element.50), channel_id=1, source_target_pairs={{0,4},{4,64},{64,68},{68,0},{1,5},{5,65},{65,69},{69,1},{2,6},{6,6... | collective-permute-start | bytes 688136 | tf_op jit(solution)/shard_map/ppermute | solution.py:28
  106.6 24.3 %collective-permute-start.9 = (bf16[896,128]{1,0:T(8,128)(2,1)}, bf16[896,128]{1,0:T(8,128)(2,1)}, u32[]{:S(2)}, u32[]{:S(2)}) collective-permute-start(bf16[896,128]{1,0:T(8,128)(2,1)} %get-tuple-element.51), channel_id=1, source_target_pairs={{0,64},{4,68},{64,0},{68,4},{1,65},{5,69},{65,1},{69,5},{2,66},{6,... | collective-permute-start | bytes 688136 | tf_op jit(solution)/shard_map/ppermute | solution.py:28
  109.4 2.3 %copy-start.2 = (bf16[1024,2048]{1,0:T(8,128)(2,1)S(1)}, bf16[1024,2048]{1,0:T(8,128)(2,1)}, u32[]{:S(2)}) copy-start(bf16[1024,2048]{1,0:T(8,128)(2,1)} %all-gather.2.cloned.1.call-done.held_ref) | copy-start | bytes 12582916
  122.6 31.1 %copy-start.5 = (bf16[128,896]{1,0:T(8,128)(2,1)S(1)}, bf16[128,896]{1,0:T(8,128)(2,1)}, u32[]{:S(2)}) copy-start(bf16[128,896]{1,0:T(8,128)(2,1)} %copy-done.4) | copy-start | bytes 688132
  122.6 31.1 %copy-start.8 = (f32[1,896]{1,0:T(1,128)S(1)}, f32[1,896]{1,0:T(1,128)}, u32[]{:S(2)}) copy-start(f32[1,896]{1,0:T(1,128)} %reshape.52.gain_ref) | copy-start | bytes 10756
  122.6 75.6 %all-to-all-start.1 = ((bf16[128,8,512]{2,1,0:T(8,128)(2,1)}), bf16[128,8,512]{2,1,0:T(8,128)(2,1)S(1)}, u32[]{:S(2)}, u32[]{:S(2)}) async-start(bf16[128,8,512]{2,1,0:T(8,128)(2,1)} %bitcast.14), calls=%async_computation.1 | async-start | bytes 2097152 | tf_op jit(solution)/shard_map/all_to_all | solution.py:416
  132.4 13.8 %collective-permute-start.11 = (bf16[224,128]{1,0:T(8,128)(2,1)S(1)}, bf16[224,128]{1,0:T(8,128)(2,1)S(1)}, u32[]{:S(2)}, u32[]{:S(2)}) collective-permute-start(bf16[224,128]{1,0:T(8,128)(2,1)S(1)} %get-tuple-element.63), channel_id=1, source_target_pairs={{0,1},{1,2},{2,3},{3,0},{4,5},{5,6},{6,7},{7,4},{8,9},{9,10},{10,1... | collective-permute-start | bytes 172040 | tf_op jit(solution)/shard_map/ppermute | solution.py:28
  134.0 18.0 %collective-permute-start.12 = (bf16[224,128]{1,0:T(8,128)(2,1)S(1)}, bf16[224,128]{1,0:T(8,128)(2,1)S(1)}, u32[]{:S(2)}, u32[]{:S(2)}) collective-permute-start(bf16[224,128]{1,0:T(8,128)(2,1)S(1)} %get-tuple-element.65), channel_id=1, source_target_pairs={{0,2},{1,3},{2,0},{3,1},{4,6},{5,7},{6,4},{7,5},{8,10},{9,11},{10,... | collective-permute-start | bytes 172040 | tf_op jit(solution)/shard_map/ppermute | solution.py:28
  136.9 15.0 %collective-permute-start.13 = (bf16[224,128]{1,0:T(8,128)(2,1)S(1)}, bf16[224,128]{1,0:T(8,128)(2,1)S(1)}, u32[]{:S(2)}, u32[]{:S(2)}) collective-permute-start(bf16[224,128]{1,0:T(8,128)(2,1)S(1)} %get-tuple-element.64), channel_id=1, source_target_pairs={{0,3},{1,0},{2,1},{3,2},{4,7},{5,4},{6,5},{7,6},{8,11},{9,8},{10,9... | collective-permute-start | bytes 172040 | tf_op jit(solution)/shard_map/ppermute | solution.py:28
  152.0 10.9 %collective-permute-start.14 = (bf16[224,128]{1,0:T(8,128)(2,1)S(1)}, bf16[224,128]{1,0:T(8,128)(2,1)S(1)}, u32[]{:S(2)}, u32[]{:S(2)}) collective-permute-start(bf16[224,128]{1,0:T(8,128)(2,1)S(1)} %add_convert_fusion.1), channel_id=1, source_target_pairs={{0,3},{1,0},{2,1},{3,2},{4,7},{5,4},{6,5},{7,6},{8,11},{9,8},{10,9... | collective-permute-start | bytes 172040 | tf_op jit(solution)/shard_map/ppermute | solution.py:28
  152.1 10.9 %collective-permute-start.15 = (bf16[224,128]{1,0:T(8,128)(2,1)S(1)}, bf16[224,128]{1,0:T(8,128)(2,1)S(1)}, u32[]{:S(2)}, u32[]{:S(2)}) collective-permute-start(bf16[224,128]{1,0:T(8,128)(2,1)S(1)} %add_convert_fusion.1), channel_id=1, source_target_pairs={{0,2},{1,3},{2,0},{3,1},{4,6},{5,7},{6,4},{7,5},{8,10},{9,11},{10,... | collective-permute-start | bytes 172040 | tf_op jit(solution)/shard_map/ppermute | solution.py:28
  153.2 9.7 %collective-permute-start.16 = (bf16[224,128]{1,0:T(8,128)(2,1)S(1)}, bf16[224,128]{1,0:T(8,128)(2,1)S(1)}, u32[]{:S(2)}, u32[]{:S(2)}) collective-permute-start(bf16[224,128]{1,0:T(8,128)(2,1)S(1)} %add_convert_fusion.1), channel_id=1, source_target_pairs={{0,1},{1,2},{2,3},{3,0},{4,5},{5,6},{6,7},{7,4},{8,9},{9,10},{10,1... | collective-permute-start | bytes 172040 | tf_op jit(solution)/shard_map/ppermute | solution.py:28
  153.7 2.4 %copy-start = (bf16[896,2688]{1,0:T(8,128)(2,1)S(1)}, bf16[896,2688]{1,0:T(8,128)(2,1)}, u32[]{:S(2)}) copy-start(bf16[896,2688]{1,0:T(8,128)(2,1)} %project_ref.3) | copy-start | bytes 14450692
  159.0 12.0 %collective-permute-start.24 = (bf16[128,896]{1,0:T(8,128)(2,1)S(1)}, bf16[128,896]{1,0:T(8,128)(2,1)S(1)}, u32[]{:S(2)}, u32[]{:S(2)}) collective-permute-start(bf16[128,896]{1,0:T(8,128)(2,1)S(1)} %shard_map.134), channel_id=1, source_target_pairs={{0,0},{1,8},{2,16},{3,24},{4,32},{5,40},{6,48},{7,56},{8,1},{9,9},... | collective-permute-start | bytes 688136 | tf_op jit(solution)/shard_map/ppermute | solution.py:37
  163.0 23.4 %collective-permute-start.17 = (bf16[4,224,128]{2,1,0:T(8,128)(2,1)S(1)}, bf16[4,224,128]{2,1,0:T(8,128)(2,1)S(1)}, u32[]{:S(2)}, u32[]{:S(2)}) collective-permute-start(bf16[4,224,128]{2,1,0:T(8,128)(2,1)S(1)} %pad_maximum_fusion.rest_0_), channel_id=1, source_target_pairs={{0,68},{4,0},{64,4},{68,64},{1,69},{5,1},{65,5},{69,65},{2,70},{6,... | collective-permute-start | bytes 688136 | tf_op jit(solution)/shard_map/ppermute | solution.py:28
  166.6 19.8 %collective-permute-start.18 = (bf16[4,224,128]{2,1,0:T(8,128)(2,1)S(1)}, bf16[4,224,128]{2,1,0:T(8,128)(2,1)S(1)}, u32[]{:S(2)}, u32[]{:S(2)}) collective-permute-start(bf16[4,224,128]{2,1,0:T(8,128)(2,1)S(1)} %pad_maximum_fusion.rest_0_), channel_id=1, source_target_pairs={{0,64},{4,68},{64,0},{68,4},{1,65},{5,69},{65,1},{69,5},{2,66},{6,... | collective-permute-start | bytes 688136 | tf_op jit(solution)/shard_map/ppermute | solution.py:28
  167.5 18.9 %collective-permute-start.19 = (bf16[4,224,128]{2,1,0:T(8,128)(2,1)S(1)}, bf16[4,224,128]{2,1,0:T(8,128)(2,1)S(1)}, u32[]{:S(2)}, u32[]{:S(2)}) collective-permute-start(bf16[4,224,128]{2,1,0:T(8,128)(2,1)S(1)} %pad_maximum_fusion.rest_0_), channel_id=1, source_target_pairs={{0,4},{4,64},{64,68},{68,0},{1,5},{5,65},{65,69},{69,1},{2,6},{6,6... | collective-permute-start | bytes 688136 | tf_op jit(solution)/shard_map/ppermute | solution.py:28
  190.2 1.8 copy-start.3
Sparse Core Ops, SparseCore 0:
  53.2 31.4 all-gather.1
Sparse Core Ops, SparseCore 1:
  79.0 111.1 all-reduce.1

commit v5 on v3

--- a/solution.py
+++ b/solution.py
@@ -102,7 +102,7 @@
     shape = jax.ShapeDtypeStruct((TOK, ENC), bf16)
     wide = jax.ShapeDtypeStruct((TOK, 3 * ENC), bf16)
     vmem = pl.BlockSpec(memory_space=pltpu.VMEM)
-    far = pl.BlockSpec(memory_space=pl.ANY)
+    far = pl.BlockSpec(memory_space=pltpu.HBM)
     return pl.pallas_call(
         encode_kernel,
         in_specs=[vmem, vmem, far, far],
@@ -113,7 +113,7 @@
             pltpu.VMEM((ENC, ENC), bf16),
             pltpu.SemaphoreType.DMA((4,)),
         ],
-        compiler_params=params(58),
+        compiler_params=params(24),
         cost_estimate=cost(10**9, 8 * 10**6),
     )(x, gain, project, mix)
 
@@ -213,15 +213,14 @@
             jax.ShapeDtypeStruct((rows, 2 * inner), bf16),
             jax.ShapeDtypeStruct((ENC, 2 * inner), bf16),
         ),
-        compiler_params=params(44, 1),
+        compiler_params=params(58, 1),
         cost_estimate=cost(16 * 10**9, 16 * 10**6),
     )(slots, queries, upstream, weight, *sources)
 
 
 def place_kernel(sum_ref, out_ref):
     size, many = sum_ref.shape[0], sum_ref.shape[1] // HS
-    for j in range(many):
-        out_ref[pl.ds(j, size, stride=many), :] = sum_ref[:, j * HS : (j + 1) * HS].astype(f32)
+    out_ref[...] = sum_ref[...].astype(f32).reshape(size, many, HS).reshape(size * many, HS)
 
 
 def placed(summed):
@@ -233,9 +232,11 @@
         in_specs=[pl.BlockSpec((size, summed.shape[1]), lambda i: (i, 0))],
         out_specs=pl.BlockSpec((size * many, HS), lambda i: (i, 0)),
         out_shape=jax.ShapeDtypeStruct((ENC * many, HS), f32),
-        compiler_params=params(16, 1),
+        compiler_params=params(58, 1),
         cost_estimate=cost(10**6, 11 * 10**6),
     )(summed)
+
+
 def near_kernel(pairs_ref, weight_ref, brought_ref, own_ref, *outs):
     total = nt(pairs_ref[...], weight_ref[...]) + brought_ref[...].astype(f32)
     own_ref[...] = total[:TOK]
@@ -255,7 +256,7 @@
         out_specs=[whole(TOK, ENC)] * 4,
         out_shape=[jax.ShapeDtypeStruct((TOK, ENC), f32)] + [jax.ShapeDtypeStruct((TOK, ENC), bf16)] * 3,
         compiler_params=params(32, 1),
-        cost_estimate=cost(2 * 10**9, 8 * 10**6),
+        cost_estimate=cost(10**4, 10**4),
     )(pairs, weight, brought)
 
 
@@ -295,7 +296,7 @@
         backward_kernel,
         out_shape=jax.ShapeDtypeStruct((PARTS, TOK, LANES), bf16),
         compiler_params=params(24),
-        cost_estimate=cost(6 * 10**8, 4 * 10**6),
+        cost_estimate=cost(10**4, 10**4),
     )(grad, projected, mix)
 
 
@@ -318,7 +319,7 @@
         inputs_kernel,
         out_shape=jax.ShapeDtypeStruct((TOK, ENC), bf16),
         compiler_params=params(24),
-        cost_estimate=cost(6 * 10**8, 6 * 10**6),
+        cost_estimate=cost(10**4, 10**4),
     )(x, gain, project, parts, grad)
 
 
@@ -350,8 +351,7 @@
     result, grad_queries, grad_pairs, grad_weight = cross(
         slots.astype(jnp.int32), decoder_queries, grad_output, weight, sources, heads
     )
-    grad_cross = placed(lax.psum(grad_weight, PLANE))
-    grad_cross = grad_cross.reshape(ENC, heads, 2, HS).swapaxes(1, 2).reshape(cross_pairs.shape)
+    summed = lax.psum(grad_weight, PLANE)
 
     brought = across(nt(grad_pairs[4 * TOK :], weight).astype(bf16))
     total, *others = near_sums(grad_pairs, weight, brought)
@@ -366,15 +366,13 @@
     arrived = lax.all_to_all(encoder_grad, FINE, 0, 0, tiled=True).astype(f32)
     arrived = arrived.reshape(2, 8, 8, 8, LANES).sum(axis=(0, 2))
     rows = jnp.swapaxes(arrived, 0, 1).reshape(8, 8 * LANES)[:7]
-    grad_inputs = flipped(inputs_grad(x, gain, encoder_project, parts, grad_encoded))
-    return (
-        result,
-        grad_queries,
-        grad_cross,
-        rows[:, : 3 * ENC],
-        rows[:, 6 * LANES : 6 * LANES + ENC],
-        grad_inputs[None],
+    grad_project, grad_mix = rows[:, : 3 * ENC], rows[:, 6 * LANES : 6 * LANES + ENC]
+    grad_inputs = flipped(inputs_grad(x, gain, encoder_project, parts, grad_encoded))[None]
+    summed, grad_project, grad_mix, grad_inputs = lax.optimization_barrier(
+        (summed, grad_project, grad_mix, grad_inputs)
     )
+    grad_cross = placed(summed).reshape(ENC, heads, 2, HS).swapaxes(1, 2).reshape(cross_pairs.shape)
+    return result, grad_queries, grad_cross, grad_project, grad_mix, grad_inputs
 
 
 def solution(mesh):

time: 201 us -> 198 us (0.985)
  local copies, waits for them, and re-layouts: 24.2 us -> 18.5 us
  Pallas kernels: 35.9 us -> 39.3 us
    ppermute x2, waiting for transfers between devices: 12.5 us -> 0.01 us  [flipped(): return lax.ppermute(x, ('y', 'c', 'xl', 'z'), pairs)]
    all_to_all x1, waiting for transfers between devices: 0.01 us -> 11.8 us  [shards(): arrived = lax.all_to_all(encoder_grad, FINE, 0, 0, tiled=True).astype(f32)]
    pallas_call x1, Pallas kernels: 13.3 us -> 18.6 us  [cross(): pl.pallas_call(functools.partial(cross_kernel, per), grid_spec=pltpu.Pref...]
    unnamed x38 -> x24, local copies, waits for them, and re-layouts: 15.1 us -> 9.86 us
    pallas_call x1, Pallas kernels: 5.45 us -> 2.99 us  [encode(): pl.pallas_call(encode_kernel, in_specs=[vmem, vmem, far, far], out_specs=...]
where the time goes in v5:
time: 198 us; the launch traced here: 197 us
  waiting for transfers between devices  72 us (36%)
  starting transfers between devices  40.2 us (20%)
  Pallas kernels  39.3 us (20%)
  local copies, waits for them, and re-layouts  18.5 us (9%)
  between operations  15.6 us (8%)
  matrix products  8.45 us (4%)
  other arithmetic  3.34 us (2%)
    psum x1, waiting for transfers between devices, shards(): summed = lax.psum(grad_weight, PLANE)  26.4 us
    pallas_call x1, Pallas kernels, cross(): pl.pallas_call(functools.partial(cross_kernel, per), grid_spec=pltpu.Pref...  18.6 us
    ppermute x6, waiting for transfers between devices, turned(): return lambda x: lax.ppermute(x, axis, pairs)  18.5 us
    all_to_all x1, waiting for transfers between devices, shards(): lax.all_to_all(parts, TP, 0, 0, tiled=True).reshape(8 * TOK, LANES)  12.7 us
    all_to_all x1, waiting for transfers between devices, shards(): arrived = lax.all_to_all(encoder_grad, FINE, 0, 0, tiled=True).astype(f32)  11.8 us
    ppermute x6, starting transfers between devices, turned(): return lambda x: lax.ppermute(x, axis, pairs)  11.3 us
    unnamed x24, local copies, waits for them, and re-layouts  9.86 us
    ppermute x2, starting transfers between devices, flipped(): return lax.ppermute(x, ('y', 'c', 'xl', 'z'), pairs)  8.55 us
  transfers between devices with their start and end apart: 17, of which 9 were waited for; matrix products, arithmetic and copies ran while one was open for 10% of the time, Pallas kernels for 15%

profile of v5, /device:TPU:1, one launch (start us, length us, event | category | flops | bytes accessed | tf_op | source)
XLA Modules:
  0.0 197.3 jit_solution(3296269955175570520)
XLA Ops:
  8.0 4.9 %collective-permute-start = (bf16[128,896]{1,0:T(8,128)(2,1)}, bf16[128,896]{1,0:T(8,128)(2,1)S(1)}, u32[]{:S(2)}, u32[]{:S(2)}) collective-permute-start(bf16[128,896]{1,0:T(8,128)(2,1)} %bitcast.29), channel_id=1, source_target_pairs={{0,0},{1,8},{2,16},{3,24},{4,32},{5,40},{6,48},{7,56},{8,1},{9,9},... | collective-permute-start | bytes 688136 | tf_op jit(solution)/shard_map/ppermute | solution.py:37
  13.0 7.3 %reshape.46.weight_ref = bf16[896,2048]{1,0:T(8,128)(2,1)} reshape(bf16[896,8,2,128]{3,2,1,0:T(2,128)(2,1)} %bitcast.25) | data formatting | bytes 7340032 | tf_op jit(solution)/shard_map/reshape | solution.py:340
  20.3 2.4 %copy-done = bf16[896,2688]{1,0:T(8,128)(2,1)S(1)} copy-done((bf16[896,2688]{1,0:T(8,128)(2,1)S(1)}, bf16[896,2688]{1,0:T(8,128)(2,1)}, u32[]{:S(2)}) %copy-start) | copy-done | bytes 4816920
  22.7 3.0 %shard_map.127 = (bf16[128,896]{1,0:T(8,128)(2,1)S(1)}, bf16[128,896]{1,0:T(8,128)(2,1)S(1)}, bf16[128,2688]{1,0:T(8,128)(2,1)S(1)}, bf16[128,896]{1,0:T(8,128)(2,1)S(1)}) custom-call(bf16[128,896]{1,0:T(8,128)(2,1)S(1)} %collective-permute-done.x_ref, f32[1,896]{1,0:T(1,128)S(1)} %reshape.47.gain_ref, bf16[896,2688]{1,0:T(8,128)(2,1)S(1)} %copy-done, ...), custom_call_target="tpu_custom_call" | custom-call | flops 1000000000 | bytes 8000000 | tf_op jit(solution)/shard_map/pallas_call | solution.py:106
  25.7 8.5 %collective-permute-start.1 = (bf16[128,896]{1,0:T(8,128)(2,1)S(1)}, bf16[128,896]{1,0:T(8,128)(2,1)S(1)}, u32[]{:S(2)}, u32[]{:S(2)}) collective-permute-start(bf16[128,896]{1,0:T(8,128)(2,1)S(1)} %get-tuple-element.38.rest_0_), channel_id=1, source_target_pairs={{0,48},{16,0},{32,16},{48,32},{1,49},{17,1},{33,17},{49,33},{2,50}... | collective-permute-start | bytes 688136 | tf_op jit(solution)/shard_map/ppermute | solution.py:28
  34.2 0.1 collective-permute-start.2
  34.3 0.8 collective-permute-start.3
  35.1 3.1 %collective-permute-start.4 = (bf16[128,896]{1,0:T(8,128)(2,1)S(1)}, bf16[128,896]{1,0:T(8,128)(2,1)}, u32[]{:S(2)}, u32[]{:S(2)}) collective-permute-start(bf16[128,896]{1,0:T(8,128)(2,1)S(1)} %get-tuple-element.38.rest_0_), channel_id=1, source_target_pairs={{0,8},{8,0},{1,9},{9,1},{2,10},{10,2},{3,11},{11,3},{4,12},{12,4},... | collective-permute-start | bytes 688136 | tf_op jit(solution)/shard_map/ppermute | solution.py:32
  38.2 5.5 %collective-permute-done.1.rest_1_ = bf16[128,896]{1,0:T(8,128)(2,1)S(1)} collective-permute-done((bf16[128,896]{1,0:T(8,128)(2,1)S(1)}, bf16[128,896]{1,0:T(8,128)(2,1)S(1)}, u32[]{:S(2)}, u32[]{:S(2)}) %collective-permute-start.1) | collective-permute-done | bytes 229408 | tf_op jit(solution)/shard_map/ppermute | solution.py:28
  43.7 1.3 collective-permute-start.5
  44.9 1.3 collective-permute-start.6
  46.3 0.9 collective-permute-done.3.rest_3_
  47.1 1.4 collective-permute-start.7
  48.6 1.7 shard_map.128
  50.3 0.2 all-reduce.2.cloned.1.call-start
  50.6 0.1 copy.20
  50.7 0.1 reshape.44
  50.8 0.5 fusion.7.slots_ref
  51.3 18.6 %shard_map.129 = (bf16[4,64,1024]{2,1,0:T(8,128)(2,1)}, bf16[4,64,1024]{2,1,0:T(8,128)(2,1)}, bf16[1024,2048]{1,0:T(8,128)(2,1)}, bf16[896,2048]{1,0:T(8,128)(2,1)}) custom-call(s32[8]{0:T(128)} %fusion.7.slots_ref, bf16[4,64,1024]{2,1,0:T(8,128)(2,1)} %q_ref.1, bf16[4,64,1024]{2,1,0:T(8,128)(2,1)} %up_ref.1, bf16[896,2048]{1,0:T(8,128)(2,1)} %reshape.46.weight_ref, ...), custom_call_target="tpu_custom_call" | custom-call | flops 16000000000 | bytes 16000000 | tf_op jit(solution)/shard_map/pallas_call | solution.py:187
  69.9 5.0 %fusion.3 = bf16[512,896]{1,0:T(8,128)(2,1)} fusion(bf16[896,2048]{1,0:T(8,128)(2,1)S(1)} %copy-done.2, bf16[1024,2048]{1,0:T(8,128)(2,1)} %get-tuple-element.50.pairs_ref), kind=kOutput, calls=%fused_computation.6 | convolution fusion | flops 1879506944 | bytes 6684672 | tf_op jit(solution)/shard_map/dot_general | solution.py:41
  74.9 0.1 collective-permute-start.8
  75.0 2.6 %collective-permute-done.8.brought_ref = bf16[512,896]{1,0:T(8,128)(2,1)S(1)} collective-permute-done((bf16[512,896]{1,0:T(8,128)(2,1)}, bf16[512,896]{1,0:T(8,128)(2,1)S(1)}, u32[]{:S(2)}, u32[]{:S(2)}) %collective-permute-start.8) | collective-permute-done | bytes 917536 | tf_op jit(solution)/shard_map/ppermute | solution.py:32
  77.6 2.1 %copy-done.3 = bf16[896,2048]{1,0:T(8,128)(2,1)S(1)} copy-done((bf16[896,2048]{1,0:T(8,128)(2,1)S(1)}, bf16[896,2048]{1,0:T(8,128)(2,1)}, u32[]{:S(2)}) %copy-start.3) | copy-done | bytes 3670040
  79.6 2.2 %copy-done.5 = bf16[1024,2048]{1,0:T(8,128)(2,1)S(1)} copy-done((bf16[1024,2048]{1,0:T(8,128)(2,1)S(1)}, bf16[1024,2048]{1,0:T(8,128)(2,1)}, u32[]{:S(2)}) %copy-start.5) | copy-done | bytes 4194328
  81.8 2.4 %shard_map.130 = (f32[128,896]{1,0:T(8,128)S(1)}, bf16[128,896]{1,0:T(8,128)(2,1)S(1)}, bf16[128,896]{1,0:T(8,128)(2,1)S(1)}, bf16[128,896]{1,0:T(8,128)(2,1)S(1)}) custom-call(bf16[1024,2048]{1,0:T(8,128)(2,1)S(1)} %copy-done.5, bf16[896,2048]{1,0:T(8,128)(2,1)S(1)} %copy-done.3, bf16[512,896]{1,0:T(8,128)(2,1)S(1)} %collective-permute-done.8.brought_ref), custom_call_target="tpu_custom_call" | custom-call | flops 10000 | bytes 10000 | tf_op jit(solution)/shard_map/pallas_call | solution.py:252
  84.2 0.5 collective-permute-start.10
  84.7 0.8 collective-permute-start.11
  85.4 0.7 collective-permute-start.9
  86.1 6.7 %collective-permute-done.10 = bf16[128,896]{1,0:T(8,128)(2,1)S(1)} collective-permute-done((bf16[128,896]{1,0:T(8,128)(2,1)S(1)}, bf16[128,896]{1,0:T(8,128)(2,1)S(1)}, u32[]{:S(2)}, u32[]{:S(2)}) %collective-permute-start.10) | collective-permute-done | bytes 229408 | tf_op jit(solution)/shard_map/ppermute | solution.py:28
  92.8 3.2 %collective-permute-done.11 = bf16[128,896]{1,0:T(8,128)(2,1)S(1)} collective-permute-done((bf16[128,896]{1,0:T(8,128)(2,1)S(1)}, bf16[128,896]{1,0:T(8,128)(2,1)S(1)}, u32[]{:S(2)}, u32[]{:S(2)}) %collective-permute-start.11) | collective-permute-done | bytes 229408 | tf_op jit(solution)/shard_map/ppermute | solution.py:28
  96.0 2.3 %collective-permute-done.9 = bf16[128,896]{1,0:T(8,128)(2,1)S(1)} collective-permute-done((bf16[128,896]{1,0:T(8,128)(2,1)S(1)}, bf16[128,896]{1,0:T(8,128)(2,1)S(1)}, u32[]{:S(2)}, u32[]{:S(2)}) %collective-permute-start.9) | collective-permute-done | bytes 229408 | tf_op jit(solution)/shard_map/ppermute | solution.py:28
  98.3 0.1 add_convert_fusion.grad_ref
  98.4 4.6 %shard_map.131.parts_ref = bf16[8,128,512]{2,1,0:T(8,128)(2,1)} custom-call(bf16[128,896]{1,0:T(8,128)(2,1)S(1)} %add_convert_fusion.grad_ref, bf16[128,2688]{1,0:T(8,128)(2,1)S(1)} %get-tuple-element.55.projected_ref, bf16[896,896]{1,0:T(8,128)(2,1)S(1)} %copy-done.4), custom_call_target="tpu_custom_call" | custom-call | flops 10000 | bytes 10000 | tf_op jit(solution)/shard_map/pallas_call | solution.py:295
  103.1 4.5 %all-to-all-start = ((bf16[8,128,512]{2,1,0:T(8,128)(2,1)}), bf16[8,128,512]{2,1,0:T(8,128)(2,1)}, u32[]{:S(2)}, u32[]{:S(2)}) async-start(bf16[8,128,512]{2,1,0:T(8,128)(2,1)} %shard_map.131.parts_ref), calls=%async_computation | async-start | bytes 2097152 | tf_op jit(solution)/shard_map/all_to_all | solution.py:363
  107.6 2.6 %fusion = bf16[1024,1024]{0,1:T(8,128)(2,1)S(1)} fusion(bf16[1024,2048]{1,0:T(8,128)(2,1)} %all-gather.2.cloned.1.call-done, pred[]{:T(512)S(6)} %lt.20), kind=kLoop, calls=%fused_computation.1 | loop fusion | flops 1048576 | bytes 6291457 | tf_op jit(solution)/shard_map/transpose | solution.py:365
  110.2 12.7 %all-to-all-done = bf16[8,128,512]{2,1,0:T(8,128)(2,1)} async-done(((bf16[8,128,512]{2,1,0:T(8,128)(2,1)}), bf16[8,128,512]{2,1,0:T(8,128)(2,1)}, u32[]{:S(2)}, u32[]{:S(2)}) %all-to-all-start) | async-done | bytes 1048608 | tf_op jit(solution)/shard_map/all_to_all | solution.py:363
  122.8 3.5 %fusion.6 = bf16[128,8,512]{2,1,0:T(8,128)(2,1)} fusion(bf16[1024,1024]{0,1:T(8,128)(2,1)S(1)} %fusion, bf16[1024,512]{1,0:T(8,128)(2,1)} %bitcast.4), kind=kOutput, calls=%fused_computation.7 | convolution fusion | flops 1074266112 | bytes 4194304 | tf_op jit(solution)/shard_map/dot_general | solution.py:41
  126.3 8.3 %all-to-all-start.1 = ((bf16[128,8,512]{2,1,0:T(8,128)(2,1)}), bf16[128,8,512]{2,1,0:T(8,128)(2,1)S(1)}, u32[]{:S(2)}, u32[]{:S(2)}) async-start(bf16[128,8,512]{2,1,0:T(8,128)(2,1)} %fusion.6), calls=%async_computation.1 | async-start | bytes 2097152 | tf_op jit(solution)/shard_map/all_to_all | solution.py:366
  134.6 2.4 %copy-done.1 = bf16[896,2688]{1,0:T(8,128)(2,1)S(1)} copy-done((bf16[896,2688]{1,0:T(8,128)(2,1)S(1)}, bf16[896,2688]{1,0:T(8,128)(2,1)}, u32[]{:S(2)}) %copy-start.1) | copy-done | bytes 4816920
  137.0 3.0 %shard_map.132 = bf16[128,896]{1,0:T(8,128)(2,1)S(1)} custom-call(bf16[128,896]{1,0:T(8,128)(2,1)S(1)} %collective-permute-done.x_ref, f32[1,896]{1,0:T(1,128)S(1)} %reshape.47.gain_ref, bf16[896,2688]{1,0:T(8,128)(2,1)S(1)} %copy-done.1, bf16[8,128,512]{2,1,0:T(8,128)(2,1)} %shard_map.131.parts_ref, bf16[128,896]{1,0:T(8,128)(2,1)S(1)} %add_convert_fusion.grad_ref), custom_call_target="tpu_custom_call" | custom-call | flops 10000 | bytes 10000 | tf_op jit(solution)/shard_map/pallas_call | solution.py:318
  140.0 3.6 %collective-permute-start.12 = (bf16[128,896]{1,0:T(8,128)(2,1)S(1)}, bf16[128,896]{1,0:T(8,128)(2,1)S(1)}, u32[]{:S(2)}, u32[]{:S(2)}) collective-permute-start(bf16[128,896]{1,0:T(8,128)(2,1)S(1)} %shard_map.132), channel_id=1, source_target_pairs={{0,0},{1,8},{2,16},{3,24},{4,32},{5,40},{6,48},{7,56},{8,1},{9,9},... | collective-permute-start | bytes 688136 | tf_op jit(solution)/shard_map/ppermute | solution.py:37
  143.6 11.8 %all-to-all-done.1 = bf16[128,8,512]{2,1,0:T(8,128)(2,1)S(1)} async-done(((bf16[128,8,512]{2,1,0:T(8,128)(2,1)}), bf16[128,8,512]{2,1,0:T(8,128)(2,1)S(1)}, u32[]{:S(2)}, u32[]{:S(2)}) %all-to-all-start.1) | async-done | bytes 1048608 | tf_op jit(solution)/shard_map/all_to_all | solution.py:366
  155.5 0.1 convert_reduce_fusion
  155.6 0.6 slice.31
  156.3 0.6 slice.32
  156.9 26.4 %all-reduce.2.cloned.1.call-done.sum_ref = bf16[896,2048]{1,0:T(8,128)(2,1)} async-done(((bf16[896,2048]{1,0:T(8,128)(2,1)}), bf16[896,2048]{1,0:T(8,128)(2,1)}) %all-reduce.2.cloned.1.call-update) | async-done | bytes 3670032 | tf_op jit(solution)/shard_map/psum | solution.py:354
  183.2 6.0 %shard_map.133 = f32[14336,128]{1,0:T(8,128)} custom-call(bf16[896,2048]{1,0:T(8,128)(2,1)} %all-reduce.2.cloned.1.call-done.sum_ref), custom_call_target="tpu_custom_call" | custom-call | flops 1000000 | bytes 11000000 | tf_op jit(solution)/shard_map/pallas_call | solution.py:229
  189.2 0.7 copy.25
  (30 shorter events, 0.1 us)
Async XLA Ops:
  8.0 99.6 %all-gather.2.cloned.1.call-start = ((), (), s32[]{:S(2)}) async-start(), calls=%async_computation.3 | async-start | bytes 4718592 | tf_op jit(solution)/shard_map/all_gather | solution.py:347
  8.0 12.3 %collective-permute-start = (bf16[128,896]{1,0:T(8,128)(2,1)}, bf16[128,896]{1,0:T(8,128)(2,1)S(1)}, u32[]{:S(2)}, u32[]{:S(2)}) collective-permute-start(bf16[128,896]{1,0:T(8,128)(2,1)} %bitcast.29), channel_id=1, source_target_pairs={{0,0},{1,8},{2,16},{3,24},{4,32},{5,40},{6,48},{7,56},{8,1},{9,9},... | collective-permute-start | bytes 688136 | tf_op jit(solution)/shard_map/ppermute | solution.py:37
  13.0 7.3 %copy-start.7 = (f32[896]{0:T(1024)S(1)}, f32[896]{0:T(1024)}, u32[]{:S(2)}) copy-start(f32[896]{0:T(1024)} %param.9) | copy-start | bytes 10756
  13.0 7.3 %copy-start.4 = (bf16[896,896]{1,0:T(8,128)(2,1)S(1)}, bf16[896,896]{1,0:T(8,128)(2,1)}, u32[]{:S(2)}) copy-start(bf16[896,896]{1,0:T(8,128)(2,1)} %mix_ref.3) | copy-start | bytes 4816900
  20.3 2.4 %copy-start = (bf16[896,2688]{1,0:T(8,128)(2,1)S(1)}, bf16[896,2688]{1,0:T(8,128)(2,1)}, u32[]{:S(2)}) copy-start(bf16[896,2688]{1,0:T(8,128)(2,1)} %project_ref.3) | copy-start | bytes 14450692
  22.7 27.9 %copy-start.8 = (s32[4,2]{0,1:T(2,128)S(1)}, s32[4,2]{0,1:T(2,128)}, u32[]{:S(2)}) copy-start(s32[4,2]{0,1:T(2,128)} %param.14) | copy-start | bytes 100
  25.7 25.1 %copy-start.6 = (bf16[128,896]{1,0:T(8,128)(2,1)}, bf16[128,896]{1,0:T(8,128)(2,1)S(1)}, u32[]{:S(2)}) copy-start(bf16[128,896]{1,0:T(8,128)(2,1)S(1)} %get-tuple-element.38.rest_0_) | copy-start | bytes 688132
  25.7 18.0 %collective-permute-start.1 = (bf16[128,896]{1,0:T(8,128)(2,1)S(1)}, bf16[128,896]{1,0:T(8,128)(2,1)S(1)}, u32[]{:S(2)}, u32[]{:S(2)}) collective-permute-start(bf16[128,896]{1,0:T(8,128)(2,1)S(1)} %get-tuple-element.38.rest_0_), channel_id=1, source_target_pairs={{0,48},{16,0},{32,16},{48,32},{1,49},{17,1},{33,17},{49,33},{2,50}... | collective-permute-start | bytes 688136 | tf_op jit(solution)/shard_map/ppermute | solution.py:28
  34.2 10.7 %collective-permute-start.2 = (bf16[128,896]{1,0:T(8,128)(2,1)S(1)}, bf16[128,896]{1,0:T(8,128)(2,1)S(1)}, u32[]{:S(2)}, u32[]{:S(2)}) collective-permute-start(bf16[128,896]{1,0:T(8,128)(2,1)S(1)} %get-tuple-element.38.rest_0_), channel_id=1, source_target_pairs={{0,32},{16,48},{32,0},{48,16},{1,33},{17,49},{33,1},{49,17},{2,34}... | collective-permute-start | bytes 688136 | tf_op jit(solution)/shard_map/ppermute | solution.py:28
  34.3 12.8 %collective-permute-start.3 = (bf16[128,896]{1,0:T(8,128)(2,1)S(1)}, bf16[128,896]{1,0:T(8,128)(2,1)}, u32[]{:S(2)}, u32[]{:S(2)}) collective-permute-start(bf16[128,896]{1,0:T(8,128)(2,1)S(1)} %get-tuple-element.38.rest_0_), channel_id=1, source_target_pairs={{0,16},{16,32},{32,48},{48,0},{1,17},{17,33},{33,49},{49,1},{2,18}... | collective-permute-start | bytes 688136 | tf_op jit(solution)/shard_map/ppermute | solution.py:28
  35.1 15.2 %collective-permute-start.4 = (bf16[128,896]{1,0:T(8,128)(2,1)S(1)}, bf16[128,896]{1,0:T(8,128)(2,1)}, u32[]{:S(2)}, u32[]{:S(2)}) collective-permute-start(bf16[128,896]{1,0:T(8,128)(2,1)S(1)} %get-tuple-element.38.rest_0_), channel_id=1, source_target_pairs={{0,8},{8,0},{1,9},{9,1},{2,10},{10,2},{3,11},{11,3},{4,12},{12,4},... | collective-permute-start | bytes 688136 | tf_op jit(solution)/shard_map/ppermute | solution.py:32
  43.7 7.1 %copy-start.9 = (bf16[128,896]{1,0:T(8,128)(2,1)}, bf16[128,896]{1,0:T(8,128)(2,1)S(1)}, u32[]{:S(2)}) copy-start(bf16[128,896]{1,0:T(8,128)(2,1)S(1)} %collective-permute-done.1.rest_1_) | copy-start | bytes 688132
  43.7 6.6 %collective-permute-start.5 = (bf16[128,896]{1,0:T(8,128)(2,1)S(1)}, bf16[128,896]{1,0:T(8,128)(2,1)}, u32[]{:S(2)}, u32[]{:S(2)}) collective-permute-start(bf16[128,896]{1,0:T(8,128)(2,1)S(1)} %collective-permute-done.1.rest_1_), channel_id=1, source_target_pairs={{0,8},{8,0},{1,9},{9,1},{2,10},{10,2},{3,11},{11,3},{4,12},{12,4},... | collective-permute-start | bytes 688136 | tf_op jit(solution)/shard_map/ppermute | solution.py:32
  44.9 5.9 %copy-start.10 = (bf16[128,896]{1,0:T(8,128)(2,1)}, bf16[128,896]{1,0:T(8,128)(2,1)S(1)}, u32[]{:S(2)}) copy-start(bf16[128,896]{1,0:T(8,128)(2,1)S(1)} %collective-permute-done.2.rest_2_) | copy-start | bytes 688132
  44.9 5.4 %collective-permute-start.6 = (bf16[128,896]{1,0:T(8,128)(2,1)S(1)}, bf16[128,896]{1,0:T(8,128)(2,1)}, u32[]{:S(2)}, u32[]{:S(2)}) collective-permute-start(bf16[128,896]{1,0:T(8,128)(2,1)S(1)} %collective-permute-done.2.rest_2_), channel_id=1, source_target_pairs={{0,8},{8,0},{1,9},{9,1},{2,10},{10,2},{3,11},{11,3},{4,12},{12,4},... | collective-permute-start | bytes 688136 | tf_op jit(solution)/shard_map/ppermute | solution.py:32
  47.1 3.2 %collective-permute-start.7 = (bf16[128,896]{1,0:T(8,128)(2,1)}, bf16[128,896]{1,0:T(8,128)(2,1)}, u32[]{:S(2)}, u32[]{:S(2)}) collective-permute-start(bf16[128,896]{1,0:T(8,128)(2,1)} %collective-permute-done.3.rest_3_), channel_id=1, source_target_pairs={{0,8},{8,0},{1,9},{9,1},{2,10},{10,2},{3,11},{11,3},{4,12},{12,4},... | collective-permute-start | bytes 688136 | tf_op jit(solution)/shard_map/ppermute | solution.py:32
  50.3 132.9 %all-reduce.2.cloned.1.call-start = ((), (), s32[]{:S(2)}) async-start(), calls=%async_computation.2 | async-start | bytes 7340032 | tf_op jit(solution)/shard_map/psum | solution.py:354
  51.3 18.6 %copy-start.2 = (bf16[896,2048]{1,0:T(8,128)(2,1)S(1)}, bf16[896,2048]{1,0:T(8,128)(2,1)}, u32[]{:S(2)}) copy-start(bf16[896,2048]{1,0:T(8,128)(2,1)} %reshape.46.weight_ref) | copy-start | bytes 11010052
  74.9 2.7 %collective-permute-start.8 = (bf16[512,896]{1,0:T(8,128)(2,1)}, bf16[512,896]{1,0:T(8,128)(2,1)S(1)}, u32[]{:S(2)}, u32[]{:S(2)}) collective-permute-start(bf16[512,896]{1,0:T(8,128)(2,1)} %fusion.3), channel_id=1, source_target_pairs={{0,8},{8,0},{1,9},{9,1},{2,10},{10,2},{3,11},{11,3},{4,12},{12,4},... | collective-permute-start | bytes 2752520 | tf_op jit(solution)/shard_map/ppermute | solution.py:32
  77.6 2.1 %copy-start.3 = (bf16[896,2048]{1,0:T(8,128)(2,1)S(1)}, bf16[896,2048]{1,0:T(8,128)(2,1)}, u32[]{:S(2)}) copy-start(bf16[896,2048]{1,0:T(8,128)(2,1)} %reshape.46.weight_ref) | copy-start | bytes 11010052
  79.6 2.2 %copy-start.5 = (bf16[1024,2048]{1,0:T(8,128)(2,1)S(1)}, bf16[1024,2048]{1,0:T(8,128)(2,1)}, u32[]{:S(2)}) copy-start(bf16[1024,2048]{1,0:T(8,128)(2,1)} %get-tuple-element.50.pairs_ref) | copy-start | bytes 12582916
  84.2 8.6 %collective-permute-start.10 = (bf16[128,896]{1,0:T(8,128)(2,1)S(1)}, bf16[128,896]{1,0:T(8,128)(2,1)S(1)}, u32[]{:S(2)}, u32[]{:S(2)}) collective-permute-start(bf16[128,896]{1,0:T(8,128)(2,1)S(1)} %get-tuple-element.53), channel_id=1, source_target_pairs={{0,32},{16,48},{32,0},{48,16},{1,33},{17,49},{33,1},{49,17},{2,34}... | collective-permute-start | bytes 688136 | tf_op jit(solution)/shard_map/ppermute | solution.py:28
  84.7 11.3 %collective-permute-start.11 = (bf16[128,896]{1,0:T(8,128)(2,1)S(1)}, bf16[128,896]{1,0:T(8,128)(2,1)S(1)}, u32[]{:S(2)}, u32[]{:S(2)}) collective-permute-start(bf16[128,896]{1,0:T(8,128)(2,1)S(1)} %get-tuple-element.54), channel_id=1, source_target_pairs={{0,48},{16,0},{32,16},{48,32},{1,49},{17,1},{33,17},{49,33},{2,50}... | collective-permute-start | bytes 688136 | tf_op jit(solution)/shard_map/ppermute | solution.py:28
  85.4 12.9 %collective-permute-start.9 = (bf16[128,896]{1,0:T(8,128)(2,1)S(1)}, bf16[128,896]{1,0:T(8,128)(2,1)S(1)}, u32[]{:S(2)}, u32[]{:S(2)}) collective-permute-start(bf16[128,896]{1,0:T(8,128)(2,1)S(1)} %get-tuple-element.52), channel_id=1, source_target_pairs={{0,16},{16,32},{32,48},{48,0},{1,17},{17,33},{33,49},{49,1},{2,18}... | collective-permute-start | bytes 688136 | tf_op jit(solution)/shard_map/ppermute | solution.py:28
  103.1 19.7 %all-to-all-start = ((bf16[8,128,512]{2,1,0:T(8,128)(2,1)}), bf16[8,128,512]{2,1,0:T(8,128)(2,1)}, u32[]{:S(2)}, u32[]{:S(2)}) async-start(bf16[8,128,512]{2,1,0:T(8,128)(2,1)} %shard_map.131.parts_ref), calls=%async_computation | async-start | bytes 2097152 | tf_op jit(solution)/shard_map/all_to_all | solution.py:363
  126.3 29.2 %all-to-all-start.1 = ((bf16[128,8,512]{2,1,0:T(8,128)(2,1)}), bf16[128,8,512]{2,1,0:T(8,128)(2,1)S(1)}, u32[]{:S(2)}, u32[]{:S(2)}) async-start(bf16[128,8,512]{2,1,0:T(8,128)(2,1)} %fusion.6), calls=%async_computation.1 | async-start | bytes 2097152 | tf_op jit(solution)/shard_map/all_to_all | solution.py:366
  134.6 2.4 %copy-start.1 = (bf16[896,2688]{1,0:T(8,128)(2,1)S(1)}, bf16[896,2688]{1,0:T(8,128)(2,1)}, u32[]{:S(2)}) copy-start(bf16[896,2688]{1,0:T(8,128)(2,1)} %project_ref.3) | copy-start | bytes 14450692
  140.0 16.9 %collective-permute-start.12 = (bf16[128,896]{1,0:T(8,128)(2,1)S(1)}, bf16[128,896]{1,0:T(8,128)(2,1)S(1)}, u32[]{:S(2)}, u32[]{:S(2)}) collective-permute-start(bf16[128,896]{1,0:T(8,128)(2,1)S(1)} %shard_map.132), channel_id=1, source_target_pairs={{0,0},{1,8},{2,16},{3,24},{4,32},{5,40},{6,48},{7,56},{8,1},{9,9},... | collective-permute-start | bytes 688136 | tf_op jit(solution)/shard_map/ppermute | solution.py:37
Sparse Core Ops, SparseCore 0:
  50.5 31.4 all-gather.1
Sparse Core Ops, SparseCore 1:
  75.1 108.1 all-reduce.1

commit v6 on v5

--- a/solution.py
+++ b/solution.py
@@ -136,7 +136,8 @@
 
 
 def cross_kernel(per, slots_ref, q_ref, up_ref, weight_ref, *rest):
-    sources, (out_ref, grad_ref, pairs_ref, sum_ref, rows_ref, turned_ref, held_ref) = rest[:8], rest[8:]
+    sources, rest = rest[:8], rest[8:]
+    (out_ref, grad_ref, pairs_ref), halves, (rows_ref, turned_ref, held_ref) = rest[:3], rest[3:5], rest[5:]
 
     @pl.when(pl.program_id(0) == 0)
     def _():
@@ -177,10 +178,15 @@
             g = jnp.concatenate([g[:, :HS] * scale, g[:, HS:]], axis=1).astype(bf16)
             for n in range(2):
                 pairs_ref[rows[c][n], pair] = g[n * TOK : (n + 1) * TOK]
-    sum_ref[...] = nn(turned_ref[...], pairs_ref[...]).astype(bf16)
-
-
-def cross(slots, queries, upstream, weight, sources, per):
+    for i, half in enumerate(halves):
+
+        @pl.when(pl.program_id(0) == i)
+        def _():
+            half[...] = nn(turned_ref[...], pairs_ref[...]).astype(bf16)
+
+
+def cross(slots, queries, upstream, weight, sources):
+    per = queries.shape[2] // HS // 2
     spans, length, inner = queries.shape
     rows = len(sources) * TOK
     column = pl.BlockSpec((spans, length, per * HS), lambda i, s: (0, 0, i))
@@ -199,7 +205,7 @@
                 column,
                 column,
                 pl.BlockSpec((rows, 2 * HS * per), lambda i, s: (0, i)),
-                pl.BlockSpec((ENC, 2 * HS * per), lambda i, s: (0, i)),
+                *[pl.BlockSpec((ENC, inner), lambda i, s: (0, 0))] * 2,
             ),
             scratch_shapes=[
                 pltpu.VMEM((rows, ENC), bf16),
@@ -211,30 +217,34 @@
             jax.ShapeDtypeStruct(queries.shape, bf16),
             jax.ShapeDtypeStruct(queries.shape, bf16),
             jax.ShapeDtypeStruct((rows, 2 * inner), bf16),
-            jax.ShapeDtypeStruct((ENC, 2 * inner), bf16),
+            *[jax.ShapeDtypeStruct((ENC, inner), bf16)] * 2,
         ),
         compiler_params=params(58, 1),
         cost_estimate=cost(16 * 10**9, 16 * 10**6),
     )(slots, queries, upstream, weight, *sources)
 
 
-def place_kernel(sum_ref, out_ref):
-    size, many = sum_ref.shape[0], sum_ref.shape[1] // HS
-    out_ref[...] = sum_ref[...].astype(f32).reshape(size, many, HS).reshape(size * many, HS)
-
-
-def placed(summed):
+def place_kernel(one_ref, other_ref, out_ref):
+    both = jnp.concatenate([one_ref[...], other_ref[...]], axis=1).astype(f32)
+    size, many = both.shape[0], both.shape[1] // HS
+    out_ref[...] = both.reshape(size, many, HS).reshape(size * many, HS)
+
+
+def placed(one, other):
     size = ENC // 4
-    many = summed.shape[1] // HS
+    many = (one.shape[1] + other.shape[1]) // HS
     return pl.pallas_call(
         place_kernel,
         grid=(4,),
-        in_specs=[pl.BlockSpec((size, summed.shape[1]), lambda i: (i, 0))],
+        in_specs=[
+            pl.BlockSpec((size, one.shape[1]), lambda i: (i, 0)),
+            pl.BlockSpec((size, other.shape[1]), lambda i: (i, 0)),
+        ],
         out_specs=pl.BlockSpec((size * many, HS), lambda i: (i, 0)),
         out_shape=jax.ShapeDtypeStruct((ENC * many, HS), f32),
         compiler_params=params(58, 1),
         cost_estimate=cost(10**6, 11 * 10**6),
-    )(summed)
+    )(one, other)
 
 
 def near_kernel(pairs_ref, weight_ref, brought_ref, own_ref, *outs):
@@ -348,16 +358,23 @@
 
     named = span_neighbours.reshape(-1) % 8
     slots = (named % 2 != core) * 4 + (named // 2 - y) % 4
-    result, grad_queries, grad_pairs, grad_weight = cross(
-        slots.astype(jnp.int32), decoder_queries, grad_output, weight, sources, heads
+    result, grad_queries, grad_pairs, one_half, other_half = cross(
+        slots.astype(jnp.int32), decoder_queries, grad_output, weight, sources
     )
-    summed = lax.psum(grad_weight, PLANE)
-
-    brought = across(nt(grad_pairs[4 * TOK :], weight).astype(bf16))
+    one_half = lax.psum(one_half, PLANE)
+    far = nt(grad_pairs[4 * TOK :], weight).astype(bf16)
+    far, other_half = lax.optimization_barrier((far, other_half))
+    brought = across(far)
+    shares = lax.all_to_all(other_half.reshape(16, -1, inner), PLANE, 0, 0, tiled=True)
+
     total, *others = near_sums(grad_pairs, weight, brought)
     for step, other in enumerate(others):
         total += turned("y", 4, step + 1)(other).astype(f32)
     grad_encoded = total.astype(bf16)
+
+    shares, _ = lax.optimization_barrier((shares, grad_encoded))
+    share = jnp.sum(shares.astype(f32), axis=0).astype(bf16)
+    other_half = lax.all_gather(share, PLANE, tiled=True)
 
     parts = backward(grad_encoded, projected, encoder_mix)
     all_parts = lax.all_to_all(parts, TP, 0, 0, tiled=True).reshape(8 * TOK, LANES)
@@ -368,10 +385,10 @@
     rows = jnp.swapaxes(arrived, 0, 1).reshape(8, 8 * LANES)[:7]
     grad_project, grad_mix = rows[:, : 3 * ENC], rows[:, 6 * LANES : 6 * LANES + ENC]
     grad_inputs = flipped(inputs_grad(x, gain, encoder_project, parts, grad_encoded))[None]
-    summed, grad_project, grad_mix, grad_inputs = lax.optimization_barrier(
-        (summed, grad_project, grad_mix, grad_inputs)
+    one_half, other_half, grad_project, grad_mix, grad_inputs = lax.optimization_barrier(
+        (one_half, other_half, grad_project, grad_mix, grad_inputs)
     )
-    grad_cross = placed(summed).reshape(ENC, heads, 2, HS).swapaxes(1, 2).reshape(cross_pairs.shape)
+    grad_cross = placed(one_half, other_half).reshape(ENC, heads, 2, HS).swapaxes(1, 2).reshape(cross_pairs.shape)
     return result, grad_queries, grad_cross, grad_project, grad_mix, grad_inputs
 
 

time: 198 us -> 200 us (1.010)
  waiting for transfers between devices: 72 us -> 59.1 us
  starting transfers between devices: 40.2 us -> 49.5 us
  other arithmetic: 3.34 us -> 7.1 us
    psum x1, waiting for transfers between devices: 26.4 us -> 8.02 us  [shards(): one_half = lax.psum(one_half, PLANE)]
    all_to_all x0 -> x1, starting transfers between devices: none -> 6.98 us  [shards(): lax.all_to_all(other_half.reshape(16, -1, inner), PLANE, 0, 0, tiled=True)]
    all_to_all x0 -> x1, waiting for transfers between devices: none -> 6.11 us  [shards(): lax.all_to_all(other_half.reshape(16, -1, inner), PLANE, 0, 0, tiled=True)]
    reduce_sum x0 -> x1, other arithmetic: none -> 2.51 us  [shards(): share = jnp.sum(shares.astype(f32), axis=0).astype(bf16)]
  transfers between devices with their start and end apart: 17 -> 19, of which waited for: 9 -> 10; matrix products, arithmetic and copies ran while one was open for 10% -> 12% of each run, Pallas kernels for 15% -> 16%
where the time goes in v6:
time: 200 us; the launch traced here: 199 us
  waiting for transfers between devices  59.1 us (30%)
  starting transfers between devices  49.5 us (25%)
  Pallas kernels  40.6 us (20%)
  local copies, waits for them, and re-layouts  18.5 us (9%)
  between operations  15.7 us (8%)
  matrix products  8.65 us (4%)
  other arithmetic  7.1 us (4%)
    pallas_call x1, Pallas kernels, cross(): pl.pallas_call(functools.partial(cross_kernel, per), grid_spec=pltpu.Pref...  19.9 us
    ppermute x6, waiting for transfers between devices, turned(): return lambda x: lax.ppermute(x, axis, pairs)  18.3 us
    all_to_all x1, waiting for transfers between devices, shards(): lax.all_to_all(parts, TP, 0, 0, tiled=True).reshape(8 * TOK, LANES)  12.7 us
    all_to_all x1, waiting for transfers between devices, shards(): arrived = lax.all_to_all(encoder_grad, FINE, 0, 0, tiled=True).astype(f32)  11.8 us
    ppermute x6, starting transfers between devices, turned(): return lambda x: lax.ppermute(x, axis, pairs)  11.5 us
    unnamed x24, local copies, waits for them, and re-layouts  9.87 us
    all_to_all x1, starting transfers between devices, shards(): arrived = lax.all_to_all(encoder_grad, FINE, 0, 0, tiled=True).astype(f32)  9.47 us
    dot_general x2, matrix products, dot(): lax.dot_general(a, b, ((contract[:1], contract[1:]), ((), ())), preferred...  8.65 us
  transfers between devices with their start and end apart: 19, of which 10 were waited for; matrix products, arithmetic and copies ran while one was open for 12% of the time, Pallas kernels for 16%

profile of v6, /device:TPU:1, one launch (start us, length us, event | category | flops | bytes accessed | tf_op | source)
XLA Modules:
  0.0 199.1 jit_solution(15712473850653325623)
XLA Ops:
  8.0 4.9 %collective-permute-start = (bf16[128,896]{1,0:T(8,128)(2,1)}, bf16[128,896]{1,0:T(8,128)(2,1)S(1)}, u32[]{:S(2)}, u32[]{:S(2)}) collective-permute-start(bf16[128,896]{1,0:T(8,128)(2,1)} %bitcast.30), channel_id=1, source_target_pairs={{0,0},{1,8},{2,16},{3,24},{4,32},{5,40},{6,48},{7,56},{8,1},{9,9},... | collective-permute-start | bytes 688136 | tf_op jit(solution)/shard_map/ppermute | solution.py:37
  13.0 7.3 %reshape.49.weight_ref = bf16[896,2048]{1,0:T(8,128)(2,1)} reshape(bf16[896,8,2,128]{3,2,1,0:T(2,128)(2,1)} %bitcast.25) | data formatting | bytes 7340032 | tf_op jit(solution)/shard_map/reshape | solution.py:350
  20.3 2.4 %copy-done = bf16[896,2688]{1,0:T(8,128)(2,1)S(1)} copy-done((bf16[896,2688]{1,0:T(8,128)(2,1)S(1)}, bf16[896,2688]{1,0:T(8,128)(2,1)}, u32[]{:S(2)}) %copy-start) | copy-done | bytes 4816920
  22.7 3.0 %shard_map.127 = (bf16[128,896]{1,0:T(8,128)(2,1)S(1)}, bf16[128,896]{1,0:T(8,128)(2,1)S(1)}, bf16[128,2688]{1,0:T(8,128)(2,1)S(1)}, bf16[128,896]{1,0:T(8,128)(2,1)S(1)}) custom-call(bf16[128,896]{1,0:T(8,128)(2,1)S(1)} %collective-permute-done.x_ref, f32[1,896]{1,0:T(1,128)S(1)} %reshape.50.gain_ref, bf16[896,2688]{1,0:T(8,128)(2,1)S(1)} %copy-done, ...), custom_call_target="tpu_custom_call" | custom-call | flops 1000000000 | bytes 8000000 | tf_op jit(solution)/shard_map/pallas_call | solution.py:106
  25.7 8.5 %collective-permute-start.1 = (bf16[128,896]{1,0:T(8,128)(2,1)S(1)}, bf16[128,896]{1,0:T(8,128)(2,1)S(1)}, u32[]{:S(2)}, u32[]{:S(2)}) collective-permute-start(bf16[128,896]{1,0:T(8,128)(2,1)S(1)} %get-tuple-element.43.rest_0_), channel_id=1, source_target_pairs={{0,48},{16,0},{32,16},{48,32},{1,49},{17,1},{33,17},{49,33},{2,50}... | collective-permute-start | bytes 688136 | tf_op jit(solution)/shard_map/ppermute | solution.py:28
  34.2 0.1 collective-permute-start.2
  34.4 0.8 collective-permute-start.3
  35.1 3.1 %collective-permute-start.4 = (bf16[128,896]{1,0:T(8,128)(2,1)S(1)}, bf16[128,896]{1,0:T(8,128)(2,1)}, u32[]{:S(2)}, u32[]{:S(2)}) collective-permute-start(bf16[128,896]{1,0:T(8,128)(2,1)S(1)} %get-tuple-element.43.rest_0_), channel_id=1, source_target_pairs={{0,8},{8,0},{1,9},{9,1},{2,10},{10,2},{3,11},{11,3},{4,12},{12,4},... | collective-permute-start | bytes 688136 | tf_op jit(solution)/shard_map/ppermute | solution.py:32
  38.2 5.5 %collective-permute-done.1.rest_1_ = bf16[128,896]{1,0:T(8,128)(2,1)S(1)} collective-permute-done((bf16[128,896]{1,0:T(8,128)(2,1)S(1)}, bf16[128,896]{1,0:T(8,128)(2,1)S(1)}, u32[]{:S(2)}, u32[]{:S(2)}) %collective-permute-start.1) | collective-permute-done | bytes 229408 | tf_op jit(solution)/shard_map/ppermute | solution.py:28
  43.7 1.3 collective-permute-start.5
  45.0 1.3 collective-permute-start.6
  46.3 0.8 collective-permute-done.3.rest_3_
  47.1 1.4 collective-permute-start.7
  48.5 1.7 shard_map.128
  50.3 0.2 all-reduce.2.cloned.1.call-start
  50.7 0.5 fusion.7.slots_ref
  51.3 19.9 %shard_map.129 = (bf16[4,64,1024]{2,1,0:T(8,128)(2,1)}, bf16[4,64,1024]{2,1,0:T(8,128)(2,1)}, bf16[1024,2048]{1,0:T(8,128)(2,1)}, bf16[896,1024]{1,0:T(8,128)(2,1)}, bf16[896,1024]{1,0:T(8,128)(2,1)}) custom-call(s32[8]{0:T(128)} %fusion.7.slots_ref, bf16[4,64,1024]{2,1,0:T(8,128)(2,1)} %q_ref.1, bf16[4,64,1024]{2,1,0:T(8,128)(2,1)} %up_ref.1, ...), custom_call_target="tpu_custom_call" | custom-call | flops 16000000000 | bytes 16000000 | tf_op jit(solution)/shard_map/pallas_call | solution.py:193
  71.2 5.1 %fusion.3 = bf16[512,896]{1,0:T(8,128)(2,1)S(1)} fusion(bf16[896,2048]{1,0:T(8,128)(2,1)} %reshape.49.weight_ref, bf16[1024,2048]{1,0:T(8,128)(2,1)} %get-tuple-element.54.pairs_ref), kind=kOutput, calls=%fused_computation.6 | convolution fusion | flops 1879506944 | bytes 6684672 | tf_op jit(solution)/shard_map/dot_general | solution.py:41
  76.3 7.0 %all-to-all-start = ((bf16[16,56,1024]{2,1,0:T(8,128)(2,1)}), bf16[16,56,1024]{2,1,0:T(8,128)(2,1)}, u32[]{:S(2)}, u32[]{:S(2)}) async-start(bf16[16,56,1024]{2,1,0:T(8,128)(2,1)} %bitcast.26), calls=%async_computation | async-start | bytes 3670016 | tf_op jit(solution)/shard_map/all_to_all | solution.py:368
  83.4 0.4 collective-permute-start.8
  83.7 2.2 %collective-permute-done.8.brought_ref = bf16[512,896]{1,0:T(8,128)(2,1)S(1)} collective-permute-done((bf16[512,896]{1,0:T(8,128)(2,1)S(1)}, bf16[512,896]{1,0:T(8,128)(2,1)S(1)}, u32[]{:S(2)}, u32[]{:S(2)}) %collective-permute-start.8) | collective-permute-done | bytes 917536 | tf_op jit(solution)/shard_map/ppermute | solution.py:32
  85.9 2.1 %copy-done.2 = bf16[896,2048]{1,0:T(8,128)(2,1)S(1)} copy-done((bf16[896,2048]{1,0:T(8,128)(2,1)S(1)}, bf16[896,2048]{1,0:T(8,128)(2,1)}, u32[]{:S(2)}) %copy-start.2) | copy-done | bytes 3670040
  88.0 2.2 %copy-done.4 = bf16[1024,2048]{1,0:T(8,128)(2,1)S(1)} copy-done((bf16[1024,2048]{1,0:T(8,128)(2,1)S(1)}, bf16[1024,2048]{1,0:T(8,128)(2,1)}, u32[]{:S(2)}) %copy-start.4) | copy-done | bytes 4194328
  90.2 2.4 %shard_map.130 = (f32[128,896]{1,0:T(8,128)S(1)}, bf16[128,896]{1,0:T(8,128)(2,1)S(1)}, bf16[128,896]{1,0:T(8,128)(2,1)S(1)}, bf16[128,896]{1,0:T(8,128)(2,1)S(1)}) custom-call(bf16[1024,2048]{1,0:T(8,128)(2,1)S(1)} %copy-done.4, bf16[896,2048]{1,0:T(8,128)(2,1)S(1)} %copy-done.2, bf16[512,896]{1,0:T(8,128)(2,1)S(1)} %collective-permute-done.8.brought_ref), custom_call_target="tpu_custom_call" | custom-call | flops 10000 | bytes 10000 | tf_op jit(solution)/shard_map/pallas_call | solution.py:262
  92.6 0.7 collective-permute-start.10
  93.2 1.1 collective-permute-start.11
  94.3 0.4 collective-permute-start.9
  94.7 6.5 %collective-permute-done.10 = bf16[128,896]{1,0:T(8,128)(2,1)S(1)} collective-permute-done((bf16[128,896]{1,0:T(8,128)(2,1)S(1)}, bf16[128,896]{1,0:T(8,128)(2,1)S(1)}, u32[]{:S(2)}, u32[]{:S(2)}) %collective-permute-start.10) | collective-permute-done | bytes 229408 | tf_op jit(solution)/shard_map/ppermute | solution.py:28
  101.2 3.1 %collective-permute-done.11 = bf16[128,896]{1,0:T(8,128)(2,1)S(1)} collective-permute-done((bf16[128,896]{1,0:T(8,128)(2,1)S(1)}, bf16[128,896]{1,0:T(8,128)(2,1)S(1)}, u32[]{:S(2)}, u32[]{:S(2)}) %collective-permute-start.11) | collective-permute-done | bytes 229408 | tf_op jit(solution)/shard_map/ppermute | solution.py:28
  104.4 2.3 %collective-permute-done.9 = bf16[128,896]{1,0:T(8,128)(2,1)S(1)} collective-permute-done((bf16[128,896]{1,0:T(8,128)(2,1)S(1)}, bf16[128,896]{1,0:T(8,128)(2,1)S(1)}, u32[]{:S(2)}, u32[]{:S(2)}) %collective-permute-start.9) | collective-permute-done | bytes 229408 | tf_op jit(solution)/shard_map/ppermute | solution.py:28
  106.8 6.1 %all-to-all-done = bf16[16,56,1024]{2,1,0:T(8,128)(2,1)} async-done(((bf16[16,56,1024]{2,1,0:T(8,128)(2,1)}), bf16[16,56,1024]{2,1,0:T(8,128)(2,1)}, u32[]{:S(2)}, u32[]{:S(2)}) %all-to-all-start) | async-done | bytes 1835040 | tf_op jit(solution)/shard_map/all_to_all | solution.py:368
  112.9 2.5 %reduce_sum.21 = bf16[56,1024]{1,0:T(8,128)(2,1)} reduce(bf16[16,56,1024]{2,1,0:T(8,128)(2,1)} %all-to-all-done, bf16[]{:T(256)} %constant.64.clone.1), dimensions={0}, to_apply=%region_1.2 | reduce | flops 860160 | bytes 1949698 | tf_op jit(solution)/shard_map/reduce_sum | solution.py:376
  115.4 4.6 %shard_map.131.parts_ref = bf16[8,128,512]{2,1,0:T(8,128)(2,1)} custom-call(bf16[128,896]{1,0:T(8,128)(2,1)S(1)} %add_convert_fusion.grad_ref, bf16[128,2688]{1,0:T(8,128)(2,1)S(1)} %get-tuple-element.64.projected_ref, bf16[896,896]{1,0:T(8,128)(2,1)S(1)} %copy-done.3), custom_call_target="tpu_custom_call" | custom-call | flops 10000 | bytes 10000 | tf_op jit(solution)/shard_map/pallas_call | solution.py:305
  120.1 5.2 %all-to-all-start.1 = ((bf16[8,128,512]{2,1,0:T(8,128)(2,1)}), bf16[8,128,512]{2,1,0:T(8,128)(2,1)}, u32[]{:S(2)}, u32[]{:S(2)}) async-start(bf16[8,128,512]{2,1,0:T(8,128)(2,1)} %shard_map.131.parts_ref), calls=%async_computation.1 | async-start | bytes 2097152 | tf_op jit(solution)/shard_map/all_to_all | solution.py:380
  125.3 2.5 %fusion = bf16[1024,1024]{0,1:T(8,128)(2,1)S(1)} fusion(bf16[1024,2048]{1,0:T(8,128)(2,1)} %all-gather.5.cloned.1.call-done, pred[]{:T(512)S(6)} %lt.20), kind=kLoop, calls=%fused_computation.1 | loop fusion | flops 1048576 | bytes 6291457 | tf_op jit(solution)/shard_map/transpose | solution.py:382
  127.8 12.7 %all-to-all-done.1 = bf16[8,128,512]{2,1,0:T(8,128)(2,1)} async-done(((bf16[8,128,512]{2,1,0:T(8,128)(2,1)}), bf16[8,128,512]{2,1,0:T(8,128)(2,1)}, u32[]{:S(2)}, u32[]{:S(2)}) %all-to-all-start.1) | async-done | bytes 1048608 | tf_op jit(solution)/shard_map/all_to_all | solution.py:380
  140.5 3.5 %fusion.6 = bf16[128,8,512]{2,1,0:T(8,128)(2,1)} fusion(bf16[1024,1024]{0,1:T(8,128)(2,1)S(1)} %fusion, bf16[1024,512]{1,0:T(8,128)(2,1)} %bitcast.5), kind=kOutput, calls=%fused_computation.7 | convolution fusion | flops 1074266112 | bytes 4194304 | tf_op jit(solution)/shard_map/dot_general | solution.py:41
  144.0 9.5 %all-to-all-start.2 = ((bf16[128,8,512]{2,1,0:T(8,128)(2,1)}), bf16[128,8,512]{2,1,0:T(8,128)(2,1)}, u32[]{:S(2)}, u32[]{:S(2)}) async-start(bf16[128,8,512]{2,1,0:T(8,128)(2,1)} %fusion.6), calls=%async_computation.2 | async-start | bytes 2097152 | tf_op jit(solution)/shard_map/all_to_all | solution.py:383
  153.5 2.4 %copy-done.1 = bf16[896,2688]{1,0:T(8,128)(2,1)S(1)} copy-done((bf16[896,2688]{1,0:T(8,128)(2,1)S(1)}, bf16[896,2688]{1,0:T(8,128)(2,1)}, u32[]{:S(2)}) %copy-start.1) | copy-done | bytes 4816920
  155.9 3.0 %shard_map.132 = bf16[128,896]{1,0:T(8,128)(2,1)S(1)} custom-call(bf16[128,896]{1,0:T(8,128)(2,1)S(1)} %collective-permute-done.x_ref, f32[1,896]{1,0:T(1,128)S(1)} %reshape.50.gain_ref, bf16[896,2688]{1,0:T(8,128)(2,1)S(1)} %copy-done.1, bf16[8,128,512]{2,1,0:T(8,128)(2,1)} %shard_map.131.parts_ref, bf16[128,896]{1,0:T(8,128)(2,1)S(1)} %add_convert_fusion.grad_ref), custom_call_target="tpu_custom_call" | custom-call | flops 10000 | bytes 10000 | tf_op jit(solution)/shard_map/pallas_call | solution.py:328
  158.9 3.6 %collective-permute-start.12 = (bf16[128,896]{1,0:T(8,128)(2,1)S(1)}, bf16[128,896]{1,0:T(8,128)(2,1)S(1)}, u32[]{:S(2)}, u32[]{:S(2)}) collective-permute-start(bf16[128,896]{1,0:T(8,128)(2,1)S(1)} %shard_map.132), channel_id=1, source_target_pairs={{0,0},{1,8},{2,16},{3,24},{4,32},{5,40},{6,48},{7,56},{8,1},{9,9},... | collective-permute-start | bytes 688136 | tf_op jit(solution)/shard_map/ppermute | solution.py:37
  162.6 11.8 %all-to-all-done.2 = bf16[128,8,512]{2,1,0:T(8,128)(2,1)} async-done(((bf16[128,8,512]{2,1,0:T(8,128)(2,1)}), bf16[128,8,512]{2,1,0:T(8,128)(2,1)}, u32[]{:S(2)}, u32[]{:S(2)}) %all-to-all-start.2) | async-done | bytes 1048608 | tf_op jit(solution)/shard_map/all_to_all | solution.py:383
  174.3 1.4 convert_reduce_fusion
  175.7 0.6 slice.31
  176.4 0.6 slice.32
  177.0 8.0 %all-reduce.2.cloned.1.call-done.one_ref = bf16[896,1024]{1,0:T(8,128)(2,1)} async-done(((bf16[896,1024]{1,0:T(8,128)(2,1)}), bf16[896,1024]{1,0:T(8,128)(2,1)}) %all-reduce.2.cloned.1.call-update) | async-done | bytes 1835024 | tf_op jit(solution)/shard_map/psum | solution.py:364
  185.0 6.0 %shard_map.133 = f32[14336,128]{1,0:T(8,128)} custom-call(bf16[896,1024]{1,0:T(8,128)(2,1)} %all-reduce.2.cloned.1.call-done.one_ref, bf16[896,1024]{1,0:T(8,128)(2,1)} %all-gather.3.cloned.1.call-done.other_ref), custom_call_target="tpu_custom_call" | custom-call | flops 1000000 | bytes 11000000 | tf_op jit(solution)/shard_map/pallas_call | solution.py:236
  191.0 0.7 copy.25
  (36 shorter events, 0.5 us)
Async XLA Ops:
  8.0 117.3 %all-gather.5.cloned.1.call-start = ((), (), s32[]{:S(2)}) async-start(), calls=%async_computation.5 | async-start | bytes 4718592 | tf_op jit(solution)/shard_map/all_gather | solution.py:357
  8.0 12.3 %collective-permute-start = (bf16[128,896]{1,0:T(8,128)(2,1)}, bf16[128,896]{1,0:T(8,128)(2,1)S(1)}, u32[]{:S(2)}, u32[]{:S(2)}) collective-permute-start(bf16[128,896]{1,0:T(8,128)(2,1)} %bitcast.30), channel_id=1, source_target_pairs={{0,0},{1,8},{2,16},{3,24},{4,32},{5,40},{6,48},{7,56},{8,1},{9,9},... | collective-permute-start | bytes 688136 | tf_op jit(solution)/shard_map/ppermute | solution.py:37
  13.0 7.3 %copy-start.6 = (f32[896]{0:T(1024)S(1)}, f32[896]{0:T(1024)}, u32[]{:S(2)}) copy-start(f32[896]{0:T(1024)} %param.9) | copy-start | bytes 10756
  13.0 7.3 %copy-start.3 = (bf16[896,896]{1,0:T(8,128)(2,1)S(1)}, bf16[896,896]{1,0:T(8,128)(2,1)}, u32[]{:S(2)}) copy-start(bf16[896,896]{1,0:T(8,128)(2,1)} %mix_ref.3) | copy-start | bytes 4816900
  20.3 2.4 %copy-start = (bf16[896,2688]{1,0:T(8,128)(2,1)S(1)}, bf16[896,2688]{1,0:T(8,128)(2,1)}, u32[]{:S(2)}) copy-start(bf16[896,2688]{1,0:T(8,128)(2,1)} %project_ref.3) | copy-start | bytes 14450692
  25.7 25.5 %copy-start.5 = (bf16[128,896]{1,0:T(8,128)(2,1)}, bf16[128,896]{1,0:T(8,128)(2,1)S(1)}, u32[]{:S(2)}) copy-start(bf16[128,896]{1,0:T(8,128)(2,1)S(1)} %get-tuple-element.43.rest_0_) | copy-start | bytes 688132
  25.7 24.8 %copy-start.7 = (s32[4,2]{0,1:T(2,128)S(1)}, s32[4,2]{0,1:T(2,128)}, u32[]{:S(2)}) copy-start(s32[4,2]{0,1:T(2,128)} %param.14) | copy-start | bytes 100
  25.7 17.9 %collective-permute-start.1 = (bf16[128,896]{1,0:T(8,128)(2,1)S(1)}, bf16[128,896]{1,0:T(8,128)(2,1)S(1)}, u32[]{:S(2)}, u32[]{:S(2)}) collective-permute-start(bf16[128,896]{1,0:T(8,128)(2,1)S(1)} %get-tuple-element.43.rest_0_), channel_id=1, source_target_pairs={{0,48},{16,0},{32,16},{48,32},{1,49},{17,1},{33,17},{49,33},{2,50}... | collective-permute-start | bytes 688136 | tf_op jit(solution)/shard_map/ppermute | solution.py:28
  34.2 10.7 %collective-permute-start.2 = (bf16[128,896]{1,0:T(8,128)(2,1)S(1)}, bf16[128,896]{1,0:T(8,128)(2,1)S(1)}, u32[]{:S(2)}, u32[]{:S(2)}) collective-permute-start(bf16[128,896]{1,0:T(8,128)(2,1)S(1)} %get-tuple-element.43.rest_0_), channel_id=1, source_target_pairs={{0,32},{16,48},{32,0},{48,16},{1,33},{17,49},{33,1},{49,17},{2,34}... | collective-permute-start | bytes 688136 | tf_op jit(solution)/shard_map/ppermute | solution.py:28
  34.4 12.7 %collective-permute-start.3 = (bf16[128,896]{1,0:T(8,128)(2,1)S(1)}, bf16[128,896]{1,0:T(8,128)(2,1)S(1)}, u32[]{:S(2)}, u32[]{:S(2)}) collective-permute-start(bf16[128,896]{1,0:T(8,128)(2,1)S(1)} %get-tuple-element.43.rest_0_), channel_id=1, source_target_pairs={{0,16},{16,32},{32,48},{48,0},{1,17},{17,33},{33,49},{49,1},{2,18}... | collective-permute-start | bytes 688136 | tf_op jit(solution)/shard_map/ppermute | solution.py:28
  35.1 15.1 %collective-permute-start.4 = (bf16[128,896]{1,0:T(8,128)(2,1)S(1)}, bf16[128,896]{1,0:T(8,128)(2,1)}, u32[]{:S(2)}, u32[]{:S(2)}) collective-permute-start(bf16[128,896]{1,0:T(8,128)(2,1)S(1)} %get-tuple-element.43.rest_0_), channel_id=1, source_target_pairs={{0,8},{8,0},{1,9},{9,1},{2,10},{10,2},{3,11},{11,3},{4,12},{12,4},... | collective-permute-start | bytes 688136 | tf_op jit(solution)/shard_map/ppermute | solution.py:32
  43.7 7.6 %copy-start.8 = (bf16[128,896]{1,0:T(8,128)(2,1)}, bf16[128,896]{1,0:T(8,128)(2,1)S(1)}, u32[]{:S(2)}) copy-start(bf16[128,896]{1,0:T(8,128)(2,1)S(1)} %collective-permute-done.1.rest_1_) | copy-start | bytes 688132
  43.7 6.5 %collective-permute-start.5 = (bf16[128,896]{1,0:T(8,128)(2,1)S(1)}, bf16[128,896]{1,0:T(8,128)(2,1)}, u32[]{:S(2)}, u32[]{:S(2)}) collective-permute-start(bf16[128,896]{1,0:T(8,128)(2,1)S(1)} %collective-permute-done.1.rest_1_), channel_id=1, source_target_pairs={{0,8},{8,0},{1,9},{9,1},{2,10},{10,2},{3,11},{11,3},{4,12},{12,4},... | collective-permute-start | bytes 688136 | tf_op jit(solution)/shard_map/ppermute | solution.py:32
  44.9 6.3 %copy-start.9 = (bf16[128,896]{1,0:T(8,128)(2,1)}, bf16[128,896]{1,0:T(8,128)(2,1)S(1)}, u32[]{:S(2)}) copy-start(bf16[128,896]{1,0:T(8,128)(2,1)S(1)} %collective-permute-done.2.rest_2_) | copy-start | bytes 688132
  45.0 5.3 %collective-permute-start.6 = (bf16[128,896]{1,0:T(8,128)(2,1)S(1)}, bf16[128,896]{1,0:T(8,128)(2,1)}, u32[]{:S(2)}, u32[]{:S(2)}) collective-permute-start(bf16[128,896]{1,0:T(8,128)(2,1)S(1)} %collective-permute-done.2.rest_2_), channel_id=1, source_target_pairs={{0,8},{8,0},{1,9},{9,1},{2,10},{10,2},{3,11},{11,3},{4,12},{12,4},... | collective-permute-start | bytes 688136 | tf_op jit(solution)/shard_map/ppermute | solution.py:32
  47.1 4.1 %copy-start.10 = (bf16[128,896]{1,0:T(8,128)(2,1)}, bf16[128,896]{1,0:T(8,128)(2,1)S(1)}, u32[]{:S(2)}) copy-start(bf16[128,896]{1,0:T(8,128)(2,1)S(1)} %collective-permute-done.3.rest_3_) | copy-start | bytes 688132
  47.1 3.1 %collective-permute-start.7 = (bf16[128,896]{1,0:T(8,128)(2,1)S(1)}, bf16[128,896]{1,0:T(8,128)(2,1)}, u32[]{:S(2)}, u32[]{:S(2)}) collective-permute-start(bf16[128,896]{1,0:T(8,128)(2,1)S(1)} %collective-permute-done.3.rest_3_), channel_id=1, source_target_pairs={{0,8},{8,0},{1,9},{9,1},{2,10},{10,2},{3,11},{11,3},{4,12},{12,4},... | collective-permute-start | bytes 688136 | tf_op jit(solution)/shard_map/ppermute | solution.py:32
  50.3 134.8 %all-reduce.2.cloned.1.call-start = ((), (), s32[]{:S(2)}) async-start(), calls=%async_computation.3 | async-start | bytes 3670016 | tf_op jit(solution)/shard_map/psum | solution.py:364
  76.3 36.6 %all-to-all-start = ((bf16[16,56,1024]{2,1,0:T(8,128)(2,1)}), bf16[16,56,1024]{2,1,0:T(8,128)(2,1)}, u32[]{:S(2)}, u32[]{:S(2)}) async-start(bf16[16,56,1024]{2,1,0:T(8,128)(2,1)} %bitcast.26), calls=%async_computation | async-start | bytes 3670016 | tf_op jit(solution)/shard_map/all_to_all | solution.py:368
  83.3 101.7 %all-gather.3.cloned.1.call-start = ((), (), s32[]{:S(2)}) async-start(), calls=%async_computation.4 | async-start | bytes 1949696 | tf_op jit(solution)/shard_map/all_gather | solution.py:377
  83.4 2.6 %collective-permute-start.8 = (bf16[512,896]{1,0:T(8,128)(2,1)S(1)}, bf16[512,896]{1,0:T(8,128)(2,1)S(1)}, u32[]{:S(2)}, u32[]{:S(2)}) collective-permute-start(bf16[512,896]{1,0:T(8,128)(2,1)S(1)} %fusion.3), channel_id=1, source_target_pairs={{0,8},{8,0},{1,9},{9,1},{2,10},{10,2},{3,11},{11,3},{4,12},{12,4},... | collective-permute-start | bytes 2752520 | tf_op jit(solution)/shard_map/ppermute | solution.py:32
  85.9 2.1 %copy-start.2 = (bf16[896,2048]{1,0:T(8,128)(2,1)S(1)}, bf16[896,2048]{1,0:T(8,128)(2,1)}, u32[]{:S(2)}) copy-start(bf16[896,2048]{1,0:T(8,128)(2,1)} %reshape.49.weight_ref) | copy-start | bytes 11010052
  88.0 2.2 %copy-start.4 = (bf16[1024,2048]{1,0:T(8,128)(2,1)S(1)}, bf16[1024,2048]{1,0:T(8,128)(2,1)}, u32[]{:S(2)}) copy-start(bf16[1024,2048]{1,0:T(8,128)(2,1)} %get-tuple-element.54.pairs_ref) | copy-start | bytes 12582916
  92.6 8.7 %collective-permute-start.10 = (bf16[128,896]{1,0:T(8,128)(2,1)S(1)}, bf16[128,896]{1,0:T(8,128)(2,1)S(1)}, u32[]{:S(2)}, u32[]{:S(2)}) collective-permute-start(bf16[128,896]{1,0:T(8,128)(2,1)S(1)} %get-tuple-element.60), channel_id=1, source_target_pairs={{0,32},{16,48},{32,0},{48,16},{1,33},{17,49},{33,1},{49,17},{2,34}... | collective-permute-start | bytes 688136 | tf_op jit(solution)/shard_map/ppermute | solution.py:28
  93.2 11.2 %collective-permute-start.11 = (bf16[128,896]{1,0:T(8,128)(2,1)S(1)}, bf16[128,896]{1,0:T(8,128)(2,1)S(1)}, u32[]{:S(2)}, u32[]{:S(2)}) collective-permute-start(bf16[128,896]{1,0:T(8,128)(2,1)S(1)} %get-tuple-element.61), channel_id=1, source_target_pairs={{0,48},{16,0},{32,16},{48,32},{1,49},{17,1},{33,17},{49,33},{2,50}... | collective-permute-start | bytes 688136 | tf_op jit(solution)/shard_map/ppermute | solution.py:28
  94.3 12.4 %collective-permute-start.9 = (bf16[128,896]{1,0:T(8,128)(2,1)S(1)}, bf16[128,896]{1,0:T(8,128)(2,1)S(1)}, u32[]{:S(2)}, u32[]{:S(2)}) collective-permute-start(bf16[128,896]{1,0:T(8,128)(2,1)S(1)} %get-tuple-element.59), channel_id=1, source_target_pairs={{0,16},{16,32},{32,48},{48,0},{1,17},{17,33},{33,49},{49,1},{2,18}... | collective-permute-start | bytes 688136 | tf_op jit(solution)/shard_map/ppermute | solution.py:28
  120.1 20.4 %all-to-all-start.1 = ((bf16[8,128,512]{2,1,0:T(8,128)(2,1)}), bf16[8,128,512]{2,1,0:T(8,128)(2,1)}, u32[]{:S(2)}, u32[]{:S(2)}) async-start(bf16[8,128,512]{2,1,0:T(8,128)(2,1)} %shard_map.131.parts_ref), calls=%async_computation.1 | async-start | bytes 2097152 | tf_op jit(solution)/shard_map/all_to_all | solution.py:380
  144.0 30.3 %all-to-all-start.2 = ((bf16[128,8,512]{2,1,0:T(8,128)(2,1)}), bf16[128,8,512]{2,1,0:T(8,128)(2,1)}, u32[]{:S(2)}, u32[]{:S(2)}) async-start(bf16[128,8,512]{2,1,0:T(8,128)(2,1)} %fusion.6), calls=%async_computation.2 | async-start | bytes 2097152 | tf_op jit(solution)/shard_map/all_to_all | solution.py:383
  153.5 2.4 %copy-start.1 = (bf16[896,2688]{1,0:T(8,128)(2,1)S(1)}, bf16[896,2688]{1,0:T(8,128)(2,1)}, u32[]{:S(2)}) copy-start(bf16[896,2688]{1,0:T(8,128)(2,1)} %project_ref.3) | copy-start | bytes 14450692
  158.9 18.1 %collective-permute-start.12 = (bf16[128,896]{1,0:T(8,128)(2,1)S(1)}, bf16[128,896]{1,0:T(8,128)(2,1)S(1)}, u32[]{:S(2)}, u32[]{:S(2)}) collective-permute-start(bf16[128,896]{1,0:T(8,128)(2,1)S(1)} %shard_map.132), channel_id=1, source_target_pairs={{0,0},{1,8},{2,16},{3,24},{4,32},{5,40},{6,48},{7,56},{8,1},{9,9},... | collective-permute-start | bytes 688136 | tf_op jit(solution)/shard_map/ppermute | solution.py:37
Sparse Core Ops, SparseCore 0:
  50.4 31.4 all-gather.4
  115.6 49.0 all-gather.2
Sparse Core Ops, SparseCore 1:
  71.3 113.7 all-reduce.1

commit v7 on v5

--- a/solution.py
+++ b/solution.py
@@ -136,7 +136,8 @@
 
 
 def cross_kernel(per, slots_ref, q_ref, up_ref, weight_ref, *rest):
-    sources, (out_ref, grad_ref, pairs_ref, sum_ref, rows_ref, turned_ref, held_ref) = rest[:8], rest[8:]
+    sources, rest = rest[:8], rest[8:]
+    out_ref, grad_ref, pairs_ref, sum_ref, far_ref, rows_ref, turned_ref, held_ref = rest
 
     @pl.when(pl.program_id(0) == 0)
     def _():
@@ -178,33 +179,35 @@
             for n in range(2):
                 pairs_ref[rows[c][n], pair] = g[n * TOK : (n + 1) * TOK]
     sum_ref[...] = nn(turned_ref[...], pairs_ref[...]).astype(bf16)
-
-
-def cross(slots, queries, upstream, weight, sources, per):
+    far_ref[...] = nt(pairs_ref[4 * TOK :], weight_ref[...]).astype(bf16)
+
+
+def cross(slots, queries, upstream, weight, sources):
     spans, length, inner = queries.shape
     rows = len(sources) * TOK
-    column = pl.BlockSpec((spans, length, per * HS), lambda i, s: (0, 0, i))
-    return pl.pallas_call(
-        functools.partial(cross_kernel, per),
+    column = pl.BlockSpec((spans, length, inner), lambda i, s: (0, 0, i))
+    return pl.pallas_call(
+        functools.partial(cross_kernel, inner // HS),
         grid_spec=pltpu.PrefetchScalarGridSpec(
             num_scalar_prefetch=1,
-            grid=(inner // HS // per,),
+            grid=(1,),
             in_specs=[
                 column,
                 column,
-                pl.BlockSpec((ENC, 2 * HS * per), lambda i, s: (0, i)),
+                pl.BlockSpec((ENC, 2 * inner), lambda i, s: (0, i)),
                 *[pl.BlockSpec((TOK, ENC), lambda i, s: (0, 0))] * len(sources),
             ],
             out_specs=(
                 column,
                 column,
-                pl.BlockSpec((rows, 2 * HS * per), lambda i, s: (0, i)),
-                pl.BlockSpec((ENC, 2 * HS * per), lambda i, s: (0, i)),
+                pl.BlockSpec((rows, 2 * inner), lambda i, s: (0, i)),
+                pl.BlockSpec((ENC, 2 * inner), lambda i, s: (0, i)),
+                pl.BlockSpec((4 * TOK, ENC), lambda i, s: (0, 0)),
             ),
             scratch_shapes=[
                 pltpu.VMEM((rows, ENC), bf16),
                 pltpu.VMEM((ENC, rows), bf16),
-                pltpu.VMEM((rows, 2 * HS * per), bf16),
+                pltpu.VMEM((rows, 2 * inner), bf16),
             ],
         ),
         out_shape=(
@@ -212,27 +215,45 @@
             jax.ShapeDtypeStruct(queries.shape, bf16),
             jax.ShapeDtypeStruct((rows, 2 * inner), bf16),
             jax.ShapeDtypeStruct((ENC, 2 * inner), bf16),
+            jax.ShapeDtypeStruct((4 * TOK, ENC), bf16),
         ),
         compiler_params=params(58, 1),
         cost_estimate=cost(16 * 10**9, 16 * 10**6),
     )(slots, queries, upstream, weight, *sources)
 
 
-def place_kernel(sum_ref, out_ref):
-    size, many = sum_ref.shape[0], sum_ref.shape[1] // HS
-    out_ref[...] = sum_ref[...].astype(f32).reshape(size, many, HS).reshape(size * many, HS)
+def place_kernel(sum_ref, out_ref, held_ref, made_ref, sems):
+    steps = 8
+    size, many = sum_ref.shape[0] // steps, sum_ref.shape[1] // HS
+    ins, outs = [], []
+    for i in range(steps):
+        at = slice(i * size, (i + 1) * size)
+        ins.append(pltpu.make_async_copy(sum_ref.at[at], held_ref.at[at], sems.at[i]))
+        ins[i].start()
+    for i in range(steps):
+        at, to = slice(i * size, (i + 1) * size), slice(i * size * many, (i + 1) * size * many)
+        ins[i].wait()
+        made_ref[to] = held_ref[at].astype(f32).reshape(size, many, HS).reshape(size * many, HS)
+        outs.append(pltpu.make_async_copy(made_ref.at[to], out_ref.at[to], sems.at[steps + i]))
+        outs[i].start()
+    for copy in outs:
+        copy.wait()
 
 
 def placed(summed):
-    size = ENC // 4
     many = summed.shape[1] // HS
+    hbm = pl.BlockSpec(memory_space=pltpu.HBM)
     return pl.pallas_call(
         place_kernel,
-        grid=(4,),
-        in_specs=[pl.BlockSpec((size, summed.shape[1]), lambda i: (i, 0))],
-        out_specs=pl.BlockSpec((size * many, HS), lambda i: (i, 0)),
+        in_specs=[hbm],
+        out_specs=hbm,
         out_shape=jax.ShapeDtypeStruct((ENC * many, HS), f32),
-        compiler_params=params(58, 1),
+        scratch_shapes=[
+            pltpu.VMEM(summed.shape, bf16),
+            pltpu.VMEM((ENC * many, HS), f32),
+            pltpu.SemaphoreType.DMA((16,)),
+        ],
+        compiler_params=params(58),
         cost_estimate=cost(10**6, 11 * 10**6),
     )(summed)
 
@@ -348,12 +369,12 @@
 
     named = span_neighbours.reshape(-1) % 8
     slots = (named % 2 != core) * 4 + (named // 2 - y) % 4
-    result, grad_queries, grad_pairs, grad_weight = cross(
-        slots.astype(jnp.int32), decoder_queries, grad_output, weight, sources, heads
+    result, grad_queries, grad_pairs, grad_weight, far = cross(
+        slots.astype(jnp.int32), decoder_queries, grad_output, weight, sources
     )
     summed = lax.psum(grad_weight, PLANE)
 
-    brought = across(nt(grad_pairs[4 * TOK :], weight).astype(bf16))
+    brought = across(far)
     total, *others = near_sums(grad_pairs, weight, brought)
     for step, other in enumerate(others):
         total += turned("y", 4, step + 1)(other).astype(f32)

time: 198 us -> 192 us (0.970)
  matrix products: 8.45 us -> 3.52 us
    dot_general x2 -> x1, matrix products: 8.45 us -> 3.52 us  [dot(): lax.dot_general(a, b, ((contract[:1], contract[1:]), ((), ())), preferred...]
  transfers between devices with their start and end apart: 17 -> 17, of which waited for: 9 -> 9; matrix products, arithmetic and copies ran while one was open for 10% -> 9% of each run, Pallas kernels for 15% -> 16%
where the time goes in v7:
time: 192 us; the launch traced here: 191 us
  waiting for transfers between devices  70.5 us (37%)
  starting transfers between devices  40 us (21%)
  Pallas kernels  38.4 us (20%)
  local copies, waits for them, and re-layouts  18.5 us (10%)
  between operations  15.7 us (8%)
  other arithmetic  4.61 us (2%)
  matrix products  3.52 us (2%)
    psum x1, waiting for transfers between devices, shards(): summed = lax.psum(grad_weight, PLANE)  25.1 us
    pallas_call x1, Pallas kernels, cross(): pl.pallas_call(functools.partial(cross_kernel, inner // HS), grid_spec=pl...  19.4 us
    ppermute x6, waiting for transfers between devices, turned(): return lambda x: lax.ppermute(x, axis, pairs)  18.7 us
    all_to_all x1, waiting for transfers between devices, shards(): lax.all_to_all(parts, TP, 0, 0, tiled=True).reshape(8 * TOK, LANES)  12.6 us
    all_to_all x1, waiting for transfers between devices, shards(): arrived = lax.all_to_all(encoder_grad, FINE, 0, 0, tiled=True).astype(f32)  11.3 us
    ppermute x6, starting transfers between devices, turned(): return lambda x: lax.ppermute(x, axis, pairs)  11 us
    unnamed x24, local copies, waits for them, and re-layouts  9.91 us
    ppermute x2, starting transfers between devices, flipped(): return lax.ppermute(x, ('y', 'c', 'xl', 'z'), pairs)  8.62 us
  transfers between devices with their start and end apart: 17, of which 9 were waited for; matrix products, arithmetic and copies ran while one was open for 9% of the time, Pallas kernels for 16%

profile of v7, /device:TPU:1, one launch (start us, length us, event | category | flops | bytes accessed | tf_op | source)
XLA Modules:
  0.0 191.2 jit_solution(17229653242794929203)
XLA Ops:
  8.0 0.0 all-gather.2.cloned.1.call-start
  8.0 4.9 %collective-permute-start = (bf16[128,896]{1,0:T(8,128)(2,1)}, bf16[128,896]{1,0:T(8,128)(2,1)S(1)}, u32[]{:S(2)}, u32[]{:S(2)}) collective-permute-start(bf16[128,896]{1,0:T(8,128)(2,1)} %bitcast.27), channel_id=1, source_target_pairs={{0,0},{1,8},{2,16},{3,24},{4,32},{5,40},{6,48},{7,56},{8,1},{9,9},... | collective-permute-start | bytes 688136 | tf_op jit(solution)/shard_map/ppermute | solution.py:37
  13.0 7.3 %reshape.46.weight_ref = bf16[896,2048]{1,0:T(8,128)(2,1)} reshape(bf16[896,8,2,128]{3,2,1,0:T(2,128)(2,1)} %bitcast.23) | data formatting | bytes 7340032 | tf_op jit(solution)/shard_map/reshape | solution.py:361
  20.3 2.4 %copy-done = bf16[896,2688]{1,0:T(8,128)(2,1)S(1)} copy-done((bf16[896,2688]{1,0:T(8,128)(2,1)S(1)}, bf16[896,2688]{1,0:T(8,128)(2,1)}, u32[]{:S(2)}) %copy-start) | copy-done | bytes 4816920
  22.7 3.0 %shard_map.127 = (bf16[128,896]{1,0:T(8,128)(2,1)S(1)}, bf16[128,896]{1,0:T(8,128)(2,1)S(1)}, bf16[128,2688]{1,0:T(8,128)(2,1)S(1)}, bf16[128,896]{1,0:T(8,128)(2,1)S(1)}) custom-call(bf16[128,896]{1,0:T(8,128)(2,1)S(1)} %collective-permute-done.x_ref, f32[1,896]{1,0:T(1,128)S(1)} %reshape.47.gain_ref, bf16[896,2688]{1,0:T(8,128)(2,1)S(1)} %copy-done, ...), custom_call_target="tpu_custom_call" | custom-call | flops 1000000000 | bytes 8000000 | tf_op jit(solution)/shard_map/pallas_call | solution.py:106
  25.7 8.5 %collective-permute-start.1 = (bf16[128,896]{1,0:T(8,128)(2,1)S(1)}, bf16[128,896]{1,0:T(8,128)(2,1)S(1)}, u32[]{:S(2)}, u32[]{:S(2)}) collective-permute-start(bf16[128,896]{1,0:T(8,128)(2,1)S(1)} %get-tuple-element.39.rest_0_), channel_id=1, source_target_pairs={{0,48},{16,0},{32,16},{48,32},{1,49},{17,1},{33,17},{49,33},{2,50}... | collective-permute-start | bytes 688136 | tf_op jit(solution)/shard_map/ppermute | solution.py:28
  34.2 0.1 collective-permute-start.2
  34.3 0.8 collective-permute-start.3
  35.1 3.1 %collective-permute-start.4 = (bf16[128,896]{1,0:T(8,128)(2,1)S(1)}, bf16[128,896]{1,0:T(8,128)(2,1)}, u32[]{:S(2)}, u32[]{:S(2)}) collective-permute-start(bf16[128,896]{1,0:T(8,128)(2,1)S(1)} %get-tuple-element.39.rest_0_), channel_id=1, source_target_pairs={{0,8},{8,0},{1,9},{9,1},{2,10},{10,2},{3,11},{11,3},{4,12},{12,4},... | collective-permute-start | bytes 688136 | tf_op jit(solution)/shard_map/ppermute | solution.py:32
  38.2 5.5 %collective-permute-done.1.rest_1_ = bf16[128,896]{1,0:T(8,128)(2,1)S(1)} collective-permute-done((bf16[128,896]{1,0:T(8,128)(2,1)S(1)}, bf16[128,896]{1,0:T(8,128)(2,1)S(1)}, u32[]{:S(2)}, u32[]{:S(2)}) %collective-permute-start.1) | collective-permute-done | bytes 229408 | tf_op jit(solution)/shard_map/ppermute | solution.py:28
  43.7 1.3 collective-permute-start.5
  44.9 1.3 collective-permute-start.6
  46.3 0.8 collective-permute-done.3.rest_3_
  47.1 1.4 collective-permute-start.7
  48.5 1.7 shard_map.128
  50.2 0.2 all-reduce.2.cloned.1.call-start
  50.5 0.1 copy.20
  50.6 0.1 reshape.44
  50.7 0.5 fusion.2.slots_ref
  51.2 19.4 %shard_map.129 = (bf16[4,64,1024]{2,1,0:T(8,128)(2,1)}, bf16[4,64,1024]{2,1,0:T(8,128)(2,1)}, bf16[1024,2048]{1,0:T(8,128)(2,1)}, bf16[896,2048]{1,0:T(8,128)(2,1)}, bf16[512,896]{1,0:T(8,128)(2,1)}) custom-call(s32[8]{0:T(128)} %fusion.2.slots_ref, bf16[4,64,1024]{2,1,0:T(8,128)(2,1)} %q_ref.1, bf16[4,64,1024]{2,1,0:T(8,128)(2,1)} %up_ref.1, ...), custom_call_target="tpu_custom_call" | custom-call | flops 16000000000 | bytes 16000000 | tf_op jit(solution)/shard_map/pallas_call | solution.py:189
  70.6 0.0 all-reduce.2.cloned.1.call-update
  70.7 2.8 %collective-permute-done.8.brought_ref = bf16[512,896]{1,0:T(8,128)(2,1)S(1)} collective-permute-done((bf16[512,896]{1,0:T(8,128)(2,1)}, bf16[512,896]{1,0:T(8,128)(2,1)S(1)}, u32[]{:S(2)}, u32[]{:S(2)}) %collective-permute-start.8) | collective-permute-done | bytes 917536 | tf_op jit(solution)/shard_map/ppermute | solution.py:32
  73.5 2.1 %copy-done.2 = bf16[896,2048]{1,0:T(8,128)(2,1)S(1)} copy-done((bf16[896,2048]{1,0:T(8,128)(2,1)S(1)}, bf16[896,2048]{1,0:T(8,128)(2,1)}, u32[]{:S(2)}) %copy-start.2) | copy-done | bytes 3670040
  75.6 2.2 %copy-done.4 = bf16[1024,2048]{1,0:T(8,128)(2,1)S(1)} copy-done((bf16[1024,2048]{1,0:T(8,128)(2,1)S(1)}, bf16[1024,2048]{1,0:T(8,128)(2,1)}, u32[]{:S(2)}) %copy-start.4) | copy-done | bytes 4194328
  77.9 2.4 %shard_map.130 = (f32[128,896]{1,0:T(8,128)S(1)}, bf16[128,896]{1,0:T(8,128)(2,1)S(1)}, bf16[128,896]{1,0:T(8,128)(2,1)S(1)}, bf16[128,896]{1,0:T(8,128)(2,1)S(1)}) custom-call(bf16[1024,2048]{1,0:T(8,128)(2,1)S(1)} %copy-done.4, bf16[896,2048]{1,0:T(8,128)(2,1)S(1)} %copy-done.2, bf16[512,896]{1,0:T(8,128)(2,1)S(1)} %collective-permute-done.8.brought_ref), custom_call_target="tpu_custom_call" | custom-call | flops 10000 | bytes 10000 | tf_op jit(solution)/shard_map/pallas_call | solution.py:273
  80.2 0.2 collective-permute-start.10
  80.4 0.9 collective-permute-start.11
  81.3 0.6 collective-permute-start.9
  81.9 7.0 %collective-permute-done.10 = bf16[128,896]{1,0:T(8,128)(2,1)S(1)} collective-permute-done((bf16[128,896]{1,0:T(8,128)(2,1)S(1)}, bf16[128,896]{1,0:T(8,128)(2,1)S(1)}, u32[]{:S(2)}, u32[]{:S(2)}) %collective-permute-start.10) | collective-permute-done | bytes 229408 | tf_op jit(solution)/shard_map/ppermute | solution.py:28
  88.9 2.9 %collective-permute-done.11 = bf16[128,896]{1,0:T(8,128)(2,1)S(1)} collective-permute-done((bf16[128,896]{1,0:T(8,128)(2,1)S(1)}, bf16[128,896]{1,0:T(8,128)(2,1)S(1)}, u32[]{:S(2)}, u32[]{:S(2)}) %collective-permute-start.11) | collective-permute-done | bytes 229408 | tf_op jit(solution)/shard_map/ppermute | solution.py:28
  91.8 2.6 %collective-permute-done.9 = bf16[128,896]{1,0:T(8,128)(2,1)S(1)} collective-permute-done((bf16[128,896]{1,0:T(8,128)(2,1)S(1)}, bf16[128,896]{1,0:T(8,128)(2,1)S(1)}, u32[]{:S(2)}, u32[]{:S(2)}) %collective-permute-start.9) | collective-permute-done | bytes 229408 | tf_op jit(solution)/shard_map/ppermute | solution.py:28
  94.4 0.1 add_convert_fusion.grad_ref
  94.5 4.6 %shard_map.131.parts_ref = bf16[8,128,512]{2,1,0:T(8,128)(2,1)} custom-call(bf16[128,896]{1,0:T(8,128)(2,1)S(1)} %add_convert_fusion.grad_ref, bf16[128,2688]{1,0:T(8,128)(2,1)S(1)} %get-tuple-element.57.projected_ref, bf16[896,896]{1,0:T(8,128)(2,1)S(1)} %copy-done.3), custom_call_target="tpu_custom_call" | custom-call | flops 10000 | bytes 10000 | tf_op jit(solution)/shard_map/pallas_call | solution.py:316
  99.1 4.5 %all-to-all-start = ((bf16[8,128,512]{2,1,0:T(8,128)(2,1)}), bf16[8,128,512]{2,1,0:T(8,128)(2,1)}, u32[]{:S(2)}, u32[]{:S(2)}) async-start(bf16[8,128,512]{2,1,0:T(8,128)(2,1)} %shard_map.131.parts_ref), calls=%async_computation | async-start | bytes 2097152 | tf_op jit(solution)/shard_map/all_to_all | solution.py:384
  103.6 2.6 %fusion = bf16[1024,1024]{0,1:T(8,128)(2,1)S(1)} fusion(bf16[1024,2048]{1,0:T(8,128)(2,1)} %all-gather.2.cloned.1.call-done, pred[]{:T(512)S(6)} %lt.20), kind=kLoop, calls=%fused_computation.1 | loop fusion | flops 1048576 | bytes 6291457 | tf_op jit(solution)/shard_map/transpose | solution.py:386
  106.2 12.6 %all-to-all-done = bf16[8,128,512]{2,1,0:T(8,128)(2,1)} async-done(((bf16[8,128,512]{2,1,0:T(8,128)(2,1)}), bf16[8,128,512]{2,1,0:T(8,128)(2,1)}, u32[]{:S(2)}, u32[]{:S(2)}) %all-to-all-start) | async-done | bytes 1048608 | tf_op jit(solution)/shard_map/all_to_all | solution.py:384
  118.8 3.5 %fusion.1 = bf16[128,8,512]{2,1,0:T(8,128)(2,1)} fusion(bf16[1024,1024]{0,1:T(8,128)(2,1)S(1)} %fusion, bf16[1024,512]{1,0:T(8,128)(2,1)} %bitcast.4), kind=kOutput, calls=%fused_computation.4 | convolution fusion | flops 1074266112 | bytes 4194304 | tf_op jit(solution)/shard_map/dot_general | solution.py:41
  122.4 8.4 %all-to-all-start.1 = ((bf16[128,8,512]{2,1,0:T(8,128)(2,1)}), bf16[128,8,512]{2,1,0:T(8,128)(2,1)}, u32[]{:S(2)}, u32[]{:S(2)}) async-start(bf16[128,8,512]{2,1,0:T(8,128)(2,1)} %fusion.1), calls=%async_computation.1 | async-start | bytes 2097152 | tf_op jit(solution)/shard_map/all_to_all | solution.py:387
  130.8 2.4 %copy-done.1 = bf16[896,2688]{1,0:T(8,128)(2,1)S(1)} copy-done((bf16[896,2688]{1,0:T(8,128)(2,1)S(1)}, bf16[896,2688]{1,0:T(8,128)(2,1)}, u32[]{:S(2)}) %copy-start.1) | copy-done | bytes 4816920
  133.2 3.0 %shard_map.132 = bf16[128,896]{1,0:T(8,128)(2,1)S(1)} custom-call(bf16[128,896]{1,0:T(8,128)(2,1)S(1)} %collective-permute-done.x_ref, f32[1,896]{1,0:T(1,128)S(1)} %reshape.47.gain_ref, bf16[896,2688]{1,0:T(8,128)(2,1)S(1)} %copy-done.1, bf16[8,128,512]{2,1,0:T(8,128)(2,1)} %shard_map.131.parts_ref, bf16[128,896]{1,0:T(8,128)(2,1)S(1)} %add_convert_fusion.grad_ref), custom_call_target="tpu_custom_call" | custom-call | flops 10000 | bytes 10000 | tf_op jit(solution)/shard_map/pallas_call | solution.py:339
  136.1 3.7 %collective-permute-start.12 = (bf16[128,896]{1,0:T(8,128)(2,1)S(1)}, bf16[128,896]{1,0:T(8,128)(2,1)S(1)}, u32[]{:S(2)}, u32[]{:S(2)}) collective-permute-start(bf16[128,896]{1,0:T(8,128)(2,1)S(1)} %shard_map.132), channel_id=1, source_target_pairs={{0,0},{1,8},{2,16},{3,24},{4,32},{5,40},{6,48},{7,56},{8,1},{9,9},... | collective-permute-start | bytes 688136 | tf_op jit(solution)/shard_map/ppermute | solution.py:37
  139.8 11.3 %all-to-all-done.1 = bf16[128,8,512]{2,1,0:T(8,128)(2,1)} async-done(((bf16[128,8,512]{2,1,0:T(8,128)(2,1)}), bf16[128,8,512]{2,1,0:T(8,128)(2,1)}, u32[]{:S(2)}, u32[]{:S(2)}) %all-to-all-start.1) | async-done | bytes 1048608 | tf_op jit(solution)/shard_map/all_to_all | solution.py:387
  151.1 1.4 convert_reduce_fusion
  152.5 0.6 slice.27
  153.1 0.6 slice.28
  153.7 25.1 %all-reduce.2.cloned.1.call-done.sum_ref = bf16[896,2048]{1,0:T(8,128)(2,1)} async-done(((bf16[896,2048]{1,0:T(8,128)(2,1)}), bf16[896,2048]{1,0:T(8,128)(2,1)}) %all-reduce.2.cloned.1.call-update) | async-done | bytes 3670032 | tf_op jit(solution)/shard_map/psum | solution.py:375
  178.8 4.3 %shard_map.133 = f32[14336,128]{1,0:T(8,128)} custom-call(bf16[896,2048]{1,0:T(8,128)(2,1)} %all-reduce.2.cloned.1.call-done.sum_ref), custom_call_target="tpu_custom_call" | custom-call | flops 1000000 | bytes 11000000 | tf_op jit(solution)/shard_map/pallas_call | solution.py:246
  183.1 0.7 copy.25
  (29 shorter events, 0.1 us)
Async XLA Ops:
  8.0 95.6 %all-gather.2.cloned.1.call-start = ((), (), s32[]{:S(2)}) async-start(), calls=%async_computation.3 | async-start | bytes 4718592 | tf_op jit(solution)/shard_map/all_gather | solution.py:368
  8.0 12.3 %collective-permute-start = (bf16[128,896]{1,0:T(8,128)(2,1)}, bf16[128,896]{1,0:T(8,128)(2,1)S(1)}, u32[]{:S(2)}, u32[]{:S(2)}) collective-permute-start(bf16[128,896]{1,0:T(8,128)(2,1)} %bitcast.27), channel_id=1, source_target_pairs={{0,0},{1,8},{2,16},{3,24},{4,32},{5,40},{6,48},{7,56},{8,1},{9,9},... | collective-permute-start | bytes 688136 | tf_op jit(solution)/shard_map/ppermute | solution.py:37
  13.0 7.3 %copy-start.6 = (f32[896]{0:T(1024)S(1)}, f32[896]{0:T(1024)}, u32[]{:S(2)}) copy-start(f32[896]{0:T(1024)} %param.9) | copy-start | bytes 10756
  13.0 7.3 %copy-start.3 = (bf16[896,896]{1,0:T(8,128)(2,1)S(1)}, bf16[896,896]{1,0:T(8,128)(2,1)}, u32[]{:S(2)}) copy-start(bf16[896,896]{1,0:T(8,128)(2,1)} %mix_ref.3) | copy-start | bytes 4816900
  20.3 2.4 %copy-start = (bf16[896,2688]{1,0:T(8,128)(2,1)S(1)}, bf16[896,2688]{1,0:T(8,128)(2,1)}, u32[]{:S(2)}) copy-start(bf16[896,2688]{1,0:T(8,128)(2,1)} %project_ref.3) | copy-start | bytes 14450692
  25.7 25.5 %copy-start.5 = (bf16[128,896]{1,0:T(8,128)(2,1)}, bf16[128,896]{1,0:T(8,128)(2,1)S(1)}, u32[]{:S(2)}) copy-start(bf16[128,896]{1,0:T(8,128)(2,1)S(1)} %get-tuple-element.39.rest_0_) | copy-start | bytes 688132
  25.7 24.8 %copy-start.7 = (s32[4,2]{0,1:T(2,128)S(1)}, s32[4,2]{0,1:T(2,128)}, u32[]{:S(2)}) copy-start(s32[4,2]{0,1:T(2,128)} %param.14) | copy-start | bytes 100
  25.7 18.0 %collective-permute-start.1 = (bf16[128,896]{1,0:T(8,128)(2,1)S(1)}, bf16[128,896]{1,0:T(8,128)(2,1)S(1)}, u32[]{:S(2)}, u32[]{:S(2)}) collective-permute-start(bf16[128,896]{1,0:T(8,128)(2,1)S(1)} %get-tuple-element.39.rest_0_), channel_id=1, source_target_pairs={{0,48},{16,0},{32,16},{48,32},{1,49},{17,1},{33,17},{49,33},{2,50}... | collective-permute-start | bytes 688136 | tf_op jit(solution)/shard_map/ppermute | solution.py:28
  34.2 10.7 %collective-permute-start.2 = (bf16[128,896]{1,0:T(8,128)(2,1)S(1)}, bf16[128,896]{1,0:T(8,128)(2,1)S(1)}, u32[]{:S(2)}, u32[]{:S(2)}) collective-permute-start(bf16[128,896]{1,0:T(8,128)(2,1)S(1)} %get-tuple-element.39.rest_0_), channel_id=1, source_target_pairs={{0,32},{16,48},{32,0},{48,16},{1,33},{17,49},{33,1},{49,17},{2,34}... | collective-permute-start | bytes 688136 | tf_op jit(solution)/shard_map/ppermute | solution.py:28
  34.3 12.7 %collective-permute-start.3 = (bf16[128,896]{1,0:T(8,128)(2,1)S(1)}, bf16[128,896]{1,0:T(8,128)(2,1)S(1)}, u32[]{:S(2)}, u32[]{:S(2)}) collective-permute-start(bf16[128,896]{1,0:T(8,128)(2,1)S(1)} %get-tuple-element.39.rest_0_), channel_id=1, source_target_pairs={{0,16},{16,32},{32,48},{48,0},{1,17},{17,33},{33,49},{49,1},{2,18}... | collective-permute-start | bytes 688136 | tf_op jit(solution)/shard_map/ppermute | solution.py:28
  35.1 15.1 %collective-permute-start.4 = (bf16[128,896]{1,0:T(8,128)(2,1)S(1)}, bf16[128,896]{1,0:T(8,128)(2,1)}, u32[]{:S(2)}, u32[]{:S(2)}) collective-permute-start(bf16[128,896]{1,0:T(8,128)(2,1)S(1)} %get-tuple-element.39.rest_0_), channel_id=1, source_target_pairs={{0,8},{8,0},{1,9},{9,1},{2,10},{10,2},{3,11},{11,3},{4,12},{12,4},... | collective-permute-start | bytes 688136 | tf_op jit(solution)/shard_map/ppermute | solution.py:32
  43.7 7.5 %copy-start.8 = (bf16[128,896]{1,0:T(8,128)(2,1)}, bf16[128,896]{1,0:T(8,128)(2,1)S(1)}, u32[]{:S(2)}) copy-start(bf16[128,896]{1,0:T(8,128)(2,1)S(1)} %collective-permute-done.1.rest_1_) | copy-start | bytes 688132
  43.7 6.5 %collective-permute-start.5 = (bf16[128,896]{1,0:T(8,128)(2,1)S(1)}, bf16[128,896]{1,0:T(8,128)(2,1)}, u32[]{:S(2)}, u32[]{:S(2)}) collective-permute-start(bf16[128,896]{1,0:T(8,128)(2,1)S(1)} %collective-permute-done.1.rest_1_), channel_id=1, source_target_pairs={{0,8},{8,0},{1,9},{9,1},{2,10},{10,2},{3,11},{11,3},{4,12},{12,4},... | collective-permute-start | bytes 688136 | tf_op jit(solution)/shard_map/ppermute | solution.py:32
  44.9 6.3 %copy-start.9 = (bf16[128,896]{1,0:T(8,128)(2,1)}, bf16[128,896]{1,0:T(8,128)(2,1)S(1)}, u32[]{:S(2)}) copy-start(bf16[128,896]{1,0:T(8,128)(2,1)S(1)} %collective-permute-done.2.rest_2_) | copy-start | bytes 688132
  44.9 5.3 %collective-permute-start.6 = (bf16[128,896]{1,0:T(8,128)(2,1)S(1)}, bf16[128,896]{1,0:T(8,128)(2,1)}, u32[]{:S(2)}, u32[]{:S(2)}) collective-permute-start(bf16[128,896]{1,0:T(8,128)(2,1)S(1)} %collective-permute-done.2.rest_2_), channel_id=1, source_target_pairs={{0,8},{8,0},{1,9},{9,1},{2,10},{10,2},{3,11},{11,3},{4,12},{12,4},... | collective-permute-start | bytes 688136 | tf_op jit(solution)/shard_map/ppermute | solution.py:32
  47.1 4.2 %copy-start.10 = (bf16[128,896]{1,0:T(8,128)(2,1)}, bf16[128,896]{1,0:T(8,128)(2,1)S(1)}, u32[]{:S(2)}) copy-start(bf16[128,896]{1,0:T(8,128)(2,1)S(1)} %collective-permute-done.3.rest_3_) | copy-start | bytes 688132
  47.1 3.1 %collective-permute-start.7 = (bf16[128,896]{1,0:T(8,128)(2,1)S(1)}, bf16[128,896]{1,0:T(8,128)(2,1)}, u32[]{:S(2)}, u32[]{:S(2)}) collective-permute-start(bf16[128,896]{1,0:T(8,128)(2,1)S(1)} %collective-permute-done.3.rest_3_), channel_id=1, source_target_pairs={{0,8},{8,0},{1,9},{9,1},{2,10},{10,2},{3,11},{11,3},{4,12},{12,4},... | collective-permute-start | bytes 688136 | tf_op jit(solution)/shard_map/ppermute | solution.py:32
  50.2 128.5 %all-reduce.2.cloned.1.call-start = ((), (), s32[]{:S(2)}) async-start(), calls=%async_computation.2 | async-start | bytes 7340032 | tf_op jit(solution)/shard_map/psum | solution.py:375
  70.6 2.9 %collective-permute-start.8 = (bf16[512,896]{1,0:T(8,128)(2,1)}, bf16[512,896]{1,0:T(8,128)(2,1)S(1)}, u32[]{:S(2)}, u32[]{:S(2)}) collective-permute-start(bf16[512,896]{1,0:T(8,128)(2,1)} %get-tuple-element.52), channel_id=1, source_target_pairs={{0,8},{8,0},{1,9},{9,1},{2,10},{10,2},{3,11},{11,3},{4,12},{12,4},... | collective-permute-start | bytes 2752520 | tf_op jit(solution)/shard_map/ppermute | solution.py:32
  73.5 2.1 %copy-start.2 = (bf16[896,2048]{1,0:T(8,128)(2,1)S(1)}, bf16[896,2048]{1,0:T(8,128)(2,1)}, u32[]{:S(2)}) copy-start(bf16[896,2048]{1,0:T(8,128)(2,1)} %reshape.46.weight_ref) | copy-start | bytes 11010052
  75.6 2.2 %copy-start.4 = (bf16[1024,2048]{1,0:T(8,128)(2,1)S(1)}, bf16[1024,2048]{1,0:T(8,128)(2,1)}, u32[]{:S(2)}) copy-start(bf16[1024,2048]{1,0:T(8,128)(2,1)} %get-tuple-element.51.pairs_ref) | copy-start | bytes 12582916
  80.2 8.7 %collective-permute-start.10 = (bf16[128,896]{1,0:T(8,128)(2,1)S(1)}, bf16[128,896]{1,0:T(8,128)(2,1)S(1)}, u32[]{:S(2)}, u32[]{:S(2)}) collective-permute-start(bf16[128,896]{1,0:T(8,128)(2,1)S(1)} %get-tuple-element.55), channel_id=1, source_target_pairs={{0,32},{16,48},{32,0},{48,16},{1,33},{17,49},{33,1},{49,17},{2,34}... | collective-permute-start | bytes 688136 | tf_op jit(solution)/shard_map/ppermute | solution.py:28
  80.4 11.3 %collective-permute-start.11 = (bf16[128,896]{1,0:T(8,128)(2,1)S(1)}, bf16[128,896]{1,0:T(8,128)(2,1)S(1)}, u32[]{:S(2)}, u32[]{:S(2)}) collective-permute-start(bf16[128,896]{1,0:T(8,128)(2,1)S(1)} %get-tuple-element.56), channel_id=1, source_target_pairs={{0,48},{16,0},{32,16},{48,32},{1,49},{17,1},{33,17},{49,33},{2,50}... | collective-permute-start | bytes 688136 | tf_op jit(solution)/shard_map/ppermute | solution.py:28
  81.3 13.1 %collective-permute-start.9 = (bf16[128,896]{1,0:T(8,128)(2,1)S(1)}, bf16[128,896]{1,0:T(8,128)(2,1)S(1)}, u32[]{:S(2)}, u32[]{:S(2)}) collective-permute-start(bf16[128,896]{1,0:T(8,128)(2,1)S(1)} %get-tuple-element.54), channel_id=1, source_target_pairs={{0,16},{16,32},{32,48},{48,0},{1,17},{17,33},{33,49},{49,1},{2,18}... | collective-permute-start | bytes 688136 | tf_op jit(solution)/shard_map/ppermute | solution.py:28
  99.1 19.7 %all-to-all-start = ((bf16[8,128,512]{2,1,0:T(8,128)(2,1)}), bf16[8,128,512]{2,1,0:T(8,128)(2,1)}, u32[]{:S(2)}, u32[]{:S(2)}) async-start(bf16[8,128,512]{2,1,0:T(8,128)(2,1)} %shard_map.131.parts_ref), calls=%async_computation | async-start | bytes 2097152 | tf_op jit(solution)/shard_map/all_to_all | solution.py:384
  122.4 28.7 %all-to-all-start.1 = ((bf16[128,8,512]{2,1,0:T(8,128)(2,1)}), bf16[128,8,512]{2,1,0:T(8,128)(2,1)}, u32[]{:S(2)}, u32[]{:S(2)}) async-start(bf16[128,8,512]{2,1,0:T(8,128)(2,1)} %fusion.1), calls=%async_computation.1 | async-start | bytes 2097152 | tf_op jit(solution)/shard_map/all_to_all | solution.py:387
  130.8 2.4 %copy-start.1 = (bf16[896,2688]{1,0:T(8,128)(2,1)S(1)}, bf16[896,2688]{1,0:T(8,128)(2,1)}, u32[]{:S(2)}) copy-start(bf16[896,2688]{1,0:T(8,128)(2,1)} %project_ref.3) | copy-start | bytes 14450692
  136.1 17.6 %collective-permute-start.12 = (bf16[128,896]{1,0:T(8,128)(2,1)S(1)}, bf16[128,896]{1,0:T(8,128)(2,1)S(1)}, u32[]{:S(2)}, u32[]{:S(2)}) collective-permute-start(bf16[128,896]{1,0:T(8,128)(2,1)S(1)} %shard_map.132), channel_id=1, source_target_pairs={{0,0},{1,8},{2,16},{3,24},{4,32},{5,40},{6,48},{7,56},{8,1},{9,9},... | collective-permute-start | bytes 688136 | tf_op jit(solution)/shard_map/ppermute | solution.py:37
Sparse Core Ops, SparseCore 0:
  50.4 31.4 all-gather.1
Sparse Core Ops, SparseCore 1:
  70.8 108.0 all-reduce.1

commit v8 on v7

--- a/solution.py
+++ b/solution.py
@@ -135,16 +135,15 @@
     )(normed, mixed)
 
 
-def cross_kernel(per, slots_ref, q_ref, up_ref, weight_ref, *rest):
-    sources, rest = rest[:8], rest[8:]
-    out_ref, grad_ref, pairs_ref, sum_ref, far_ref, rows_ref, turned_ref, held_ref = rest
-
-    @pl.when(pl.program_id(0) == 0)
-    def _():
-        for n, source in enumerate(sources):
-            rows_ref[n * TOK : (n + 1) * TOK] = source[...]
-            turned_ref[:, n * TOK : (n + 1) * TOK] = source[...].T
-
+def cross_kernel(per, slots_ref, q_ref, up_ref, weight_hbm, *rest):
+    sources, (out_ref, grad_ref, pairs_hbm, sum_hbm, far_ref), rest = rest[:8], rest[8:13], rest[13:]
+    weight_ref, rows_ref, turned_ref, held_ref, pairs_ref, sum_ref, sems = rest
+    fetch = pltpu.make_async_copy(weight_hbm, weight_ref, sems.at[0])
+    fetch.start()
+    for n, source in enumerate(sources):
+        rows_ref[n * TOK : (n + 1) * TOK] = source[...]
+        turned_ref[:, n * TOK : (n + 1) * TOK] = source[...].T
+    fetch.wait()
     scale = 1.0 / math.sqrt(HS)
     length = q_ref.shape[1]
     none = jnp.zeros((length, HS), bf16)
@@ -178,14 +177,21 @@
             g = jnp.concatenate([g[:, :HS] * scale, g[:, HS:]], axis=1).astype(bf16)
             for n in range(2):
                 pairs_ref[rows[c][n], pair] = g[n * TOK : (n + 1) * TOK]
+    give_pairs = pltpu.make_async_copy(pairs_ref, pairs_hbm, sems.at[1])
+    give_pairs.start()
     sum_ref[...] = nn(turned_ref[...], pairs_ref[...]).astype(bf16)
+    give_sum = pltpu.make_async_copy(sum_ref, sum_hbm, sems.at[2])
+    give_sum.start()
     far_ref[...] = nt(pairs_ref[4 * TOK :], weight_ref[...]).astype(bf16)
+    give_pairs.wait()
+    give_sum.wait()
 
 
 def cross(slots, queries, upstream, weight, sources):
     spans, length, inner = queries.shape
     rows = len(sources) * TOK
     column = pl.BlockSpec((spans, length, inner), lambda i, s: (0, 0, i))
+    hbm = pl.BlockSpec(memory_space=pltpu.HBM)
     return pl.pallas_call(
         functools.partial(cross_kernel, inner // HS),
         grid_spec=pltpu.PrefetchScalarGridSpec(
@@ -194,20 +200,24 @@
             in_specs=[
                 column,
                 column,
-                pl.BlockSpec((ENC, 2 * inner), lambda i, s: (0, i)),
+                hbm,
                 *[pl.BlockSpec((TOK, ENC), lambda i, s: (0, 0))] * len(sources),
             ],
             out_specs=(
                 column,
                 column,
-                pl.BlockSpec((rows, 2 * inner), lambda i, s: (0, i)),
-                pl.BlockSpec((ENC, 2 * inner), lambda i, s: (0, i)),
+                hbm,
+                hbm,
                 pl.BlockSpec((4 * TOK, ENC), lambda i, s: (0, 0)),
             ),
             scratch_shapes=[
+                pltpu.VMEM((ENC, 2 * inner), bf16),
                 pltpu.VMEM((rows, ENC), bf16),
                 pltpu.VMEM((ENC, rows), bf16),
                 pltpu.VMEM((rows, 2 * inner), bf16),
+                pltpu.VMEM((rows, 2 * inner), bf16),
+                pltpu.VMEM((ENC, 2 * inner), bf16),
+                pltpu.SemaphoreType.DMA((3,)),
             ],
         ),
         out_shape=(

time: 192 us -> 194 us (1.010)
  transfers between devices with their start and end apart: 17 -> 17, of which waited for: 9 -> 9; matrix products, arithmetic and copies ran while one was open for 9% -> 9% of each run, Pallas kernels for 16% -> 17%
where the time goes in v8:
time: 194 us; the launch traced here: 193 us
  waiting for transfers between devices  70.1 us (36%)
  starting transfers between devices  40.7 us (21%)
  Pallas kernels  39.9 us (21%)
  local copies, waits for them, and re-layouts  18.5 us (10%)
  between operations  15.7 us (8%)
  other arithmetic  4.59 us (2%)
  matrix products  3.52 us (2%)
    psum x1, waiting for transfers between devices, shards(): summed = lax.psum(grad_weight, PLANE)  25.1 us
    pallas_call x1, Pallas kernels, cross(): pl.pallas_call(functools.partial(cross_kernel, inner // HS), grid_spec=pl...  20.9 us
    ppermute x6, waiting for transfers between devices, turned(): return lambda x: lax.ppermute(x, axis, pairs)  18.5 us
    all_to_all x1, waiting for transfers between devices, shards(): lax.all_to_all(parts, TP, 0, 0, tiled=True).reshape(8 * TOK, LANES)  12.6 us
    ppermute x6, starting transfers between devices, turned(): return lambda x: lax.ppermute(x, axis, pairs)  11.3 us
    all_to_all x1, waiting for transfers between devices, shards(): arrived = lax.all_to_all(encoder_grad, FINE, 0, 0, tiled=True).astype(f32)  11.3 us
    unnamed x24, local copies, waits for them, and re-layouts  9.89 us
    ppermute x2, starting transfers between devices, flipped(): return lax.ppermute(x, ('y', 'c', 'xl', 'z'), pairs)  8.62 us
  transfers between devices with their start and end apart: 17, of which 9 were waited for; matrix products, arithmetic and copies ran while one was open for 9% of the time, Pallas kernels for 17%

profile of v8, /device:TPU:1, one launch (start us, length us, event | category | flops | bytes accessed | tf_op | source)
XLA Modules:
  0.0 193.0 jit_solution(11633432242901974993)
XLA Ops:
  8.0 0.0 all-gather.2.cloned.1.call-start
  8.0 4.9 %collective-permute-start = (bf16[128,896]{1,0:T(8,128)(2,1)}, bf16[128,896]{1,0:T(8,128)(2,1)S(1)}, u32[]{:S(2)}, u32[]{:S(2)}) collective-permute-start(bf16[128,896]{1,0:T(8,128)(2,1)} %bitcast.27), channel_id=1, source_target_pairs={{0,0},{1,8},{2,16},{3,24},{4,32},{5,40},{6,48},{7,56},{8,1},{9,9},... | collective-permute-start | bytes 688136 | tf_op jit(solution)/shard_map/ppermute | solution.py:37
  13.0 7.3 %reshape.46.weight_hbm.weight_ref = bf16[896,2048]{1,0:T(8,128)(2,1)} reshape(bf16[896,8,2,128]{3,2,1,0:T(2,128)(2,1)} %bitcast.23) | data formatting | bytes 7340032 | tf_op jit(solution)/shard_map/reshape | solution.py:371
  20.3 2.4 %copy-done = bf16[896,2688]{1,0:T(8,128)(2,1)S(1)} copy-done((bf16[896,2688]{1,0:T(8,128)(2,1)S(1)}, bf16[896,2688]{1,0:T(8,128)(2,1)}, u32[]{:S(2)}) %copy-start) | copy-done | bytes 4816920
  22.7 3.0 %shard_map.127 = (bf16[128,896]{1,0:T(8,128)(2,1)S(1)}, bf16[128,896]{1,0:T(8,128)(2,1)S(1)}, bf16[128,2688]{1,0:T(8,128)(2,1)S(1)}, bf16[128,896]{1,0:T(8,128)(2,1)S(1)}) custom-call(bf16[128,896]{1,0:T(8,128)(2,1)S(1)} %collective-permute-done.x_ref, f32[1,896]{1,0:T(1,128)S(1)} %reshape.47.gain_ref, bf16[896,2688]{1,0:T(8,128)(2,1)S(1)} %copy-done, ...), custom_call_target="tpu_custom_call" | custom-call | flops 1000000000 | bytes 8000000 | tf_op jit(solution)/shard_map/pallas_call | solution.py:106
  25.7 8.5 %collective-permute-start.1 = (bf16[128,896]{1,0:T(8,128)(2,1)S(1)}, bf16[128,896]{1,0:T(8,128)(2,1)S(1)}, u32[]{:S(2)}, u32[]{:S(2)}) collective-permute-start(bf16[128,896]{1,0:T(8,128)(2,1)S(1)} %get-tuple-element.39.rest_0_), channel_id=1, source_target_pairs={{0,48},{16,0},{32,16},{48,32},{1,49},{17,1},{33,17},{49,33},{2,50}... | collective-permute-start | bytes 688136 | tf_op jit(solution)/shard_map/ppermute | solution.py:28
  34.2 0.1 collective-permute-start.2
  34.3 0.8 collective-permute-start.3
  35.1 3.1 %collective-permute-start.4 = (bf16[128,896]{1,0:T(8,128)(2,1)S(1)}, bf16[128,896]{1,0:T(8,128)(2,1)}, u32[]{:S(2)}, u32[]{:S(2)}) collective-permute-start(bf16[128,896]{1,0:T(8,128)(2,1)S(1)} %get-tuple-element.39.rest_0_), channel_id=1, source_target_pairs={{0,8},{8,0},{1,9},{9,1},{2,10},{10,2},{3,11},{11,3},{4,12},{12,4},... | collective-permute-start | bytes 688136 | tf_op jit(solution)/shard_map/ppermute | solution.py:32
  38.2 5.5 %collective-permute-done.1.rest_1_ = bf16[128,896]{1,0:T(8,128)(2,1)S(1)} collective-permute-done((bf16[128,896]{1,0:T(8,128)(2,1)S(1)}, bf16[128,896]{1,0:T(8,128)(2,1)S(1)}, u32[]{:S(2)}, u32[]{:S(2)}) %collective-permute-start.1) | collective-permute-done | bytes 229408 | tf_op jit(solution)/shard_map/ppermute | solution.py:28
  43.7 1.3 collective-permute-start.5
  44.9 1.3 collective-permute-start.6
  46.3 0.8 collective-permute-done.3.rest_3_
  47.1 1.4 collective-permute-start.7
  48.5 1.7 shard_map.128
  50.2 0.2 all-reduce.2.cloned.1.call-start
  50.5 0.1 copy.20
  50.6 0.1 reshape.44
  50.7 0.5 fusion.2.slots_ref
  51.2 20.9 %shard_map.129 = (bf16[4,64,1024]{2,1,0:T(8,128)(2,1)}, bf16[4,64,1024]{2,1,0:T(8,128)(2,1)}, bf16[1024,2048]{1,0:T(8,128)(2,1)}, bf16[896,2048]{1,0:T(8,128)(2,1)}, bf16[512,896]{1,0:T(8,128)(2,1)}) custom-call(s32[8]{0:T(128)} %fusion.2.slots_ref, bf16[4,64,1024]{2,1,0:T(8,128)(2,1)} %q_ref.1, bf16[4,64,1024]{2,1,0:T(8,128)(2,1)} %up_ref.1, ...), custom_call_target="tpu_custom_call" | custom-call | flops 16000000000 | bytes 16000000 | tf_op jit(solution)/shard_map/pallas_call | solution.py:195
  72.1 0.3 collective-permute-start.8
  72.4 2.6 %collective-permute-done.8.brought_ref = bf16[512,896]{1,0:T(8,128)(2,1)S(1)} collective-permute-done((bf16[512,896]{1,0:T(8,128)(2,1)}, bf16[512,896]{1,0:T(8,128)(2,1)S(1)}, u32[]{:S(2)}, u32[]{:S(2)}) %collective-permute-start.8) | collective-permute-done | bytes 917536 | tf_op jit(solution)/shard_map/ppermute | solution.py:32
  75.1 2.1 %copy-done.2 = bf16[896,2048]{1,0:T(8,128)(2,1)S(1)} copy-done((bf16[896,2048]{1,0:T(8,128)(2,1)S(1)}, bf16[896,2048]{1,0:T(8,128)(2,1)}, u32[]{:S(2)}) %copy-start.2) | copy-done | bytes 3670040
  77.2 2.2 %copy-done.4 = bf16[1024,2048]{1,0:T(8,128)(2,1)S(1)} copy-done((bf16[1024,2048]{1,0:T(8,128)(2,1)S(1)}, bf16[1024,2048]{1,0:T(8,128)(2,1)}, u32[]{:S(2)}) %copy-start.4) | copy-done | bytes 4194328
  79.4 2.4 %shard_map.130 = (f32[128,896]{1,0:T(8,128)S(1)}, bf16[128,896]{1,0:T(8,128)(2,1)S(1)}, bf16[128,896]{1,0:T(8,128)(2,1)S(1)}, bf16[128,896]{1,0:T(8,128)(2,1)S(1)}) custom-call(bf16[1024,2048]{1,0:T(8,128)(2,1)S(1)} %copy-done.4, bf16[896,2048]{1,0:T(8,128)(2,1)S(1)} %copy-done.2, bf16[512,896]{1,0:T(8,128)(2,1)S(1)} %collective-permute-done.8.brought_ref), custom_call_target="tpu_custom_call" | custom-call | flops 10000 | bytes 10000 | tf_op jit(solution)/shard_map/pallas_call | solution.py:283
  81.8 0.4 collective-permute-start.10
  82.2 1.0 collective-permute-start.11
  83.2 0.4 collective-permute-start.9
  83.7 6.8 %collective-permute-done.10 = bf16[128,896]{1,0:T(8,128)(2,1)S(1)} collective-permute-done((bf16[128,896]{1,0:T(8,128)(2,1)S(1)}, bf16[128,896]{1,0:T(8,128)(2,1)S(1)}, u32[]{:S(2)}, u32[]{:S(2)}) %collective-permute-start.10) | collective-permute-done | bytes 229408 | tf_op jit(solution)/shard_map/ppermute | solution.py:28
  90.5 3.1 %collective-permute-done.11 = bf16[128,896]{1,0:T(8,128)(2,1)S(1)} collective-permute-done((bf16[128,896]{1,0:T(8,128)(2,1)S(1)}, bf16[128,896]{1,0:T(8,128)(2,1)S(1)}, u32[]{:S(2)}, u32[]{:S(2)}) %collective-permute-start.11) | collective-permute-done | bytes 229408 | tf_op jit(solution)/shard_map/ppermute | solution.py:28
  93.6 2.3 %collective-permute-done.9 = bf16[128,896]{1,0:T(8,128)(2,1)S(1)} collective-permute-done((bf16[128,896]{1,0:T(8,128)(2,1)S(1)}, bf16[128,896]{1,0:T(8,128)(2,1)S(1)}, u32[]{:S(2)}, u32[]{:S(2)}) %collective-permute-start.9) | collective-permute-done | bytes 229408 | tf_op jit(solution)/shard_map/ppermute | solution.py:28
  95.9 0.1 add_convert_fusion.grad_ref
  96.0 4.6 %shard_map.131.parts_ref = bf16[8,128,512]{2,1,0:T(8,128)(2,1)} custom-call(bf16[128,896]{1,0:T(8,128)(2,1)S(1)} %add_convert_fusion.grad_ref, bf16[128,2688]{1,0:T(8,128)(2,1)S(1)} %get-tuple-element.57.projected_ref, bf16[896,896]{1,0:T(8,128)(2,1)S(1)} %copy-done.3), custom_call_target="tpu_custom_call" | custom-call | flops 10000 | bytes 10000 | tf_op jit(solution)/shard_map/pallas_call | solution.py:326
  100.7 4.5 %all-to-all-start = ((bf16[8,128,512]{2,1,0:T(8,128)(2,1)}), bf16[8,128,512]{2,1,0:T(8,128)(2,1)}, u32[]{:S(2)}, u32[]{:S(2)}) async-start(bf16[8,128,512]{2,1,0:T(8,128)(2,1)} %shard_map.131.parts_ref), calls=%async_computation | async-start | bytes 2097152 | tf_op jit(solution)/shard_map/all_to_all | solution.py:394
  105.2 2.6 %fusion = bf16[1024,1024]{0,1:T(8,128)(2,1)S(1)} fusion(bf16[1024,2048]{1,0:T(8,128)(2,1)} %all-gather.2.cloned.1.call-done, pred[]{:T(512)S(6)} %lt.20), kind=kLoop, calls=%fused_computation.1 | loop fusion | flops 1048576 | bytes 6291457 | tf_op jit(solution)/shard_map/transpose | solution.py:396
  107.7 12.6 %all-to-all-done = bf16[8,128,512]{2,1,0:T(8,128)(2,1)} async-done(((bf16[8,128,512]{2,1,0:T(8,128)(2,1)}), bf16[8,128,512]{2,1,0:T(8,128)(2,1)}, u32[]{:S(2)}, u32[]{:S(2)}) %all-to-all-start) | async-done | bytes 1048608 | tf_op jit(solution)/shard_map/all_to_all | solution.py:394
  120.4 3.5 %fusion.1 = bf16[128,8,512]{2,1,0:T(8,128)(2,1)} fusion(bf16[1024,1024]{0,1:T(8,128)(2,1)S(1)} %fusion, bf16[1024,512]{1,0:T(8,128)(2,1)} %bitcast.4), kind=kOutput, calls=%fused_computation.4 | convolution fusion | flops 1074266112 | bytes 4194304 | tf_op jit(solution)/shard_map/dot_general | solution.py:41
  123.9 8.6 %all-to-all-start.1 = ((bf16[128,8,512]{2,1,0:T(8,128)(2,1)}), bf16[128,8,512]{2,1,0:T(8,128)(2,1)}, u32[]{:S(2)}, u32[]{:S(2)}) async-start(bf16[128,8,512]{2,1,0:T(8,128)(2,1)} %fusion.1), calls=%async_computation.1 | async-start | bytes 2097152 | tf_op jit(solution)/shard_map/all_to_all | solution.py:397
  132.5 2.4 %copy-done.1 = bf16[896,2688]{1,0:T(8,128)(2,1)S(1)} copy-done((bf16[896,2688]{1,0:T(8,128)(2,1)S(1)}, bf16[896,2688]{1,0:T(8,128)(2,1)}, u32[]{:S(2)}) %copy-start.1) | copy-done | bytes 4816920
  134.9 3.0 %shard_map.132 = bf16[128,896]{1,0:T(8,128)(2,1)S(1)} custom-call(bf16[128,896]{1,0:T(8,128)(2,1)S(1)} %collective-permute-done.x_ref, f32[1,896]{1,0:T(1,128)S(1)} %reshape.47.gain_ref, bf16[896,2688]{1,0:T(8,128)(2,1)S(1)} %copy-done.1, bf16[8,128,512]{2,1,0:T(8,128)(2,1)} %shard_map.131.parts_ref, bf16[128,896]{1,0:T(8,128)(2,1)S(1)} %add_convert_fusion.grad_ref), custom_call_target="tpu_custom_call" | custom-call | flops 10000 | bytes 10000 | tf_op jit(solution)/shard_map/pallas_call | solution.py:349
  137.8 3.7 %collective-permute-start.12 = (bf16[128,896]{1,0:T(8,128)(2,1)S(1)}, bf16[128,896]{1,0:T(8,128)(2,1)S(1)}, u32[]{:S(2)}, u32[]{:S(2)}) collective-permute-start(bf16[128,896]{1,0:T(8,128)(2,1)S(1)} %shard_map.132), channel_id=1, source_target_pairs={{0,0},{1,8},{2,16},{3,24},{4,32},{5,40},{6,48},{7,56},{8,1},{9,9},... | collective-permute-start | bytes 688136 | tf_op jit(solution)/shard_map/ppermute | solution.py:37
  141.5 11.3 %all-to-all-done.1 = bf16[128,8,512]{2,1,0:T(8,128)(2,1)} async-done(((bf16[128,8,512]{2,1,0:T(8,128)(2,1)}), bf16[128,8,512]{2,1,0:T(8,128)(2,1)}, u32[]{:S(2)}, u32[]{:S(2)}) %all-to-all-start.1) | async-done | bytes 1048608 | tf_op jit(solution)/shard_map/all_to_all | solution.py:397
  152.8 1.4 convert_reduce_fusion
  154.2 0.6 slice.27
  154.8 0.6 slice.28
  155.4 25.1 %all-reduce.2.cloned.1.call-done.sum_ref = bf16[896,2048]{1,0:T(8,128)(2,1)} async-done(((bf16[896,2048]{1,0:T(8,128)(2,1)}), bf16[896,2048]{1,0:T(8,128)(2,1)}) %all-reduce.2.cloned.1.call-update) | async-done | bytes 3670032 | tf_op jit(solution)/shard_map/psum | solution.py:385
  180.5 4.3 %shard_map.133 = f32[14336,128]{1,0:T(8,128)} custom-call(bf16[896,2048]{1,0:T(8,128)(2,1)} %all-reduce.2.cloned.1.call-done.sum_ref), custom_call_target="tpu_custom_call" | custom-call | flops 1000000 | bytes 11000000 | tf_op jit(solution)/shard_map/pallas_call | solution.py:256
  184.8 0.7 copy.25
  (29 shorter events, 0.1 us)
Async XLA Ops:
  8.0 97.2 %all-gather.2.cloned.1.call-start = ((), (), s32[]{:S(2)}) async-start(), calls=%async_computation.3 | async-start | bytes 4718592 | tf_op jit(solution)/shard_map/all_gather | solution.py:378
  8.0 12.3 %collective-permute-start = (bf16[128,896]{1,0:T(8,128)(2,1)}, bf16[128,896]{1,0:T(8,128)(2,1)S(1)}, u32[]{:S(2)}, u32[]{:S(2)}) collective-permute-start(bf16[128,896]{1,0:T(8,128)(2,1)} %bitcast.27), channel_id=1, source_target_pairs={{0,0},{1,8},{2,16},{3,24},{4,32},{5,40},{6,48},{7,56},{8,1},{9,9},... | collective-permute-start | bytes 688136 | tf_op jit(solution)/shard_map/ppermute | solution.py:37
  13.0 7.3 %copy-start.6 = (f32[896]{0:T(1024)S(1)}, f32[896]{0:T(1024)}, u32[]{:S(2)}) copy-start(f32[896]{0:T(1024)} %param.9) | copy-start | bytes 10756
  13.0 7.3 %copy-start.3 = (bf16[896,896]{1,0:T(8,128)(2,1)S(1)}, bf16[896,896]{1,0:T(8,128)(2,1)}, u32[]{:S(2)}) copy-start(bf16[896,896]{1,0:T(8,128)(2,1)} %mix_ref.3) | copy-start | bytes 4816900
  20.3 2.4 %copy-start = (bf16[896,2688]{1,0:T(8,128)(2,1)S(1)}, bf16[896,2688]{1,0:T(8,128)(2,1)}, u32[]{:S(2)}) copy-start(bf16[896,2688]{1,0:T(8,128)(2,1)} %project_ref.3) | copy-start | bytes 14450692
  25.7 25.5 %copy-start.5 = (bf16[128,896]{1,0:T(8,128)(2,1)}, bf16[128,896]{1,0:T(8,128)(2,1)S(1)}, u32[]{:S(2)}) copy-start(bf16[128,896]{1,0:T(8,128)(2,1)S(1)} %get-tuple-element.39.rest_0_) | copy-start | bytes 688132
  25.7 24.8 %copy-start.7 = (s32[4,2]{0,1:T(2,128)S(1)}, s32[4,2]{0,1:T(2,128)}, u32[]{:S(2)}) copy-start(s32[4,2]{0,1:T(2,128)} %param.14) | copy-start | bytes 100
  25.7 18.0 %collective-permute-start.1 = (bf16[128,896]{1,0:T(8,128)(2,1)S(1)}, bf16[128,896]{1,0:T(8,128)(2,1)S(1)}, u32[]{:S(2)}, u32[]{:S(2)}) collective-permute-start(bf16[128,896]{1,0:T(8,128)(2,1)S(1)} %get-tuple-element.39.rest_0_), channel_id=1, source_target_pairs={{0,48},{16,0},{32,16},{48,32},{1,49},{17,1},{33,17},{49,33},{2,50}... | collective-permute-start | bytes 688136 | tf_op jit(solution)/shard_map/ppermute | solution.py:28
  34.2 10.7 %collective-permute-start.2 = (bf16[128,896]{1,0:T(8,128)(2,1)S(1)}, bf16[128,896]{1,0:T(8,128)(2,1)S(1)}, u32[]{:S(2)}, u32[]{:S(2)}) collective-permute-start(bf16[128,896]{1,0:T(8,128)(2,1)S(1)} %get-tuple-element.39.rest_0_), channel_id=1, source_target_pairs={{0,32},{16,48},{32,0},{48,16},{1,33},{17,49},{33,1},{49,17},{2,34}... | collective-permute-start | bytes 688136 | tf_op jit(solution)/shard_map/ppermute | solution.py:28
  34.3 12.7 %collective-permute-start.3 = (bf16[128,896]{1,0:T(8,128)(2,1)S(1)}, bf16[128,896]{1,0:T(8,128)(2,1)S(1)}, u32[]{:S(2)}, u32[]{:S(2)}) collective-permute-start(bf16[128,896]{1,0:T(8,128)(2,1)S(1)} %get-tuple-element.39.rest_0_), channel_id=1, source_target_pairs={{0,16},{16,32},{32,48},{48,0},{1,17},{17,33},{33,49},{49,1},{2,18}... | collective-permute-start | bytes 688136 | tf_op jit(solution)/shard_map/ppermute | solution.py:28
  35.1 15.1 %collective-permute-start.4 = (bf16[128,896]{1,0:T(8,128)(2,1)S(1)}, bf16[128,896]{1,0:T(8,128)(2,1)}, u32[]{:S(2)}, u32[]{:S(2)}) collective-permute-start(bf16[128,896]{1,0:T(8,128)(2,1)S(1)} %get-tuple-element.39.rest_0_), channel_id=1, source_target_pairs={{0,8},{8,0},{1,9},{9,1},{2,10},{10,2},{3,11},{11,3},{4,12},{12,4},... | collective-permute-start | bytes 688136 | tf_op jit(solution)/shard_map/ppermute | solution.py:32
  43.7 7.5 %copy-start.8 = (bf16[128,896]{1,0:T(8,128)(2,1)}, bf16[128,896]{1,0:T(8,128)(2,1)S(1)}, u32[]{:S(2)}) copy-start(bf16[128,896]{1,0:T(8,128)(2,1)S(1)} %collective-permute-done.1.rest_1_) | copy-start | bytes 688132
  43.7 6.5 %collective-permute-start.5 = (bf16[128,896]{1,0:T(8,128)(2,1)S(1)}, bf16[128,896]{1,0:T(8,128)(2,1)}, u32[]{:S(2)}, u32[]{:S(2)}) collective-permute-start(bf16[128,896]{1,0:T(8,128)(2,1)S(1)} %collective-permute-done.1.rest_1_), channel_id=1, source_target_pairs={{0,8},{8,0},{1,9},{9,1},{2,10},{10,2},{3,11},{11,3},{4,12},{12,4},... | collective-permute-start | bytes 688136 | tf_op jit(solution)/shard_map/ppermute | solution.py:32
  44.9 6.3 %copy-start.9 = (bf16[128,896]{1,0:T(8,128)(2,1)}, bf16[128,896]{1,0:T(8,128)(2,1)S(1)}, u32[]{:S(2)}) copy-start(bf16[128,896]{1,0:T(8,128)(2,1)S(1)} %collective-permute-done.2.rest_2_) | copy-start | bytes 688132
  44.9 5.3 %collective-permute-start.6 = (bf16[128,896]{1,0:T(8,128)(2,1)S(1)}, bf16[128,896]{1,0:T(8,128)(2,1)}, u32[]{:S(2)}, u32[]{:S(2)}) collective-permute-start(bf16[128,896]{1,0:T(8,128)(2,1)S(1)} %collective-permute-done.2.rest_2_), channel_id=1, source_target_pairs={{0,8},{8,0},{1,9},{9,1},{2,10},{10,2},{3,11},{11,3},{4,12},{12,4},... | collective-permute-start | bytes 688136 | tf_op jit(solution)/shard_map/ppermute | solution.py:32
  47.1 4.2 %copy-start.10 = (bf16[128,896]{1,0:T(8,128)(2,1)}, bf16[128,896]{1,0:T(8,128)(2,1)S(1)}, u32[]{:S(2)}) copy-start(bf16[128,896]{1,0:T(8,128)(2,1)S(1)} %collective-permute-done.3.rest_3_) | copy-start | bytes 688132
  47.1 3.1 %collective-permute-start.7 = (bf16[128,896]{1,0:T(8,128)(2,1)S(1)}, bf16[128,896]{1,0:T(8,128)(2,1)}, u32[]{:S(2)}, u32[]{:S(2)}) collective-permute-start(bf16[128,896]{1,0:T(8,128)(2,1)S(1)} %collective-permute-done.3.rest_3_), channel_id=1, source_target_pairs={{0,8},{8,0},{1,9},{9,1},{2,10},{10,2},{3,11},{11,3},{4,12},{12,4},... | collective-permute-start | bytes 688136 | tf_op jit(solution)/shard_map/ppermute | solution.py:32
  50.2 130.2 %all-reduce.2.cloned.1.call-start = ((), (), s32[]{:S(2)}) async-start(), calls=%async_computation.2 | async-start | bytes 7340032 | tf_op jit(solution)/shard_map/psum | solution.py:385
  72.1 3.0 %collective-permute-start.8 = (bf16[512,896]{1,0:T(8,128)(2,1)}, bf16[512,896]{1,0:T(8,128)(2,1)S(1)}, u32[]{:S(2)}, u32[]{:S(2)}) collective-permute-start(bf16[512,896]{1,0:T(8,128)(2,1)} %get-tuple-element.52), channel_id=1, source_target_pairs={{0,8},{8,0},{1,9},{9,1},{2,10},{10,2},{3,11},{11,3},{4,12},{12,4},... | collective-permute-start | bytes 2752520 | tf_op jit(solution)/shard_map/ppermute | solution.py:32
  75.1 2.1 %copy-start.2 = (bf16[896,2048]{1,0:T(8,128)(2,1)S(1)}, bf16[896,2048]{1,0:T(8,128)(2,1)}, u32[]{:S(2)}) copy-start(bf16[896,2048]{1,0:T(8,128)(2,1)} %reshape.46.weight_hbm.weight_ref) | copy-start | bytes 11010052
  77.2 2.2 %copy-start.4 = (bf16[1024,2048]{1,0:T(8,128)(2,1)S(1)}, bf16[1024,2048]{1,0:T(8,128)(2,1)}, u32[]{:S(2)}) copy-start(bf16[1024,2048]{1,0:T(8,128)(2,1)} %get-tuple-element.51.pairs_ref) | copy-start | bytes 12582916
  81.8 8.7 %collective-permute-start.10 = (bf16[128,896]{1,0:T(8,128)(2,1)S(1)}, bf16[128,896]{1,0:T(8,128)(2,1)S(1)}, u32[]{:S(2)}, u32[]{:S(2)}) collective-permute-start(bf16[128,896]{1,0:T(8,128)(2,1)S(1)} %get-tuple-element.55), channel_id=1, source_target_pairs={{0,32},{16,48},{32,0},{48,16},{1,33},{17,49},{33,1},{49,17},{2,34}... | collective-permute-start | bytes 688136 | tf_op jit(solution)/shard_map/ppermute | solution.py:28
  82.2 11.4 %collective-permute-start.11 = (bf16[128,896]{1,0:T(8,128)(2,1)S(1)}, bf16[128,896]{1,0:T(8,128)(2,1)S(1)}, u32[]{:S(2)}, u32[]{:S(2)}) collective-permute-start(bf16[128,896]{1,0:T(8,128)(2,1)S(1)} %get-tuple-element.56), channel_id=1, source_target_pairs={{0,48},{16,0},{32,16},{48,32},{1,49},{17,1},{33,17},{49,33},{2,50}... | collective-permute-start | bytes 688136 | tf_op jit(solution)/shard_map/ppermute | solution.py:28
  83.2 12.7 %collective-permute-start.9 = (bf16[128,896]{1,0:T(8,128)(2,1)S(1)}, bf16[128,896]{1,0:T(8,128)(2,1)S(1)}, u32[]{:S(2)}, u32[]{:S(2)}) collective-permute-start(bf16[128,896]{1,0:T(8,128)(2,1)S(1)} %get-tuple-element.54), channel_id=1, source_target_pairs={{0,16},{16,32},{32,48},{48,0},{1,17},{17,33},{33,49},{49,1},{2,18}... | collective-permute-start | bytes 688136 | tf_op jit(solution)/shard_map/ppermute | solution.py:28
  100.7 19.7 %all-to-all-start = ((bf16[8,128,512]{2,1,0:T(8,128)(2,1)}), bf16[8,128,512]{2,1,0:T(8,128)(2,1)}, u32[]{:S(2)}, u32[]{:S(2)}) async-start(bf16[8,128,512]{2,1,0:T(8,128)(2,1)} %shard_map.131.parts_ref), calls=%async_computation | async-start | bytes 2097152 | tf_op jit(solution)/shard_map/all_to_all | solution.py:394
  123.9 28.9 %all-to-all-start.1 = ((bf16[128,8,512]{2,1,0:T(8,128)(2,1)}), bf16[128,8,512]{2,1,0:T(8,128)(2,1)}, u32[]{:S(2)}, u32[]{:S(2)}) async-start(bf16[128,8,512]{2,1,0:T(8,128)(2,1)} %fusion.1), calls=%async_computation.1 | async-start | bytes 2097152 | tf_op jit(solution)/shard_map/all_to_all | solution.py:397
  132.5 2.4 %copy-start.1 = (bf16[896,2688]{1,0:T(8,128)(2,1)S(1)}, bf16[896,2688]{1,0:T(8,128)(2,1)}, u32[]{:S(2)}) copy-start(bf16[896,2688]{1,0:T(8,128)(2,1)} %project_ref.3) | copy-start | bytes 14450692
  137.8 17.6 %collective-permute-start.12 = (bf16[128,896]{1,0:T(8,128)(2,1)S(1)}, bf16[128,896]{1,0:T(8,128)(2,1)S(1)}, u32[]{:S(2)}, u32[]{:S(2)}) collective-permute-start(bf16[128,896]{1,0:T(8,128)(2,1)S(1)} %shard_map.132), channel_id=1, source_target_pairs={{0,0},{1,8},{2,16},{3,24},{4,32},{5,40},{6,48},{7,56},{8,1},{9,9},... | collective-permute-start | bytes 688136 | tf_op jit(solution)/shard_map/ppermute | solution.py:37
Sparse Core Ops, SparseCore 0:
  50.4 31.4 all-gather.1
Sparse Core Ops, SparseCore 1:
  72.5 107.9 all-reduce.1

commit v9 on v7

--- a/solution.py
+++ b/solution.py
@@ -23,18 +23,22 @@
 PARTS = 8
 
 
-def turned(axis, length, by):
-    pairs = [(i, (i + by) % length) for i in range(length)]
-    return lambda x: lax.ppermute(x, axis, pairs)
-
-
 def across(x):
     return lax.ppermute(x, "c", [(0, 1), (1, 0)])
 
 
-def flipped(x):
-    pairs = [(t * 8 + s, s * 8 + t) for t in range(8) for s in range(8)]
-    return lax.ppermute(x, ("y", "c", "xl", "z"), pairs)
+def routes(step):
+    return [
+        (t * 8 + s, ((s // 2 - step) % 4 * 2 + s % 2) * 8 + t) for t in range(8) for s in range(8)
+    ]
+
+
+def sent(x, step):
+    return lax.ppermute(x, ("y", "c", "xl", "z"), routes(step))
+
+
+def sent_back(x, step):
+    return lax.ppermute(x, ("y", "c", "xl", "z"), [(b, a) for a, b in routes(step)])
 
 
 def dot(a, b, contract):
@@ -258,11 +262,10 @@
     )(summed)
 
 
-def near_kernel(pairs_ref, weight_ref, brought_ref, own_ref, *outs):
+def near_kernel(pairs_ref, weight_ref, brought_ref, *outs):
     total = nt(pairs_ref[...], weight_ref[...]) + brought_ref[...].astype(f32)
-    own_ref[...] = total[:TOK]
     for n, out in enumerate(outs):
-        out[...] = total[(n + 1) * TOK : (n + 2) * TOK].astype(bf16)
+        out[...] = total[n * TOK : (n + 1) * TOK].astype(bf16)
 
 
 def near_sums(pairs, weight, brought):
@@ -275,7 +278,7 @@
         grid=(1,),
         in_specs=[whole(4 * TOK, inner), whole(ENC, inner), whole(4 * TOK, ENC)],
         out_specs=[whole(TOK, ENC)] * 4,
-        out_shape=[jax.ShapeDtypeStruct((TOK, ENC), f32)] + [jax.ShapeDtypeStruct((TOK, ENC), bf16)] * 3,
+        out_shape=[jax.ShapeDtypeStruct((TOK, ENC), bf16)] * 4,
         compiler_params=params(32, 1),
         cost_estimate=cost(10**4, 10**4),
     )(pairs, weight, brought)
@@ -357,12 +360,14 @@
     gain = encoder_gain.reshape(1, ENC)
     y, core = lax.axis_index("y"), lax.axis_index("c")
     inner = cross_pairs.shape[2]
+    inner = cross_pairs.shape[2]
+    x = neighbour_inputs[0]
     heads = inner // HS
     weight = cross_pairs.reshape(ENC, 2, heads, HS).swapaxes(1, 2).reshape(ENC, 2 * inner)
-    x, weight = lax.optimization_barrier((flipped(neighbour_inputs[0]), weight))
     encoded, normed, projected, mixed = encode(x, gain, encoder_project, encoder_mix)
 
-    column = [encoded] + [turned("y", 4, -step)(encoded) for step in range(1, 4)]
+    column = [sent(encoded, step) for step in range(4)]
+    column[3], weight = lax.optimization_barrier((column[3], weight))
     sources = column + [across(one) for one in column]
     operands, sources = lax.optimization_barrier((spread(normed, mixed), sources))
     operands = lax.all_gather(operands, TP, tiled=True)
@@ -375,9 +380,10 @@
     summed = lax.psum(grad_weight, PLANE)
 
     brought = across(far)
-    total, *others = near_sums(grad_pairs, weight, brought)
-    for step, other in enumerate(others):
-        total += turned("y", 4, step + 1)(other).astype(f32)
+    total = sum(
+        sent_back(one, step).astype(f32)
+        for step, one in enumerate(near_sums(grad_pairs, weight, brought))
+    )
     grad_encoded = total.astype(bf16)
 
     parts = backward(grad_encoded, projected, encoder_mix)
@@ -388,7 +394,7 @@
     arrived = arrived.reshape(2, 8, 8, 8, LANES).sum(axis=(0, 2))
     rows = jnp.swapaxes(arrived, 0, 1).reshape(8, 8 * LANES)[:7]
     grad_project, grad_mix = rows[:, : 3 * ENC], rows[:, 6 * LANES : 6 * LANES + ENC]
-    grad_inputs = flipped(inputs_grad(x, gain, encoder_project, parts, grad_encoded))[None]
+    grad_inputs = inputs_grad(x, gain, encoder_project, parts, grad_encoded)[None]
     summed, grad_project, grad_mix, grad_inputs = lax.optimization_barrier(
         (summed, grad_project, grad_mix, grad_inputs)
     )

time: 192 us -> 214 us (1.11)
  waiting for transfers between devices: 70.5 us -> 88.9 us
  local copies, waits for them, and re-layouts: 18.5 us -> 21 us
    ppermute x8, waiting for transfers between devices: 18.7 us -> 34.4 us  [the longest x4 25.4 us: sent_back(): lax.ppermute(x, ('y', 'c', 'xl', 'z'), [(b, a) for a, b in routes(step)])]
    ppermute x8, starting transfers between devices: 19.7 us -> 25.3 us  [the longest x4 13.4 us: sent(): return lax.ppermute(x, ('y', 'c', 'xl', 'z'), routes(step))]
    ppermute x5, starting transfers between devices: 7.13 us -> 1.56 us  [across(): return lax.ppermute(x, 'c', [(0, 1), (1, 0)])]
    all_to_all x1, waiting for transfers between devices: 11.3 us -> 15.3 us  [shards(): arrived = lax.all_to_all(encoder_grad, FINE, 0, 0, tiled=True).astype(f32)]
    unnamed x24 -> x35, local copies, waits for them, and re-layouts: 9.91 us -> 11.8 us
  transfers between devices with their start and end apart: 17 -> 17, of which waited for: 9 -> 8; matrix products, arithmetic and copies ran while one was open for 9% -> 7% of each run, Pallas kernels for 16% -> 15%
where the time goes in v9:
time: 214 us; the launch traced here: 213 us
  waiting for transfers between devices  88.9 us (42%)
  starting transfers between devices  41.6 us (19%)
  Pallas kernels  39.2 us (18%)
  local copies, waits for them, and re-layouts  21 us (10%)
  between operations  15.7 us (7%)
  matrix products  3.52 us (2%)
  other arithmetic  3.24 us (2%)
    psum x1, waiting for transfers between devices, shards(): summed = lax.psum(grad_weight, PLANE)  26.2 us
    ppermute x4, waiting for transfers between devices, sent_back(): lax.ppermute(x, ('y', 'c', 'xl', 'z'), [(b, a) for a, b in routes(step)])  25.4 us
    pallas_call x1, Pallas kernels, cross(): pl.pallas_call(functools.partial(cross_kernel, inner // HS), grid_spec=pl...  19.5 us
    all_to_all x1, waiting for transfers between devices, shards(): arrived = lax.all_to_all(encoder_grad, FINE, 0, 0, tiled=True).astype(f32)  15.3 us
    ppermute x4, starting transfers between devices, sent(): return lax.ppermute(x, ('y', 'c', 'xl', 'z'), routes(step))  13.4 us
    ppermute x4, starting transfers between devices, sent_back(): lax.ppermute(x, ('y', 'c', 'xl', 'z'), [(b, a) for a, b in routes(step)])  11.9 us
    unnamed x35, local copies, waits for them, and re-layouts  11.8 us
    all_to_all x1, waiting for transfers between devices, shards(): lax.all_to_all(parts, TP, 0, 0, tiled=True).reshape(8 * TOK, LANES)  10.5 us
  transfers between devices with their start and end apart: 17, of which 8 were waited for; matrix products, arithmetic and copies ran while one was open for 7% of the time, Pallas kernels for 15%

profile of v9, /device:TPU:1, one launch (start us, length us, event | category | flops | bytes accessed | tf_op | source)
XLA Modules:
  0.0 213.1 jit_solution(13777324908077968877)
XLA Ops:
  8.0 0.0 all-gather.2.cloned.1.call-start
  8.0 0.7 reshape.45.gain_ref
  8.7 2.4 %copy-done = bf16[896,2688]{1,0:T(8,128)(2,1)S(1)} copy-done((bf16[896,2688]{1,0:T(8,128)(2,1)S(1)}, bf16[896,2688]{1,0:T(8,128)(2,1)}, u32[]{:S(2)}) %copy-start) | copy-done | bytes 4816920
  11.1 1.4 copy-done.3
  12.5 0.9 copy-done.6
  13.5 3.0 %shard_map.127 = (bf16[128,896]{1,0:T(8,128)(2,1)S(1)}, bf16[128,896]{1,0:T(8,128)(2,1)S(1)}, bf16[128,2688]{1,0:T(8,128)(2,1)S(1)}, bf16[128,896]{1,0:T(8,128)(2,1)S(1)}) custom-call(bf16[128,896]{1,0:T(8,128)(2,1)S(1)} %bitcast.22, f32[1,896]{1,0:T(1,128)S(1)} %reshape.45.gain_ref, bf16[896,2688]{1,0:T(8,128)(2,1)S(1)} %copy-done, ...), custom_call_target="tpu_custom_call" | custom-call | flops 1000000000 | bytes 8000000 | tf_op jit(solution)/shard_map/pallas_call | solution.py:110
  16.5 4.1 %collective-permute-start = (bf16[128,896]{1,0:T(8,128)(2,1)S(1)}, bf16[128,896]{1,0:T(8,128)(2,1)S(1)}, u32[]{:S(2)}, u32[]{:S(2)}) collective-permute-start(bf16[128,896]{1,0:T(8,128)(2,1)S(1)} %get-tuple-element.34), channel_id=1, source_target_pairs={{0,16},{1,24},{2,32},{3,40},{4,48},{5,56},{6,0},{7,8},{8,17},{9,25... | collective-permute-start | bytes 688136 | tf_op jit(solution)/shard_map/ppermute | solution.py:37
  20.6 1.9 collective-permute-start.1
  22.5 4.4 %collective-permute-start.2 = (bf16[128,896]{1,0:T(8,128)(2,1)S(1)}, bf16[128,896]{1,0:T(8,128)(2,1)S(1)}, u32[]{:S(2)}, u32[]{:S(2)}) collective-permute-start(bf16[128,896]{1,0:T(8,128)(2,1)S(1)} %get-tuple-element.34), channel_id=1, source_target_pairs={{0,48},{1,56},{2,0},{3,8},{4,16},{5,24},{6,32},{7,40},{8,49},{9,57... | collective-permute-start | bytes 688136 | tf_op jit(solution)/shard_map/ppermute | solution.py:37
  27.0 3.0 %collective-permute-start.3 = (bf16[128,896]{1,0:T(8,128)(2,1)S(1)}, bf16[128,896]{1,0:T(8,128)(2,1)S(1)}, u32[]{:S(2)}, u32[]{:S(2)}) collective-permute-start(bf16[128,896]{1,0:T(8,128)(2,1)S(1)} %get-tuple-element.34), channel_id=1, source_target_pairs={{0,32},{1,40},{2,48},{3,56},{4,0},{5,8},{6,16},{7,24},{8,33},{9,41... | collective-permute-start | bytes 688136 | tf_op jit(solution)/shard_map/ppermute | solution.py:37
  29.9 7.2 %reshape.47.weight_ref = bf16[896,2048]{1,0:T(8,128)(2,1)} reshape(bf16[896,8,2,128]{3,2,1,0:T(2,128)(2,1)} %bitcast.26) | data formatting | bytes 7340032 | tf_op jit(solution)/shard_map/reshape | solution.py:366
  37.1 0.1 collective-permute-start.7
  37.2 0.5 collective-permute-start.4
  37.7 4.5 %collective-permute-done.2.rest_1_ = bf16[128,896]{1,0:T(8,128)(2,1)S(1)} collective-permute-done((bf16[128,896]{1,0:T(8,128)(2,1)S(1)}, bf16[128,896]{1,0:T(8,128)(2,1)S(1)}, u32[]{:S(2)}, u32[]{:S(2)}) %collective-permute-start.2) | collective-permute-done | bytes 229408 | tf_op jit(solution)/shard_map/ppermute | solution.py:37
  42.2 0.5 collective-permute-start.5
  42.7 4.6 %collective-permute-done.3.rest_2_ = bf16[128,896]{1,0:T(8,128)(2,1)S(1)} collective-permute-done((bf16[128,896]{1,0:T(8,128)(2,1)S(1)}, bf16[128,896]{1,0:T(8,128)(2,1)S(1)}, u32[]{:S(2)}, u32[]{:S(2)}) %collective-permute-start.3) | collective-permute-done | bytes 229408 | tf_op jit(solution)/shard_map/ppermute | solution.py:37
  47.3 1.7 shard_map.128
  49.1 0.2 all-reduce.2.cloned.1.call-start
  49.3 0.1 copy.20
  49.4 0.1 reshape.44
  49.5 0.5 fusion.2.slots_ref
  50.1 19.5 %shard_map.129 = (bf16[4,64,1024]{2,1,0:T(8,128)(2,1)}, bf16[4,64,1024]{2,1,0:T(8,128)(2,1)}, bf16[1024,2048]{1,0:T(8,128)(2,1)}, bf16[896,2048]{1,0:T(8,128)(2,1)}, bf16[512,896]{1,0:T(8,128)(2,1)}) custom-call(s32[8]{0:T(128)} %fusion.2.slots_ref, bf16[4,64,1024]{2,1,0:T(8,128)(2,1)} %q_ref.1, bf16[4,64,1024]{2,1,0:T(8,128)(2,1)} %up_ref.1, ...), custom_call_target="tpu_custom_call" | custom-call | flops 16000000000 | bytes 16000000 | tf_op jit(solution)/shard_map/pallas_call | solution.py:193
  69.6 0.5 collective-permute-start.8
  70.1 2.3 %collective-permute-done.8.brought_ref = bf16[512,896]{1,0:T(8,128)(2,1)S(1)} collective-permute-done((bf16[512,896]{1,0:T(8,128)(2,1)}, bf16[512,896]{1,0:T(8,128)(2,1)S(1)}, u32[]{:S(2)}, u32[]{:S(2)}) %collective-permute-start.8) | collective-permute-done | bytes 917536 | tf_op jit(solution)/shard_map/ppermute | solution.py:27
  72.4 2.1 copy-done.2
  74.6 2.3 %copy-done.5 = bf16[1024,2048]{1,0:T(8,128)(2,1)S(1)} copy-done((bf16[1024,2048]{1,0:T(8,128)(2,1)S(1)}, bf16[1024,2048]{1,0:T(8,128)(2,1)}, u32[]{:S(2)}) %copy-start.5) | copy-done | bytes 4194328
  76.8 2.4 %shard_map.130 = (bf16[128,896]{1,0:T(8,128)(2,1)S(1)}, bf16[128,896]{1,0:T(8,128)(2,1)S(1)}, bf16[128,896]{1,0:T(8,128)(2,1)S(1)}, bf16[128,896]{1,0:T(8,128)(2,1)S(1)}) custom-call(bf16[1024,2048]{1,0:T(8,128)(2,1)S(1)} %copy-done.5, bf16[896,2048]{1,0:T(8,128)(2,1)S(1)} %copy-done.2, bf16[512,896]{1,0:T(8,128)(2,1)S(1)} %collective-permute-done.8.brought_ref), custom_call_target="tpu_custom_call" | custom-call | flops 10000 | bytes 10000 | tf_op jit(solution)/shard_map/pallas_call | solution.py:276
  79.2 6.4 %collective-permute-start.10 = (bf16[128,896]{1,0:T(8,128)(2,1)S(1)}, bf16[128,896]{1,0:T(8,128)(2,1)S(1)}, u32[]{:S(2)}, u32[]{:S(2)}) collective-permute-start(bf16[128,896]{1,0:T(8,128)(2,1)S(1)} %get-tuple-element.54), channel_id=1, source_target_pairs={{48,0},{56,1},{0,2},{8,3},{16,4},{24,5},{32,6},{40,7},{49,8},{57,9... | collective-permute-start | bytes 688136 | tf_op jit(solution)/shard_map/ppermute | solution.py:41
  85.6 0.7 collective-permute-start.11
  86.4 2.0 collective-permute-start.12
  88.4 2.6 %collective-permute-start.9 = (bf16[128,896]{1,0:T(8,128)(2,1)S(1)}, bf16[128,896]{1,0:T(8,128)(2,1)S(1)}, u32[]{:S(2)}, u32[]{:S(2)}) collective-permute-start(bf16[128,896]{1,0:T(8,128)(2,1)S(1)} %get-tuple-element.53), channel_id=1, source_target_pairs={{0,0},{8,1},{16,2},{24,3},{32,4},{40,5},{48,6},{56,7},{1,8},{9,9},... | collective-permute-start | bytes 688136 | tf_op jit(solution)/shard_map/ppermute | solution.py:41
  91.1 17.6 %collective-permute-done.10 = bf16[128,896]{1,0:T(8,128)(2,1)S(1)} collective-permute-done((bf16[128,896]{1,0:T(8,128)(2,1)S(1)}, bf16[128,896]{1,0:T(8,128)(2,1)S(1)}, u32[]{:S(2)}, u32[]{:S(2)}) %collective-permute-start.10) | collective-permute-done | bytes 229408 | tf_op jit(solution)/shard_map/ppermute | solution.py:41
  108.7 7.8 %collective-permute-done.9 = bf16[128,896]{1,0:T(8,128)(2,1)S(1)} collective-permute-done((bf16[128,896]{1,0:T(8,128)(2,1)S(1)}, bf16[128,896]{1,0:T(8,128)(2,1)S(1)}, u32[]{:S(2)}, u32[]{:S(2)}) %collective-permute-start.9) | collective-permute-done | bytes 229408 | tf_op jit(solution)/shard_map/ppermute | solution.py:41
  116.5 0.1 add_convert_fusion.grad_ref
  116.6 4.6 %shard_map.131.parts_ref = bf16[8,128,512]{2,1,0:T(8,128)(2,1)} custom-call(bf16[128,896]{1,0:T(8,128)(2,1)S(1)} %add_convert_fusion.grad_ref, bf16[128,2688]{1,0:T(8,128)(2,1)S(1)} %get-tuple-element.57.projected_ref, bf16[896,896]{1,0:T(8,128)(2,1)S(1)} %copy-done.4), custom_call_target="tpu_custom_call" | custom-call | flops 10000 | bytes 10000 | tf_op jit(solution)/shard_map/pallas_call | solution.py:319
  121.3 4.2 %all-to-all-start = ((bf16[8,128,512]{2,1,0:T(8,128)(2,1)}), bf16[8,128,512]{2,1,0:T(8,128)(2,1)}, u32[]{:S(2)}, u32[]{:S(2)}) async-start(bf16[8,128,512]{2,1,0:T(8,128)(2,1)} %shard_map.131.parts_ref), calls=%async_computation | async-start | bytes 2097152 | tf_op jit(solution)/shard_map/all_to_all | solution.py:390
  125.5 2.4 %fusion = bf16[1024,1024]{0,1:T(8,128)(2,1)S(1)} fusion(bf16[1024,2048]{1,0:T(8,128)(2,1)} %all-gather.2.cloned.1.call-done, pred[]{:T(512)S(6)} %lt.20), kind=kLoop, calls=%fused_computation.1 | loop fusion | flops 1048576 | bytes 6291457 | tf_op jit(solution)/shard_map/transpose | solution.py:392
  127.9 10.5 %all-to-all-done = bf16[8,128,512]{2,1,0:T(8,128)(2,1)} async-done(((bf16[8,128,512]{2,1,0:T(8,128)(2,1)}), bf16[8,128,512]{2,1,0:T(8,128)(2,1)}, u32[]{:S(2)}, u32[]{:S(2)}) %all-to-all-start) | async-done | bytes 1048608 | tf_op jit(solution)/shard_map/all_to_all | solution.py:390
  138.5 3.5 %fusion.1 = bf16[128,8,512]{2,1,0:T(8,128)(2,1)} fusion(bf16[1024,1024]{0,1:T(8,128)(2,1)S(1)} %fusion, bf16[1024,512]{1,0:T(8,128)(2,1)} %bitcast.4), kind=kOutput, calls=%fused_computation.4 | convolution fusion | flops 1074266112 | bytes 4194304 | tf_op jit(solution)/shard_map/dot_general | solution.py:45
  142.0 10.3 %all-to-all-start.1 = ((bf16[128,8,512]{2,1,0:T(8,128)(2,1)}), bf16[128,8,512]{2,1,0:T(8,128)(2,1)S(1)}, u32[]{:S(2)}, u32[]{:S(2)}) async-start(bf16[128,8,512]{2,1,0:T(8,128)(2,1)} %fusion.1), calls=%async_computation.1 | async-start | bytes 2097152 | tf_op jit(solution)/shard_map/all_to_all | solution.py:393
  152.3 2.5 %copy-done.1 = bf16[896,2688]{1,0:T(8,128)(2,1)S(1)} copy-done((bf16[896,2688]{1,0:T(8,128)(2,1)S(1)}, bf16[896,2688]{1,0:T(8,128)(2,1)}, u32[]{:S(2)}) %copy-start.1) | copy-done | bytes 4816920
  154.8 3.7 %shard_map.132 = bf16[128,896]{1,0:T(8,128)(2,1)} custom-call(bf16[128,896]{1,0:T(8,128)(2,1)S(1)} %bitcast.23, f32[1,896]{1,0:T(1,128)S(1)} %reshape.45.gain_ref, bf16[896,2688]{1,0:T(8,128)(2,1)S(1)} %copy-done.1, bf16[8,128,512]{2,1,0:T(8,128)(2,1)} %shard_map.131.parts_ref, bf16[128,896]{1,0:T(8,128)(2,1)S(1)} %add_convert_fusion.grad_ref), custom_call_target="tpu_custom_call" | custom-call | flops 10000 | bytes 10000 | tf_op jit(solution)/shard_map/pallas_call | solution.py:342
  158.5 15.3 %all-to-all-done.1 = bf16[128,8,512]{2,1,0:T(8,128)(2,1)S(1)} async-done(((bf16[128,8,512]{2,1,0:T(8,128)(2,1)}), bf16[128,8,512]{2,1,0:T(8,128)(2,1)S(1)}, u32[]{:S(2)}, u32[]{:S(2)}) %all-to-all-start.1) | async-done | bytes 1048608 | tf_op jit(solution)/shard_map/all_to_all | solution.py:393
  173.8 0.1 convert_reduce_fusion
  173.9 0.6 slice.27
  174.5 0.6 slice.28
  175.2 26.2 %all-reduce.2.cloned.1.call-done.sum_ref = bf16[896,2048]{1,0:T(8,128)(2,1)} async-done(((bf16[896,2048]{1,0:T(8,128)(2,1)}), bf16[896,2048]{1,0:T(8,128)(2,1)}) %all-reduce.2.cloned.1.call-update) | async-done | bytes 3670032 | tf_op jit(solution)/shard_map/psum | solution.py:380
  201.3 4.3 %shard_map.133 = f32[14336,128]{1,0:T(8,128)} custom-call(bf16[896,2048]{1,0:T(8,128)(2,1)} %all-reduce.2.cloned.1.call-done.sum_ref), custom_call_target="tpu_custom_call" | custom-call | flops 1000000 | bytes 11000000 | tf_op jit(solution)/shard_map/pallas_call | solution.py:250
  (40 shorter events, 0.1 us)
Async XLA Ops:
  8.0 117.5 %all-gather.2.cloned.1.call-start = ((), (), s32[]{:S(2)}) async-start(), calls=%async_computation.3 | async-start | bytes 4718592 | tf_op jit(solution)/shard_map/all_gather | solution.py:373
  8.7 2.4 %copy-start = (bf16[896,2688]{1,0:T(8,128)(2,1)S(1)}, bf16[896,2688]{1,0:T(8,128)(2,1)}, u32[]{:S(2)}) copy-start(bf16[896,2688]{1,0:T(8,128)(2,1)} %project_ref.3) | copy-start | bytes 14450692
  11.1 1.4 copy-start.3
  12.5 0.9 copy-start.6
  16.5 20.6 %collective-permute-start = (bf16[128,896]{1,0:T(8,128)(2,1)S(1)}, bf16[128,896]{1,0:T(8,128)(2,1)S(1)}, u32[]{:S(2)}, u32[]{:S(2)}) collective-permute-start(bf16[128,896]{1,0:T(8,128)(2,1)S(1)} %get-tuple-element.34), channel_id=1, source_target_pairs={{0,16},{1,24},{2,32},{3,40},{4,48},{5,56},{6,0},{7,8},{8,17},{9,25... | collective-permute-start | bytes 688136 | tf_op jit(solution)/shard_map/ppermute | solution.py:37
  20.6 16.6 %collective-permute-start.1 = (bf16[128,896]{1,0:T(8,128)(2,1)S(1)}, bf16[128,896]{1,0:T(8,128)(2,1)S(1)}, u32[]{:S(2)}, u32[]{:S(2)}) collective-permute-start(bf16[128,896]{1,0:T(8,128)(2,1)S(1)} %get-tuple-element.34), channel_id=1, source_target_pairs={{0,0},{1,8},{2,16},{3,24},{4,32},{5,40},{6,48},{7,56},{8,1},{9,9},... | collective-permute-start | bytes 688136 | tf_op jit(solution)/shard_map/ppermute | solution.py:37
  22.5 19.7 %collective-permute-start.2 = (bf16[128,896]{1,0:T(8,128)(2,1)S(1)}, bf16[128,896]{1,0:T(8,128)(2,1)S(1)}, u32[]{:S(2)}, u32[]{:S(2)}) collective-permute-start(bf16[128,896]{1,0:T(8,128)(2,1)S(1)} %get-tuple-element.34), channel_id=1, source_target_pairs={{0,48},{1,56},{2,0},{3,8},{4,16},{5,24},{6,32},{7,40},{8,49},{9,57... | collective-permute-start | bytes 688136 | tf_op jit(solution)/shard_map/ppermute | solution.py:37
  27.0 20.3 %collective-permute-start.3 = (bf16[128,896]{1,0:T(8,128)(2,1)S(1)}, bf16[128,896]{1,0:T(8,128)(2,1)S(1)}, u32[]{:S(2)}, u32[]{:S(2)}) collective-permute-start(bf16[128,896]{1,0:T(8,128)(2,1)S(1)} %get-tuple-element.34), channel_id=1, source_target_pairs={{0,32},{1,40},{2,48},{3,56},{4,0},{5,8},{6,16},{7,24},{8,33},{9,41... | collective-permute-start | bytes 688136 | tf_op jit(solution)/shard_map/ppermute | solution.py:37
  37.1 12.2 %copy-start.8 = (s32[4,2]{0,1:T(2,128)S(1)}, s32[4,2]{0,1:T(2,128)}, u32[]{:S(2)}) copy-start(s32[4,2]{0,1:T(2,128)} %param.14) | copy-start | bytes 100
  37.1 12.9 %copy-start.9 = (bf16[128,896]{1,0:T(8,128)(2,1)}, bf16[128,896]{1,0:T(8,128)(2,1)S(1)}, u32[]{:S(2)}) copy-start(bf16[128,896]{1,0:T(8,128)(2,1)S(1)} %collective-permute-done.rest_3_) | copy-start | bytes 688132
  37.1 11.9 %collective-permute-start.7 = (bf16[128,896]{1,0:T(8,128)(2,1)S(1)}, bf16[128,896]{1,0:T(8,128)(2,1)S(1)}, u32[]{:S(2)}, u32[]{:S(2)}) collective-permute-start(bf16[128,896]{1,0:T(8,128)(2,1)S(1)} %collective-permute-done.rest_3_), channel_id=1, source_target_pairs={{0,8},{8,0},{1,9},{9,1},{2,10},{10,2},{3,11},{11,3},{4,12},{12,4},... | collective-permute-start | bytes 688136 | tf_op jit(solution)/shard_map/ppermute | solution.py:27
  37.2 12.8 %copy-start.10 = (bf16[128,896]{1,0:T(8,128)(2,1)}, bf16[128,896]{1,0:T(8,128)(2,1)S(1)}, u32[]{:S(2)}) copy-start(bf16[128,896]{1,0:T(8,128)(2,1)S(1)} %collective-permute-done.1.rest_0_) | copy-start | bytes 688132
  37.2 11.8 %collective-permute-start.4 = (bf16[128,896]{1,0:T(8,128)(2,1)S(1)}, bf16[128,896]{1,0:T(8,128)(2,1)S(1)}, u32[]{:S(2)}, u32[]{:S(2)}) collective-permute-start(bf16[128,896]{1,0:T(8,128)(2,1)S(1)} %collective-permute-done.1.rest_0_), channel_id=1, source_target_pairs={{0,8},{8,0},{1,9},{9,1},{2,10},{10,2},{3,11},{11,3},{4,12},{12,4},... | collective-permute-start | bytes 688136 | tf_op jit(solution)/shard_map/ppermute | solution.py:27
  42.2 7.8 %copy-start.11 = (bf16[128,896]{1,0:T(8,128)(2,1)}, bf16[128,896]{1,0:T(8,128)(2,1)S(1)}, u32[]{:S(2)}) copy-start(bf16[128,896]{1,0:T(8,128)(2,1)S(1)} %collective-permute-done.2.rest_1_) | copy-start | bytes 688132
  42.2 6.8 %collective-permute-start.5 = (bf16[128,896]{1,0:T(8,128)(2,1)S(1)}, bf16[128,896]{1,0:T(8,128)(2,1)S(1)}, u32[]{:S(2)}, u32[]{:S(2)}) collective-permute-start(bf16[128,896]{1,0:T(8,128)(2,1)S(1)} %collective-permute-done.2.rest_1_), channel_id=1, source_target_pairs={{0,8},{8,0},{1,9},{9,1},{2,10},{10,2},{3,11},{11,3},{4,12},{12,4},... | collective-permute-start | bytes 688136 | tf_op jit(solution)/shard_map/ppermute | solution.py:27
  47.3 2.8 %copy-start.12 = (bf16[128,896]{1,0:T(8,128)(2,1)}, bf16[128,896]{1,0:T(8,128)(2,1)S(1)}, u32[]{:S(2)}) copy-start(bf16[128,896]{1,0:T(8,128)(2,1)S(1)} %collective-permute-done.3.rest_2_) | copy-start | bytes 688132
  47.3 1.8 collective-permute-start.6
  49.0 1.1 copy-start.13
  49.0 1.1 copy-start.14
  49.0 1.1 copy-start.15
  49.0 1.0 copy-start.16
  49.1 152.3 %all-reduce.2.cloned.1.call-start = ((), (), s32[]{:S(2)}) async-start(), calls=%async_computation.2 | async-start | bytes 7340032 | tf_op jit(solution)/shard_map/psum | solution.py:380
  69.6 2.9 %collective-permute-start.8 = (bf16[512,896]{1,0:T(8,128)(2,1)}, bf16[512,896]{1,0:T(8,128)(2,1)S(1)}, u32[]{:S(2)}, u32[]{:S(2)}) collective-permute-start(bf16[512,896]{1,0:T(8,128)(2,1)} %get-tuple-element.52), channel_id=1, source_target_pairs={{0,8},{8,0},{1,9},{9,1},{2,10},{10,2},{3,11},{11,3},{4,12},{12,4},... | collective-permute-start | bytes 2752520 | tf_op jit(solution)/shard_map/ppermute | solution.py:27
  72.4 2.1 copy-start.2
  74.6 2.3 %copy-start.5 = (bf16[1024,2048]{1,0:T(8,128)(2,1)S(1)}, bf16[1024,2048]{1,0:T(8,128)(2,1)}, u32[]{:S(2)}) copy-start(bf16[1024,2048]{1,0:T(8,128)(2,1)} %get-tuple-element.51.pairs_ref) | copy-start | bytes 12582916
  76.8 39.8 %copy-start.4 = (bf16[896,896]{1,0:T(8,128)(2,1)S(1)}, bf16[896,896]{1,0:T(8,128)(2,1)}, u32[]{:S(2)}) copy-start(bf16[896,896]{1,0:T(8,128)(2,1)} %mix_ref.3) | copy-start | bytes 4816900
  79.2 29.5 %collective-permute-start.10 = (bf16[128,896]{1,0:T(8,128)(2,1)S(1)}, bf16[128,896]{1,0:T(8,128)(2,1)S(1)}, u32[]{:S(2)}, u32[]{:S(2)}) collective-permute-start(bf16[128,896]{1,0:T(8,128)(2,1)S(1)} %get-tuple-element.54), channel_id=1, source_target_pairs={{48,0},{56,1},{0,2},{8,3},{16,4},{24,5},{32,6},{40,7},{49,8},{57,9... | collective-permute-start | bytes 688136 | tf_op jit(solution)/shard_map/ppermute | solution.py:41
  85.6 23.1 %collective-permute-start.11 = (bf16[128,896]{1,0:T(8,128)(2,1)S(1)}, bf16[128,896]{1,0:T(8,128)(2,1)S(1)}, u32[]{:S(2)}, u32[]{:S(2)}) collective-permute-start(bf16[128,896]{1,0:T(8,128)(2,1)S(1)} %get-tuple-element.55), channel_id=1, source_target_pairs={{32,0},{40,1},{48,2},{56,3},{0,4},{8,5},{16,6},{24,7},{33,8},{41,9... | collective-permute-start | bytes 688136 | tf_op jit(solution)/shard_map/ppermute | solution.py:41
  86.4 22.3 %collective-permute-start.12 = (bf16[128,896]{1,0:T(8,128)(2,1)S(1)}, bf16[128,896]{1,0:T(8,128)(2,1)S(1)}, u32[]{:S(2)}, u32[]{:S(2)}) collective-permute-start(bf16[128,896]{1,0:T(8,128)(2,1)S(1)} %get-tuple-element.56), channel_id=1, source_target_pairs={{16,0},{24,1},{32,2},{40,3},{48,4},{56,5},{0,6},{8,7},{17,8},{25,9... | collective-permute-start | bytes 688136 | tf_op jit(solution)/shard_map/ppermute | solution.py:41
  88.4 28.1 %collective-permute-start.9 = (bf16[128,896]{1,0:T(8,128)(2,1)S(1)}, bf16[128,896]{1,0:T(8,128)(2,1)S(1)}, u32[]{:S(2)}, u32[]{:S(2)}) collective-permute-start(bf16[128,896]{1,0:T(8,128)(2,1)S(1)} %get-tuple-element.53), channel_id=1, source_target_pairs={{0,0},{8,1},{16,2},{24,3},{32,4},{40,5},{48,6},{56,7},{1,8},{9,9},... | collective-permute-start | bytes 688136 | tf_op jit(solution)/shard_map/ppermute | solution.py:41
  121.3 17.2 %all-to-all-start = ((bf16[8,128,512]{2,1,0:T(8,128)(2,1)}), bf16[8,128,512]{2,1,0:T(8,128)(2,1)}, u32[]{:S(2)}, u32[]{:S(2)}) async-start(bf16[8,128,512]{2,1,0:T(8,128)(2,1)} %shard_map.131.parts_ref), calls=%async_computation | async-start | bytes 2097152 | tf_op jit(solution)/shard_map/all_to_all | solution.py:390
  142.0 10.3 %copy-start.7 = (bf16[1,128,896]{2,1,0:T(8,128)(2,1)S(1)}, bf16[1,128,896]{2,1,0:T(8,128)(2,1)}, u32[]{:S(2)}) copy-start(bf16[1,128,896]{2,1,0:T(8,128)(2,1)} %param.8) | copy-start | bytes 688132
  142.0 31.8 %all-to-all-start.1 = ((bf16[128,8,512]{2,1,0:T(8,128)(2,1)}), bf16[128,8,512]{2,1,0:T(8,128)(2,1)S(1)}, u32[]{:S(2)}, u32[]{:S(2)}) async-start(bf16[128,8,512]{2,1,0:T(8,128)(2,1)} %fusion.1), calls=%async_computation.1 | async-start | bytes 2097152 | tf_op jit(solution)/shard_map/all_to_all | solution.py:393
  152.3 2.5 %copy-start.1 = (bf16[896,2688]{1,0:T(8,128)(2,1)S(1)}, bf16[896,2688]{1,0:T(8,128)(2,1)}, u32[]{:S(2)}) copy-start(bf16[896,2688]{1,0:T(8,128)(2,1)} %project_ref.3) | copy-start | bytes 14450692
Sparse Core Ops, SparseCore 0:
  49.2 34.9 all-gather.1
Sparse Core Ops, SparseCore 1:
  70.2 131.1 all-reduce.1
